TPU v7x, 32 devices: a whole 2x2x4 slice. The times are simulated.
32 devices in a mesh: replica: 4 (over y, x), fsdp: 8 (over z, core).
Axes of the slice: x: 2, y: 2, z: 4, core: 2. Of those that a mesh axis runs over, the one named last changes fastest.
Arguments:
- tokens: bfloat16 [8192, 2048], P(('replica', 'fsdp')), may hold values from -6 to 6
- cotangent: bfloat16 [8192, 2048], P(('replica', 'fsdp')), may hold values from -6 to 6
- segment_ids: int32 [32, 256], P(('replica', 'fsdp')), may hold values from 0 to 7, never falling along the last dimension, each value on 1 to 128 neighbouring positions
- expert_index: int32 [8192, 8], P(('replica', 'fsdp')), may hold values from 0 to 15, all different within a row; in each aligned block of 256 rows (0 to 255, 256 to 511, ...) at most 144 rows name the same one
- clip_threshold: int32 [16], replicated, may hold values from 2 to 11
- attn_norm_gain: bfloat16 [2048], replicated, may hold values from 0.5 to 1.5
- w_query: bfloat16 [2048, 2048], P('fsdp'), may hold values from -0.125 to 0.125
- w_key: bfloat16 [2048, 2048], P('fsdp'), may hold values from -0.125 to 0.125
- w_value: bfloat16 [2048, 2048], P('fsdp'), may hold values from -0.125 to 0.125
- w_output: bfloat16 [2048, 2048], P('fsdp'), may hold values from -0.5 to 0.5
- query_gain: bfloat16 [128], replicated, may hold values from 0.5 to 1.5
- key_gain: bfloat16 [128], replicated, may hold values from 0.5 to 1.5
- ffn_norm_gain: bfloat16 [2048], replicated, may hold values from 0.5 to 1.5
- router: bfloat16 [2048, 16], P('fsdp'), may hold values from -0.0625 to 0.0625
- expert_in: bfloat16 [16, 2048, 2048], P('fsdp'), may hold values from -0.125 to 0.125
- expert_out: bfloat16 [16, 1024, 2048], P('fsdp'), may hold values from -0.75 to 0.75
Outputs:
- output: bfloat16 [8192, 2048], P(('replica', 'fsdp'))
- input_grad: bfloat16 [8192, 2048], P(('replica', 'fsdp'))
- attn_norm_gain_grad: float32 [2048], replicated
- w_query_grad: float32 [2048, 2048], P('fsdp')
- w_key_grad: float32 [2048, 2048], P('fsdp')
- w_value_grad: float32 [2048, 2048], P('fsdp')
- w_output_grad: float32 [2048, 2048], P('fsdp')
- query_gain_grad: float32 [128], replicated
- key_gain_grad: float32 [128], replicated
- ffn_norm_gain_grad: float32 [2048], replicated
- router_grad: float32 [2048, 16], P('fsdp')
- expert_in_grad: float32 [16, 2048, 2048], P('fsdp', 'replica')
- expert_out_grad: float32 [16, 1024, 2048], P('fsdp', 'replica')
- head_max: float32 [16], replicated
- clipped_query: bfloat16 [2048, 2048], P('fsdp')
- clipped_key: bfloat16 [2048, 2048], P('fsdp')
Inputs may be any that keep to these rules, and one draw needn't show every extreme that they name: `segment_ids`: within each row the ids never fall; each id covers 1 to 128 positions, one exactly that many. `expert_index`: each row names 8 different experts; among the 256 rows of one sequence no expert is named more than 144 times, a bound that some block reaches.
All inputs are finite; a program needn't handle non-finite values.
Results may differ from a plain program's by a relative error of at most 0.023.
Values may be sent and summed in bfloat16 or wider, within the bound.
No kernel may reach another device: no remote copies, remote signals or barrier semaphores. Data moves between devices by JAX's collectives and lax.ppermute only.
A program may use at most 320 MiB of HBM per device.

v0:
```python
import jax
import jax.numpy as jnp
from jax import lax
from jax.sharding import PartitionSpec as P

H = 16
HD = 128
FF = 1024
TOPK = 8
EXPERTS = 16
CAP = 144


epsilon = 1e-06
rope_base = 10000.0


def rms_norm(values, gain):
    return values * lax.rsqrt(jnp.mean(values * values, axis=-1, keepdims=True) + epsilon) * gain


def rope_tables(length, width):
    places = jnp.arange(length, dtype=jnp.float32)
    rates = rope_base ** (-jnp.arange(width // 2, dtype=jnp.float32) * 2.0 / width)
    angle = places[:, None] * rates[None, :]
    return (jnp.cos(angle)[:, None, :], jnp.sin(angle)[:, None, :])


def rotate(values, cosine, sine):
    half = values.shape[-1] // 2
    first = values[..., :half]
    second = values[..., half:]
    return jnp.concatenate(
        [first * cosine - second * sine, second * cosine + first * sine], axis=-1
    )


def head_prep(heads, gain, cosine, sine):
    return rotate(rms_norm(heads, gain), cosine, sine)


def outer_sum(left, right):
    return jnp.einsum("sd,se->de", left, right, preferred_element_type=jnp.float32)


def times_transposed(left, right):
    return jnp.einsum("se,de->sd", left, right, preferred_element_type=jnp.float32)


def local(
    tokens,
    cotangent,
    segment_ids,
    expert_index,
    clip_threshold,
    attn_norm_gain,
    w_query,
    w_key,
    w_value,
    w_output,
    query_gain,
    key_gain,
    ffn_norm_gain,
    router,
    expert_in,
    expert_out,
):
    groups = lax.axis_size("fsdp")
    length, width = tokens.shape
    scale = HD ** (-0.5)
    inputs = tokens.astype(jnp.float32)
    attn_gain = attn_norm_gain.astype(jnp.float32)
    ffn_gain = ffn_norm_gain.astype(jnp.float32)
    gain_query = query_gain.astype(jnp.float32)
    gain_key = key_gain.astype(jnp.float32)
    full_query, full_key, full_value, full_output, full_router = (
        lax.all_gather(w_query, "fsdp", axis=0, tiled=True),
        lax.all_gather(w_key, "fsdp", axis=0, tiled=True),
        lax.all_gather(w_value, "fsdp", axis=0, tiled=True),
        lax.all_gather(w_output, "fsdp", axis=0, tiled=True),
        lax.all_gather(router, "fsdp", axis=0, tiled=True),
    )
    normed = rms_norm(inputs, attn_gain).astype(jnp.bfloat16)
    query_raw = jnp.dot(normed, full_query, preferred_element_type=jnp.float32).reshape(
        length, H, HD
    )
    key_raw = jnp.dot(normed, full_key, preferred_element_type=jnp.float32).reshape(length, H, HD)
    value = (
        jnp.dot(normed, full_value, preferred_element_type=jnp.float32)
        .astype(jnp.bfloat16)
        .reshape(length, H, HD)
    )
    cosine, sine = rope_tables(length, HD)
    query_rot = head_prep(query_raw, gain_query, cosine, sine).astype(jnp.bfloat16)
    key_rot = head_prep(key_raw, gain_key, cosine, sine).astype(jnp.bfloat16)
    segment = segment_ids[0]
    allowed = (segment[:, None] == segment[None, :])[None]
    scores = (
        jnp.einsum("shd,thd->hst", query_rot, key_rot, preferred_element_type=jnp.float32) * scale
    )
    masked = jnp.where(allowed, scores, -jnp.inf)
    peak = jnp.max(masked, axis=-1, keepdims=True)
    log_total = peak + jnp.log(jnp.sum(jnp.exp(masked - peak), axis=-1, keepdims=True))
    weights = jnp.exp(masked - log_total).astype(jnp.bfloat16)
    mixed = (
        jnp.einsum("hst,thd->shd", weights, value, preferred_element_type=jnp.float32)
        .astype(jnp.bfloat16)
        .reshape(length, width)
    )
    head_max = lax.pmax(jnp.max(peak[:, :, 0], axis=1), ("replica", "fsdp"))
    hidden = inputs + jnp.dot(mixed, full_output, preferred_element_type=jnp.float32)
    normed_ffn = rms_norm(hidden, ffn_gain).astype(jnp.bfloat16)
    logits = jnp.dot(normed_ffn, full_router, preferred_element_type=jnp.float32)
    picked = expert_index[:, :, None] == jnp.arange(EXPERTS, dtype=jnp.int32)[None, None, :]
    picked_float = picked.astype(jnp.float32)
    chosen = jnp.sum(picked_float * logits[:, None, :], axis=2)
    gates = jax.nn.softmax(chosen, axis=1)
    flat_expert = expert_index.reshape(-1)
    counts_hot = picked.reshape(-1, EXPERTS).astype(jnp.int32)
    rank = jnp.sum((jnp.cumsum(counts_hot, axis=0) - 1) * counts_hot, axis=1)
    slot_index = flat_expert * CAP + rank
    local_experts = expert_in.shape[0]
    send = (
        jnp.zeros((EXPERTS * CAP, width), jnp.bfloat16)
        .at[slot_index]
        .set(jnp.repeat(normed_ffn, TOPK, axis=0))
    )
    send = send.reshape(groups, local_experts, CAP, width)
    received_rows = lax.all_to_all(send, "fsdp", split_axis=0, concat_axis=0, tiled=True)
    projected_rows = jnp.einsum(
        "njcd,jde->njce", received_rows, expert_in, preferred_element_type=jnp.float32
    )
    active_rows = (jax.nn.silu(projected_rows[..., :FF]) * projected_rows[..., FF:]).astype(
        jnp.bfloat16
    )
    result_rows = jnp.einsum(
        "njcf,jfd->njcd", active_rows, expert_out, preferred_element_type=jnp.float32
    ).astype(jnp.bfloat16)
    returned = lax.all_to_all(result_rows, "fsdp", split_axis=0, concat_axis=0, tiled=True).reshape(
        EXPERTS * CAP, width
    )
    slot_values = returned[slot_index].reshape(length, TOPK, width)
    output = hidden + jnp.sum(gates[:, :, None] * slot_values, axis=1)
    grad_out = cotangent.astype(jnp.float32)
    grad_gates = jnp.sum(grad_out[:, None, :] * slot_values, axis=2)
    grad_result = (
        (gates[:, :, None] * grad_out[:, None, :])
        .astype(jnp.bfloat16)
        .reshape(length * TOPK, width)
    )
    grad_send = jnp.zeros((EXPERTS * CAP, width), jnp.bfloat16).at[slot_index].set(grad_result)
    grad_received = lax.all_to_all(
        grad_send.reshape(groups, local_experts, CAP, width),
        "fsdp",
        split_axis=0,
        concat_axis=0,
        tiled=True,
    )
    gate_part = projected_rows[..., :FF]
    up_part = projected_rows[..., FF:]
    sigmoid = jax.nn.sigmoid(gate_part)
    grad_active = jnp.einsum(
        "njcd,jfd->njcf", grad_received, expert_out, preferred_element_type=jnp.float32
    )
    out_grad = jnp.einsum(
        "njcf,njcd->jfd", active_rows, grad_received, preferred_element_type=jnp.float32
    )
    grad_projected = jnp.concatenate(
        [
            grad_active * up_part * sigmoid * (1.0 + gate_part * (1.0 - sigmoid)),
            grad_active * (gate_part * sigmoid),
        ],
        axis=-1,
    ).astype(jnp.bfloat16)
    in_grad = jnp.einsum(
        "njcd,njce->jde", received_rows, grad_projected, preferred_element_type=jnp.float32
    )
    grad_rows = jnp.einsum(
        "njce,jde->njcd", grad_projected, expert_in, preferred_element_type=jnp.float32
    ).astype(jnp.bfloat16)
    rows_back = lax.all_to_all(grad_rows, "fsdp", split_axis=0, concat_axis=0, tiled=True).reshape(
        EXPERTS * CAP, width
    )
    centered = grad_gates - jnp.sum(gates * grad_gates, axis=1, keepdims=True)
    grad_logits = jnp.sum((gates * centered)[:, :, None] * picked_float, axis=1).astype(
        jnp.bfloat16
    )
    router_grad = outer_sum(normed_ffn, grad_logits)
    grad_normed_ffn = jnp.sum(
        rows_back[slot_index].reshape(length, TOPK, width), axis=1, dtype=jnp.float32
    ) + times_transposed(grad_logits, full_router)
    norm_value, ffn_back = jax.vjp(rms_norm, hidden, ffn_gain)
    grad_hidden_norm, ffn_gain_grad = ffn_back(grad_normed_ffn)
    grad_hidden = grad_out + grad_hidden_norm
    back_query, back_key, back_value, back_output = (
        lax.all_gather(w_query, "fsdp", axis=0, tiled=True),
        lax.all_gather(w_key, "fsdp", axis=0, tiled=True),
        lax.all_gather(w_value, "fsdp", axis=0, tiled=True),
        lax.all_gather(w_output, "fsdp", axis=0, tiled=True),
    )
    grad_attn = grad_hidden.astype(jnp.bfloat16)
    output_grad = outer_sum(mixed, grad_attn)
    grad_mixed = (
        times_transposed(grad_attn, back_output).astype(jnp.bfloat16).reshape(length, H, HD)
    )
    again = (
        jnp.einsum("shd,thd->hst", query_rot, key_rot, preferred_element_type=jnp.float32) * scale
    )
    probs = jnp.exp(jnp.where(allowed, again, -jnp.inf) - log_total)
    grad_weights = jnp.einsum("shd,thd->hst", grad_mixed, value, preferred_element_type=jnp.float32)
    grad_value = (
        jnp.einsum(
            "hst,shd->thd",
            probs.astype(jnp.bfloat16),
            grad_mixed,
            preferred_element_type=jnp.float32,
        )
        .astype(jnp.bfloat16)
        .reshape(length, width)
    )
    grad_scores = (
        probs * (grad_weights - jnp.sum(probs * grad_weights, axis=-1, keepdims=True))
    ).astype(jnp.bfloat16)
    grad_query_rot = (
        jnp.einsum("hst,thd->shd", grad_scores, key_rot, preferred_element_type=jnp.float32) * scale
    )
    grad_key_rot = (
        jnp.einsum("hst,shd->thd", grad_scores, query_rot, preferred_element_type=jnp.float32)
        * scale
    )
    query_value, query_back = jax.vjp(
        lambda heads, gain: head_prep(heads, gain, cosine, sine), query_raw, gain_query
    )
    key_value, key_back = jax.vjp(
        lambda heads, gain: head_prep(heads, gain, cosine, sine), key_raw, gain_key
    )
    grad_query_raw, query_gain_grad = query_back(grad_query_rot)
    grad_key_raw, key_gain_grad = key_back(grad_key_rot)
    grad_query = grad_query_raw.reshape(length, width).astype(jnp.bfloat16)
    grad_key = grad_key_raw.reshape(length, width).astype(jnp.bfloat16)
    query_grad = outer_sum(normed, grad_query)
    key_grad = outer_sum(normed, grad_key)
    value_grad = outer_sum(normed, grad_value)
    grad_normed = (
        times_transposed(grad_query, back_query)
        + times_transposed(grad_key, back_key)
        + times_transposed(grad_value, back_value)
    )
    attn_value, attn_back = jax.vjp(rms_norm, inputs, attn_gain)
    grad_inputs_norm, attn_gain_grad = attn_back(grad_normed)
    input_grad = (grad_hidden + grad_inputs_norm).astype(jnp.bfloat16)
    expert_in_grad, expert_out_grad = (
        lax.psum_scatter(
            in_grad.astype(jnp.bfloat16), "replica", scatter_dimension=1, tiled=True
        ).astype(jnp.float32),
        lax.psum_scatter(
            out_grad.astype(jnp.bfloat16), "replica", scatter_dimension=1, tiled=True
        ).astype(jnp.float32),
    )
    attn_gain_total, query_gain_total, key_gain_total, ffn_gain_total = lax.psum(
        (attn_gain_grad, query_gain_grad, key_gain_grad, ffn_gain_grad), ("replica", "fsdp")
    )
    share_query, share_key, share_value, share_output, share_router = (
        lax.psum_scatter(
            query_grad.astype(jnp.bfloat16), "fsdp", scatter_dimension=0, tiled=True
        ).astype(jnp.float32),
        lax.psum_scatter(
            key_grad.astype(jnp.bfloat16), "fsdp", scatter_dimension=0, tiled=True
        ).astype(jnp.float32),
        lax.psum_scatter(
            value_grad.astype(jnp.bfloat16), "fsdp", scatter_dimension=0, tiled=True
        ).astype(jnp.float32),
        lax.psum_scatter(
            output_grad.astype(jnp.bfloat16), "fsdp", scatter_dimension=0, tiled=True
        ).astype(jnp.float32),
        lax.psum_scatter(
            router_grad.astype(jnp.bfloat16), "fsdp", scatter_dimension=0, tiled=True
        ).astype(jnp.float32),
    )
    total_query, total_key, total_value, total_output, total_router = (
        lax.psum(share_query.astype(jnp.bfloat16), "replica").astype(jnp.float32),
        lax.psum(share_key.astype(jnp.bfloat16), "replica").astype(jnp.float32),
        lax.psum(share_value.astype(jnp.bfloat16), "replica").astype(jnp.float32),
        lax.psum(share_output.astype(jnp.bfloat16), "replica").astype(jnp.float32),
        lax.psum(share_router.astype(jnp.bfloat16), "replica").astype(jnp.float32),
    )
    threshold = clip_threshold.astype(jnp.float32)
    factor = threshold / jnp.maximum(head_max, threshold)
    column_scale = jnp.repeat(jnp.sqrt(factor), HD)
    clipped_query = (w_query.astype(jnp.float32) * column_scale[None, :]).astype(jnp.bfloat16)
    clipped_key = (w_key.astype(jnp.float32) * column_scale[None, :]).astype(jnp.bfloat16)
    return (
        output.astype(jnp.bfloat16),
        input_grad,
        attn_gain_total,
        total_query,
        total_key,
        total_value,
        total_output,
        query_gain_total,
        key_gain_total,
        ffn_gain_total,
        total_router,
        expert_in_grad,
        expert_out_grad,
        head_max,
        clipped_query,
        clipped_key,
    )


def solution(mesh):
    return jax.shard_map(
        local,
        mesh=mesh,
        in_specs=(
            P(("replica", "fsdp"), None),
            P(("replica", "fsdp"), None),
            P(("replica", "fsdp"), None),
            P(("replica", "fsdp"), None),
            P(),
            P(),
            P("fsdp", None),
            P("fsdp", None),
            P("fsdp", None),
            P("fsdp", None),
            P(),
            P(),
            P(),
            P("fsdp", None),
            P("fsdp", None, None),
            P("fsdp", None, None),
        ),
        out_specs=(
            P(("replica", "fsdp"), None),
            P(("replica", "fsdp"), None),
            P(),
            P("fsdp", None),
            P("fsdp", None),
            P("fsdp", None),
            P("fsdp", None),
            P(),
            P(),
            P(),
            P("fsdp", None),
            P("fsdp", "replica", None),
            P("fsdp", "replica", None),
            P(),
            P("fsdp", None),
            P("fsdp", None),
        ),
        check_vma=False,
    )
```

profile of v0, /device:TPU:8, one launch (start us, length us, event | category | flops | bytes accessed | tf_op | source)
XLA Modules:
  0.0 2100.0 jit_solution(15007729034176878505)
XLA Ops:
  11.8 4.5 reduce-window.6
  19.4 70.9 %all-gather.9.cloned.1.call-done = bf16[2048,2048]{1,0:T(8,128)(2,1)} async-done(((bf16[256,2048]{1,0:T(8,128)(2,1)}), bf16[2048,2048]{1,0:T(8,128)(2,1)}) %all-gather.9.cloned.1.call-update) | async-done | bytes 8388624 | tf_op jit(solution)/shard_map/all_gather | solution.py:78
  90.3 5.8 fusion.87
  98.7 73.9 %all-gather.7.cloned.1.call-done = bf16[2048,2048]{1,0:T(8,128)(2,1)} async-done(((bf16[256,2048]{1,0:T(8,128)(2,1)}), bf16[2048,2048]{1,0:T(8,128)(2,1)}) %all-gather.7.cloned.1.call-update) | async-done | bytes 8388624 | tf_op jit(solution)/shard_map/all_gather | solution.py:77
  172.5 5.8 fusion.89
  189.9 64.9 %all-gather.5.cloned.1.call-done = bf16[2048,2048]{1,0:T(8,128)(2,1)} async-done(((bf16[256,2048]{1,0:T(8,128)(2,1)}), bf16[2048,2048]{1,0:T(8,128)(2,1)}) %all-gather.5.cloned.1.call-update) | async-done | bytes 8388624 | tf_op jit(solution)/shard_map/all_gather | solution.py:79
  254.7 5.9 fusion.57
  262.5 74.3 %all-gather.11.cloned.1.call-done = bf16[2048,2048]{1,0:T(8,128)(2,1)} async-done(((bf16[256,2048]{1,0:T(8,128)(2,1)}), bf16[2048,2048]{1,0:T(8,128)(2,1)}) %all-gather.11.cloned.1.call-update) | async-done | bytes 8388624 | tf_op jit(solution)/shard_map/all_gather | solution.py:80
  336.8 5.8 multiply_reduce_fusion.5
  344.2 17.8 scatter_custom_fusion
  362.1 8.1 all-to-all-start
  371.7 209.7 %all_gather.23 = bf16[2048,16]{0,1:T(8,128)(2,1)S(1)} all-gather(bf16[256,16]{0,1:T(8,128)(2,1)S(1)} %copy-done.89), channel_id=1, replica_groups=mesh['replica'=4,'fsdp'=8] {'fsdp'}, dimensions={0}, use_global_device_ids=true | all-gather | bytes 73728 | tf_op jit(solution)/shard_map/all_gather | solution.py:81
  583.6 18.9 scatter_custom_fusion.1
  602.4 6.5 all-to-all-start.2
  608.9 27.4 %fusion.27 = f32[8,2,144,2048]{3,2,0,1:T(8,128)} fusion(bf16[2,2048,2048]{2,1,0:T(8,128)(2,1)} %param.30, bf16[8,2,144,2048]{3,2,1,0:T(8,128)(2,1)} %all-to-all-done), kind=kOutput, calls=%fused_computation.47 | convolution fusion | flops 19327352832 | bytes 45088768 | tf_op jit(solution)/shard_map/njcd,jde->njce/dot_general | solution.py:130
  636.3 175.4 %all-to-all-done.2 = bf16[8,2,144,2048]{3,2,1,0:T(8,128)(2,1)} async-done(((bf16[8,2,144,2048]{3,2,1,0:T(8,128)(2,1)}), bf16[8,2,144,2048]{3,2,1,0:T(8,128)(2,1)}, u32[]{:S(2)}, u32[]{:S(2)}) %all-to-all-start.2) | async-done | bytes 9437216 | tf_op jit(solution)/shard_map/all_to_all | solution.py:152
  811.7 22.8 %fusion.9 = (bf16[8,2,144,1024]{3,2,0,1:T(8,128)(2,1)}, bf16[8,2,144,1024]{3,2,0,1:T(8,128)(2,1)}, bf16[8,2,144,1024]{3,2,0,1:T(8,128)(2,1)}) fusion(f32[8,2,144,2048]{3,2,0,1:T(8,128)} %fusion.27, bf16[2,1024,2048]{2,1,0:T(8,128)(2,1)} %param.31, bf16[8,2,144,2048]{3,2,1,0:T(8,128)(2,1)} %all-to-all-done.2), kind=kOutput, calls=%fused_computation.22 | convolution fusion | flops 9699065856 | bytes 50855936 | tf_op jit(solution)/shard_map/njcd,jfd->njcf/dot_general | solution.py:162
  834.6 25.8 %convert_bitcast_fusion = bf16[8,2,144,2048]{3,2,0,1:T(8,128)(2,1)} fusion(bf16[2,2048,2048]{2,1,0:T(8,128)(2,1)} %param.30, bf16[8,2,144,1024]{3,2,0,1:T(8,128)(2,1)} %get-tuple-element.37, bf16[8,2,144,1024]{3,2,0,1:T(8,128)(2,1)} %get-tuple-element.36), kind=kOutput, calls=%fused_computation.26 | convolution fusion | flops 19350945792 | bytes 35651584 | tf_op jit(solution)/shard_map/njce,jde->njcd/dot_general | solution.py:178
  860.4 9.3 copy.243
  869.6 8.6 all-to-all-start.3
  878.2 16.3 convert_bitcast_fusion.1
  894.5 9.3 copy.240
  903.8 177.3 %all-to-all-done.3 = bf16[8,2,144,2048]{3,2,1,0:T(8,128)(2,1)} async-done(((bf16[8,2,144,2048]{3,2,1,0:T(8,128)(2,1)}), bf16[8,2,144,2048]{3,2,1,0:T(8,128)(2,1)}, u32[]{:S(2)}, u32[]{:S(2)}) %all-to-all-start.3) | async-done | bytes 9437216 | tf_op jit(solution)/shard_map/all_to_all | solution.py:181
  1081.1 8.5 all-to-all-start.1
  1089.6 21.6 %gather_fusion.1 = bf16[2048,2048]{1,0:T(8,128)(2,1)} fusion(bf16[2304,2048]{1,0:T(8,128)(2,1)} %bitcast.22, s32[2048]{0:T(1024)S(1)} %broadcast_clamp_fusion), kind=kCustom, calls=%fused_computation.1 | custom fusion | bytes 16785408 | tf_op jit(solution)/shard_map/gather | solution.py:190
  1111.2 11.3 convert_reduce_fusion
  1122.5 169.9 %all-to-all-done.1 = bf16[8,2,144,2048]{3,2,1,0:T(8,128)(2,1)} async-done(((bf16[8,2,144,2048]{3,2,1,0:T(8,128)(2,1)}), bf16[8,2,144,2048]{3,2,1,0:T(8,128)(2,1)}, u32[]{:S(2)}, u32[]{:S(2)}) %all-to-all-start.1) | async-done | bytes 9437216 | tf_op jit(solution)/shard_map/all_to_all | solution.py:139
  1292.5 21.2 %gather_fusion = bf16[2048,2048]{1,0:T(8,128)(2,1)} fusion(bf16[2304,2048]{1,0:T(8,128)(2,1)} %bitcast.14, s32[2048]{0:T(1024)S(1)} %broadcast_clamp_fusion), kind=kCustom, calls=%fused_computation | custom fusion | bytes 16785408 | tf_op jit(solution)/shard_map/gather | solution.py:142
  1313.8 10.0 fusion.1
  1330.2 5.6 convolution_convert_fusion
  1337.4 5.7 convolution_convert_fusion.4
  1348.4 5.8 convolution_convert_fusion.1
  1371.9 5.9 convolution_convert_fusion.2
  1387.8 5.9 convolution_convert_fusion.3
  1395.9 17.8 bitcast_convert_fusion.1
  1413.8 29.2 %bitcast_convert_fusion = bf16[2,2048,2048]{2,1,0:T(8,128)(2,1)} fusion(bf16[8,2,144,2048]{3,2,1,0:T(8,128)(2,1)} %all-to-all-done, bf16[8,2,144,1024]{3,2,0,1:T(8,128)(2,1)} %get-tuple-element.37, bf16[8,2,144,1024]{3,2,0,1:T(8,128)(2,1)} %get-tuple-element.36), kind=kOutput, calls=%fused_computation.4 | convolution fusion | flops 19354615808 | bytes 35651584 | tf_op jit(solution)/shard_map/njcd,njce->jde/dot_general | solution.py:175
  1443.7 43.8 %pmax.7 = f32[16]{0:T(128)S(1)} all-reduce(f32[16]{0:T(128)S(1)} %copy-done.97), channel_id=1, replica_groups=mesh['replica'=4,'fsdp'=8] {'replica','fsdp'}, use_global_device_ids=true, to_apply=%region_45.46 | all-reduce | flops 16 | bytes 128 | tf_op jit(solution)/shard_map/pmax | solution.py:110
  1487.5 28.4 %reduce-scatter.12.cloned.1.call-done = bf16[256,2048]{1,0:T(8,128)(2,1)} async-done(((bf16[2048,2048]{1,0:T(8,128)(2,1)}), bf16[256,2048]{1,0:T(8,128)(2,1)}) %reduce-scatter.12.cloned.1.call-update) | async-done | bytes 1048592 | tf_op jit(solution)/shard_map/reduce_scatter | solution.py:270
  1515.9 90.3 %reduce-scatter.10.cloned.1.call-done = bf16[256,2048]{1,0:T(8,128)(2,1)} async-done(((bf16[2048,2048]{1,0:T(8,128)(2,1)}), bf16[256,2048]{1,0:T(8,128)(2,1)}) %reduce-scatter.10.cloned.1.call-update) | async-done | bytes 1048592 | tf_op jit(solution)/shard_map/reduce_scatter | solution.py:267
  1606.2 90.9 %reduce-scatter.8.cloned.1.call-done = bf16[256,2048]{1,0:T(8,128)(2,1)} async-done(((bf16[2048,2048]{1,0:T(8,128)(2,1)}), bf16[256,2048]{1,0:T(8,128)(2,1)}) %reduce-scatter.8.cloned.1.call-update) | async-done | bytes 1048592 | tf_op jit(solution)/shard_map/reduce_scatter | solution.py:264
  1698.2 5.9 fusion.95
  1704.2 5.9 convolution_add_fusion.2
  1714.4 42.7 %all-reduce.4 = (f32[2048]{0:T(1024)}, f32[128]{0:T(128)}, f32[128]{0:T(128)}, f32[2048]{0:T(1024)}) all-reduce(f32[2048]{0:T(1024)S(1)} %get-tuple-element.26, f32[128]{0:T(128)S(1)} %copy-done.96, f32[128]{0:T(128)S(1)} %copy-done.95, f32[2048]{0:T(1024)S(1)} %copy-done.77), channel_id=1, replica_groups=mesh['replica'=4,'fsdp'=8] {'replica','fsdp'}, use_global_device_ids=true, to_apply=%region_25.26 | all-reduce | flops 4352 | bytes 34816 | tf_op jit(solution)/shard_map/psum | solution.py:260
  1761.8 11.1 psum.71
  1773.6 46.5 %reduce-scatter.20.cloned.1.call-done = bf16[2,256,2048]{2,1,0:T(8,128)(2,1)} async-done(((bf16[2,1024,2048]{2,1,0:T(8,128)(2,1)}), bf16[2,256,2048]{2,1,0:T(8,128)(2,1)}) %reduce-scatter.20.cloned.1.call-update) | async-done | bytes 2097168 | tf_op jit(solution)/shard_map/reduce_scatter | solution.py:256
  1824.2 152.8 %reduce-scatter.18.cloned.1.call-done = bf16[2,512,2048]{2,1,0:T(8,128)(2,1)} async-done(((bf16[2,2048,2048]{2,1,0:T(8,128)(2,1)}), bf16[2,512,2048]{2,1,0:T(8,128)(2,1)}) %reduce-scatter.18.cloned.1.call-update) | async-done | bytes 4194320 | tf_op jit(solution)/shard_map/reduce_scatter | solution.py:253
  1977.0 6.7 convert_element_type.231
  1983.6 101.8 %all-reduce.8.cloned.1.call-done = (bf16[256,2048]{1,0:T(8,128)(2,1)}, bf16[256,2048]{1,0:T(8,128)(2,1)}, bf16[256,2048]{1,0:T(8,128)(2,1)}, bf16[256,2048]{1,0:T(8,128)(2,1)}) async-done(((bf16[256,2048]{1,0:T(8,128)(2,1)}, bf16[256,2048]{1,0:T(8,128)(2,1)}, bf16[256,2048]{1,0:T(8,128)(2,1)}, bf16[256,2048]{1,0:T(8,128)(2,1)}), (bf16[256,2048]{1,0:T(8,128)(2,1)}, bf16[256,2048]{1,0:T(8,128)(2,1)}, ...) | async-done | bytes 4194320 | tf_op jit(solution)/shard_map/psum | solution.py:281
  (317 shorter events, 94.2 us)
Async XLA Ops:
  7.2 83.0 %all-gather.9.cloned.1.call-start = ((), (), s32[]{:S(2)}) async-start(), calls=%async_computation.13 | async-start | bytes 9437184 | tf_op jit(solution)/shard_map/all_gather | solution.py:78
  8.0 164.6 %all-gather.7.cloned.1.call-start = ((), (), s32[]{:S(2)}) async-start(), calls=%async_computation.12 | async-start | bytes 9437184 | tf_op jit(solution)/shard_map/all_gather | solution.py:77
  8.7 8.4 copy-start.3
  8.7 246.0 %all-gather.5.cloned.1.call-start = ((), (), s32[]{:S(2)}) async-start(), calls=%async_computation.11 | async-start | bytes 9437184 | tf_op jit(solution)/shard_map/all_gather | solution.py:79
  9.5 327.4 %all-gather.11.cloned.1.call-start = ((), (), s32[]{:S(2)}) async-start(), calls=%async_computation.14 | async-start | bytes 9437184 | tf_op jit(solution)/shard_map/all_gather | solution.py:80
  11.5 243.3 %copy-start.52 = (f32[2048]{0:T(1024)}, f32[2048]{0:T(1024)S(1)}, u32[]{:S(2)}) copy-start(f32[2048]{0:T(1024)S(1)} %convert_element_type.186) | copy-start | bytes 24580
  11.5 331.2 %copy-start.68 = (f32[2048]{0:T(1024)}, f32[2048]{0:T(1024)S(1)}, u32[]{:S(2)}) copy-start(f32[2048]{0:T(1024)S(1)} %convert_element_type.194) | copy-start | bytes 24580
  17.4 78.6 %copy-start.85 = (f32[256]{0:T(256)}, f32[256]{0:T(256)S(1)}, u32[]{:S(2)}) copy-start(f32[256]{0:T(256)S(1)} %fusion.51) | copy-start | bytes 3076
  17.4 155.1 %copy-start.73 = (f32[256]{0:T(256)}, f32[256]{0:T(256)S(1)}, u32[]{:S(2)}) copy-start(f32[256]{0:T(256)S(1)} %fusion.78) | copy-start | bytes 3076
  18.7 165.6 %copy-start.43 = (f32[256,64]{1,0:T(8,128)}, f32[256,64]{1,0:T(8,128)S(1)}, u32[]{:S(2)}) copy-start(f32[256,64]{1,0:T(8,128)S(1)} %get-tuple-element.55) | copy-start | bytes 196612
  18.7 165.6 %copy-start.45 = (f32[256,64]{1,0:T(8,128)}, f32[256,64]{1,0:T(8,128)S(1)}, u32[]{:S(2)}) copy-start(f32[256,64]{1,0:T(8,128)S(1)} %get-tuple-element.56) | copy-start | bytes 196612
  187.8 66.9 %copy-start.74 = (f32[256]{0:T(256)S(1)}, f32[256]{0:T(256)}, u32[]{:S(2)}) copy-start(f32[256]{0:T(256)} %copy-done.73) | copy-start | bytes 3076
  189.8 70.8 %copy-start.57 = (f32[16,256]{1,0:T(8,128)}, f32[16,256]{1,0:T(8,128)S(1)}, u32[]{:S(2)}) copy-start(f32[16,256]{1,0:T(8,128)S(1)} %log_add_fusion) | copy-start | bytes 49156
  262.5 80.2 %copy-start.20 = (bf16[16,128,256]{2,1,0:T(8,128)(2,1)}, bf16[16,128,256]{2,1,0:T(8,128)(2,1)S(1)}, u32[]{:S(2)}) copy-start(bf16[16,128,256]{2,1,0:T(8,128)(2,1)S(1)} %convolution_convert_fusion.8) | copy-start | bytes 3145732
  342.7 19.4 copy-start.87
  342.7 19.4 copy-start.81
  344.2 237.2 %copy-start.18 = (bf16[256,2048]{1,0:T(8,128)(2,1)}, bf16[256,2048]{1,0:T(8,128)(2,1)S(1)}, u32[]{:S(2)}) copy-start(bf16[256,2048]{1,0:T(8,128)(2,1)S(1)} %multiply_convert_fusion.4) | copy-start | bytes 3145732
  362.1 240.3 %all-to-all-start = ((bf16[8,2,144,2048]{3,2,1,0:T(8,128)(2,1)}), bf16[8,2,144,2048]{3,2,1,0:T(8,128)(2,1)}, u32[]{:S(2)}, u32[]{:S(2)}) async-start(bf16[8,2,144,2048]{3,2,1,0:T(8,128)(2,1)} %bitcast.177), calls=%async_computation | async-start | bytes 18874368 | tf_op jit(solution)/shard_map/all_to_all | solution.py:129
  370.2 211.9 %copy-start.71 = (s32[256,8]{0,1:T(8,128)S(1)}, s32[256,8]{0,1:T(8,128)}, u32[]{:S(2)}) copy-start(s32[256,8]{0,1:T(8,128)} %param.19) | copy-start | bytes 24580
  371.7 230.7 %copy-start.15 = (f32[256,2048]{1,0:T(8,128)}, f32[256,2048]{1,0:T(8,128)S(1)}, u32[]{:S(2)}) copy-start(f32[256,2048]{1,0:T(8,128)S(1)} %convert_element_type.203) | copy-start | bytes 6291460
  583.4 19.0 copy-start.47
  602.4 209.3 %all-to-all-start.2 = ((bf16[8,2,144,2048]{3,2,1,0:T(8,128)(2,1)}), bf16[8,2,144,2048]{3,2,1,0:T(8,128)(2,1)}, u32[]{:S(2)}, u32[]{:S(2)}) async-start(bf16[8,2,144,2048]{3,2,1,0:T(8,128)(2,1)} %bitcast.178), calls=%async_computation.2 | async-start | bytes 18874368 | tf_op jit(solution)/shard_map/all_to_all | solution.py:152
  869.6 211.4 %all-to-all-start.3 = ((bf16[8,2,144,2048]{3,2,1,0:T(8,128)(2,1)}), bf16[8,2,144,2048]{3,2,1,0:T(8,128)(2,1)}, u32[]{:S(2)}, u32[]{:S(2)}) async-start(bf16[8,2,144,2048]{3,2,1,0:T(8,128)(2,1)} %copy.243), calls=%async_computation.3 | async-start | bytes 18874368 | tf_op jit(solution)/shard_map/all_to_all | solution.py:181
  903.8 185.8 %copy-start.78 = (s32[2048,1]{0,1:T(1,128)S(1)}, s32[2048,1]{0,1:T(1,128)}, u32[]{:S(2)}) copy-start(s32[2048,1]{0,1:T(1,128)} %compare_select_fusion) | copy-start | bytes 24580
  1081.1 211.4 %all-to-all-start.1 = ((bf16[8,2,144,2048]{3,2,1,0:T(8,128)(2,1)}), bf16[8,2,144,2048]{3,2,1,0:T(8,128)(2,1)}, u32[]{:S(2)}, u32[]{:S(2)}) async-start(bf16[8,2,144,2048]{3,2,1,0:T(8,128)(2,1)} %copy.240), calls=%async_computation.1 | async-start | bytes 18874368 | tf_op jit(solution)/shard_map/all_to_all | solution.py:139
  1089.6 397.9 %reduce-scatter.14.cloned.1.call-start = ((), (), s32[]{:S(2)}) async-start(), calls=%async_computation.18 | async-start | bytes 9437184 | tf_op jit(solution)/shard_map/reduce_scatter | solution.py:273
  1292.5 21.2 %copy-start.48 = (f32[256,8]{1,0:T(8,128)S(1)}, f32[256,8]{1,0:T(8,128)}, u32[]{:S(2)}) copy-start(f32[256,8]{1,0:T(8,128)} %copy-done.47) | copy-start | bytes 24580
  1313.7 10.1 copy-start.60
  1313.7 10.1 copy-start.80
  1313.7 10.1 copy-start.84
  1313.7 10.2 copy-start.72
  1313.7 10.2 copy-start.7
  1313.8 10.2 copy-start.56
  1313.8 10.2 copy-start.69
  1313.8 10.2 copy-start.82
  1335.9 180.0 %reduce-scatter.12.cloned.1.call-start = ((), (), s32[]{:S(2)}) async-start(), calls=%async_computation.17 | async-start | bytes 9437184 | tf_op jit(solution)/shard_map/reduce_scatter | solution.py:270
  1354.2 252.0 %reduce-scatter.10.cloned.1.call-start = ((), (), s32[]{:S(2)}) async-start(), calls=%async_computation.16 | async-start | bytes 9437184 | tf_op jit(solution)/shard_map/reduce_scatter | solution.py:267
  1377.8 319.2 %reduce-scatter.8.cloned.1.call-start = ((), (), s32[]{:S(2)}) async-start(), calls=%async_computation.15 | async-start | bytes 9437184 | tf_op jit(solution)/shard_map/reduce_scatter | solution.py:264
  1393.7 368.1 %reduce-scatter.16.cloned.1.call-start = ((), (), s32[]{:S(2)}) async-start(), calls=%async_computation.19 | async-start | bytes 73728 | tf_op jit(solution)/shard_map/reduce_scatter | solution.py:276
  1395.9 424.2 %reduce-scatter.20.cloned.1.call-start = ((), (), s32[]{:S(2)}) async-start(), calls=%async_computation.21 | async-start | bytes 10485760 | tf_op jit(solution)/shard_map/reduce_scatter | solution.py:256
  1413.8 563.2 %reduce-scatter.18.cloned.1.call-start = ((), (), s32[]{:S(2)}) async-start(), calls=%async_computation.20 | async-start | bytes 20971520 | tf_op jit(solution)/shard_map/reduce_scatter | solution.py:253
  1443.1 642.4 %all-reduce.8.cloned.1.call-start = ((), (), s32[]{:S(2)}) async-start(), calls=%async_computation.22 | async-start | bytes 8388608 | tf_op jit(solution)/shard_map/psum | solution.py:281
  1487.5 269.6 %copy-start.101 = (f32[16]{0:T(128)}, f32[16]{0:T(128)S(1)}, u32[]{:S(2)}) copy-start(f32[16]{0:T(128)S(1)} %pmax.7) | copy-start | bytes 196
  1698.2 11.9 slice-start
  1710.3 46.8 %copy-start.100 = (s32[16]{0:T(128)S(1)}, s32[16]{0:T(128)}, u32[]{:S(2)}) copy-start(s32[16]{0:T(128)} %param.20) | copy-start | bytes 196
  1710.3 46.8 %copy-start.86 = (f32[256]{0:T(256)S(1)}, f32[256]{0:T(256)}, u32[]{:S(2)}) copy-start(f32[256]{0:T(256)} %copy-done.85) | copy-start | bytes 3076
  1710.3 46.9 %copy-start.32 = (bf16[256,2048]{1,0:T(8,128)(2,1)S(1)}, bf16[256,2048]{1,0:T(8,128)(2,1)}, u32[]{:S(2)}) copy-start(bf16[256,2048]{1,0:T(8,128)(2,1)} %param.23) | copy-start | bytes 3145732
  1710.3 46.9 %copy-start.33 = (bf16[256,2048]{1,0:T(8,128)(2,1)S(1)}, bf16[256,2048]{1,0:T(8,128)(2,1)}, u32[]{:S(2)}) copy-start(bf16[256,2048]{1,0:T(8,128)(2,1)} %param.22) | copy-start | bytes 3145732
  (72 other events, 208.6 us)
Sparse Core Ops, SparseCore 0:
  9.7 80.5 all-gather.8
  91.9 80.6 all-gather.6
  174.1 80.5 all-gather.4
  256.2 80.5 all-gather.10
  1336.0 88.6 reduce-scatter.13
  1426.8 89.0 reduce-scatter.11
  1518.2 87.9 reduce-scatter.9
  1609.0 87.9 reduce-scatter.7
  1699.8 27.6 reduce-scatter.15
  1730.7 89.2 reduce-scatter.19
  1823.1 153.8 reduce-scatter.17
  1980.5 104.8 all-reduce.7
where the time goes:
time: 2110 us; the launch traced here: 2100 us
  waiting for transfers between devices  1320 us (63%)
  blocking collectives  307 us (15%)
  matrix products  224 us (11%)
  local copies, waits for them, and re-layouts  103 us (5%)
  other arithmetic  97.2 us (5%)
  starting transfers between devices  32.8 us (2%)
    all_gather x1, blocking collectives, local(): lax.all_gather(router, 'fsdp', axis=0, tiled=True)  210 us
    all_to_all x1, waiting for transfers between devices, local(): lax.all_to_all(grad_rows, 'fsdp', split_axis=0, concat_axis=0, tiled=True)  177 us
    all_to_all x1, waiting for transfers between devices, local(): lax.all_to_all(grad_send.reshape(groups, local_experts, CAP, width), 'fsd...  175 us
    all_to_all x1, waiting for transfers between devices, local(): lax.all_to_all(result_rows, 'fsdp', split_axis=0, concat_axis=0, tiled=True)  170 us
    reduce_scatter x1, waiting for transfers between devices, local(): lax.psum_scatter(in_grad.astype(jnp.bfloat16), 'replica', scatter_dimensi...  153 us
    psum x1, waiting for transfers between devices, local(): lax.psum(share_query.astype(jnp.bfloat16), 'replica').astype(jnp.float32)  102 us
    reduce_scatter x1, waiting for transfers between devices, local(): lax.psum_scatter(query_grad.astype(jnp.bfloat16), 'fsdp', scatter_dimensi...  90.9 us
    reduce_scatter x1, waiting for transfers between devices, local(): lax.psum_scatter(key_grad.astype(jnp.bfloat16), 'fsdp', scatter_dimension...  90.3 us
  transfers between devices with their start and end apart: 16, of which 13 were waited for; matrix products, arithmetic and copies ran while one was open for 13% of the time, Pallas kernels for 0%

commit v1 on v0

v1 whole, which is shorter than its diff:
```python
import jax
import jax.numpy as jnp
from jax import lax
from jax.sharding import PartitionSpec as P

HD = 128
EXPERTS = 16
CAP = 144

epsilon = 1e-06
rope_base = 10000.0
BF = jnp.bfloat16
F32 = jnp.float32


def rms_norm(values, gain):
    return values * lax.rsqrt(jnp.mean(values * values, axis=-1, keepdims=True) + epsilon) * gain


def rope_tables(length, width):
    places = jnp.arange(length, dtype=F32)
    rates = rope_base ** (-jnp.arange(width // 2, dtype=F32) * 2.0 / width)
    angle = places[:, None] * rates[None, :]
    return jnp.cos(angle), jnp.sin(angle)


def rotate(values, cosine, sine):
    half = values.shape[-1] // 2
    first = values[..., :half]
    second = values[..., half:]
    return jnp.concatenate(
        [first * cosine - second * sine, second * cosine + first * sine], axis=-1
    )


def dot(left, right):
    return jnp.dot(left, right, preferred_element_type=F32)


def dot_tn(left, right):
    return lax.dot_general(left, right, (((0,), (0,)), ((), ())), preferred_element_type=F32)


def dot_nt(left, right):
    return lax.dot_general(left, right, (((1,), (1,)), ((), ())), preferred_element_type=F32)


def local(
    tokens,
    cotangent,
    segment_ids,
    expert_index,
    clip_threshold,
    attn_norm_gain,
    w_query,
    w_key,
    w_value,
    w_output,
    query_gain,
    key_gain,
    ffn_norm_gain,
    router,
    expert_in,
    expert_out,
):
    replicas = lax.axis_size("replica")
    groups = lax.axis_size("fsdp")
    me_r = lax.axis_index("replica")
    me_f = lax.axis_index("fsdp")
    length, width = tokens.shape
    part = width // replicas
    heads = part // HD
    ff = expert_out.shape[1]
    local_experts = expert_in.shape[0]
    scale = HD ** (-0.5)
    attn_gain = attn_norm_gain.astype(F32)
    ffn_gain = ffn_norm_gain.astype(F32)
    gain_query = query_gain.astype(F32)
    gain_key = key_gain.astype(F32)

    def swap(value, k):
        return lax.ppermute(value, "replica", [(r, r ^ k) for r in range(replicas)])

    def columns(value, k, axis=1):
        return lax.dynamic_slice_in_dim(value, (me_r ^ k) * part, part, axis)

    def spread(value):
        return [value] + [swap(value, k) for k in range(1, replicas)]

    def trade_columns(value):
        return [columns(value, 0)] + [swap(columns(value, k), k) for k in range(1, replicas)]

    def join_columns(blocks):
        out = jnp.zeros((blocks[0].shape[0], part * replicas), blocks[0].dtype)
        for k, block in enumerate(blocks):
            out = lax.dynamic_update_slice_in_dim(out, block, (me_r ^ k) * part, 1)
        return out

    def gather(value):
        return lax.all_gather(value, "fsdp", axis=0, tiled=True)

    def reduce(value):
        return lax.psum_scatter(value, "fsdp", scatter_dimension=0, tiled=True)

    w_qkv = gather(jnp.concatenate([columns(w, 0) for w in (w_query, w_key, w_value)], axis=1))
    tokens_all = jnp.concatenate(spread(tokens), axis=0)
    segments = jnp.concatenate(spread(segment_ids), axis=0)
    full_index = gather(expert_index)
    w_or = gather(jnp.concatenate([w_output, router], axis=1))
    full_output, full_router = w_or[:, :width], w_or[:, width:]
    cot_all = gather(cotangent)

    inputs_all = tokens_all.astype(F32)
    normed = rms_norm(inputs_all, attn_gain).astype(BF)
    raw = dot(normed, w_qkv)
    by_head = raw.reshape(replicas, length, 3, heads, HD)
    query_raw = by_head[:, :, 0].transpose(0, 2, 1, 3)
    key_raw = by_head[:, :, 1].transpose(0, 2, 1, 3)
    value = by_head[:, :, 2].transpose(0, 2, 1, 3).astype(BF)
    cosine, sine = rope_tables(length, HD)

    def head_prep(values, gain):
        return rotate(rms_norm(values, gain), cosine, sine)

    query_rot = head_prep(query_raw, gain_query).astype(BF)
    key_rot = head_prep(key_raw, gain_key).astype(BF)
    allowed = (segments[:, :, None] == segments[:, None, :])[:, None]
    scores = jnp.einsum("nhsd,nhtd->nhst", query_rot, key_rot, preferred_element_type=F32) * scale
    masked = jnp.where(allowed, scores, -jnp.inf)
    peak = jnp.max(masked, axis=-1, keepdims=True)
    log_total = peak + jnp.log(jnp.sum(jnp.exp(masked - peak), axis=-1, keepdims=True))
    probs = jnp.exp(masked - log_total)
    weights = probs.astype(BF)
    mixed_heads = jnp.einsum("nhst,nhtd->nshd", weights, value, preferred_element_type=F32).astype(
        BF
    )
    mixed_heads = mixed_heads.reshape(replicas, length, part)
    my_max = jnp.max(peak, axis=(0, 2, 3))
    mixed = join_columns(
        [mixed_heads[0]] + [swap(mixed_heads[k], k) for k in range(1, replicas)]
    )
    inputs = tokens.astype(F32)
    hidden = inputs + dot(mixed, full_output)
    normed_ffn = rms_norm(hidden, ffn_gain).astype(BF)
    mixed_all = jnp.concatenate(spread(mixed), axis=0)

    nf_all = gather(normed_ffn)
    ids = jnp.arange(EXPERTS, dtype=jnp.int32)
    mask = jnp.any(full_index[:, :, None] == ids, axis=1)
    logits = dot(nf_all, full_router)
    logits = jnp.where(mask, logits, -jnp.inf)
    top = jnp.max(logits, axis=1, keepdims=True)
    powers = jnp.exp(logits - top)
    gates = powers / jnp.sum(powers, axis=1, keepdims=True)
    first = me_f * local_experts
    hot = lax.dynamic_slice_in_dim(mask, first, local_experts, 1).reshape(
        groups, length, local_experts
    )
    own_gates = lax.dynamic_slice_in_dim(gates, first, local_experts, 1).reshape(
        groups, length, local_experts
    )
    order = jnp.arange(length, dtype=jnp.int32)
    before = (order[:, None] < order[None, :]).astype(BF)
    rank = jnp.einsum("nsj,st->ntj", hot.astype(BF), before, preferred_element_type=F32).astype(
        jnp.int32
    )
    slots = jnp.arange(CAP, dtype=jnp.int32)
    nf_seq = nf_all.reshape(groups, length, width)
    cot_seq = cot_all.reshape(groups, length, width)
    moe = jnp.zeros((groups, length, width), F32)
    back = jnp.zeros((groups, length, width), F32)
    gate_grads = []
    in_grads = []
    out_grads = []
    for j in range(local_experts):
        pick = (
            (rank[:, None, :, j] == slots[None, :, None]) & hot[:, None, :, j]
        ).astype(BF)
        gate = jnp.einsum(
            "ncs,ns->nc", pick.astype(F32), own_gates[:, :, j], precision=lax.Precision.HIGHEST
        ).reshape(-1, 1)

        def take(source):
            return jnp.einsum("ncs,nsd->ncd", pick, source, preferred_element_type=F32).astype(
                BF
            ).reshape(groups * CAP, width)

        def put(rows):
            return jnp.einsum(
                "ncs,ncd->nsd",
                pick,
                rows.reshape(groups, CAP, width),
                preferred_element_type=F32,
            )

        rows = take(nf_seq)
        projected = dot(rows, expert_in[j])
        gate_part, up_part = projected[:, :ff], projected[:, ff:]
        sigmoid = jax.nn.sigmoid(gate_part)
        silu = gate_part * sigmoid
        active = silu * up_part
        scaled = (active * gate).astype(BF)
        result = dot(scaled, expert_out[j]).astype(BF)
        moe = moe + put(result)
        cot_rows = take(cot_seq)
        pulled = dot_nt(cot_rows, expert_out[j])
        gate_grad = jnp.sum(active * pulled, axis=1)
        grad_active = pulled * gate
        grad_projected = jnp.concatenate(
            [
                grad_active * up_part * sigmoid * (1.0 + gate_part * (1.0 - sigmoid)),
                grad_active * silu,
            ],
            axis=1,
        ).astype(BF)
        back = back + put(dot_nt(grad_projected, expert_in[j]).astype(BF))
        gate_grads.append(
            jnp.einsum(
                "ncs,nc->ns",
                pick.astype(F32),
                gate_grad.reshape(groups, CAP),
                precision=lax.Precision.HIGHEST,
            )
        )
        in_grads.append(dot_tn(rows, grad_projected).astype(BF))
        out_grads.append(dot_tn(scaled, cot_rows).astype(BF))
    gate_grads = jnp.stack(gate_grads, axis=-1).reshape(groups * length, local_experts)
    sent = gate_grads.astype(BF)
    rest = (gate_grads - sent.astype(F32)).astype(BF)
    blank = jnp.zeros((groups * length, EXPERTS), BF)
    extra = jnp.concatenate(
        [
            lax.dynamic_update_slice_in_dim(blank, sent, first, 1),
            lax.dynamic_update_slice_in_dim(blank, rest, first, 1),
        ],
        axis=1,
    )
    packed = jnp.concatenate([back.reshape(groups * length, width).astype(BF), extra], axis=1)
    summed = reduce(packed).astype(F32)
    output = (hidden + reduce(moe.reshape(groups * length, width).astype(BF)).astype(F32)).astype(
        BF
    )

    grad_gates = summed[:, width : width + EXPERTS] + summed[:, width + EXPERTS :]
    my_gates = lax.dynamic_slice_in_dim(gates, me_f * length, length, 0)
    centered = grad_gates - jnp.sum(my_gates * grad_gates, axis=1, keepdims=True)
    grad_logits = (my_gates * centered).astype(BF)
    router_grad = dot_tn(normed_ffn, grad_logits)
    grad_normed_ffn = summed[:, :width] + dot_nt(grad_logits, full_router)
    grad_out = cotangent.astype(F32)
    norm_value, ffn_back = jax.vjp(rms_norm, hidden, ffn_gain)
    grad_hidden_norm, ffn_gain_grad = ffn_back(grad_normed_ffn)
    grad_hidden = grad_out + grad_hidden_norm
    grad_attn = grad_hidden.astype(BF)
    attn_columns = jnp.concatenate(trade_columns(grad_attn), axis=0)
    output_grad = dot_tn(mixed_all, attn_columns)
    grad_mixed = dot_nt(grad_attn, full_output).astype(BF)
    grad_mixed = jnp.stack(trade_columns(grad_mixed), axis=0)
    grad_mixed = grad_mixed.reshape(replicas, length, heads, HD).transpose(0, 2, 1, 3)
    grad_weights = jnp.einsum("nhsd,nhtd->nhst", grad_mixed, value, preferred_element_type=F32)
    grad_value = jnp.einsum(
        "nhst,nhsd->nthd", weights, grad_mixed, preferred_element_type=F32
    ).astype(BF)
    grad_scores = (
        probs * (grad_weights - jnp.sum(probs * grad_weights, axis=-1, keepdims=True))
    ).astype(BF)
    grad_query_rot = (
        jnp.einsum("nhst,nhtd->nhsd", grad_scores, key_rot, preferred_element_type=F32) * scale
    )
    grad_key_rot = (
        jnp.einsum("nhst,nhsd->nhtd", grad_scores, query_rot, preferred_element_type=F32) * scale
    )
    query_value, query_back = jax.vjp(head_prep, query_raw, gain_query)
    key_value, key_back = jax.vjp(head_prep, key_raw, gain_key)
    grad_query_raw, query_gain_grad = query_back(grad_query_rot)
    grad_key_raw, key_gain_grad = key_back(grad_key_rot)
    rows_all = replicas * length
    grad_qkv = jnp.concatenate(
        [
            grad_query_raw.astype(BF).transpose(0, 2, 1, 3).reshape(rows_all, part),
            grad_key_raw.astype(BF).transpose(0, 2, 1, 3).reshape(rows_all, part),
            grad_value.reshape(rows_all, part),
        ],
        axis=1,
    )
    qkv_grad = dot_tn(normed, grad_qkv)
    part_normed = dot_nt(grad_qkv, w_qkv).astype(BF).reshape(replicas, length, width)
    grad_normed = part_normed[0].astype(F32)
    for k in range(1, replicas):
        grad_normed = grad_normed + swap(part_normed[k], k).astype(F32)
    attn_value, attn_back = jax.vjp(rms_norm, inputs, attn_gain)
    grad_inputs_norm, attn_gain_grad = attn_back(grad_normed)
    input_grad = (grad_hidden + grad_inputs_norm).astype(BF)

    share_o = reduce(jnp.concatenate([output_grad, router_grad], axis=1).astype(BF))
    share_qkv = reduce(qkv_grad.astype(BF))
    blocks_o = spread(share_o)
    total_output = join_columns([b[:, :part].astype(F32) for b in blocks_o])
    total_router = sum(b[:, part:].astype(F32) for b in blocks_o)
    blocks_qkv = spread(share_qkv)
    total_query, total_key, total_value = (
        join_columns([b[:, i * part : (i + 1) * part].astype(F32) for b in blocks_qkv])
        for i in range(3)
    )

    def replica_sum(value, flip):
        bits = replicas.bit_length() - 1
        value = value.reshape((2,) * bits + (-1, value.shape[-1]))
        for step in range(bits):
            bit = bits - 1 - step if flip else step
            axis = bits - 1 - bit
            mine = (me_r >> bit) & 1
            keep = lax.dynamic_slice_in_dim(value, mine, 1, axis)
            send = lax.dynamic_slice_in_dim(value, 1 - mine, 1, axis)
            value = keep.astype(F32) + swap(send, 1 << bit).astype(F32)
            if step < bits - 1:
                value = value.astype(BF)
        return value.reshape(-1, value.shape[-1])

    expert_out_grad = jnp.stack([replica_sum(g, j % 2 == 1) for j, g in enumerate(out_grads)])
    expert_in_grad = jnp.stack([replica_sum(g, j % 2 == 1) for j, g in enumerate(in_grads)])

    top_heads = lax.dynamic_update_slice_in_dim(
        jnp.full((replicas * heads,), -jnp.inf, F32), my_max, me_r * heads, 0
    )
    sums = jnp.concatenate([attn_gain_grad, query_gain_grad, key_gain_grad, ffn_gain_grad])
    small = jnp.concatenate([sums, top_heads])
    n_sums = sums.shape[0]
    is_sum = jnp.arange(small.shape[0]) < n_sums

    def merge(a, b):
        return jnp.where(is_sum, a + b, jnp.maximum(a, b))

    step = 1
    while step < replicas:
        small = merge(small, swap(small, step))
        step *= 2
    step = 1
    while step < groups:
        other = lax.ppermute(small, "fsdp", [(f, f ^ step) for f in range(groups)])
        small = merge(small, other)
        step *= 2
    attn_gain_total = small[:width]
    query_gain_total = small[width : width + HD]
    key_gain_total = small[width + HD : width + 2 * HD]
    ffn_gain_total = small[width + 2 * HD : n_sums]
    head_max = small[n_sums:]
    threshold = clip_threshold.astype(F32)
    factor = threshold / jnp.maximum(head_max, threshold)
    column_scale = jnp.repeat(jnp.sqrt(factor), HD)
    clipped_query = (w_query.astype(F32) * column_scale[None, :]).astype(BF)
    clipped_key = (w_key.astype(F32) * column_scale[None, :]).astype(BF)
    return (
        output,
        input_grad,
        attn_gain_total,
        total_query,
        total_key,
        total_value,
        total_output,
        query_gain_total,
        key_gain_total,
        ffn_gain_total,
        total_router,
        expert_in_grad,
        expert_out_grad,
        head_max,
        clipped_query,
        clipped_key,
    )


def solution(mesh):
    both = ("replica", "fsdp")
    return jax.shard_map(
        local,
        mesh=mesh,
        in_specs=(
            P(both, None),
            P(both, None),
            P(both, None),
            P(both, None),
            P(),
            P(),
            P("fsdp", None),
            P("fsdp", None),
            P("fsdp", None),
            P("fsdp", None),
            P(),
            P(),
            P(),
            P("fsdp", None),
            P("fsdp", None, None),
            P("fsdp", None, None),
        ),
        out_specs=(
            P(both, None),
            P(both, None),
            P(),
            P("fsdp", None),
            P("fsdp", None),
            P("fsdp", None),
            P("fsdp", None),
            P(),
            P(),
            P(),
            P("fsdp", None),
            P("fsdp", "replica", None),
            P("fsdp", "replica", None),
            P(),
            P("fsdp", None),
            P("fsdp", None),
        ),
        check_vma=False,
    )
```

time: 2110 us -> 968 us (0.46)
  waiting for transfers between devices: 1320 us -> 402 us
  blocking collectives: 307 us -> 14.1 us
  matrix products: 224 us -> 280 us
  starting transfers between devices: 32.8 us -> 62.6 us
    all_to_all x4 -> x0, waiting for transfers between devices: 523 us -> none  [the longest x1 177 us: local(): lax.all_to_all(grad_rows, 'fsdp', split_axis=0, concat_axis=0, tiled=True)]
    reduce_scatter x7 -> x4, waiting for transfers between devices: 409 us -> 0.03 us  [reduce(): return lax.psum_scatter(value, 'fsdp', scatter_dimension=0, tiled=True)]
    ppermute x0 -> x40, waiting for transfers between devices: none -> 231 us  [the longest x37 229 us: swap(): return lax.ppermute(value, 'replica', [(r, r ^ k) for r in range(replicas)])]
    all_gather x1, blocking collectives: 210 us -> 14.1 us  [gather(): return lax.all_gather(value, 'fsdp', axis=0, tiled=True)]
    all_gather x4, waiting for transfers between devices: 284 us -> 170 us  [gather(): return lax.all_gather(value, 'fsdp', axis=0, tiled=True)]
    psum x1 -> x0, waiting for transfers between devices: 102 us -> none  [local(): lax.psum(share_query.astype(jnp.bfloat16), 'replica').astype(jnp.float32)]
    ppermute x0 -> x40, starting transfers between devices: none -> 62.3 us  [the longest x37 51.5 us: swap(): return lax.ppermute(value, 'replica', [(r, r ^ k) for r in range(replicas)])]
    dot_general x27 -> x40, matrix products: 224 us -> 280 us  [the longest x7 75.8 us: dot_nt(): lax.dot_general(left, right, (((1,), (1,)), ((), ())), preferred_element_...]
  transfers between devices with their start and end apart: 16 -> 48, of which waited for: 13 -> 22; matrix products, arithmetic and copies ran while one was open for 13% -> 30% of each run, Pallas kernels for 0% -> 0%
where the time goes in v1:
time: 968 us; the launch traced here: 956 us
  waiting for transfers between devices  402 us (42%)
  matrix products  280 us (29%)
  local copies, waits for them, and re-layouts  97.6 us (10%)
  other arithmetic  82.9 us (9%)
  starting transfers between devices  62.6 us (6%)
  between operations  16.7 us (2%)
  blocking collectives  14.1 us (1%)
    ppermute x37, waiting for transfers between devices, swap(): return lax.ppermute(value, 'replica', [(r, r ^ k) for r in range(replicas)])  229 us
    all_gather x4, waiting for transfers between devices, gather(): return lax.all_gather(value, 'fsdp', axis=0, tiled=True)  170 us
    dot_general x7, matrix products, dot_nt(): lax.dot_general(left, right, (((1,), (1,)), ((), ())), preferred_element_...  75.8 us
    dot_general x7, matrix products, dot(): return jnp.dot(left, right, preferred_element_type=F32)  66.9 us
    dot_general x7, matrix products, dot_tn(): lax.dot_general(left, right, (((0,), (0,)), ((), ())), preferred_element_...  57.5 us
    ppermute x37, starting transfers between devices, swap(): return lax.ppermute(value, 'replica', [(r, r ^ k) for r in range(replicas)])  51.5 us
    dot_general x4, matrix products, put(): jnp.einsum('ncs,ncd->nsd', pick, rows.reshape(groups, CAP, width), prefer...  40.3 us
    dot_general x4, matrix products, take(): jnp.einsum('ncs,nsd->ncd', pick, source, preferred_element_type=F32)  21.2 us
  transfers between devices with their start and end apart: 48, of which 22 were waited for; matrix products, arithmetic and copies ran while one was open for 30% of the time, Pallas kernels for 0%

profile of v1, /device:TPU:8, one launch (start us, length us, event | category | flops | bytes accessed | tf_op | source)
XLA Modules:
  0.0 955.8 jit_solution(9239159984155684670)
XLA Ops:
  19.0 40.9 %collective-permute-done.3 = s32[1,256]{1,0:T(1,128)S(1)} collective-permute-done((s32[1,256]{1,0:T(1,128)S(1)}, s32[1,256]{1,0:T(1,128)S(1)}, u32[]{:S(2)}, u32[]{:S(2)}) %collective-permute-start.3) | collective-permute-done | bytes 1056 | tf_op jit(solution)/shard_map/ppermute | solution.py:82
  67.1 7.2 all-gather.5.cloned.1.call-done
  74.2 13.5 %fusion.66 = f32[1024,1536]{1,0:T(8,128)} fusion(bf16[2048,1536]{1,0:T(8,128)(2,1)} %all-gather.5.cloned.1.call-done, f32[2048]{0:T(1024)S(1)} %convert_element_type.316, f32[1024]{0:T(1024)S(1)} %add_rsqrt_fusion, bf16[256,2048]{1,0:T(8,128)(2,1)} %copy-done.57, bf16[256,2048]{1,0:T(8,128)(2,1)} %copy-done.55, ...), kind=kOutput, calls=%fused_computation.146 | convolution fusion | flops 6465519616 | bytes 16789504 | tf_op jit(solution)/shard_map/dot_general | solution.py:37
  87.7 7.7 reshape.295
  121.5 5.4 collective-permute-done.7
  128.4 32.6 %all-gather.7.cloned.1.call-done = bf16[2048,2064]{1,0:T(8,128)(2,1)} async-done(((bf16[256,2064]{1,0:T(8,128)(2,1)}), bf16[2048,2064]{1,0:T(8,128)(2,1)}) %all-gather.7.cloned.1.call-update) | async-done | bytes 8454160 | tf_op jit(solution)/shard_map/all_gather | solution.py:100
  161.0 6.2 multiply_reduce_fusion.9
  169.8 14.1 %all_gather.17 = s32[2048,8]{0,1:T(8,128)S(1)} all-gather(s32[256,8]{0,1:T(8,128)S(1)} %copy-done.93), channel_id=1, replica_groups=mesh['replica'=4,'fsdp'=8] {'fsdp'}, dimensions={0}, use_global_device_ids=true | all-gather | bytes 73728 | tf_op jit(solution)/shard_map/all_gather | solution.py:100
  184.6 59.2 %all-gather.11.cloned.1.call-done = bf16[2048,2048]{1,0:T(8,128)(2,1)} async-done(((bf16[256,2048]{1,0:T(8,128)(2,1)}), bf16[2048,2048]{1,0:T(8,128)(2,1)}) %all-gather.11.cloned.1.call-update) | async-done | bytes 8388624 | tf_op jit(solution)/shard_map/all_gather | solution.py:100
  243.8 7.1 convolution_convert_fusion.5
  254.4 71.5 %all-gather.9.cloned.1.call-done = bf16[2048,2048]{1,0:T(8,128)(2,1)} async-done(((bf16[256,2048]{1,0:T(8,128)(2,1)}), bf16[2048,2048]{1,0:T(8,128)(2,1)}) %all-gather.9.cloned.1.call-update) | async-done | bytes 8388624 | tf_op jit(solution)/shard_map/all_gather | solution.py:100
  325.9 7.1 convolution_convert_fusion.7
  344.3 16.1 %fusion.5 = f32[1152,2048]{1,0:T(8,128)} fusion(bf16[1152,2048]{1,0:T(8,128)(2,1)} %bitcast.214, bf16[2,2048,2048]{2,1,0:T(8,128)(2,1)} %param.30), kind=kOutput, calls=%fused_computation.10 | convolution fusion | flops 9663676416 | bytes 22544384 | tf_op jit(solution)/shard_map/dot_general | solution.py:37
  360.4 14.5 %fusion.9 = f32[1152,2048]{1,0:T(8,128)} fusion(bf16[1152,2048]{1,0:T(8,128)(2,1)S(1)} %bitcast.220, bf16[2,2048,2048]{2,1,0:T(8,128)(2,1)} %param.30), kind=kOutput, calls=%fused_computation.14 | convolution fusion | flops 9663676416 | bytes 22544384 | tf_op jit(solution)/shard_map/dot_general | solution.py:37
  375.0 15.0 %multiply_convert_fusion.1 = (bf16[1152,1024]{1,0:T(8,128)(2,1)}, bf16[1152,1024]{1,0:T(8,128)(2,1)}, f32[1152]{0:T(1024)S(1)}, bf16[1152,1024]{1,0:T(8,128)(2,1)}) fusion(f32[1152,2048]{1,0:T(8,128)} %fusion.5, f32[1152]{0:T(1024)S(1)} %mul.696, bf16[1152,2048]{1,0:T(8,128)(2,1)} %bitcast.228, bf16[2,1024,2048]{2,1,0:T(8,128)(2,1)} %param.31), kind=kOutput, calls=%fused_computation.38 | convolution fusion | flops 4854250496 | bytes 25437184 | tf_op jit(solution)/shard_map/dot_general | solution.py:45
  390.6 14.7 %multiply_convert_fusion.3 = (bf16[1152,1024]{1,0:T(8,128)(2,1)}, bf16[1152,1024]{1,0:T(8,128)(2,1)}, f32[1152]{0:T(1024)S(1)}, bf16[1152,1024]{1,0:T(8,128)(2,1)}) fusion(f32[1152,2048]{1,0:T(8,128)} %fusion.9, f32[1152]{0:T(1024)S(1)} %mul.691, bf16[1152,2048]{1,0:T(8,128)(2,1)} %bitcast.224, bf16[2,1024,2048]{2,1,0:T(8,128)(2,1)} %param.31), kind=kOutput, calls=%fused_computation.40 | convolution fusion | flops 4854250496 | bytes 25437184 | tf_op jit(solution)/shard_map/dot_general | solution.py:45
  406.7 14.1 %fusion.11 = bf16[1152,2048]{1,0:T(8,128)(2,1)S(1)} fusion(bf16[2,2048,2048]{2,1,0:T(8,128)(2,1)} %param.30, bf16[1152,1024]{1,0:T(8,128)(2,1)} %get-tuple-element.31, bf16[1152,1024]{1,0:T(8,128)(2,1)} %get-tuple-element.30), kind=kOutput, calls=%fused_computation.23 | convolution fusion | flops 9675472896 | bytes 17825792 | tf_op jit(solution)/shard_map/dot_general | solution.py:45
  420.8 8.3 fusion.71
  436.5 14.4 %fusion.14 = bf16[1152,2048]{1,0:T(8,128)(2,1)S(1)} fusion(bf16[2,2048,2048]{2,1,0:T(8,128)(2,1)} %param.30, bf16[1152,1024]{1,0:T(8,128)(2,1)} %get-tuple-element.29, bf16[1152,1024]{1,0:T(8,128)(2,1)} %get-tuple-element.28), kind=kOutput, calls=%fused_computation.24 | convolution fusion | flops 9675472896 | bytes 17825792 | tf_op jit(solution)/shard_map/dot_general | solution.py:45
  450.9 11.8 %add_convert_fusion = bf16[8,256,2048]{2,1,0:T(8,128)(2,1)} fusion(f32[8,256,2048]{2,1,0:T(8,128)} %fusion.71, bf16[8,144,2048]{2,1,0:T(8,128)(2,1)S(1)} %bitcast.241, s32[8,256]{1,0:T(8,128)S(1)} %get-tuple-element.80, pred[8,256]{1,0:T(8,128)(4,1)S(1)} %get-tuple-element.84), kind=kOutput, calls=%fused_computation | convolution fusion | flops 1216937984 | bytes 29894656 | tf_op jit(solution)/shard_map/ncs,ncd->nsd/dot_general | solution.py:189
  462.7 13.7 %concatenate.57 = bf16[2048,2080]{1,0:T(8,128)(2,1)} concatenate(bf16[2048,2048]{1,0:T(8,128)(2,1)} %bitcast.213, bf16[2048,16]{1,0:T(8,128)(2,1)S(1)} %dynamic_update_slice.73, bf16[2048,16]{1,0:T(8,128)(2,1)S(1)} %dynamic_update_slice.74), dimensions={1} | concatenate | bytes 17039360 | tf_op jit(solution)/shard_map/concatenate | solution.py:238
  476.5 7.9 convolution_convert_fusion.1
  484.5 8.3 fusion.74
  492.8 5.3 convolution_convert_fusion
  498.1 11.8 %add_convert_fusion.1 = bf16[8,256,2048]{2,1,0:T(8,128)(2,1)} fusion(f32[8,256,2048]{2,1,0:T(8,128)} %fusion.74, bf16[8,144,2048]{2,1,0:T(8,128)(2,1)S(1)} %bitcast.240, s32[8,256]{1,0:T(8,128)S(1)} %get-tuple-element.80, pred[8,256]{1,0:T(8,128)(4,1)S(1)} %get-tuple-element.84), kind=kOutput, calls=%fused_computation.1 | convolution fusion | flops 1216937984 | bytes 29894656 | tf_op jit(solution)/shard_map/ncs,ncd->nsd/dot_general | solution.py:189
  515.5 8.5 convolution_convert_fusion.10
  529.3 5.9 convolution_convert_fusion.11
  538.3 16.6 %convolution_convert_fusion.3 = bf16[2048,2048]{1,0:T(8,128)(2,1)} fusion(bf16[1152,2048]{1,0:T(8,128)(2,1)S(1)} %bitcast.223, bf16[1152,1024]{1,0:T(8,128)(2,1)} %get-tuple-element.31, bf16[1152,1024]{1,0:T(8,128)(2,1)} %get-tuple-element.30), kind=kOutput, calls=%fused_computation.21 | convolution fusion | flops 9677307904 | bytes 17825792 | tf_op jit(solution)/shard_map/dot_general | solution.py:41
  555.0 12.3 %convolution_convert_fusion.2 = bf16[2048,2048]{1,0:T(8,128)(2,1)S(1)} fusion(bf16[1152,2048]{1,0:T(8,128)(2,1)S(1)} %bitcast.217, bf16[1152,1024]{1,0:T(8,128)(2,1)} %get-tuple-element.29, bf16[1152,1024]{1,0:T(8,128)(2,1)S(1)} %copy-done.111), kind=kOutput, calls=%fused_computation.20 | convolution fusion | flops 9677307904 | bytes 17825792 | tf_op jit(solution)/shard_map/dot_general | solution.py:41
  567.3 7.9 constant_dynamic-slice_fusion.7
  577.6 28.8 %collective-permute-done.38 = bf16[1,2,256,2048]{3,2,1,0:T(8,128)(2,1)} collective-permute-done((bf16[1,2,256,2048]{3,2,1,0:T(8,128)(2,1)}, bf16[1,2,256,2048]{3,2,1,0:T(8,128)(2,1)}, u32[]{:S(2)}, u32[]{:S(2)}) %collective-permute-start.38) | collective-permute-done | bytes 2097184 | tf_op jit(solution)/shard_map/ppermute | solution.py:82
  622.8 6.0 fusion.51
  630.5 5.9 collective-permute-done.39
  640.2 5.1 collective-permute-start.11
  664.3 4.8 fusion.46
  684.4 6.8 multiply_add_fusion.1
  697.7 4.8 fusion.91
  710.8 9.1 convolution_convert_fusion.4
  719.9 28.9 %collective-permute-done.32 = bf16[2,1,512,2048]{3,2,1,0:T(8,128)(2,1)} collective-permute-done((bf16[2,1,512,2048]{3,2,1,0:T(8,128)(2,1)}, bf16[2,1,512,2048]{3,2,1,0:T(8,128)(2,1)}, u32[]{:S(2)}, u32[]{:S(2)}) %collective-permute-start.32) | collective-permute-done | bytes 4194336 | tf_op jit(solution)/shard_map/ppermute | solution.py:82
  748.9 5.6 add_convert_fusion.3
  757.0 9.6 %convolution_convert_fusion.9 = bf16[1024,2048]{1,0:T(8,128)(2,1)S(1)} fusion(bf16[1024,1536]{1,0:T(8,128)(2,1)S(1)} %copy-done.64, bf16[2048,1536]{1,0:T(8,128)(2,1)} %all-gather.5.cloned.1.call-done), kind=kOutput, calls=%fused_computation.83 | convolution fusion | flops 6444548096 | bytes 13631488 | tf_op jit(solution)/shard_map/dot_general | solution.py:45
  780.7 14.2 %collective-permute-done.12 = bf16[256,2048]{1,0:T(8,128)(2,1)} collective-permute-done((bf16[256,2048]{1,0:T(8,128)(2,1)}, bf16[256,2048]{1,0:T(8,128)(2,1)}, u32[]{:S(2)}, u32[]{:S(2)}) %collective-permute-start.12) | collective-permute-done | bytes 1048608 | tf_op jit(solution)/shard_map/ppermute | solution.py:82
  794.9 47.8 %collective-permute-done.13 = bf16[256,2048]{1,0:T(8,128)(2,1)} collective-permute-done((bf16[256,2048]{1,0:T(8,128)(2,1)}, bf16[256,2048]{1,0:T(8,128)(2,1)}, u32[]{:S(2)}, u32[]{:S(2)}) %collective-permute-start.13) | collective-permute-done | bytes 1048608 | tf_op jit(solution)/shard_map/ppermute | solution.py:82
  863.5 10.6 %collective-permute-start.18 = (f32[4368]{0:T(1024)S(1)}, f32[4368]{0:T(1024)S(1)}, u32[]{:S(2)}, u32[]{:S(2)}) collective-permute-start(f32[4368]{0:T(1024)S(1)} %maximum_select_fusion.2), channel_id=1, source_target_pairs={{0,2},{1,3},{2,0},{3,1},{4,6},{5,7},{6,4},{7,5},{8,10},{9,11},{10,... | collective-permute-start | bytes 52424 | tf_op jit(solution)/shard_map/ppermute | solution.py:340
  876.0 5.8 fusion.58
  895.8 5.4 collective-permute-done.30
  913.3 16.2 %collective-permute-done.20 = bf16[256,1536]{1,0:T(8,128)(2,1)S(1)} collective-permute-done((bf16[256,1536]{1,0:T(8,128)(2,1)}, bf16[256,1536]{1,0:T(8,128)(2,1)S(1)}, u32[]{:S(2)}, u32[]{:S(2)}) %collective-permute-start.20) | collective-permute-done | bytes 786464 | tf_op jit(solution)/shard_map/ppermute | solution.py:82
  929.6 15.7 %collective-permute-done.21 = bf16[256,1536]{1,0:T(8,128)(2,1)S(1)} collective-permute-done((bf16[256,1536]{1,0:T(8,128)(2,1)}, bf16[256,1536]{1,0:T(8,128)(2,1)S(1)}, u32[]{:S(2)}, u32[]{:S(2)}) %collective-permute-start.21) | collective-permute-done | bytes 786464 | tf_op jit(solution)/shard_map/ppermute | solution.py:82
  (514 shorter events, 228.5 us)
Async XLA Ops:
  7.2 67.0 %all-gather.5.cloned.1.call-start = ((), (), s32[]{:S(2)}) async-start(), calls=%async_computation.4 | async-start | bytes 7077888 | tf_op jit(solution)/shard_map/all_gather | solution.py:100
  10.4 150.6 %all-gather.7.cloned.1.call-start = ((), (), s32[]{:S(2)}) async-start(), calls=%async_computation.5 | async-start | bytes 10027008 | tf_op jit(solution)/shard_map/all_gather | solution.py:100
  11.7 232.1 %all-gather.11.cloned.1.call-start = ((), (), s32[]{:S(2)}) async-start(), calls=%async_computation.8 | async-start | bytes 9437184 | tf_op jit(solution)/shard_map/all_gather | solution.py:100
  12.4 313.5 %all-gather.9.cloned.1.call-start = ((), (), s32[]{:S(2)}) async-start(), calls=%async_computation.6 | async-start | bytes 9437184 | tf_op jit(solution)/shard_map/all_gather | solution.py:100
  12.5 52.2 %collective-permute-start = (bf16[256,2048]{1,0:T(8,128)(2,1)S(1)}, bf16[256,2048]{1,0:T(8,128)(2,1)S(1)}, u32[]{:S(2)}, u32[]{:S(2)}) collective-permute-start(bf16[256,2048]{1,0:T(8,128)(2,1)S(1)} %copy-done.15), channel_id=1, source_target_pairs={{0,8},{8,0},{16,24},{24,16},{1,9},{9,1},{17,25},{25,17},{2,10},{10... | collective-permute-start | bytes 3145736 | tf_op jit(solution)/shard_map/ppermute | solution.py:82
  14.0 50.7 %collective-permute-start.1 = (bf16[256,2048]{1,0:T(8,128)(2,1)S(1)}, bf16[256,2048]{1,0:T(8,128)(2,1)S(1)}, u32[]{:S(2)}, u32[]{:S(2)}) collective-permute-start(bf16[256,2048]{1,0:T(8,128)(2,1)S(1)} %copy-done.15), channel_id=1, source_target_pairs={{0,16},{8,24},{16,0},{24,8},{1,17},{9,25},{17,1},{25,9},{2,18},{10... | collective-permute-start | bytes 3145736 | tf_op jit(solution)/shard_map/ppermute | solution.py:82
  15.5 49.2 %collective-permute-start.2 = (bf16[256,2048]{1,0:T(8,128)(2,1)S(1)}, bf16[256,2048]{1,0:T(8,128)(2,1)S(1)}, u32[]{:S(2)}, u32[]{:S(2)}) collective-permute-start(bf16[256,2048]{1,0:T(8,128)(2,1)S(1)} %copy-done.15), channel_id=1, source_target_pairs={{0,24},{8,16},{16,8},{24,0},{1,25},{9,17},{17,9},{25,1},{2,26},{10... | collective-permute-start | bytes 3145736 | tf_op jit(solution)/shard_map/ppermute | solution.py:82
  16.0 43.9 %collective-permute-start.3 = (s32[1,256]{1,0:T(1,128)S(1)}, s32[1,256]{1,0:T(1,128)S(1)}, u32[]{:S(2)}, u32[]{:S(2)}) collective-permute-start(s32[1,256]{1,0:T(1,128)S(1)} %copy-done.104), channel_id=1, source_target_pairs={{0,8},{8,0},{16,24},{24,16},{1,9},{9,1},{17,25},{25,17},{2,10},{10... | collective-permute-start | bytes 3080 | tf_op jit(solution)/shard_map/ppermute | solution.py:82
  17.5 45.5 %collective-permute-start.4 = (s32[1,256]{1,0:T(1,128)S(1)}, s32[1,256]{1,0:T(1,128)S(1)}, u32[]{:S(2)}, u32[]{:S(2)}) collective-permute-start(s32[1,256]{1,0:T(1,128)S(1)} %copy-done.104), channel_id=1, source_target_pairs={{0,16},{8,24},{16,0},{24,8},{1,17},{9,25},{17,1},{25,9},{2,18},{10... | collective-permute-start | bytes 3080 | tf_op jit(solution)/shard_map/ppermute | solution.py:82
  60.0 4.5 collective-permute-start.5
  111.6 9.2 collective-permute-start.6
  113.1 13.8 %collective-permute-start.7 = (bf16[256,512]{0,1:T(8,128)(2,1)S(1)}, bf16[256,512]{0,1:T(8,128)(2,1)S(1)}, u32[]{:S(2)}, u32[]{:S(2)}) collective-permute-start(bf16[256,512]{0,1:T(8,128)(2,1)S(1)} %bitcast.252), channel_id=1, source_target_pairs={{0,16},{8,24},{16,0},{24,8},{1,17},{9,25},{17,1},{25,9},{2,18},{10... | collective-permute-start | bytes 786440 | tf_op jit(solution)/shard_map/ppermute | solution.py:82
  114.6 13.1 %collective-permute-start.8 = (bf16[256,512]{0,1:T(8,128)(2,1)S(1)}, bf16[256,512]{0,1:T(8,128)(2,1)S(1)}, u32[]{:S(2)}, u32[]{:S(2)}) collective-permute-start(bf16[256,512]{0,1:T(8,128)(2,1)S(1)} %bitcast.251), channel_id=1, source_target_pairs={{0,24},{8,16},{16,8},{24,0},{1,25},{9,17},{17,9},{25,1},{2,26},{10... | collective-permute-start | bytes 786440 | tf_op jit(solution)/shard_map/ppermute | solution.py:82
  169.7 445.4 %reduce-scatter.7.cloned.1.call-start = ((), (), s32[]{:S(2)}) async-start(), calls=%async_computation.9 | async-start | bytes 10027008 | tf_op jit(solution)/shard_map/reduce_scatter | solution.py:103
  476.5 399.5 %reduce-scatter.5.cloned.1.call-start = ((), (), s32[]{:S(2)}) async-start(), calls=%async_computation.7 | async-start | bytes 9437184 | tf_op jit(solution)/shard_map/reduce_scatter | solution.py:103
  509.9 375.4 %reduce-scatter.11.cloned.1.call-start = ((), (), s32[]{:S(2)}) async-start(), calls=%async_computation.11 | async-start | bytes 2433024 | tf_op jit(solution)/shard_map/reduce_scatter | solution.py:103
  511.9 116.9 %collective-permute-start.23 = (bf16[256,2048]{0,1:T(8,128)(2,1)}, bf16[256,2048]{0,1:T(8,128)(2,1)}, u32[]{:S(2)}, u32[]{:S(2)}) collective-permute-start(bf16[256,2048]{0,1:T(8,128)(2,1)} %constant_dynamic-update-slice_fusion.4), channel_id=1, source_target_pairs={{0,8},{8,0},{16,24},{24,16},{1,9},{9,1},{17,25},{25,17},{2,10},{10... | collective-permute-start | bytes 3145736 | tf_op jit(solution)/shard_map/ppermute | solution.py:82
  513.6 150.0 %collective-permute-start.24 = (bf16[256,2048]{0,1:T(8,128)(2,1)}, bf16[256,2048]{0,1:T(8,128)(2,1)}, u32[]{:S(2)}, u32[]{:S(2)}) collective-permute-start(bf16[256,2048]{0,1:T(8,128)(2,1)} %constant_dynamic-update-slice_fusion.4), channel_id=1, source_target_pairs={{0,16},{8,24},{16,0},{24,8},{1,17},{9,25},{17,1},{25,9},{2,18},{10... | collective-permute-start | bytes 3145736 | tf_op jit(solution)/shard_map/ppermute | solution.py:82
  515.1 148.5 %collective-permute-start.25 = (bf16[256,2048]{0,1:T(8,128)(2,1)}, bf16[256,2048]{0,1:T(8,128)(2,1)}, u32[]{:S(2)}, u32[]{:S(2)}) collective-permute-start(bf16[256,2048]{0,1:T(8,128)(2,1)} %constant_dynamic-update-slice_fusion.4), channel_id=1, source_target_pairs={{0,24},{8,16},{16,8},{24,0},{1,25},{9,17},{17,9},{25,1},{2,26},{10... | collective-permute-start | bytes 3145736 | tf_op jit(solution)/shard_map/ppermute | solution.py:82
  527.6 78.8 %collective-permute-start.38 = (bf16[1,2,256,2048]{3,2,1,0:T(8,128)(2,1)}, bf16[1,2,256,2048]{3,2,1,0:T(8,128)(2,1)}, u32[]{:S(2)}, u32[]{:S(2)}) collective-permute-start(bf16[1,2,256,2048]{3,2,1,0:T(8,128)(2,1)} %constant_dynamic-slice_fusion.1), channel_id=1, source_target_pairs={{0,16},{8,24},{16,0},{24,8},{1,17},{9,25},{17,1},{25,9},{2,18},{10... | collective-permute-start | bytes 6291464 | tf_op jit(solution)/shard_map/ppermute | solution.py:82
  536.7 73.9 %collective-permute-start.36 = (bf16[2,1,256,2048]{3,2,1,0:T(8,128)(2,1)}, bf16[2,1,256,2048]{3,2,1,0:T(8,128)(2,1)S(1)}, u32[]{:S(2)}, u32[]{:S(2)}) collective-permute-start(bf16[2,1,256,2048]{3,2,1,0:T(8,128)(2,1)} %constant_dynamic-slice_fusion.3), channel_id=1, source_target_pairs={{0,8},{8,0},{16,24},{24,16},{1,9},{9,1},{17,25},{25,17},{2,10},{10... | collective-permute-start | bytes 6291464 | tf_op jit(solution)/shard_map/ppermute | solution.py:82
  610.0 26.4 %collective-permute-start.39 = (bf16[1,1,256,2048]{3,2,1,0:T(8,128)(2,1)}, bf16[1,1,256,2048]{3,2,1,0:T(8,128)(2,1)}, u32[]{:S(2)}, u32[]{:S(2)}) collective-permute-start(bf16[1,1,256,2048]{3,2,1,0:T(8,128)(2,1)} %constant_dynamic-slice_fusion), channel_id=1, source_target_pairs={{0,8},{8,0},{16,24},{24,16},{1,9},{9,1},{17,25},{25,17},{2,10},{10... | collective-permute-start | bytes 3145736 | tf_op jit(solution)/shard_map/ppermute | solution.py:82
  613.7 26.5 %collective-permute-start.37 = (bf16[1,1,256,2048]{3,2,1,0:T(8,128)(2,1)}, bf16[1,1,256,2048]{3,2,1,0:T(8,128)(2,1)}, u32[]{:S(2)}, u32[]{:S(2)}) collective-permute-start(bf16[1,1,256,2048]{3,2,1,0:T(8,128)(2,1)} %constant_dynamic-slice_fusion.2), channel_id=1, source_target_pairs={{0,16},{8,24},{16,0},{24,8},{1,17},{9,25},{17,1},{25,9},{2,18},{10... | collective-permute-start | bytes 3145736 | tf_op jit(solution)/shard_map/ppermute | solution.py:82
  628.9 20.2 %collective-permute-start.9 = (bf16[256,512]{1,0:T(8,128)(2,1)S(1)}, bf16[256,512]{1,0:T(8,128)(2,1)S(1)}, u32[]{:S(2)}, u32[]{:S(2)}) collective-permute-start(bf16[256,512]{1,0:T(8,128)(2,1)S(1)} %get-tuple-element.58), channel_id=1, source_target_pairs={{0,8},{8,0},{16,24},{24,16},{1,9},{9,1},{17,25},{25,17},{2,10},{10... | collective-permute-start | bytes 786440 | tf_op jit(solution)/shard_map/ppermute | solution.py:82
  636.4 12.7 %collective-permute-start.10 = (bf16[256,512]{1,0:T(8,128)(2,1)S(1)}, bf16[256,512]{1,0:T(8,128)(2,1)S(1)}, u32[]{:S(2)}, u32[]{:S(2)}) collective-permute-start(bf16[256,512]{1,0:T(8,128)(2,1)S(1)} %get-tuple-element.57), channel_id=1, source_target_pairs={{0,16},{8,24},{16,0},{24,8},{1,17},{9,25},{17,1},{25,9},{2,18},{10... | collective-permute-start | bytes 786440 | tf_op jit(solution)/shard_map/ppermute | solution.py:82
  640.2 11.3 %collective-permute-start.11 = (bf16[256,512]{1,0:T(8,128)(2,1)S(1)}, bf16[256,512]{1,0:T(8,128)(2,1)S(1)}, u32[]{:S(2)}, u32[]{:S(2)}) collective-permute-start(bf16[256,512]{1,0:T(8,128)(2,1)S(1)} %get-tuple-element.56), channel_id=1, source_target_pairs={{0,24},{8,16},{16,8},{24,0},{1,25},{9,17},{17,9},{25,1},{2,26},{10... | collective-permute-start | bytes 786440 | tf_op jit(solution)/shard_map/ppermute | solution.py:82
  649.1 15.2 %collective-permute-start.26 = (bf16[256,512]{1,0:T(8,128)(2,1)}, bf16[256,512]{1,0:T(8,128)(2,1)}, u32[]{:S(2)}, u32[]{:S(2)}) collective-permute-start(bf16[256,512]{1,0:T(8,128)(2,1)} %get-tuple-element.54), channel_id=1, source_target_pairs={{0,8},{8,0},{16,24},{24,16},{1,9},{9,1},{17,25},{25,17},{2,10},{10... | collective-permute-start | bytes 786440 | tf_op jit(solution)/shard_map/ppermute | solution.py:82
  649.1 15.2 %collective-permute-start.27 = (bf16[256,512]{1,0:T(8,128)(2,1)S(1)}, bf16[256,512]{1,0:T(8,128)(2,1)}, u32[]{:S(2)}, u32[]{:S(2)}) collective-permute-start(bf16[256,512]{1,0:T(8,128)(2,1)S(1)} %get-tuple-element.53), channel_id=1, source_target_pairs={{0,16},{8,24},{16,0},{24,8},{1,17},{9,25},{17,1},{25,9},{2,18},{10... | collective-permute-start | bytes 786440 | tf_op jit(solution)/shard_map/ppermute | solution.py:82
  651.5 12.8 %collective-permute-start.28 = (bf16[256,512]{1,0:T(8,128)(2,1)S(1)}, bf16[256,512]{1,0:T(8,128)(2,1)}, u32[]{:S(2)}, u32[]{:S(2)}) collective-permute-start(bf16[256,512]{1,0:T(8,128)(2,1)S(1)} %get-tuple-element.52), channel_id=1, source_target_pairs={{0,24},{8,16},{16,8},{24,0},{1,25},{9,17},{17,9},{25,1},{2,26},{10... | collective-permute-start | bytes 786440 | tf_op jit(solution)/shard_map/ppermute | solution.py:82
  663.6 85.2 %collective-permute-start.32 = (bf16[2,1,512,2048]{3,2,1,0:T(8,128)(2,1)}, bf16[2,1,512,2048]{3,2,1,0:T(8,128)(2,1)}, u32[]{:S(2)}, u32[]{:S(2)}) collective-permute-start(bf16[2,1,512,2048]{3,2,1,0:T(8,128)(2,1)} %constant_dynamic-slice_fusion.7), channel_id=1, source_target_pairs={{0,8},{8,0},{16,24},{24,16},{1,9},{9,1},{17,25},{25,17},{2,10},{10... | collective-permute-start | bytes 12582920 | tf_op jit(solution)/shard_map/ppermute | solution.py:82
  663.6 108.4 %collective-permute-start.34 = (bf16[1,2,512,2048]{3,2,1,0:T(8,128)(2,1)}, bf16[1,2,512,2048]{3,2,1,0:T(8,128)(2,1)}, u32[]{:S(2)}, u32[]{:S(2)}) collective-permute-start(bf16[1,2,512,2048]{3,2,1,0:T(8,128)(2,1)} %constant_dynamic-slice_fusion.5), channel_id=1, source_target_pairs={{0,16},{8,24},{16,0},{24,8},{1,17},{9,25},{17,1},{25,9},{2,18},{10... | collective-permute-start | bytes 12582920 | tf_op jit(solution)/shard_map/ppermute | solution.py:82
  684.3 224.4 %reduce-scatter.9.cloned.1.call-start = ((), (), s32[]{:S(2)}) async-start(), calls=%async_computation.10 | async-start | bytes 7077888 | tf_op jit(solution)/shard_map/reduce_scatter | solution.py:103
  755.9 92.6 %collective-permute-start.33 = (bf16[1,1,512,2048]{3,2,1,0:T(8,128)(2,1)}, bf16[1,1,512,2048]{3,2,1,0:T(8,128)(2,1)}, u32[]{:S(2)}, u32[]{:S(2)}) collective-permute-start(bf16[1,1,512,2048]{3,2,1,0:T(8,128)(2,1)} %constant_dynamic-slice_fusion.6), channel_id=1, source_target_pairs={{0,16},{8,24},{16,0},{24,8},{1,17},{9,25},{17,1},{25,9},{2,18},{10... | collective-permute-start | bytes 6291464 | tf_op jit(solution)/shard_map/ppermute | solution.py:82
  768.5 26.4 %collective-permute-start.12 = (bf16[256,2048]{1,0:T(8,128)(2,1)}, bf16[256,2048]{1,0:T(8,128)(2,1)}, u32[]{:S(2)}, u32[]{:S(2)}) collective-permute-start(bf16[256,2048]{1,0:T(8,128)(2,1)} %get-tuple-element.38), channel_id=1, source_target_pairs={{0,8},{8,0},{16,24},{24,16},{1,9},{9,1},{17,25},{25,17},{2,10},{10... | collective-permute-start | bytes 3145736 | tf_op jit(solution)/shard_map/ppermute | solution.py:82
  770.1 72.6 %collective-permute-start.13 = (bf16[256,2048]{1,0:T(8,128)(2,1)}, bf16[256,2048]{1,0:T(8,128)(2,1)}, u32[]{:S(2)}, u32[]{:S(2)}) collective-permute-start(bf16[256,2048]{1,0:T(8,128)(2,1)} %get-tuple-element.40), channel_id=1, source_target_pairs={{0,16},{8,24},{16,0},{24,8},{1,17},{9,25},{17,1},{25,9},{2,18},{10... | collective-permute-start | bytes 3145736 | tf_op jit(solution)/shard_map/ppermute | solution.py:82
  771.4 71.3 %collective-permute-start.14 = (bf16[256,2048]{1,0:T(8,128)(2,1)}, bf16[256,2048]{1,0:T(8,128)(2,1)}, u32[]{:S(2)}, u32[]{:S(2)}) collective-permute-start(bf16[256,2048]{1,0:T(8,128)(2,1)} %get-tuple-element.39), channel_id=1, source_target_pairs={{0,24},{8,16},{16,8},{24,0},{1,25},{9,17},{17,9},{25,1},{2,26},{10... | collective-permute-start | bytes 3145736 | tf_op jit(solution)/shard_map/ppermute | solution.py:82
  776.4 80.2 %collective-permute-start.35 = (bf16[1,1,512,2048]{3,2,1,0:T(8,128)(2,1)S(1)}, bf16[1,1,512,2048]{3,2,1,0:T(8,128)(2,1)S(1)}, u32[]{:S(2)}, u32[]{:S(2)}) collective-permute-start(bf16[1,1,512,2048]{3,2,1,0:T(8,128)(2,1)S(1)} %constant_dynamic-slice_fusion.4), channel_id=1, source_target_pairs={{0,8},{8,0},{16,24},{24,16},{1,9},{9,1},{17,25},{25,17},{2,10},{10... | collective-permute-start | bytes 6291464 | tf_op jit(solution)/shard_map/ppermute | solution.py:82
  846.0 9.6 collective-permute-start.15
  855.6 3.8 collective-permute-start.16
  859.4 4.1 collective-permute-start.17
  863.5 12.4 %collective-permute-start.18 = (f32[4368]{0:T(1024)S(1)}, f32[4368]{0:T(1024)S(1)}, u32[]{:S(2)}, u32[]{:S(2)}) collective-permute-start(f32[4368]{0:T(1024)S(1)} %maximum_select_fusion.2), channel_id=1, source_target_pairs={{0,2},{1,3},{2,0},{3,1},{4,6},{5,7},{6,4},{7,5},{8,10},{9,11},{10,... | collective-permute-start | bytes 52424 | tf_op jit(solution)/shard_map/ppermute | solution.py:340
  875.9 5.9 collective-permute-start.19
  885.3 9.6 %collective-permute-start.29 = (bf16[256,528]{0,1:T(8,128)(2,1)}, bf16[256,528]{0,1:T(8,128)(2,1)S(1)}, u32[]{:S(2)}, u32[]{:S(2)}) collective-permute-start(bf16[256,528]{0,1:T(8,128)(2,1)} %reduce-scatter.11.cloned.1.call-done), channel_id=1, source_target_pairs={{0,8},{8,0},{16,24},{24,16},{1,9},{9,1},{17,25},{25,17},{2,10},{10... | collective-permute-start | bytes 811016 | tf_op jit(solution)/shard_map/ppermute | solution.py:82
  887.0 14.2 %collective-permute-start.30 = (bf16[256,528]{0,1:T(8,128)(2,1)}, bf16[256,528]{0,1:T(8,128)(2,1)}, u32[]{:S(2)}, u32[]{:S(2)}) collective-permute-start(bf16[256,528]{0,1:T(8,128)(2,1)} %reduce-scatter.11.cloned.1.call-done), channel_id=1, source_target_pairs={{0,16},{8,24},{16,0},{24,8},{1,17},{9,25},{17,1},{25,9},{2,18},{10... | collective-permute-start | bytes 811016 | tf_op jit(solution)/shard_map/ppermute | solution.py:82
  888.3 14.9 %collective-permute-start.31 = (bf16[256,528]{0,1:T(8,128)(2,1)S(1)}, bf16[256,528]{0,1:T(8,128)(2,1)}, u32[]{:S(2)}, u32[]{:S(2)}) collective-permute-start(bf16[256,528]{0,1:T(8,128)(2,1)S(1)} %copy-done.65), channel_id=1, source_target_pairs={{0,24},{8,16},{16,8},{24,0},{1,25},{9,17},{17,9},{25,1},{2,26},{10... | collective-permute-start | bytes 811016 | tf_op jit(solution)/shard_map/ppermute | solution.py:82
  908.7 20.7 %collective-permute-start.20 = (bf16[256,1536]{1,0:T(8,128)(2,1)}, bf16[256,1536]{1,0:T(8,128)(2,1)S(1)}, u32[]{:S(2)}, u32[]{:S(2)}) collective-permute-start(bf16[256,1536]{1,0:T(8,128)(2,1)} %reduce-scatter.9.cloned.1.call-done), channel_id=1, source_target_pairs={{0,8},{8,0},{16,24},{24,16},{1,9},{9,1},{17,25},{25,17},{2,10},{10... | collective-permute-start | bytes 2359304 | tf_op jit(solution)/shard_map/ppermute | solution.py:82
  910.3 35.0 %collective-permute-start.21 = (bf16[256,1536]{1,0:T(8,128)(2,1)}, bf16[256,1536]{1,0:T(8,128)(2,1)S(1)}, u32[]{:S(2)}, u32[]{:S(2)}) collective-permute-start(bf16[256,1536]{1,0:T(8,128)(2,1)} %reduce-scatter.9.cloned.1.call-done), channel_id=1, source_target_pairs={{0,16},{8,24},{16,0},{24,8},{1,17},{9,25},{17,1},{25,9},{2,18},{10... | collective-permute-start | bytes 2359304 | tf_op jit(solution)/shard_map/ppermute | solution.py:82
  911.4 34.2 %collective-permute-start.22 = (bf16[256,1536]{1,0:T(8,128)(2,1)}, bf16[256,1536]{1,0:T(8,128)(2,1)S(1)}, u32[]{:S(2)}, u32[]{:S(2)}) collective-permute-start(bf16[256,1536]{1,0:T(8,128)(2,1)} %reduce-scatter.9.cloned.1.call-done), channel_id=1, source_target_pairs={{0,24},{8,16},{16,8},{24,0},{1,25},{9,17},{17,9},{25,1},{2,26},{10... | collective-permute-start | bytes 2359304 | tf_op jit(solution)/shard_map/ppermute | solution.py:82
  (126 other events, 1321.9 us)
Sparse Core Ops, SparseCore 0:
  10.5 63.6 all-gather.4
  76.4 84.5 all-gather.6
  162.6 81.0 all-gather.10
  245.2 80.5 all-gather.8
  476.6 92.8 reduce-scatter.6
  571.6 87.9 reduce-scatter.4
  684.4 33.6 reduce-scatter.10
  720.4 69.7 reduce-scatter.8

commit v2 on v1

v2 whole, which is shorter than its diff:
```python
import functools

import jax
import jax.numpy as jnp
from jax import lax
from jax.experimental import pallas as pl
from jax.experimental.pallas import tpu as pltpu
from jax.sharding import PartitionSpec as P

HD = 128
EXPERTS = 16
CAP = 144

epsilon = 1e-06
rope_base = 10000.0
BF = jnp.bfloat16
F32 = jnp.float32


def rms_norm(values, gain):
    return values * lax.rsqrt(jnp.mean(values * values, axis=-1, keepdims=True) + epsilon) * gain


def rope_tables(length, width):
    places = jnp.arange(length, dtype=F32)
    rates = rope_base ** (-jnp.arange(width // 2, dtype=F32) * 2.0 / width)
    angle = places[:, None] * rates[None, :]
    return jnp.cos(angle), jnp.sin(angle)


def rotate(values, cosine, sine):
    half = values.shape[-1] // 2
    first = values[..., :half]
    second = values[..., half:]
    return jnp.concatenate(
        [first * cosine - second * sine, second * cosine + first * sine], axis=-1
    )


def dot(left, right):
    return jnp.dot(left, right, preferred_element_type=F32)


def dot_tn(left, right):
    return lax.dot_general(left, right, (((0,), (0,)), ((), ())), preferred_element_type=F32)


def dot_nt(left, right):
    return lax.dot_general(left, right, (((1,), (1,)), ((), ())), preferred_element_type=F32)


EXTRA = 16


def nothing(*refs):
    pass


def after(value, *others):
    held = pl.BlockSpec(memory_space=pl.ANY)
    return pl.pallas_call(
        nothing,
        in_specs=[held] * (1 + len(others)),
        out_specs=held,
        out_shape=jax.ShapeDtypeStruct(value.shape, value.dtype),
        input_output_aliases={0: 0},
        name="after",
    )(value, *others)


def expert_kernel(tile, wide, unread, who, *refs):
    (nf_a, nf_b, cot_a, cot_b, pick_a, pick_b, spread_a, spread_b) = refs[:8]
    (mask_a, mask_b, router, w_in, w_out) = refs[8:13]
    refs = refs[13 + unread :]
    rows, gp, cot_rows, scaled, moe, back_a, back_b, gates_hi, gates_lo = refs
    j = pl.program_id(0)
    cap = pick_a.shape[2]
    length = nf_a.shape[0]
    ff = w_out.shape[1]
    core, expert = who[3], who[4] + j

    @pl.when(j == 0)
    def _():
        for at, (nf, mask) in enumerate(((nf_a, mask_a), (nf_b, mask_b))):
            seen = mask[0] > 0.0
            logits = jnp.where(seen, dot(nf[...], router[...]), -1e30)
            powers = jnp.where(seen, jnp.exp(logits - jnp.max(logits, axis=1, keepdims=True)), 0.0)
            gates = powers / jnp.sum(powers, axis=1, keepdims=True)
            high = gates.astype(BF)
            gates_hi[at] = high
            gates_lo[at] = (gates - high.astype(F32)).astype(BF)

    pa, pb = pick_a[0, 0], pick_b[0, 0]
    lane = lax.broadcasted_iota(jnp.int32, (cap, router.shape[1]), 1)

    def slot_gates(p, at):
        every = dot(p, gates_hi[at]) + dot(p, gates_lo[at])
        return jnp.sum(jnp.where(lane == expert, every, 0.0), axis=1, keepdims=True)

    gate = jnp.concatenate([slot_gates(pa, 0), slot_gates(pb, 1)], axis=0)
    rows[0, :cap] = dot(pa, nf_a[...]).astype(BF)
    rows[0, cap:] = dot(pb, nf_b[...]).astype(BF)
    cot_rows[0, :cap] = dot(pa, cot_a[...]).astype(BF)
    cot_rows[0, cap:] = dot(pb, cot_b[...]).astype(BF)

    def forward(t, total):
        at = pl.multiple_of(t * tile, tile)
        g = dot(rows[0], w_in[0, :, pl.ds(at, tile)])
        u = dot(rows[0], w_in[0, :, pl.ds(ff + at, tile)])
        pulled = dot_nt(cot_rows[0], w_out[0, pl.ds(at, tile), :])
        sigma = jax.nn.sigmoid(g)
        silu = g * sigma
        active = silu * u
        scaled[0, :, pl.ds(at, tile)] = (active * gate).astype(BF)
        ga = pulled * gate
        gp[0, :, pl.ds(at, tile)] = (ga * u * sigma * (1.0 + g * (1.0 - sigma))).astype(BF)
        gp[0, :, pl.ds(ff + at, tile)] = (ga * silu).astype(BF)
        return total + jnp.sum(active * pulled, axis=1, keepdims=True)

    total = lax.fori_loop(0, ff // tile, forward, jnp.zeros((2 * cap, 1), F32))
    line = lax.broadcasted_iota(jnp.int32, (EXTRA, length), 0)
    place = 2 * (core * pl.num_programs(0) + j)
    for back, p, part in ((back_a, pa, total[:cap]), (back_b, pb, total[cap:])):
        by_token = jnp.sum(p.astype(F32) * part, axis=0, keepdims=True)
        high = by_token.astype(BF).astype(F32)
        new = jnp.where(line == place, high, jnp.where(line == place + 1, by_token - high, 0.0))

        @pl.when(j == 0)
        def _(back=back):
            back[length:, :] = jnp.zeros((EXTRA, back.shape[1]), BF)

        old = back[length:, :length].astype(F32)
        back[length:, :length] = (old + new).astype(BF)
    sa, sb = spread_a[0, 0], spread_b[0, 0]
    moe_a = pl.ds(pl.multiple_of(core * length, length), length)
    moe_b = pl.ds(pl.multiple_of((1 - core) * length, length), length)

    def backward(t, _):
        here = pl.ds(pl.multiple_of(t * wide, wide), wide)
        gr = dot_nt(gp[0], w_in[0, here, :]).astype(BF)
        res = dot(scaled[0], w_out[0, :, here]).astype(BF)
        for out, where, s, value in (
            (back_a, pl.ds(0, length), sa, gr[:cap]),
            (back_b, pl.ds(0, length), sb, gr[cap:]),
            (moe, moe_a, sa, res[:cap]),
            (moe, moe_b, sb, res[cap:]),
        ):
            old = jnp.where(j > 0, out[where, here].astype(F32), 0.0)
            out[where, here] = (dot(s, value) + old).astype(BF)
        return 0

    lax.fori_loop(0, w_in.shape[1] // wide, backward, 0)


def expert_block(k, rounds, who, nf, cot, pick, spread, mask, router, w_in, w_out, kept, first):
    length, width = nf[0].shape
    count, _, two_ff = w_in.shape
    groups = pick.shape[0]
    ff = two_ff // 2
    cap = pick.shape[2]
    lanes = router.shape[1]

    def whole(j, who):
        return (0, 0)

    def seq(i):
        return lambda j, who: (who[i], j, 0, 0)

    in_specs = [pl.BlockSpec((length, width), whole)] * 2
    if len(cot) == 2:
        in_specs += [pl.BlockSpec((length, width), whole)] * 2
    else:
        cot = [cot[0]] * 2
        in_specs += [
            pl.BlockSpec((length, width), lambda j, who, i=i: (who[i], 0)) for i in range(2)
        ]
    in_specs += [pl.BlockSpec((1, 1, cap, length), seq(i)) for i in range(2)]
    in_specs += [pl.BlockSpec((1, 1, length, cap), seq(i)) for i in range(2)]
    in_specs += [
        pl.BlockSpec((1, length, lanes), lambda j, who, i=i: (who[i], 0, 0)) for i in range(2)
    ]
    in_specs += [
        pl.BlockSpec((width, lanes), whole),
        pl.BlockSpec((1, width, two_ff), lambda j, who: (j, 0, 0)),
        pl.BlockSpec((1, ff, width), lambda j, who: (j, 0, 0)),
    ]
    args = [*nf, *cot, pick, pick, spread, spread, mask, mask, router, w_in, w_out]
    total = rounds * 2 * cap
    saved = [(count, total, n) for n in (width, two_ff, width, ff)]
    out_shape = [jax.ShapeDtypeStruct(s, BF) for s in saved]
    out_shape += [jax.ShapeDtypeStruct((groups * length, width), BF)]
    out_shape += [jax.ShapeDtypeStruct((length + EXTRA, width), BF)] * 2
    out_specs = [pl.BlockSpec((1, 2 * cap, s[2]), lambda j, who: (j, k, 0)) for s in saved]
    out_specs += [pl.BlockSpec((2 * length, width), lambda j, who: (who[2], 0))]
    out_specs += [pl.BlockSpec((length + EXTRA, width), whole)] * 2
    aliases = {}
    if kept is not None:
        aliases = {1 + len(args) + i: i for i in range(len(kept))}
        in_specs += [pl.BlockSpec(memory_space=pl.ANY)] * len(kept)
        args += list(kept)
    in_specs += [pl.BlockSpec(memory_space=pl.ANY)] * len(first)
    args += list(first)
    results = pl.pallas_call(
        functools.partial(expert_kernel, min(512, ff), min(1024, width), len(aliases) + len(first)),
        grid_spec=pltpu.PrefetchScalarGridSpec(
            num_scalar_prefetch=1,
            grid=(count,),
            in_specs=in_specs,
            out_specs=out_specs,
            scratch_shapes=[pltpu.VMEM((2, length, lanes), BF)] * 2,
        ),
        out_shape=out_shape,
        input_output_aliases=aliases,
        compiler_params=pltpu.CompilerParams(vmem_limit_bytes=60 * 2**20),
        cost_estimate=pl.CostEstimate(
            flops=count * 2 * cap * width * ff * 12 * 2,
            bytes_accessed=count * 3 * width * ff * 2 + 20 * length * width * 2,
            transcendentals=0,
        ),
        name="experts",
    )(who, *args)
    return results[:5], results[5], results[6]


def out_kernel(replicas, groups, who, *refs):
    pieces = refs[:replicas]
    near, far, tokens, gain = refs[replicas : replicas + 4]
    hidden, normed, mixed = refs[replicas + 4 :]
    part = pieces[0].shape[1]
    depth = near.shape[1] // (groups // 2)
    for q in range(replicas):
        mixed[:, pl.ds(pl.multiple_of((who[0] ^ q) * part, part), part)] = pieces[q][...]
    for q in range(replicas):
        total = jnp.zeros((tokens.shape[0], part), F32)
        for k in range(groups // 2):
            for flip, source in enumerate((near, far)):
                at = ((who[2] ^ flip) * (groups // 2) + k) * depth
                left = mixed[:, pl.ds(pl.multiple_of(at, depth), depth)]
                total += dot(left, source[q, k * depth : (k + 1) * depth])
        here = pl.ds(pl.multiple_of((who[0] ^ q) * part, part), part)
        hidden[:, here] = tokens[:, here].astype(F32) + total
    value = hidden[...]
    scale = lax.rsqrt(jnp.mean(value * value, axis=1, keepdims=True) + epsilon)
    normed[...] = (value * scale * gain[...]).astype(BF)


def out_step(who, pieces, near, far, tokens, gain):
    replicas = len(pieces)
    length, width = tokens.shape
    groups = lax.axis_size("fsdp")
    vmem = pl.BlockSpec(memory_space=pltpu.VMEM)
    return pl.pallas_call(
        functools.partial(out_kernel, replicas, groups),
        in_specs=[pl.BlockSpec(memory_space=pltpu.SMEM)] + [vmem] * (replicas + 4),
        out_specs=[vmem] * 3,
        out_shape=[
            jax.ShapeDtypeStruct((length, width), F32),
            jax.ShapeDtypeStruct((length, width), BF),
            jax.ShapeDtypeStruct((length, width), BF),
        ],
        compiler_params=pltpu.CompilerParams(vmem_limit_bytes=48 * 2**20),
        name="attention_out",
    )(who, *pieces, near, far, tokens, gain)


def back_kernel(replicas, groups, experts, who, *refs):
    rounds = groups // 2
    shares = refs[:rounds]
    hidden, normed, cot, gain, gates, router, near, far = refs[rounds : rounds + 8]
    grad_hidden, gain_grad, router_grad = refs[rounds + 8 : rounds + 11]
    attn = refs[rounds + 11 : rounds + 11 + replicas]
    out = refs[rounds + 11 + replicas :]
    length, width = hidden.shape
    lanes = router.shape[1]
    part = width // replicas
    depth = width // groups
    per_chip = experts // rounds
    line = lax.broadcasted_iota(jnp.int32, (EXTRA, lanes), 0)
    lane = lax.broadcasted_iota(jnp.int32, (EXTRA, lanes), 1)
    summed = jnp.zeros((length, width), F32)
    grad_gates = jnp.zeros((length, lanes), F32)
    for k in range(rounds):
        summed += shares[k][:length].astype(F32)
        chip = who[1] ^ k
        place = (lane == chip * per_chip + line // 2) & (line < 2 * per_chip)
        grad_gates += dot_tn(shares[k][length:, :length], place.astype(BF))
    own = gates[...]
    centered = grad_gates - jnp.sum(own * grad_gates, axis=1, keepdims=True)
    grad_logits = (own * centered).astype(BF)
    router_grad[...] = dot_tn(normed[...], grad_logits).astype(BF)
    grad_normed = summed + dot_nt(grad_logits, router[...])
    value = hidden[...]
    scale = lax.rsqrt(jnp.mean(value * value, axis=1, keepdims=True) + epsilon)
    gain_grad[...] = jnp.sum(grad_normed * value * scale, axis=0, keepdims=True)
    pulled = grad_normed * gain[...]
    inner = jnp.mean(pulled * value, axis=1, keepdims=True)
    total = cot[...].astype(F32) + scale * pulled - value * (scale * scale * scale * inner)
    grad_hidden[...] = total
    for q in range(replicas):
        here = pl.ds(pl.multiple_of((who[0] ^ q) * part, part), part)
        attn[q][...] = grad_hidden[:, here].astype(BF)
    for k in range(rounds):
        for flip, source in enumerate((near, far)):
            block = jnp.zeros((length, depth), F32)
            for q in range(replicas):
                block += dot_nt(attn[q][...], source[q, k * depth : (k + 1) * depth])
            at = ((who[2] ^ flip) * (groups // 2) + k) * depth
            out[0][:, pl.ds(pl.multiple_of(at, depth), depth)] = block.astype(BF)


def back_step(who, shares, hidden, normed, cot, gain, gates, router, near, far, experts):
    replicas = near.shape[0]
    length, width = hidden.shape
    groups = 2 * len(shares)
    vmem = pl.BlockSpec(memory_space=pltpu.VMEM)
    piece = jax.ShapeDtypeStruct((length, width // replicas), BF)
    results = pl.pallas_call(
        functools.partial(back_kernel, replicas, groups, experts),
        in_specs=[pl.BlockSpec(memory_space=pltpu.SMEM)] + [vmem] * (len(shares) + 8),
        out_specs=[vmem] * (4 + replicas),
        out_shape=[
            jax.ShapeDtypeStruct((length, width), F32),
            jax.ShapeDtypeStruct((1, width), F32),
            jax.ShapeDtypeStruct((width, router.shape[1]), BF),
            *[piece] * replicas,
            jax.ShapeDtypeStruct((length, width), BF),
        ],
        compiler_params=pltpu.CompilerParams(vmem_limit_bytes=48 * 2**20),
        name="attention_back",
    )(who, *shares, hidden, normed, cot, gain, gates, router, near, far)
    return results[0], results[1], results[2], results[3 : 3 + replicas], results[3 + replicas]


def turn(value, cosine, sine):
    return value * cosine + pltpu.roll(value, value.shape[1] // 2, 1) * sine


def attend_kernel(heads, normed, weight, seg_row, seg_col, cosine, sine, gains, *outs):
    raw, ready, mixed, totals, tops = outs
    allowed = seg_col[0] == seg_row[0]
    lane = lax.broadcasted_iota(jnp.int32, totals.shape, 1)
    top_lane = lax.broadcasted_iota(jnp.int32, tops.shape[1:], 1)
    part = heads * HD
    totals[...] = jnp.zeros(totals.shape, F32)
    tops[0] = jnp.zeros(tops.shape[1:], F32)
    for i in range(2):
        raw[:, i * part : (i + 1) * part] = dot(normed[...], weight[:, i * part : (i + 1) * part])
    ready[:, 2 * part :] = dot(normed[...], weight[:, 2 * part : 3 * part]).astype(BF)
    for h in range(heads):
        rotated = []
        for i in range(2):
            at = slice(i * part + h * HD, i * part + (h + 1) * HD)
            head = raw[:, at]
            norm = lax.rsqrt(jnp.mean(head * head, axis=1, keepdims=True) + epsilon)
            rotated.append(turn(head * norm * gains[i : i + 1], cosine[...], sine[...]).astype(BF))
            ready[:, at] = rotated[i]
        scores = dot_nt(rotated[0], rotated[1]) * HD**-0.5
        scores = jnp.where(allowed, scores, -1e30)
        peak = jnp.max(scores, axis=1, keepdims=True)
        powers = jnp.exp(scores - peak)
        total = peak + jnp.log(jnp.sum(powers, axis=1, keepdims=True))
        weights = jnp.exp(scores - total).astype(BF)
        here = slice(h * HD, (h + 1) * HD)
        mixed[:, here] = dot(weights, ready[:, 2 * part + h * HD : 2 * part + (h + 1) * HD]).astype(BF)
        totals[...] = jnp.where(lane == h, total, totals[...])
        tops[0] = jnp.where(top_lane == h, jnp.max(peak, axis=0, keepdims=True), tops[0])


def attend(normed, weight, segments, cosine, sine, gains, heads):
    count, length = segments.shape
    rows, width = normed.shape
    part = heads * HD
    one = lambda n: (n, 0)
    fixed = lambda n: (0, 0)
    return pl.pallas_call(
        functools.partial(attend_kernel, heads),
        grid=(count,),
        in_specs=[
            pl.BlockSpec((length, width), one),
            pl.BlockSpec((width, 3 * part), fixed, pipeline_mode=pl.Buffered(1)),
            pl.BlockSpec((1, 1, length), lambda n: (n, 0, 0)),
            pl.BlockSpec((1, length, 1), lambda n: (n, 0, 0)),
            pl.BlockSpec((length, HD), fixed),
            pl.BlockSpec((length, HD), fixed),
            pl.BlockSpec((2, HD), fixed),
        ],
        out_specs=[
            pl.BlockSpec((length, 2 * part), one),
            pl.BlockSpec((length, 3 * part), one),
            pl.BlockSpec((length, part), one),
            pl.BlockSpec((length, 128), one),
            pl.BlockSpec((1, 1, 128), lambda n: (n, 0, 0)),
        ],
        out_shape=[
            jax.ShapeDtypeStruct((rows, 2 * part), F32),
            jax.ShapeDtypeStruct((rows, 3 * part), BF),
            jax.ShapeDtypeStruct((rows, part), BF),
            jax.ShapeDtypeStruct((rows, 128), F32),
            jax.ShapeDtypeStruct((count, 1, 128), F32),
        ],
        compiler_params=pltpu.CompilerParams(vmem_limit_bytes=48 * 2**20),
        cost_estimate=pl.CostEstimate(
            flops=rows * width * 3 * part * 4, bytes_accessed=8 * rows * width, transcendentals=0
        ),
        name="attention",
    )(normed, weight, segments[:, None, :], segments[:, :, None], cosine, sine, gains)


def attend_back_kernel(heads, pull, raw, ready, totals, seg_row, seg_col, cosine, sine, gains, grad, gain_grads):
    allowed = seg_col[0] == seg_row[0]
    lane = lax.broadcasted_iota(jnp.int32, totals.shape, 1)
    part = heads * HD
    sums = [jnp.zeros((1, HD), F32)] * 2
    for h in range(heads):
        at = [slice(i * part + h * HD, i * part + (h + 1) * HD) for i in range(3)]
        query, key, value = (ready[:, a] for a in at)
        pulled = pull[:, h * HD : (h + 1) * HD]
        total = jnp.sum(jnp.where(lane == h, totals[...], 0.0), axis=1, keepdims=True)
        scores = dot_nt(query, key) * HD**-0.5
        probs = jnp.where(allowed, jnp.exp(jnp.where(allowed, scores - total, 0.0)), 0.0)
        grad_weights = dot_nt(pulled, value)
        grad[:, at[2]] = dot_tn(probs.astype(BF), pulled).astype(BF)
        inner = jnp.sum(probs * grad_weights, axis=1, keepdims=True)
        grad_scores = (probs * (grad_weights - inner)).astype(BF)
        both = (dot(grad_scores, key), dot_tn(grad_scores, query))
        for i, g in enumerate(both):
            g = g * HD**-0.5
            back = g * cosine[...] - pltpu.roll(g, HD // 2, 1) * sine[...]
            head = raw[:, at[i]]
            norm = lax.rsqrt(jnp.mean(head * head, axis=1, keepdims=True) + epsilon)
            sums[i] = sums[i] + jnp.sum(back * head * norm, axis=0, keepdims=True)
            scaled = back * gains[i : i + 1]
            mean = jnp.mean(scaled * head, axis=1, keepdims=True)
            grad[:, at[i]] = (norm * scaled - head * (norm * norm * norm * mean)).astype(BF)
    for i in range(2):
        gain_grads[0, i : i + 1] = sums[i]


def attend_back(pull, raw, ready, totals, segments, cosine, sine, gains, heads):
    count, length = segments.shape
    rows = raw.shape[0]
    part = heads * HD
    one = lambda n: (n, 0)
    fixed = lambda n: (0, 0)
    return pl.pallas_call(
        functools.partial(attend_back_kernel, heads),
        grid=(count,),
        in_specs=[
            pl.BlockSpec((length, part), one),
            pl.BlockSpec((length, 2 * part), one),
            pl.BlockSpec((length, 3 * part), one),
            pl.BlockSpec((length, 128), one),
            pl.BlockSpec((1, 1, length), lambda n: (n, 0, 0)),
            pl.BlockSpec((1, length, 1), lambda n: (n, 0, 0)),
            pl.BlockSpec((length, HD), fixed),
            pl.BlockSpec((length, HD), fixed),
            pl.BlockSpec((2, HD), fixed),
        ],
        out_specs=[
            pl.BlockSpec((length, 3 * part), one),
            pl.BlockSpec((1, 2, HD), lambda n: (n, 0, 0)),
        ],
        out_shape=[
            jax.ShapeDtypeStruct((rows, 3 * part), BF),
            jax.ShapeDtypeStruct((count, 2, HD), F32),
        ],
        compiler_params=pltpu.CompilerParams(vmem_limit_bytes=32 * 2**20),
        cost_estimate=pl.CostEstimate(
            flops=0, bytes_accessed=0, transcendentals=0
        ),
        name="attention_grad",
    )(pull, raw, ready, totals, segments[:, None, :], segments[:, :, None], cosine, sine, gains)


def weight_grad_kernel(half, quarters, left, right, *outs):
    j, i = pl.program_id(0), pl.program_id(1)
    block = dot_tn(left[0], right[0]).astype(BF)
    for at, out in enumerate(outs):

        @pl.when((j == at // 2) & ((i >= half) == (at % 2 == 1)))
        def _(out=out):
            out[0] = block


def weight_grads(quarters, left, right, parts):
    count, rows, width = left.shape
    size, n = width // parts, right.shape[2]
    half = parts // 2

    def spot(at):
        def index(j, i, quarters):
            step = j * parts + i - (at // 2 * parts + at % 2 * half)
            return (jnp.clip(step, 0, half - 1), 0, 0)

        return index

    return pl.pallas_call(
        functools.partial(weight_grad_kernel, half),
        grid_spec=pltpu.PrefetchScalarGridSpec(
            num_scalar_prefetch=1,
            grid=(count, parts),
            in_specs=[
                pl.BlockSpec((1, rows, size), lambda j, i, quarters: (j, 0, quarters[j, i])),
                pl.BlockSpec((1, rows, n), lambda j, i, quarters: (j, 0, 0)),
            ],
            out_specs=[pl.BlockSpec((1, size, n), spot(at)) for at in range(2 * count)],
        ),
        out_shape=[jax.ShapeDtypeStruct((half, size, n), BF)] * (2 * count),
        compiler_params=pltpu.CompilerParams(vmem_limit_bytes=56 * 2**20),
        cost_estimate=pl.CostEstimate(flops=0, bytes_accessed=0, transcendentals=0),
        name="weight_grads",
    )(quarters, left, right)


def product_kernel(left, right, out):
    out[...] = dot_tn(left[...], right[...]).astype(BF)


def product(left, right):
    rows, width = left.shape
    n = right.shape[1]
    size = min(width, 256)
    return pl.pallas_call(
        product_kernel,
        grid=(width // size,),
        in_specs=[
            pl.BlockSpec((rows, size), lambda i: (0, i)),
            pl.BlockSpec((rows, n), lambda i: (0, 0)),
        ],
        out_specs=pl.BlockSpec((size, n), lambda i: (i, 0)),
        out_shape=jax.ShapeDtypeStruct((width, n), BF),
        compiler_params=pltpu.CompilerParams(vmem_limit_bytes=32 * 2**20),
        cost_estimate=pl.CostEstimate(flops=0, bytes_accessed=0, transcendentals=0),
        name="product",
    )(left, right)


def spread_kernel(grad, weight, *outs):
    block = dot_nt(grad[...], weight[...]).astype(BF)
    for at, out in enumerate(outs):

        @pl.when(pl.program_id(0) == at)
        def _(out=out):
            out[...] = block


def normed_grads(grad, weight, count):
    rows, n = grad.shape
    width = weight.shape[0]
    length = rows // count
    return pl.pallas_call(
        spread_kernel,
        grid=(count,),
        in_specs=[
            pl.BlockSpec((length, n), lambda i: (i, 0)),
            pl.BlockSpec((width, n), lambda i: (0, 0), pipeline_mode=pl.Buffered(1)),
        ],
        out_specs=[pl.BlockSpec((length, width), lambda i: (0, 0))] * count,
        out_shape=[jax.ShapeDtypeStruct((length, width), BF)] * count,
        compiler_params=pltpu.CompilerParams(vmem_limit_bytes=48 * 2**20),
        cost_estimate=pl.CostEstimate(flops=10**11, bytes_accessed=0, transcendentals=0),
        name="normed_grads",
    )(grad, weight)


def halve_kernel(half, blocks, keep, got, send_out, keep_out):
    block = (keep[0].astype(F32) + got[0].astype(F32)).astype(BF)

    @pl.when(pl.program_id(0) < half)
    def _():
        send_out[0] = block

    @pl.when(pl.program_id(0) >= half)
    def _():
        keep_out[0] = block


def halve(blocks, keep, got):
    count, size, n = keep.shape
    half = count // 2
    here = pl.BlockSpec((1, size, n), lambda i, blocks: (blocks[i], 0, 0))
    return pl.pallas_call(
        functools.partial(halve_kernel, half),
        grid_spec=pltpu.PrefetchScalarGridSpec(
            num_scalar_prefetch=1,
            grid=(count,),
            in_specs=[here, here],
            out_specs=[
                pl.BlockSpec((1, size, n), lambda i, blocks: (jnp.minimum(i, half - 1), 0, 0)),
                pl.BlockSpec((1, size, n), lambda i, blocks: (jnp.maximum(i - half, 0), 0, 0)),
            ],
        ),
        out_shape=[jax.ShapeDtypeStruct((half, size, n), BF)] * 2,
        compiler_params=pltpu.CompilerParams(vmem_limit_bytes=32 * 2**20),
        cost_estimate=pl.CostEstimate(flops=0, bytes_accessed=0, transcendentals=0),
        name="halve",
    )(blocks, keep, got)


def join_kernel(*refs):
    out = refs[-1]
    for j in range((len(refs) - 1) // 2):

        @pl.when(pl.program_id(0) == j)
        def _(j=j):
            out[0] = refs[2 * j][...].astype(F32) + refs[2 * j + 1][...].astype(F32)


def join(pairs):
    size, n = pairs[0][0].shape
    step = min(size, 256)
    count = len(pairs)

    def spot(at):
        def index(j, i):
            k = j * (size // step) + i - at * (size // step)
            return (jnp.clip(k, 0, size // step - 1), 0)

        return index

    return pl.pallas_call(
        join_kernel,
        grid=(count, size // step),
        in_specs=[pl.BlockSpec((step, n), spot(at // 2)) for at in range(2 * count)],
        out_specs=pl.BlockSpec((1, step, n), lambda j, i: (j, i, 0)),
        out_shape=jax.ShapeDtypeStruct((count, size, n), F32),
        compiler_params=pltpu.CompilerParams(vmem_limit_bytes=48 * 2**20),
        name="join",
    )(*[v for pair in pairs for v in pair])


def local(
    tokens,
    cotangent,
    segment_ids,
    expert_index,
    clip_threshold,
    attn_norm_gain,
    w_query,
    w_key,
    w_value,
    w_output,
    query_gain,
    key_gain,
    ffn_norm_gain,
    router,
    expert_in,
    expert_out,
):
    replicas = lax.axis_size("replica")
    groups = lax.axis_size("fsdp")
    me_r = lax.axis_index("replica")
    me_f = lax.axis_index("fsdp")
    core = me_f % 2
    length, width = tokens.shape
    part = width // replicas
    heads = part // HD
    ff = expert_out.shape[1]
    local_experts = expert_in.shape[0]
    scale = HD ** (-0.5)
    attn_gain = attn_norm_gain.astype(F32)
    ffn_gain = ffn_norm_gain.astype(F32)
    gain_query = query_gain.astype(F32)
    gain_key = key_gain.astype(F32)

    def swap(value, k):
        return lax.ppermute(value, "replica", [(r, r ^ k) for r in range(replicas)])

    def columns(value, k, axis=1):
        return lax.dynamic_slice_in_dim(value, (me_r ^ k) * part, part, axis)

    def spread(value):
        return [value] + [swap(value, k) for k in range(1, replicas)]

    def trade_columns(value):
        return [columns(value, 0)] + [swap(columns(value, k), k) for k in range(1, replicas)]

    def join_columns(blocks):
        out = jnp.zeros((blocks[0].shape[0], part * replicas), blocks[0].dtype)
        for k, block in enumerate(blocks):
            out = lax.dynamic_update_slice_in_dim(out, block, (me_r ^ k) * part, 1)
        return out

    def cross(value, k):
        return lax.ppermute(value, "fsdp", [(f, f ^ k) for f in range(groups)])

    def pass_on(up, down, hop):
        chips = groups // 2
        pairs = [(2 * a + i, 2 * a + 2 + i) for a in range(hop - 1, chips - 1) for i in (0, 1)]
        back = [(2 * a + 2 + i, 2 * a + i) for a in range(chips - hop) for i in (0, 1)]
        return lax.ppermute(up, "fsdp", pairs), lax.ppermute(down, "fsdp", back)

    def choose(up, down, k):
        chips = groups // 2
        found = {}
        for a in range(chips):
            b = a ^ k
            found.setdefault((b > a, abs(b - a)), []).append(a)
        picked = None
        for (above, hop), at in found.items():
            source = down[hop] if above else up[hop]
            if picked is None:
                picked = source
            else:
                here = functools.reduce(jnp.logical_or, [me_f // 2 == a for a in at])
                picked = jnp.where(here, source, picked)
        return picked

    def gather(value):
        return lax.all_gather(value, "fsdp", axis=0, tiled=True)

    def reduce(value):
        return lax.psum_scatter(value, "fsdp", scatter_dimension=0, tiled=True)

    bits = replicas.bit_length() - 1

    def next_bit(j, step):
        return 1 << (bits - 1 - step if j % 2 else step)

    def next_halves(traded, j, step):
        keep, got = traded
        left = keep.shape[0]
        place = jnp.arange(left, dtype=jnp.int32)
        here = left // 2 if j % 2 else 1
        mine = (me_r & next_bit(j, step)) != 0
        other = ((place & here) != 0) != mine
        spots = jnp.where(other, jnp.cumsum(other) - 1, left // 2 + jnp.cumsum(~other) - 1)
        return halve(jnp.zeros((left,), jnp.int32).at[spots].set(place), keep, got)

    index_table = expert_index.astype(BF).reshape(w_query.shape[0], -1)
    sent = [columns(w_output, 0), router, index_table]
    sizes = [v.shape[1] for v in sent]
    sent.append(jnp.zeros((w_query.shape[0], -sum(sizes) % 128), BF))
    quarter = gather(jnp.concatenate(sent, axis=1))
    full_router = quarter[:, part : part + EXPERTS]
    full_index = quarter[:, part + EXPERTS : part + EXPERTS + sizes[2]].astype(jnp.int32)
    full_index = full_index.reshape(groups * length, -1)
    ids = jnp.arange(EXPERTS, dtype=jnp.int32)
    mask = jnp.any(full_index[:, :, None] == ids, axis=1).reshape(groups, length, EXPERTS)
    first = me_f * local_experts
    hot = lax.dynamic_slice_in_dim(mask, first, local_experts, 2)
    order = jnp.arange(length, dtype=jnp.int32)
    before = (order[:, None] < order[None, :]).astype(BF)
    rank = jnp.einsum("nsj,st->njt", hot.astype(BF), before, preferred_element_type=F32)
    rank = jnp.where(hot.transpose(0, 2, 1), rank.astype(jnp.int32), -1)
    slots = jnp.arange(CAP, dtype=jnp.int32)
    pick = (rank[:, :, None, :] == slots[:, None]).astype(BF)
    spots = (rank[:, :, :, None] == slots).astype(BF)
    lanes = 128
    mask_wide = jnp.pad(mask.astype(F32), ((0, 0), (0, 0), (0, lanes - EXPERTS)))
    router_wide = jnp.pad(full_router, ((0, 0), (0, lanes - EXPERTS)))
    tables = (pick, spots, mask_wide, router_wide)
    segments = jnp.concatenate(spread(segment_ids), axis=0)
    tokens_all = spread(tokens)
    normed = jnp.concatenate(
        [rms_norm(v.astype(F32), attn_gain).astype(BF) for v in tokens_all], axis=0
    )
    rounds = groups // 2
    where = jnp.stack([me_r, me_f // 2, core]).astype(jnp.int32)
    half = lax.dynamic_slice(quarter, (core * (width // 2), 0), (width // 2, part))
    near = spread(after(half, normed))
    near[1] = after(near[1], *tables)
    normed = after(normed, *near[1:])
    near = jnp.stack(near)
    far = cross(near, 1)
    w_qkv = gather(jnp.concatenate([columns(w, 0) for w in (w_query, w_key, w_value)], axis=1))
    cot_all = gather(cotangent)
    cot_pair = (cotangent, cross(cotangent, 1))

    cosine, sine = rope_tables(length, HD)
    cosine = jnp.concatenate([cosine, cosine], axis=1)
    sine = jnp.concatenate([-sine, sine], axis=1)
    gains = jnp.stack([gain_query, gain_key])
    raw, ready, mixed_heads, totals, tops = attend(normed, w_qkv, segments, cosine, sine, gains, heads
    )
    my_max = jnp.max(tops, axis=(0, 1))[:heads]
    mixed_heads = mixed_heads.reshape(replicas, length, part)
    pieces = [mixed_heads[0]] + [swap(mixed_heads[k], k) for k in range(1, replicas)]
    inputs = tokens.astype(F32)
    hidden, normed_ffn, mixed = out_step(where, pieces, near, far, tokens, ffn_gain[None, :])
    mixed_all = spread(mixed)

    def first_bit(j):
        return 1 << (bits - 1 if j % 2 else 0)

    numbers = jnp.arange(replicas, dtype=jnp.int32)
    quarters = []
    for j in range(local_experts):
        other = ((numbers ^ me_r) & first_bit(j)) != 0
        place = jnp.where(other, jnp.cumsum(other) - 1, replicas // 2 + jnp.cumsum(~other) - 1)
        quarters.append(jnp.zeros((replicas,), jnp.int32).at[place].set(numbers))
    quarters = jnp.stack(quarters)
    kept = None
    shares = []
    added = []
    pending = []
    up, down = [normed_ffn], [normed_ffn]
    for k in range(rounds):
        chip = (me_f // 2) ^ k
        who = jnp.stack([2 * chip + core, 2 * chip + 1 - core, chip, core, first])
        if k + 1 < rounds:
            next_up, next_down = pass_on(up[-1], down[-1], k + 1)
        mine = choose(up, down, k) if k else normed_ffn
        nf = (mine, cross(mine, 1))
        kept, back_a, back_b = expert_block(k, rounds, who, nf, (cot_all,) if k else cot_pair, pick, spots, mask_wide, router_wide, expert_in, expert_out, kept, pending
        )
        if k + 1 < rounds:
            up.append(after(next_up, back_a))
            down.append(after(next_down, back_a))
        else:
            rows, grad_projected, cot_rows, scaled, moe = kept
            out_blocks = weight_grads(quarters, scaled, cot_rows, replicas)
        if k == rounds - 1:
            back_b = after(back_b, *out_blocks, *shares[1:])
        share = (back_a.astype(F32) + cross(back_b, 1).astype(F32)).astype(BF)
        added.append(share)
        if k == rounds - 2:
            pending = [*added[1:], mixed_all[-1]]
        else:
            pending = mixed_all[1:-1] if k == rounds - 3 else []
        shares.append(share if k == 0 else cross(share, 2 * k))
    out_traded = [
        (out_blocks[2 * j + 1], swap(out_blocks[2 * j], first_bit(j))) for j in range(local_experts)
    ]
    in_blocks = weight_grads(quarters, after(rows, share), grad_projected, replicas)
    shares[-1] = after(shares[-1], *in_blocks, *[v[1] for v in out_traded])
    output = (hidden + reduce(after(moe, shares[-1])).astype(F32)).astype(BF)

    my_mask = lax.dynamic_index_in_dim(mask_wide, me_f, 0, keepdims=False) > 0.0
    logits = jnp.where(my_mask, dot(normed_ffn, router_wide), -jnp.inf)
    powers = jnp.exp(logits - jnp.max(logits, axis=1, keepdims=True))
    my_gates = powers / jnp.sum(powers, axis=1, keepdims=True)
    grad_hidden, ffn_gain_grad, router_grad, attn_pieces, grad_mixed = back_step(
        where, shares, hidden, normed_ffn, cotangent, ffn_gain[None, :], my_gates, router_wide, near, far, EXPERTS
    )
    ffn_gain_grad = ffn_gain_grad[0]
    router_grad = router_grad[:, :EXPERTS]
    grad_mixed = jnp.stack(trade_columns(grad_mixed), axis=0)
    sends = [after(in_blocks[2 * j], grad_mixed) for j in range(local_experts)]
    in_traded = [
        (in_blocks[2 * j + 1], swap(v, first_bit(j))) for j, v in enumerate(sends)
    ]
    grad_mixed = after(grad_mixed, *sends)
    grad_qkv, gain_grads = attend_back(grad_mixed.reshape(replicas * length, part), raw, ready, totals, segments, cosine, sine, gains, heads
    )
    query_gain_grad, key_gain_grad = jnp.sum(gain_grads, axis=0)
    qkv_grad = product(normed, grad_qkv)
    w_late = after(w_qkv, qkv_grad, *[v[1] for v in in_traded])
    attn_columns = [attn_pieces[0]] + [
        swap(after(attn_pieces[k], *sends), k) for k in range(1, replicas)
    ]
    in_halves = [next_halves(v, j, 1) for j, v in enumerate(in_traded)]
    in_sends = [after(v, *attn_columns[1:]) for v, _ in in_halves]
    in_done = [(keep, swap(v, next_bit(j, 1))) for j, (v, (_, keep)) in enumerate(zip(in_sends, in_halves))]
    w_late = after(w_late, *in_sends)
    part_normed = normed_grads(grad_qkv, w_late, replicas)
    grad_normed = after(part_normed[0], *[v[1] for v in in_done]).astype(F32)
    for k in range(1, replicas):
        grad_normed = grad_normed + swap(part_normed[k], k).astype(F32)
    attn_value, attn_back = jax.vjp(rms_norm, inputs, attn_gain)
    grad_inputs_norm, attn_gain_grad = attn_back(grad_normed)
    input_grad = (grad_hidden + grad_inputs_norm).astype(BF)

    share_qkv = reduce(qkv_grad)
    attn_columns = jnp.concatenate(attn_columns, axis=0)
    output_grad = dot_tn(jnp.concatenate(mixed_all, axis=0), attn_columns)
    share_qkv = after(share_qkv, output)
    share_o = after(reduce(jnp.concatenate([output_grad.astype(BF), router_grad], axis=1)), share_qkv)
    blocks_o = spread(share_o)
    total_output = join_columns([b[:, :part].astype(F32) for b in blocks_o])
    total_router = sum(b[:, part:].astype(F32) for b in blocks_o)
    blocks_qkv = spread(share_qkv)
    total_query, total_key, total_value = (
        join_columns([b[:, i * part : (i + 1) * part].astype(F32) for b in blocks_qkv])
        for i in range(3)
    )

    out_last = [(keep, after(got, grad_normed)) for keep, got in out_traded]
    out_halves = [next_halves(v, j, 1) for j, v in enumerate(out_last)]
    out_done = [
        (keep, swap(after(v, *blocks_qkv[1:]), next_bit(j, 1)))
        for j, (v, keep) in enumerate(out_halves)
    ]

    def settle(traded):
        pairs = []
        for j, (keep, got) in enumerate(traded):
            for step in range(2, bits):
                send, keep = next_halves((keep, got), j, step)
                got = swap(send, next_bit(j, step))
            pairs.append((keep[0], got[0]))
        return join(pairs)

    expert_in_grad = settle(in_done)
    expert_out_grad = settle(out_done)

    top_heads = lax.dynamic_update_slice_in_dim(
        jnp.full((replicas * heads,), -jnp.inf, F32), my_max, me_r * heads, 0
    )
    sums = jnp.concatenate([attn_gain_grad, query_gain_grad, key_gain_grad, ffn_gain_grad])
    small = jnp.concatenate([sums, top_heads])
    n_sums = sums.shape[0]
    is_sum = jnp.arange(small.shape[0]) < n_sums

    def merge(a, b):
        return jnp.where(is_sum, a + b, jnp.maximum(a, b))

    small = functools.reduce(merge, spread(small))
    small = merge(small, cross(small, 1))
    small = functools.reduce(merge, [small] + [cross(small, 2 * k) for k in range(1, rounds)])
    attn_gain_total = small[:width]
    query_gain_total = small[width : width + HD]
    key_gain_total = small[width + HD : width + 2 * HD]
    ffn_gain_total = small[width + 2 * HD : n_sums]
    head_max = small[n_sums:]
    threshold = clip_threshold.astype(F32)
    factor = threshold / jnp.maximum(head_max, threshold)
    column_scale = jnp.repeat(jnp.sqrt(factor), HD)
    clipped_query = (w_query.astype(F32) * column_scale[None, :]).astype(BF)
    clipped_key = (w_key.astype(F32) * column_scale[None, :]).astype(BF)
    return (
        output,
        input_grad,
        attn_gain_total,
        total_query,
        total_key,
        total_value,
        total_output,
        query_gain_total,
        key_gain_total,
        ffn_gain_total,
        total_router,
        expert_in_grad,
        expert_out_grad,
        head_max,
        clipped_query,
        clipped_key,
    )


def solution(mesh):
    both = ("replica", "fsdp")
    return jax.shard_map(
        local,
        mesh=mesh,
        in_specs=(
            P(both, None),
            P(both, None),
            P(both, None),
            P(both, None),
            P(),
            P(),
            P("fsdp", None),
            P("fsdp", None),
            P("fsdp", None),
            P("fsdp", None),
            P(),
            P(),
            P(),
            P("fsdp", None),
            P("fsdp", None, None),
            P("fsdp", None, None),
        ),
        out_specs=(
            P(both, None),
            P(both, None),
            P(),
            P("fsdp", None),
            P("fsdp", None),
            P("fsdp", None),
            P("fsdp", None),
            P(),
            P(),
            P(),
            P("fsdp", None),
            P("fsdp", "replica", None),
            P("fsdp", "replica", None),
            P(),
            P("fsdp", None),
            P("fsdp", None),
        ),
        check_vma=False,
    )
```

time: 968 us -> 816 us (0.84)
  Pallas kernels: 0 us -> 278 us
  matrix products: 280 us -> 5.91 us
  waiting for transfers between devices: 402 us -> 300 us
  local copies, waits for them, and re-layouts: 97.6 us -> 67.7 us
  other arithmetic: 82.9 us -> 63.8 us
  blocking collectives: 14.1 us -> 0 us
  starting transfers between devices: 62.6 us -> 73.8 us
    pallas_call x0 -> x48, Pallas kernels: none -> 278 us  [the longest x4 131 us: expert_block(): pl.pallas_call(functools.partial(expert_kernel, min(512, ff), min(1024, w...]
    all_gather x4 -> x3, waiting for transfers between devices: 170 us -> 0.04 us  [gather(): return lax.all_gather(value, 'fsdp', axis=0, tiled=True)]
    dot_general x26 -> x1, matrix products: 156 us -> 0.16 us  [local(): jnp.einsum('nsj,st->njt', hot.astype(BF), before, preferred_element_type=...]
    dot_general x7 -> x1, matrix products: 66.9 us -> 1.4 us  [dot(): return jnp.dot(left, right, preferred_element_type=F32)]
    ppermute x37 -> x41, waiting for transfers between devices: 229 us -> 294 us  [swap(): return lax.ppermute(value, 'replica', [(r, r ^ k) for r in range(replicas)])]
    dot_general x7 -> x1, matrix products: 57.5 us -> 4.35 us  [dot_tn(): lax.dot_general(left, right, (((0,), (0,)), ((), ())), preferred_element_...]
    unnamed x263 -> x212, local copies, waits for them, and re-layouts: 20.6 us -> 46.9 us
    ppermute x3 -> x23, starting transfers between devices: 10.8 us -> 27 us  [the longest x6 16.3 us: pass_on(): return (lax.ppermute(up, 'fsdp', pairs), lax.ppermute(down, 'fsdp', back))]
  transfers between devices with their start and end apart: 48 -> 70, of which waited for: 22 -> 31; matrix products, arithmetic and copies ran while one was open for 30% -> 11% of each run, Pallas kernels for 0% -> 34%
where the time goes in v2:
time: 816 us; the launch traced here: 804 us
  waiting for transfers between devices  300 us (37%)
  Pallas kernels  278 us (34%)
  starting transfers between devices  73.8 us (9%)
  local copies, waits for them, and re-layouts  67.7 us (8%)
  other arithmetic  63.8 us (8%)
  between operations  15.7 us (2%)
    ppermute x41, waiting for transfers between devices, swap(): return lax.ppermute(value, 'replica', [(r, r ^ k) for r in range(replicas)])  294 us
    pallas_call x4, Pallas kernels, expert_block(): pl.pallas_call(functools.partial(expert_kernel, min(512, ff), min(1024, w...  131 us
    pallas_call x2, Pallas kernels, weight_grads(): pl.pallas_call(functools.partial(weight_grad_kernel, half), grid_spec=plt...  52.9 us
    unnamed x212, local copies, waits for them, and re-layouts  46.9 us
    ppermute x41, starting transfers between devices, swap(): return lax.ppermute(value, 'replica', [(r, r ^ k) for r in range(replicas)])  46.1 us
  transfers between devices with their start and end apart: 70, of which 31 were waited for; matrix products, arithmetic and copies ran while one was open for 11% of the time, Pallas kernels for 34%

profile of v2, /device:TPU:8, one launch (start us, length us, event | category | flops | bytes accessed | tf_op | source)
XLA Modules:
  0.0 804.5 jit_solution(14151388829396232741)
XLA Ops:
  17.1 22.1 %collective-permute-done = bf16[256,2048]{1,0:T(8,128)(2,1)S(1)} collective-permute-done((bf16[256,2048]{1,0:T(8,128)(2,1)S(1)}, bf16[256,2048]{1,0:T(8,128)(2,1)S(1)}, u32[]{:S(2)}, u32[]{:S(2)}) %collective-permute-start) | collective-permute-done | bytes 1048608 | tf_op jit(solution)/shard_map/ppermute | solution.py:667
  39.5 22.2 %collective-permute-done.1 = bf16[256,2048]{1,0:T(8,128)(2,1)S(1)} collective-permute-done((bf16[256,2048]{1,0:T(8,128)(2,1)S(1)}, bf16[256,2048]{1,0:T(8,128)(2,1)S(1)}, u32[]{:S(2)}, u32[]{:S(2)}) %collective-permute-start.1) | collective-permute-done | bytes 1048608 | tf_op jit(solution)/shard_map/ppermute | solution.py:667
  89.5 7.4 collective-permute-done.3.refs_0_
  97.9 20.4 %collective-permute-done.4.refs_2_ = bf16[1024,512]{1,0:T(8,128)(2,1)} collective-permute-done((bf16[1024,512]{1,0:T(8,128)(2,1)}, bf16[1024,512]{1,0:T(8,128)(2,1)}, u32[]{:S(2)}, u32[]{:S(2)}) %collective-permute-start.4) | collective-permute-done | bytes 1048608 | tf_op jit(solution)/shard_map/ppermute | solution.py:667
  118.3 3.9 pad_maximum_fusion.1.refs_4_.refs_10_
  128.8 14.3 %attention.1 = (f32[1024,1024]{1,0:T(8,128)}, bf16[1024,1536]{1,0:T(8,128)(2,1)S(1)}, bf16[1024,512]{1,0:T(8,128)(2,1)S(1)}, f32[1024,128]{1,0:T(8,128)S(1)}, f32[4,1,128]{2,1,0:T(1,128)S(1)}) custom-call(bf16[1024,2048]{1,0:T(8,128)(2,1)} %after.32.normed.left, bf16[2048,1536]{1,0:T(8,128)(2,1)} %all-gather.6.cloned.1.call-done.weight.refs_0_, ...), custom_call_target="tpu_custom_call" | custom-call | flops 12884901888 | bytes 16777216 | tf_op jit(solution)/shard_map/attention/pallas_call | solution.py:375
  149.4 5.8 collective-permute-done.9.refs_1_
  155.9 4.4 collective-permute-done.10.refs_2_
  164.6 7.3 attention_out.1
  174.1 3.5 collective-permute-start.13
  177.5 3.4 collective-permute-start.17
  180.9 32.8 %experts.4 = (bf16[2,1152,2048]{2,1,0:T(8,128)(2,1)}, bf16[2,1152,2048]{2,1,0:T(8,128)(2,1)}, bf16[2,1152,2048]{2,1,0:T(8,128)(2,1)}, bf16[2,1152,1024]{2,1,0:T(...) custom-call(s32[5]{0:T(128)} %stack.140.who, ...), custom_call_target="tpu_custom_call" | custom-call | flops 28991029248 | bytes 46137344 | tf_op jit(solution)/shard_map/experts/pallas_call | solution.py:203
  219.7 3.6 collective-permute-start.16
  225.3 32.8 %experts.5 = (bf16[2,1152,2048]{2,1,0:T(8,128)(2,1)}, bf16[2,1152,2048]{2,1,0:T(8,128)(2,1)}, bf16[2,1152,2048]{2,1,0:T(8,128)(2,1)}, bf16[2,1152,1024]{2,1,0:T(...) custom-call(s32[5]{0:T(128)} %stack.144.who, ...), custom_call_target="tpu_custom_call", output_to_operand_aliasing={{0}: (14, {}), {1}: (15, {}), {2}: (16, {}), {3}: (17, {}),... | custom-call | flops 28991029248 | bytes 46137344 | tf_op jit(solution)/shard_map/experts/pallas_call | solution.py:203
  269.1 32.9 %experts.6 = (bf16[2,1152,2048]{2,1,0:T(8,128)(2,1)}, bf16[2,1152,2048]{2,1,0:T(8,128)(2,1)}, bf16[2,1152,2048]{2,1,0:T(8,128)(2,1)}, bf16[2,1152,1024]{2,1,0:T(...) custom-call(s32[5]{0:T(128)} %stack.148.who, ...), custom_call_target="tpu_custom_call", output_to_operand_aliasing={{0}: (14, {}), {1}: (15, {}), {2}: (16, {}), {3}: (17, {}),... | custom-call | flops 28991029248 | bytes 46137344 | tf_op jit(solution)/shard_map/experts/pallas_call | solution.py:203
  305.2 3.2 add_convert_fusion.3.refs_18_
  308.4 2.7 add_convert_fusion.2.refs_19_
  311.1 3.9 collective-permute-start.30
  315.0 14.3 %collective-permute-done.28.refs_20_ = bf16[256,2048]{1,0:T(8,128)(2,1)} collective-permute-done((bf16[256,2048]{1,0:T(8,128)(2,1)S(1)}, bf16[256,2048]{1,0:T(8,128)(2,1)}, u32[]{:S(2)}, u32[]{:S(2)}) %collective-permute-start.28) | collective-permute-done | bytes 1048608 | tf_op jit(solution)/shard_map/ppermute | solution.py:667
  330.3 32.6 %experts.7 = (bf16[2,1152,2048]{2,1,0:T(8,128)(2,1)}, bf16[2,1152,2048]{2,1,0:T(8,128)(2,1)}, bf16[2,1152,2048]{2,1,0:T(8,128)(2,1)}, bf16[2,1152,1024]{2,1,0:T(...) custom-call(s32[5]{0:T(128)} %stack.137.who, ...), custom_call_target="tpu_custom_call", output_to_operand_aliasing={{0}: (14, {}), {1}: (15, {}), {2}: (16, {}), {3}: (17, {}),... | custom-call | flops 28991029248 | bytes 46137344 | tf_op jit(solution)/shard_map/experts/pallas_call | solution.py:203
  362.9 20.4 %weight_grads.2 = (bf16[2,256,2048]{2,1,0:T(8,128)(2,1)}, bf16[2,256,2048]{2,1,0:T(8,128)(2,1)}, bf16[2,256,2048]{2,1,0:T(8,128)(2,1)}, bf16[2,256,2048]{2,1,0:T(8,128)(2,1)}) custom-call(s32[2,4]{1,0:T(2,128)} %pad_add_fusion.1.quarters, bf16[2,1152,1024]{2,1,0:T(8,128)(2,1)} %get-tuple-element.109.left, bf16[2,1152,2048]{2,1,0:T(8,128)(2,1)} %get-tuple-element.110.right), custom_call_target="tpu_custom_call" | custom-call | tf_op jit(solution)/shard_map/weight_grads/pallas_call | solution.py:497
  391.2 32.6 %weight_grads.3 = (bf16[2,512,2048]{2,1,0:T(8,128)(2,1)}, bf16[2,512,2048]{2,1,0:T(8,128)(2,1)}, bf16[2,512,2048]{2,1,0:T(8,128)(2,1)}, bf16[2,512,2048]{2,1,0:T(8,128)(2,1)}) custom-call(s32[2,4]{1,0:T(2,128)} %pad_add_fusion.1.quarters, bf16[2,1152,2048]{2,1,0:T(8,128)(2,1)} %after.40.left, bf16[2,1152,2048]{2,1,0:T(8,128)(2,1)} %get-tuple-element.116.right), custom_call_target="tpu_custom_call" | custom-call | tf_op jit(solution)/shard_map/weight_grads/pallas_call | solution.py:497
  423.7 8.9 %collective-permute-done.33.refs_5_.refs_0_ = bf16[2,256,2048]{2,1,0:T(8,128)(2,1)} collective-permute-done((bf16[2,256,2048]{2,1,0:T(8,128)(2,1)}, bf16[2,256,2048]{2,1,0:T(8,128)(2,1)}, u32[]{:S(2)}, u32[]{:S(2)}) %collective-permute-start.33) | collective-permute-done | bytes 2097184 | tf_op jit(solution)/shard_map/ppermute | solution.py:667
  433.0 2.7 collective-permute-done.32.refs_0_
  440.3 3.0 add_convert_fusion.refs_0_
  443.3 11.4 %attention_back.1 = (f32[256,2048]{1,0:T(8,128)}, f32[1,2048]{1,0:T(1,128)S(1)}, bf16[2048,128]{1,0:T(8,128)(2,1)S(1)}, bf16[256,512]{1,0:T(8,128)(2,1)S(1)}, bf...) custom-call(s32[3]{0:T(128)S(1)} %copy-done.51, ...), custom_call_target="tpu_custom_call" | custom-call | tf_op jit(solution)/shard_map/attention_back/pallas_call | solution.py:317
  459.0 6.6 collective-permute-done.38
  465.6 4.7 collective-permute-done.37
  479.2 14.1 %attention_grad.1 = (bf16[1024,1536]{1,0:T(8,128)(2,1)S(1)}, f32[4,2,128]{2,1,0:T(2,128)S(1)}) custom-call(bf16[1024,512]{1,0:T(8,128)(2,1)S(1)} %bitcast.68, f32[1024,1024]{1,0:T(8,128)S(1)} %copy-done.13, bf16[1024,1536]{1,0:T(8,128)(2,1)S(1)} %copy-done.20, f32[1024,128]{1,0:T(8,128)S(1)} %copy-done.38, s32[4,1,256]{2,1,0:T(1,128)S(1)} %copy-done.49, ...), custom_call_target="tpu_custom_call" | custom-call | tf_op jit(solution)/shard_map/attention_grad/pallas_call | solution.py:445
  493.3 8.7 %product.1.refs_1_ = bf16[2048,1536]{1,0:T(8,128)(2,1)S(1)} custom-call(bf16[1024,2048]{1,0:T(8,128)(2,1)S(1)} %copy-done.2, bf16[1024,1536]{1,0:T(8,128)(2,1)S(1)} %get-tuple-element.127.right.grad), custom_call_target="tpu_custom_call" | custom-call | tf_op jit(solution)/shard_map/product/pallas_call | solution.py:523
  502.0 2.6 copy-done.3
  511.9 53.3 %collective-permute-done.39.refs_2_.got = bf16[2,512,2048]{2,1,0:T(8,128)(2,1)} collective-permute-done((bf16[2,512,2048]{2,1,0:T(8,128)(2,1)}, bf16[2,512,2048]{2,1,0:T(8,128)(2,1)}, u32[]{:S(2)}, u32[]{:S(2)}) %collective-permute-start.39) | collective-permute-done | bytes 4194336 | tf_op jit(solution)/shard_map/ppermute | solution.py:667
  567.4 4.5 halve.4
  580.5 4.4 halve.5
  588.4 12.6 %normed_grads.1 = (bf16[256,2048]{1,0:T(8,128)(2,1)S(1)}, bf16[256,2048]{1,0:T(8,128)(2,1)}, bf16[256,2048]{1,0:T(8,128)(2,1)}, bf16[256,2048]{1,0:T(8,128)(2,1)}) custom-call(bf16[1024,1536]{1,0:T(8,128)(2,1)} %copy-done.21, bf16[2048,1536]{1,0:T(8,128)(2,1)} %after.52.weight), custom_call_target="tpu_custom_call" | custom-call | flops 99999997952 | tf_op jit(solution)/shard_map/normed_grads/pallas_call | solution.py:551
  605.8 4.4 fusion.9
  611.9 13.9 %collective-permute-done.44.refs_1_ = bf16[1,512,2048]{2,1,0:T(8,128)(2,1)} collective-permute-done((bf16[1,512,2048]{2,1,0:T(8,128)(2,1)}, bf16[1,512,2048]{2,1,0:T(8,128)(2,1)}, u32[]{:S(2)}, u32[]{:S(2)}) %collective-permute-start.44) | collective-permute-done | bytes 2097184 | tf_op jit(solution)/shard_map/ppermute | solution.py:667
  625.8 10.7 %collective-permute-done.45.refs_2_ = bf16[1,512,2048]{2,1,0:T(8,128)(2,1)} collective-permute-done((bf16[1,512,2048]{2,1,0:T(8,128)(2,1)}, bf16[1,512,2048]{2,1,0:T(8,128)(2,1)}, u32[]{:S(2)}, u32[]{:S(2)}) %collective-permute-start.45) | collective-permute-done | bytes 2097184 | tf_op jit(solution)/shard_map/ppermute | solution.py:667
  636.5 22.7 %collective-permute-done.48 = bf16[256,2048]{1,0:T(8,128)(2,1)} collective-permute-done((bf16[256,2048]{1,0:T(8,128)(2,1)}, bf16[256,2048]{1,0:T(8,128)(2,1)}, u32[]{:S(2)}, u32[]{:S(2)}) %collective-permute-start.48) | collective-permute-done | bytes 1048608 | tf_op jit(solution)/shard_map/ppermute | solution.py:667
  659.2 9.4 %collective-permute-done.47 = bf16[256,2048]{1,0:T(8,128)(2,1)} collective-permute-done((bf16[256,2048]{1,0:T(8,128)(2,1)}, bf16[256,2048]{1,0:T(8,128)(2,1)}, u32[]{:S(2)}, u32[]{:S(2)}) %collective-permute-start.47) | collective-permute-done | bytes 1048608 | tf_op jit(solution)/shard_map/ppermute | solution.py:667
  668.5 10.3 %collective-permute-done.46 = bf16[256,2048]{1,0:T(8,128)(2,1)} collective-permute-done((bf16[256,2048]{1,0:T(8,128)(2,1)}, bf16[256,2048]{1,0:T(8,128)(2,1)}, u32[]{:S(2)}, u32[]{:S(2)}) %collective-permute-start.46) | collective-permute-done | bytes 1048608 | tf_op jit(solution)/shard_map/ppermute | solution.py:667
  678.9 3.5 fusion.16
  696.5 2.9 halve.6
  703.0 3.0 halve.7
  706.1 8.0 %join.2 = f32[2,512,2048]{2,1,0:T(8,128)} custom-call(bf16[512,2048]{1,0:T(8,128)(2,1)S(1)} %bitcast.69, bf16[512,2048]{1,0:T(8,128)(2,1)} %bitcast.42.refs_1_, bf16[512,2048]{1,0:T(8,128)(2,1)} %bitcast.70, bf16[512,2048]{1,0:T(8,128)(2,1)} %bitcast.44.refs_3_), custom_call_target="tpu_custom_call" | custom-call | tf_op jit(solution)/shard_map/join/pallas_call | solution.py:621
  727.5 20.5 %collective-permute-done.59 = bf16[256,528]{1,0:T(8,128)(2,1)S(1)} collective-permute-done((bf16[256,528]{1,0:T(8,128)(2,1)}, bf16[256,528]{1,0:T(8,128)(2,1)S(1)}, u32[]{:S(2)}, u32[]{:S(2)}) %collective-permute-start.59) | collective-permute-done | bytes 270368 | tf_op jit(solution)/shard_map/ppermute | solution.py:667
  751.9 19.3 %collective-permute-done.60 = bf16[256,528]{1,0:T(8,128)(2,1)S(1)} collective-permute-done((bf16[256,528]{1,0:T(8,128)(2,1)}, bf16[256,528]{1,0:T(8,128)(2,1)S(1)}, u32[]{:S(2)}, u32[]{:S(2)}) %collective-permute-start.60) | collective-permute-done | bytes 270368 | tf_op jit(solution)/shard_map/ppermute | solution.py:667
  784.1 10.7 %collective-permute-done.62 = bf16[1,256,2048]{2,1,0:T(8,128)(2,1)S(1)} collective-permute-done((bf16[1,256,2048]{2,1,0:T(8,128)(2,1)}, bf16[1,256,2048]{2,1,0:T(8,128)(2,1)S(1)}, u32[]{:S(2)}, u32[]{:S(2)}) %collective-permute-start.62) | collective-permute-done | bytes 1048608 | tf_op jit(solution)/shard_map/ppermute | solution.py:667
  (480 shorter events, 185.6 us)
Async XLA Ops:
  7.2 61.1 %all-gather.4.cloned.1.call-start = ((), (), s32[]{:S(2)}) async-start(), calls=%async_computation.3 | async-start | bytes 2949120 | tf_op jit(solution)/shard_map/all_gather | solution.py:710
  9.9 118.1 %all-gather.6.cloned.1.call-start = ((), (), s32[]{:S(2)}) async-start(), calls=%async_computation.4 | async-start | bytes 7077888 | tf_op jit(solution)/shard_map/all_gather | solution.py:710
  13.1 212.2 %all-gather.8.cloned.1.call-start = ((), (), s32[]{:S(2)}) async-start(), calls=%async_computation.5 | async-start | bytes 9437184 | tf_op jit(solution)/shard_map/all_gather | solution.py:710
  13.1 26.1 %collective-permute-start = (bf16[256,2048]{1,0:T(8,128)(2,1)S(1)}, bf16[256,2048]{1,0:T(8,128)(2,1)S(1)}, u32[]{:S(2)}, u32[]{:S(2)}) collective-permute-start(bf16[256,2048]{1,0:T(8,128)(2,1)S(1)} %copy-done.5), channel_id=1, source_target_pairs={{0,8},{8,0},{16,24},{24,16},{1,9},{9,1},{17,25},{25,17},{2,10},{10... | collective-permute-start | bytes 3145736 | tf_op jit(solution)/shard_map/ppermute | solution.py:667
  14.7 47.1 %collective-permute-start.1 = (bf16[256,2048]{1,0:T(8,128)(2,1)S(1)}, bf16[256,2048]{1,0:T(8,128)(2,1)S(1)}, u32[]{:S(2)}, u32[]{:S(2)}) collective-permute-start(bf16[256,2048]{1,0:T(8,128)(2,1)S(1)} %copy-done.5), channel_id=1, source_target_pairs={{0,16},{8,24},{16,0},{24,8},{1,17},{9,25},{17,1},{25,9},{2,18},{10... | collective-permute-start | bytes 3145736 | tf_op jit(solution)/shard_map/ppermute | solution.py:667
  16.2 45.8 %collective-permute-start.2 = (bf16[256,2048]{1,0:T(8,128)(2,1)S(1)}, bf16[256,2048]{1,0:T(8,128)(2,1)}, u32[]{:S(2)}, u32[]{:S(2)}) collective-permute-start(bf16[256,2048]{1,0:T(8,128)(2,1)S(1)} %copy-done.5), channel_id=1, source_target_pairs={{0,24},{8,16},{16,8},{24,0},{1,25},{9,17},{17,9},{25,1},{2,26},{10... | collective-permute-start | bytes 3145736 | tf_op jit(solution)/shard_map/ppermute | solution.py:667
  16.7 701.1 %reduce-scatter.4.cloned.1.call-start = ((), (), s32[]{:S(2)}) async-start(), calls=%async_computation.6 | async-start | bytes 9437184 | tf_op jit(solution)/shard_map/reduce_scatter | solution.py:713
  70.6 26.3 %collective-permute-start.3 = (bf16[1024,512]{1,0:T(8,128)(2,1)}, bf16[1024,512]{1,0:T(8,128)(2,1)S(1)}, u32[]{:S(2)}, u32[]{:S(2)}) collective-permute-start(bf16[1024,512]{1,0:T(8,128)(2,1)} %after.30), channel_id=1, source_target_pairs={{0,8},{8,0},{16,24},{24,16},{1,9},{9,1},{17,25},{25,17},{2,10},{10... | collective-permute-start | bytes 3145736 | tf_op jit(solution)/shard_map/ppermute | solution.py:667
  71.7 46.6 %collective-permute-start.4 = (bf16[1024,512]{1,0:T(8,128)(2,1)}, bf16[1024,512]{1,0:T(8,128)(2,1)}, u32[]{:S(2)}, u32[]{:S(2)}) collective-permute-start(bf16[1024,512]{1,0:T(8,128)(2,1)} %after.30), channel_id=1, source_target_pairs={{0,16},{8,24},{16,0},{24,8},{1,17},{9,25},{17,1},{25,9},{2,18},{10... | collective-permute-start | bytes 3145736 | tf_op jit(solution)/shard_map/ppermute | solution.py:667
  72.7 45.6 %collective-permute-start.5 = (bf16[1024,512]{1,0:T(8,128)(2,1)}, bf16[1024,512]{1,0:T(8,128)(2,1)}, u32[]{:S(2)}, u32[]{:S(2)}) collective-permute-start(bf16[1024,512]{1,0:T(8,128)(2,1)} %after.30), channel_id=1, source_target_pairs={{0,24},{8,16},{16,8},{24,0},{1,25},{9,17},{17,9},{25,1},{2,26},{10... | collective-permute-start | bytes 3145736 | tf_op jit(solution)/shard_map/ppermute | solution.py:667
  122.2 27.1 %collective-permute-start.12 = (bf16[4,1024,512]{2,1,0:T(8,128)(2,1)}, bf16[4,1024,512]{2,1,0:T(8,128)(2,1)}, u32[]{:S(2)}, u32[]{:S(2)}) collective-permute-start(bf16[4,1024,512]{2,1,0:T(8,128)(2,1)} %pad_maximum_fusion.1.refs_4_.refs_10_), channel_id=1, source_target_pairs={{0,1},{1,0},{2,3},{3,2},{4,5},{5,4},{6,7},{7,6},{8,9},{9,8},{10,11... | collective-permute-start | bytes 12582920 | tf_op jit(solution)/shard_map/ppermute | solution.py:685
  149.3 31.7 %collective-permute-start.15 = (bf16[256,2048]{1,0:T(8,128)(2,1)S(1)}, bf16[256,2048]{1,0:T(8,128)(2,1)}, u32[]{:S(2)}, u32[]{:S(2)}) collective-permute-start(bf16[256,2048]{1,0:T(8,128)(2,1)S(1)} %copy-done.14), channel_id=1, source_target_pairs={{0,1},{1,0},{2,3},{3,2},{4,5},{5,4},{6,7},{7,6},{8,9},{9,8},{10,11... | collective-permute-start | bytes 3145736 | tf_op jit(solution)/shard_map/ppermute | solution.py:685
  174.1 39.7 %collective-permute-start.13 = (bf16[256,2048]{1,0:T(8,128)(2,1)S(1)}, bf16[256,2048]{1,0:T(8,128)(2,1)}, u32[]{:S(2)}, u32[]{:S(2)}) collective-permute-start(bf16[256,2048]{1,0:T(8,128)(2,1)S(1)} %get-tuple-element.84.refs_0_.refs_5_), channel_id=1, source_target_pairs={{0,2},{1,3},{2,4},{3,5},{4,6},{5,7},{8,10},{9,11},{10,12},{11,13},... | collective-permute-start | bytes 3145736 | tf_op jit(solution)/shard_map/ppermute | solution.py:691
  177.5 36.3 %collective-permute-start.17 = (bf16[256,2048]{1,0:T(8,128)(2,1)S(1)}, bf16[256,2048]{1,0:T(8,128)(2,1)}, u32[]{:S(2)}, u32[]{:S(2)}) collective-permute-start(bf16[256,2048]{1,0:T(8,128)(2,1)S(1)} %get-tuple-element.84.refs_0_.refs_5_), channel_id=1, source_target_pairs={{2,0},{3,1},{4,2},{5,3},{6,4},{7,5},{10,8},{11,9},{12,10},{13,11},... | collective-permute-start | bytes 3145736 | tf_op jit(solution)/shard_map/ppermute | solution.py:691
  216.8 51.8 %collective-permute-start.22 = (bf16[256,2048]{1,0:T(8,128)(2,1)S(1)}, bf16[256,2048]{1,0:T(8,128)(2,1)}, u32[]{:S(2)}, u32[]{:S(2)}) collective-permute-start(bf16[256,2048]{1,0:T(8,128)(2,1)S(1)} %copy-done.55), channel_id=1, source_target_pairs={{0,8},{8,0},{16,24},{24,16},{1,9},{9,1},{17,25},{25,17},{2,10},{10... | collective-permute-start | bytes 3145736 | tf_op jit(solution)/shard_map/ppermute | solution.py:667
  218.2 50.8 %collective-permute-start.23 = (bf16[256,2048]{1,0:T(8,128)(2,1)S(1)}, bf16[256,2048]{1,0:T(8,128)(2,1)}, u32[]{:S(2)}, u32[]{:S(2)}) collective-permute-start(bf16[256,2048]{1,0:T(8,128)(2,1)S(1)} %copy-done.55), channel_id=1, source_target_pairs={{0,16},{8,24},{16,0},{24,8},{1,17},{9,25},{17,1},{25,9},{2,18},{10... | collective-permute-start | bytes 3145736 | tf_op jit(solution)/shard_map/ppermute | solution.py:667
  219.7 38.4 %collective-permute-start.16 = (bf16[256,2048]{1,0:T(8,128)(2,1)}, bf16[256,2048]{1,0:T(8,128)(2,1)}, u32[]{:S(2)}, u32[]{:S(2)}) collective-permute-start(bf16[256,2048]{1,0:T(8,128)(2,1)} %after.33), channel_id=1, source_target_pairs={{2,4},{3,5},{4,6},{5,7},{10,12},{11,13},{12,14},{13,15},{18,20},{1... | collective-permute-start | bytes 3145736 | tf_op jit(solution)/shard_map/ppermute | solution.py:691
  223.3 34.8 %collective-permute-start.20 = (bf16[256,2048]{1,0:T(8,128)(2,1)}, bf16[256,2048]{1,0:T(8,128)(2,1)S(1)}, u32[]{:S(2)}, u32[]{:S(2)}) collective-permute-start(bf16[256,2048]{1,0:T(8,128)(2,1)} %after.34), channel_id=1, source_target_pairs={{2,0},{3,1},{4,2},{5,3},{10,8},{11,9},{12,10},{13,11},{18,16},{19,... | collective-permute-start | bytes 3145736 | tf_op jit(solution)/shard_map/ppermute | solution.py:691
  264.6 38.7 %collective-permute-start.19 = (bf16[256,2048]{1,0:T(8,128)(2,1)}, bf16[256,2048]{1,0:T(8,128)(2,1)}, u32[]{:S(2)}, u32[]{:S(2)}) collective-permute-start(bf16[256,2048]{1,0:T(8,128)(2,1)} %after.35), channel_id=1, source_target_pairs={{4,6},{5,7},{12,14},{13,15},{20,22},{21,23},{28,30},{29,31}} | collective-permute-start | bytes 3145736 | tf_op jit(solution)/shard_map/ppermute | solution.py:691
  266.3 37.1 %collective-permute-start.24 = (bf16[256,2048]{1,0:T(8,128)(2,1)S(1)}, bf16[256,2048]{1,0:T(8,128)(2,1)}, u32[]{:S(2)}, u32[]{:S(2)}) collective-permute-start(bf16[256,2048]{1,0:T(8,128)(2,1)S(1)} %copy-done.76), channel_id=1, source_target_pairs={{2,0},{3,1},{10,8},{11,9},{18,16},{19,17},{26,24},{27,25}} | collective-permute-start | bytes 3145736 | tf_op jit(solution)/shard_map/ppermute | solution.py:691
  268.6 36.6 %collective-permute-start.26 = (bf16[272,2048]{1,0:T(8,128)(2,1)}, bf16[272,2048]{1,0:T(8,128)(2,1)}, u32[]{:S(2)}, u32[]{:S(2)}) collective-permute-start(bf16[272,2048]{1,0:T(8,128)(2,1)} %get-tuple-element.104), channel_id=1, source_target_pairs={{0,1},{1,0},{2,3},{3,2},{4,5},{5,4},{6,7},{7,6},{8,9},{9,8},{10,11... | collective-permute-start | bytes 3342344 | tf_op jit(solution)/shard_map/ppermute | solution.py:685
  302.8 26.6 %collective-permute-start.28 = (bf16[256,2048]{1,0:T(8,128)(2,1)S(1)}, bf16[256,2048]{1,0:T(8,128)(2,1)}, u32[]{:S(2)}, u32[]{:S(2)}) collective-permute-start(bf16[256,2048]{1,0:T(8,128)(2,1)S(1)} %copy-done.55), channel_id=1, source_target_pairs={{0,24},{8,16},{16,8},{24,0},{1,25},{9,17},{17,9},{25,1},{2,26},{10... | collective-permute-start | bytes 3145736 | tf_op jit(solution)/shard_map/ppermute | solution.py:667
  304.9 24.4 %collective-permute-start.25 = (bf16[256,2048]{1,0:T(8,128)(2,1)S(1)}, bf16[256,2048]{1,0:T(8,128)(2,1)S(1)}, u32[]{:S(2)}, u32[]{:S(2)}) collective-permute-start(bf16[256,2048]{1,0:T(8,128)(2,1)S(1)} %select_select_fusion.refs_0_), channel_id=1, source_target_pairs={{0,1},{1,0},{2,3},{3,2},{4,5},{5,4},{6,7},{7,6},{8,9},{9,8},{10,11... | collective-permute-start | bytes 3145736 | tf_op jit(solution)/shard_map/ppermute | solution.py:685
  308.4 74.9 %collective-permute-start.29 = (bf16[272,2048]{1,0:T(8,128)(2,1)}, bf16[272,2048]{1,0:T(8,128)(2,1)S(1)}, u32[]{:S(2)}, u32[]{:S(2)}) collective-permute-start(bf16[272,2048]{1,0:T(8,128)(2,1)} %add_convert_fusion.3.refs_18_), channel_id=1, source_target_pairs={{0,2},{1,3},{2,0},{3,1},{4,6},{5,7},{6,4},{7,5},{8,10},{9,11},{10,... | collective-permute-start | bytes 3342344 | tf_op jit(solution)/shard_map/ppermute | solution.py:685
  311.1 72.2 %collective-permute-start.30 = (bf16[272,2048]{1,0:T(8,128)(2,1)}, bf16[272,2048]{1,0:T(8,128)(2,1)}, u32[]{:S(2)}, u32[]{:S(2)}) collective-permute-start(bf16[272,2048]{1,0:T(8,128)(2,1)} %add_convert_fusion.2.refs_19_), channel_id=1, source_target_pairs={{0,4},{1,5},{2,6},{3,7},{4,0},{5,1},{6,2},{7,3},{8,12},{9,13},{10,... | collective-permute-start | bytes 3342344 | tf_op jit(solution)/shard_map/ppermute | solution.py:685
  384.3 48.4 %collective-permute-start.33 = (bf16[2,256,2048]{2,1,0:T(8,128)(2,1)}, bf16[2,256,2048]{2,1,0:T(8,128)(2,1)}, u32[]{:S(2)}, u32[]{:S(2)}) collective-permute-start(bf16[2,256,2048]{2,1,0:T(8,128)(2,1)} %get-tuple-element.111.refs_1_), channel_id=1, source_target_pairs={{0,8},{8,0},{16,24},{24,16},{1,9},{9,1},{17,25},{25,17},{2,10},{10... | collective-permute-start | bytes 6291464 | tf_op jit(solution)/shard_map/ppermute | solution.py:667
  384.9 48.1 %collective-permute-start.34 = (bf16[2,256,2048]{2,1,0:T(8,128)(2,1)}, bf16[2,256,2048]{2,1,0:T(8,128)(2,1)}, u32[]{:S(2)}, u32[]{:S(2)}) collective-permute-start(bf16[2,256,2048]{2,1,0:T(8,128)(2,1)} %get-tuple-element.113.refs_3_), channel_id=1, source_target_pairs={{0,16},{8,24},{16,0},{24,8},{1,17},{9,25},{17,1},{25,9},{2,18},{10... | collective-permute-start | bytes 6291464 | tf_op jit(solution)/shard_map/ppermute | solution.py:667
  388.9 46.7 %collective-permute-start.32 = (bf16[272,2048]{1,0:T(8,128)(2,1)S(1)}, bf16[272,2048]{1,0:T(8,128)(2,1)S(1)}, u32[]{:S(2)}, u32[]{:S(2)}) collective-permute-start(bf16[272,2048]{1,0:T(8,128)(2,1)S(1)} %add_convert_fusion.1.refs_1_), channel_id=1, source_target_pairs={{0,6},{1,7},{2,4},{3,5},{4,2},{5,3},{6,0},{7,1},{8,14},{9,15},{10,... | collective-permute-start | bytes 3342344 | tf_op jit(solution)/shard_map/ppermute | solution.py:685
  436.7 283.6 %reduce-scatter.6.cloned.1.call-start = ((), (), s32[]{:S(2)}) async-start(), calls=%async_computation.7 | async-start | bytes 7077888 | tf_op jit(solution)/shard_map/reduce_scatter | solution.py:713
  471.4 93.7 %collective-permute-start.39 = (bf16[2,512,2048]{2,1,0:T(8,128)(2,1)}, bf16[2,512,2048]{2,1,0:T(8,128)(2,1)}, u32[]{:S(2)}, u32[]{:S(2)}) collective-permute-start(bf16[2,512,2048]{2,1,0:T(8,128)(2,1)} %after.43.refs_1_), channel_id=1, source_target_pairs={{0,8},{8,0},{16,24},{24,16},{1,9},{9,1},{17,25},{25,17},{2,10},{10... | collective-permute-start | bytes 12582920 | tf_op jit(solution)/shard_map/ppermute | solution.py:667
  472.3 106.0 %collective-permute-start.40 = (bf16[2,512,2048]{2,1,0:T(8,128)(2,1)}, bf16[2,512,2048]{2,1,0:T(8,128)(2,1)}, u32[]{:S(2)}, u32[]{:S(2)}) collective-permute-start(bf16[2,512,2048]{2,1,0:T(8,128)(2,1)} %after.44.refs_2_), channel_id=1, source_target_pairs={{0,16},{8,24},{16,0},{24,8},{1,17},{9,25},{17,1},{25,9},{2,18},{10... | collective-permute-start | bytes 12582920 | tf_op jit(solution)/shard_map/ppermute | solution.py:667
  506.4 215.9 %reduce-scatter.8.cloned.1.call-start = ((), (), s32[]{:S(2)}) async-start(), calls=%async_computation.8 | async-start | bytes 2949120 | tf_op jit(solution)/shard_map/reduce_scatter | solution.py:713
  506.8 67.7 %collective-permute-start.41 = (bf16[256,512]{1,0:T(8,128)(2,1)}, bf16[256,512]{1,0:T(8,128)(2,1)S(1)}, u32[]{:S(2)}, u32[]{:S(2)}) collective-permute-start(bf16[256,512]{1,0:T(8,128)(2,1)} %after.47), channel_id=1, source_target_pairs={{0,8},{8,0},{16,24},{24,16},{1,9},{9,1},{17,25},{25,17},{2,10},{10... | collective-permute-start | bytes 786440 | tf_op jit(solution)/shard_map/ppermute | solution.py:667
  507.7 68.4 %collective-permute-start.42 = (bf16[256,512]{1,0:T(8,128)(2,1)}, bf16[256,512]{1,0:T(8,128)(2,1)S(1)}, u32[]{:S(2)}, u32[]{:S(2)}) collective-permute-start(bf16[256,512]{1,0:T(8,128)(2,1)} %after.48), channel_id=1, source_target_pairs={{0,16},{8,24},{16,0},{24,8},{1,17},{9,25},{17,1},{25,9},{2,18},{10... | collective-permute-start | bytes 786440 | tf_op jit(solution)/shard_map/ppermute | solution.py:667
  508.6 67.6 %collective-permute-start.43 = (bf16[256,512]{1,0:T(8,128)(2,1)}, bf16[256,512]{1,0:T(8,128)(2,1)S(1)}, u32[]{:S(2)}, u32[]{:S(2)}) collective-permute-start(bf16[256,512]{1,0:T(8,128)(2,1)} %after.49), channel_id=1, source_target_pairs={{0,24},{8,16},{16,8},{24,0},{1,25},{9,17},{17,9},{25,1},{2,26},{10... | collective-permute-start | bytes 786440 | tf_op jit(solution)/shard_map/ppermute | solution.py:667
  576.9 48.9 %collective-permute-start.44 = (bf16[1,512,2048]{2,1,0:T(8,128)(2,1)}, bf16[1,512,2048]{2,1,0:T(8,128)(2,1)}, u32[]{:S(2)}, u32[]{:S(2)}) collective-permute-start(bf16[1,512,2048]{2,1,0:T(8,128)(2,1)} %after.50.refs_1_), channel_id=1, source_target_pairs={{0,16},{8,24},{16,0},{24,8},{1,17},{9,25},{17,1},{25,9},{2,18},{10... | collective-permute-start | bytes 6291464 | tf_op jit(solution)/shard_map/ppermute | solution.py:667
  587.6 48.9 %collective-permute-start.45 = (bf16[1,512,2048]{2,1,0:T(8,128)(2,1)}, bf16[1,512,2048]{2,1,0:T(8,128)(2,1)}, u32[]{:S(2)}, u32[]{:S(2)}) collective-permute-start(bf16[1,512,2048]{2,1,0:T(8,128)(2,1)} %after.51.refs_2_), channel_id=1, source_target_pairs={{0,8},{8,0},{16,24},{24,16},{1,9},{9,1},{17,25},{25,17},{2,10},{10... | collective-permute-start | bytes 6291464 | tf_op jit(solution)/shard_map/ppermute | solution.py:667
  602.0 57.2 %collective-permute-start.48 = (bf16[256,2048]{1,0:T(8,128)(2,1)}, bf16[256,2048]{1,0:T(8,128)(2,1)}, u32[]{:S(2)}, u32[]{:S(2)}) collective-permute-start(bf16[256,2048]{1,0:T(8,128)(2,1)} %get-tuple-element.136), channel_id=1, source_target_pairs={{0,24},{8,16},{16,8},{24,0},{1,25},{9,17},{17,9},{25,1},{2,26},{10... | collective-permute-start | bytes 3145736 | tf_op jit(solution)/shard_map/ppermute | solution.py:667
  603.4 65.1 %collective-permute-start.47 = (bf16[256,2048]{1,0:T(8,128)(2,1)}, bf16[256,2048]{1,0:T(8,128)(2,1)}, u32[]{:S(2)}, u32[]{:S(2)}) collective-permute-start(bf16[256,2048]{1,0:T(8,128)(2,1)} %get-tuple-element.135), channel_id=1, source_target_pairs={{0,16},{8,24},{16,0},{24,8},{1,17},{9,25},{17,1},{25,9},{2,18},{10... | collective-permute-start | bytes 3145736 | tf_op jit(solution)/shard_map/ppermute | solution.py:667
  604.7 74.1 %collective-permute-start.46 = (bf16[256,2048]{1,0:T(8,128)(2,1)}, bf16[256,2048]{1,0:T(8,128)(2,1)}, u32[]{:S(2)}, u32[]{:S(2)}) collective-permute-start(bf16[256,2048]{1,0:T(8,128)(2,1)} %get-tuple-element.134), channel_id=1, source_target_pairs={{0,8},{8,0},{16,24},{24,16},{1,9},{9,1},{17,25},{25,17},{2,10},{10... | collective-permute-start | bytes 3145736 | tf_op jit(solution)/shard_map/ppermute | solution.py:667
  689.8 24.4 %collective-permute-start.55 = (f32[4368]{0:T(1024)S(1)}, f32[4368]{0:T(1024)S(1)}, u32[]{:S(2)}, u32[]{:S(2)}) collective-permute-start(f32[4368]{0:T(1024)S(1)} %maximum_select_fusion.1), channel_id=1, source_target_pairs={{0,6},{1,7},{2,4},{3,5},{4,2},{5,3},{6,0},{7,1},{8,14},{9,15},{10,... | collective-permute-start | bytes 52424 | tf_op jit(solution)/shard_map/ppermute | solution.py:685
  691.4 22.8 %collective-permute-start.53 = (f32[4368]{0:T(1024)S(1)}, f32[4368]{0:T(1024)S(1)}, u32[]{:S(2)}, u32[]{:S(2)}) collective-permute-start(f32[4368]{0:T(1024)S(1)} %maximum_select_fusion.1), channel_id=1, source_target_pairs={{0,2},{1,3},{2,0},{3,1},{4,6},{5,7},{6,4},{7,5},{8,10},{9,11},{10,... | collective-permute-start | bytes 52424 | tf_op jit(solution)/shard_map/ppermute | solution.py:685
  720.3 54.9 %collective-permute-start.56 = (bf16[256,1536]{1,0:T(8,128)(2,1)}, bf16[256,1536]{1,0:T(8,128)(2,1)S(1)}, u32[]{:S(2)}, u32[]{:S(2)}) collective-permute-start(bf16[256,1536]{1,0:T(8,128)(2,1)} %after.54.refs_1_), channel_id=1, source_target_pairs={{0,8},{8,0},{16,24},{24,16},{1,9},{9,1},{17,25},{25,17},{2,10},{10... | collective-permute-start | bytes 2359304 | tf_op jit(solution)/shard_map/ppermute | solution.py:667
  721.5 53.7 %collective-permute-start.57 = (bf16[256,1536]{1,0:T(8,128)(2,1)}, bf16[256,1536]{1,0:T(8,128)(2,1)S(1)}, u32[]{:S(2)}, u32[]{:S(2)}) collective-permute-start(bf16[256,1536]{1,0:T(8,128)(2,1)} %after.54.refs_1_), channel_id=1, source_target_pairs={{0,16},{8,24},{16,0},{24,8},{1,17},{9,25},{17,1},{25,9},{2,18},{10... | collective-permute-start | bytes 2359304 | tf_op jit(solution)/shard_map/ppermute | solution.py:667
  722.3 25.7 %collective-permute-start.59 = (bf16[256,528]{1,0:T(8,128)(2,1)}, bf16[256,528]{1,0:T(8,128)(2,1)S(1)}, u32[]{:S(2)}, u32[]{:S(2)}) collective-permute-start(bf16[256,528]{1,0:T(8,128)(2,1)} %after.55), channel_id=1, source_target_pairs={{0,8},{8,0},{16,24},{24,16},{1,9},{9,1},{17,25},{25,17},{2,10},{10... | collective-permute-start | bytes 811016 | tf_op jit(solution)/shard_map/ppermute | solution.py:667
  723.7 47.5 %collective-permute-start.60 = (bf16[256,528]{1,0:T(8,128)(2,1)}, bf16[256,528]{1,0:T(8,128)(2,1)S(1)}, u32[]{:S(2)}, u32[]{:S(2)}) collective-permute-start(bf16[256,528]{1,0:T(8,128)(2,1)} %after.55), channel_id=1, source_target_pairs={{0,16},{8,24},{16,0},{24,8},{1,17},{9,25},{17,1},{25,9},{2,18},{10... | collective-permute-start | bytes 811016 | tf_op jit(solution)/shard_map/ppermute | solution.py:667
  724.3 46.8 %collective-permute-start.61 = (bf16[256,528]{1,0:T(8,128)(2,1)}, bf16[256,528]{1,0:T(8,128)(2,1)S(1)}, u32[]{:S(2)}, u32[]{:S(2)}) collective-permute-start(bf16[256,528]{1,0:T(8,128)(2,1)} %after.55), channel_id=1, source_target_pairs={{0,24},{8,16},{16,8},{24,0},{1,25},{9,17},{17,9},{25,1},{2,26},{10... | collective-permute-start | bytes 811016 | tf_op jit(solution)/shard_map/ppermute | solution.py:667
  748.0 27.2 %collective-permute-start.58 = (bf16[256,1536]{1,0:T(8,128)(2,1)S(1)}, bf16[256,1536]{1,0:T(8,128)(2,1)}, u32[]{:S(2)}, u32[]{:S(2)}) collective-permute-start(bf16[256,1536]{1,0:T(8,128)(2,1)S(1)} %copy-done.66), channel_id=1, source_target_pairs={{0,24},{8,16},{16,8},{24,0},{1,25},{9,17},{17,9},{25,1},{2,26},{10... | collective-permute-start | bytes 2359304 | tf_op jit(solution)/shard_map/ppermute | solution.py:667
  (125 other events, 970.4 us)
Sparse Core Ops, SparseCore 0:
  10.2 34.3 all-gather.3
  46.9 62.1 all-gather.5
  110.7 90.3 all-gather.7
  436.8 86.2 reduce-scatter.3
  525.3 68.1 reduce-scatter.5
  612.0 32.6 reduce-scatter.7

commit v3 on v2

--- a/solution.py
+++ b/solution.py
@@ -258,7 +258,7 @@
             jax.ShapeDtypeStruct((length, width), BF),
             jax.ShapeDtypeStruct((length, width), BF),
         ],
-        compiler_params=pltpu.CompilerParams(vmem_limit_bytes=48 * 2**20),
+        compiler_params=pltpu.CompilerParams(vmem_limit_bytes=60 * 2**20),
         name="attention_out",
     )(who, *pieces, near, far, tokens, gain)
 
@@ -268,8 +268,8 @@
     shares = refs[:rounds]
     hidden, normed, cot, gain, gates, router, near, far = refs[rounds : rounds + 8]
     grad_hidden, gain_grad, router_grad = refs[rounds + 8 : rounds + 11]
-    attn = refs[rounds + 11 : rounds + 11 + replicas]
-    out = refs[rounds + 11 + replicas :]
+    pieces = refs[rounds + 11 : rounds + 11 + replicas]
+    mixed = refs[rounds + 11 + replicas]
     length, width = hidden.shape
     lanes = router.shape[1]
     part = width // replicas
@@ -298,14 +298,17 @@
     grad_hidden[...] = total
     for q in range(replicas):
         here = pl.ds(pl.multiple_of((who[0] ^ q) * part, part), part)
-        attn[q][...] = grad_hidden[:, here].astype(BF)
+        pieces[q][:, part:] = grad_hidden[:, here].astype(BF)
     for k in range(rounds):
         for flip, source in enumerate((near, far)):
             block = jnp.zeros((length, depth), F32)
             for q in range(replicas):
-                block += dot_nt(attn[q][...], source[q, k * depth : (k + 1) * depth])
+                block += dot_nt(pieces[q][:, part:], source[q, k * depth : (k + 1) * depth])
             at = ((who[2] ^ flip) * (groups // 2) + k) * depth
-            out[0][:, pl.ds(pl.multiple_of(at, depth), depth)] = block.astype(BF)
+            mixed[:, pl.ds(pl.multiple_of(at, depth), depth)] = block.astype(BF)
+    for q in range(replicas):
+        here = pl.ds(pl.multiple_of((who[0] ^ q) * part, part), part)
+        pieces[q][:, :part] = mixed[:, here]
 
 
 def back_step(who, shares, hidden, normed, cot, gain, gates, router, near, far, experts):
@@ -313,22 +316,23 @@
     length, width = hidden.shape
     groups = 2 * len(shares)
     vmem = pl.BlockSpec(memory_space=pltpu.VMEM)
-    piece = jax.ShapeDtypeStruct((length, width // replicas), BF)
+    piece = jax.ShapeDtypeStruct((length, 2 * width // replicas), BF)
     results = pl.pallas_call(
         functools.partial(back_kernel, replicas, groups, experts),
         in_specs=[pl.BlockSpec(memory_space=pltpu.SMEM)] + [vmem] * (len(shares) + 8),
-        out_specs=[vmem] * (4 + replicas),
+        out_specs=[vmem] * (3 + replicas),
+        scratch_shapes=[pltpu.VMEM((length, width), BF)],
         out_shape=[
             jax.ShapeDtypeStruct((length, width), F32),
             jax.ShapeDtypeStruct((1, width), F32),
             jax.ShapeDtypeStruct((width, router.shape[1]), BF),
             *[piece] * replicas,
-            jax.ShapeDtypeStruct((length, width), BF),
         ],
-        compiler_params=pltpu.CompilerParams(vmem_limit_bytes=48 * 2**20),
+        compiler_params=pltpu.CompilerParams(vmem_limit_bytes=60 * 2**20),
+        cost_estimate=pl.CostEstimate(flops=10**11, bytes_accessed=0, transcendentals=0),
         name="attention_back",
     )(who, *shares, hidden, normed, cot, gain, gates, router, near, far)
-    return results[0], results[1], results[2], results[3 : 3 + replicas], results[3 + replicas]
+    return results[0], results[1], results[2], results[3:]
 
 
 def turn(value, cosine, sine):
@@ -398,10 +402,8 @@
             jax.ShapeDtypeStruct((rows, 128), F32),
             jax.ShapeDtypeStruct((count, 1, 128), F32),
         ],
-        compiler_params=pltpu.CompilerParams(vmem_limit_bytes=48 * 2**20),
-        cost_estimate=pl.CostEstimate(
-            flops=rows * width * 3 * part * 4, bytes_accessed=8 * rows * width, transcendentals=0
-        ),
+        compiler_params=pltpu.CompilerParams(vmem_limit_bytes=60 * 2**20),
+        cost_estimate=pl.CostEstimate(flops=0, bytes_accessed=0, transcendentals=0),
         name="attention",
     )(normed, weight, segments[:, None, :], segments[:, :, None], cosine, sine, gains)
 
@@ -482,7 +484,7 @@
             out[0] = block
 
 
-def weight_grads(quarters, left, right, parts):
+def weight_grads(quarters, left, right, parts, cost):
     count, rows, width = left.shape
     size, n = width // parts, right.shape[2]
     half = parts // 2
@@ -507,7 +509,7 @@
         ),
         out_shape=[jax.ShapeDtypeStruct((half, size, n), BF)] * (2 * count),
         compiler_params=pltpu.CompilerParams(vmem_limit_bytes=56 * 2**20),
-        cost_estimate=pl.CostEstimate(flops=0, bytes_accessed=0, transcendentals=0),
+        cost_estimate=pl.CostEstimate(flops=cost, bytes_accessed=0, transcendentals=0),
         name="weight_grads",
     )(quarters, left, right)
 
@@ -558,7 +560,7 @@
         out_specs=[pl.BlockSpec((length, width), lambda i: (0, 0))] * count,
         out_shape=[jax.ShapeDtypeStruct((length, width), BF)] * count,
         compiler_params=pltpu.CompilerParams(vmem_limit_bytes=48 * 2**20),
-        cost_estimate=pl.CostEstimate(flops=10**11, bytes_accessed=0, transcendentals=0),
+        cost_estimate=pl.CostEstimate(flops=0, bytes_accessed=0, transcendentals=0),
         name="normed_grads",
     )(grad, weight)
 
@@ -575,7 +577,7 @@
         keep_out[0] = block
 
 
-def halve(blocks, keep, got):
+def halve(blocks, keep, got, cost):
     count, size, n = keep.shape
     half = count // 2
     here = pl.BlockSpec((1, size, n), lambda i, blocks: (blocks[i], 0, 0))
@@ -592,7 +594,7 @@
         ),
         out_shape=[jax.ShapeDtypeStruct((half, size, n), BF)] * 2,
         compiler_params=pltpu.CompilerParams(vmem_limit_bytes=32 * 2**20),
-        cost_estimate=pl.CostEstimate(flops=0, bytes_accessed=0, transcendentals=0),
+        cost_estimate=pl.CostEstimate(flops=cost, bytes_accessed=0, transcendentals=0),
         name="halve",
     )(blocks, keep, got)
 
@@ -606,7 +608,7 @@
             out[0] = refs[2 * j][...].astype(F32) + refs[2 * j + 1][...].astype(F32)
 
 
-def join(pairs):
+def join(pairs, cost):
     size, n = pairs[0][0].shape
     step = min(size, 256)
     count = len(pairs)
@@ -624,9 +626,83 @@
         in_specs=[pl.BlockSpec((step, n), spot(at // 2)) for at in range(2 * count)],
         out_specs=pl.BlockSpec((1, step, n), lambda j, i: (j, i, 0)),
         out_shape=jax.ShapeDtypeStruct((count, size, n), F32),
-        compiler_params=pltpu.CompilerParams(vmem_limit_bytes=48 * 2**20),
+        compiler_params=pltpu.CompilerParams(vmem_limit_bytes=60 * 2**20),
+        cost_estimate=pl.CostEstimate(flops=cost, bytes_accessed=0, transcendentals=0),
         name="join",
     )(*[v for pair in pairs for v in pair])
+
+
+def input_kernel(count, heads, who, *refs):
+    pieces = refs[:count]
+    tokens, gain, grad_hidden, ffn, gains, tops, grad, small = refs[count:]
+    width = tokens.shape[1]
+    pulled = pieces[0][...].astype(F32)
+    for piece in pieces[1:]:
+        pulled = pulled + piece[...].astype(F32)
+    value = tokens[...].astype(F32)
+    scale = lax.rsqrt(jnp.mean(value * value, axis=1, keepdims=True) + epsilon)
+    small[:, :width] = jnp.sum(pulled * value * scale, axis=0, keepdims=True)
+    small[:, width : 2 * width] = ffn[...]
+    for i in range(2):
+        at = 2 * width + i * HD
+        small[:, at : at + HD] = jnp.sum(gains[:, i], axis=0, keepdims=True)
+    top = jnp.max(tops[:, 0], axis=0, keepdims=True)
+    lane = lax.broadcasted_iota(jnp.int32, top.shape, 1)
+    top = jnp.where(lane < heads, top, -3e38)
+    small[:, 2 * width + 2 * HD :] = pltpu.roll(top, who[0] * heads, 1)
+    pulled = pulled * gain[...]
+    inner = jnp.mean(pulled * value, axis=1, keepdims=True)
+    back = scale * pulled - value * (scale * scale * scale * inner)
+    grad[...] = (grad_hidden[...] + back).astype(BF)
+
+
+def input_step(who, pieces, tokens, gain, grad_hidden, ffn, gains, tops, heads):
+    length, width = tokens.shape
+    vmem = pl.BlockSpec(memory_space=pltpu.VMEM)
+    return pl.pallas_call(
+        functools.partial(input_kernel, len(pieces), heads),
+        in_specs=[pl.BlockSpec(memory_space=pltpu.SMEM)] + [vmem] * (len(pieces) + 6),
+        out_specs=[vmem] * 2,
+        out_shape=[
+            jax.ShapeDtypeStruct((length, width), BF),
+            jax.ShapeDtypeStruct((1, 2 * width + 2 * HD + 128), F32),
+        ],
+        compiler_params=pltpu.CompilerParams(vmem_limit_bytes=60 * 2**20),
+        cost_estimate=pl.CostEstimate(flops=10**11, bytes_accessed=0, transcendentals=0),
+        name="input_grad",
+    )(who, *pieces, tokens, gain, grad_hidden, ffn, gains, tops)
+
+
+def gather_kernel(count, arrays, who, *refs):
+    blocks, outs = refs[:count], refs[count:]
+    part = outs[0].shape[1] // count
+    total = 0.0
+    for k, block in enumerate(blocks):
+        here = pl.ds(pl.multiple_of((who[0] ^ k) * part, part), part)
+        for i in range(arrays):
+            outs[i][:, here] = block[:, i * part : (i + 1) * part].astype(F32)
+        if len(outs) > arrays:
+            total += block[:, arrays * part :].astype(F32)
+    if len(outs) > arrays:
+        outs[-1][...] = total
+
+
+def gather_step(who, blocks, arrays):
+    rows, wide = blocks[0].shape
+    lanes = 128 if wide % (arrays * 256) else 0
+    part = (wide - lanes) // arrays
+    count = len(blocks)
+    vmem = pl.BlockSpec(memory_space=pltpu.VMEM)
+    return pl.pallas_call(
+        functools.partial(gather_kernel, count, arrays),
+        in_specs=[pl.BlockSpec(memory_space=pltpu.SMEM)] + [vmem] * count,
+        out_specs=[vmem] * (arrays + (lanes > 0)),
+        out_shape=[jax.ShapeDtypeStruct((rows, part * count), F32)] * arrays
+        + [jax.ShapeDtypeStruct((rows, lanes), F32)] * (lanes > 0),
+        compiler_params=pltpu.CompilerParams(vmem_limit_bytes=48 * 2**20),
+        cost_estimate=pl.CostEstimate(flops=0, bytes_accessed=0, transcendentals=0),
+        name="gather_columns",
+    )(who, *blocks)
 
 
 def local(
@@ -717,7 +793,7 @@
     def next_bit(j, step):
         return 1 << (bits - 1 - step if j % 2 else step)
 
-    def next_halves(traded, j, step):
+    def next_halves(traded, j, step, cost=0):
         keep, got = traded
         left = keep.shape[0]
         place = jnp.arange(left, dtype=jnp.int32)
@@ -725,7 +801,7 @@
         mine = (me_r & next_bit(j, step)) != 0
         other = ((place & here) != 0) != mine
         spots = jnp.where(other, jnp.cumsum(other) - 1, left // 2 + jnp.cumsum(~other) - 1)
-        return halve(jnp.zeros((left,), jnp.int32).at[spots].set(place), keep, got)
+        return halve(jnp.zeros((left,), jnp.int32).at[spots].set(place), keep, got, cost)
 
     index_table = expert_index.astype(BF).reshape(w_query.shape[0], -1)
     sent = [columns(w_output, 0), router, index_table]
@@ -750,19 +826,18 @@
     mask_wide = jnp.pad(mask.astype(F32), ((0, 0), (0, 0), (0, lanes - EXPERTS)))
     router_wide = jnp.pad(full_router, ((0, 0), (0, lanes - EXPERTS)))
     tables = (pick, spots, mask_wide, router_wide)
-    segments = jnp.concatenate(spread(segment_ids), axis=0)
-    tokens_all = spread(tokens)
+    segments = spread(segment_ids)
+    tokens_all = spread(after(tokens, *segments[1:]))
+    segments = jnp.concatenate(segments, axis=0)
     normed = jnp.concatenate(
         [rms_norm(v.astype(F32), attn_gain).astype(BF) for v in tokens_all], axis=0
     )
     rounds = groups // 2
     where = jnp.stack([me_r, me_f // 2, core]).astype(jnp.int32)
     half = lax.dynamic_slice(quarter, (core * (width // 2), 0), (width // 2, part))
-    near = spread(after(half, normed))
-    near[1] = after(near[1], *tables)
+    near = spread(after(half, *tokens_all[1:]))
+    near[1] = after(near[1], *tables, segments, normed)
     normed = after(normed, *near[1:])
-    near = jnp.stack(near)
-    far = cross(near, 1)
     w_qkv = gather(jnp.concatenate([columns(w, 0) for w in (w_query, w_key, w_value)], axis=1))
     cot_all = gather(cotangent)
     cot_pair = (cotangent, cross(cotangent, 1))
@@ -773,7 +848,8 @@
     gains = jnp.stack([gain_query, gain_key])
     raw, ready, mixed_heads, totals, tops = attend(normed, w_qkv, segments, cosine, sine, gains, heads
     )
-    my_max = jnp.max(tops, axis=(0, 1))[:heads]
+    near = jnp.stack([after(near[0], raw), *near[1:]])
+    far = cross(near, 1)
     mixed_heads = mixed_heads.reshape(replicas, length, part)
     pieces = [mixed_heads[0]] + [swap(mixed_heads[k], k) for k in range(1, replicas)]
     inputs = tokens.astype(F32)
@@ -809,98 +885,83 @@
             down.append(after(next_down, back_a))
         else:
             rows, grad_projected, cot_rows, scaled, moe = kept
-            out_blocks = weight_grads(quarters, scaled, cot_rows, replicas)
+            out_blocks = weight_grads(quarters, after(scaled, mixed_all[-1]), cot_rows, replicas, 0)
         if k == rounds - 1:
             back_b = after(back_b, *out_blocks, *shares[1:])
         share = (back_a.astype(F32) + cross(back_b, 1).astype(F32)).astype(BF)
         added.append(share)
         if k == rounds - 2:
-            pending = [*added[1:], mixed_all[-1]]
+            pending = added[1:]
         else:
             pending = mixed_all[1:-1] if k == rounds - 3 else []
         shares.append(share if k == 0 else cross(share, 2 * k))
     out_traded = [
         (out_blocks[2 * j + 1], swap(out_blocks[2 * j], first_bit(j))) for j in range(local_experts)
     ]
-    in_blocks = weight_grads(quarters, after(rows, share), grad_projected, replicas)
+    in_blocks = weight_grads(quarters, after(rows, share), grad_projected, replicas, 10**11)
     shares[-1] = after(shares[-1], *in_blocks, *[v[1] for v in out_traded])
-    output = (hidden + reduce(after(moe, shares[-1])).astype(F32)).astype(BF)
+    moe_sum = reduce(after(moe, shares[-1]))
+    output = (hidden + moe_sum.astype(F32)).astype(BF)
 
     my_mask = lax.dynamic_index_in_dim(mask_wide, me_f, 0, keepdims=False) > 0.0
     logits = jnp.where(my_mask, dot(normed_ffn, router_wide), -jnp.inf)
     powers = jnp.exp(logits - jnp.max(logits, axis=1, keepdims=True))
     my_gates = powers / jnp.sum(powers, axis=1, keepdims=True)
-    grad_hidden, ffn_gain_grad, router_grad, attn_pieces, grad_mixed = back_step(
+    grad_hidden, ffn_gain_grad, router_grad, pieces = back_step(
         where, shares, hidden, normed_ffn, cotangent, ffn_gain[None, :], my_gates, router_wide, near, far, EXPERTS
     )
-    ffn_gain_grad = ffn_gain_grad[0]
-    router_grad = router_grad[:, :EXPERTS]
-    grad_mixed = jnp.stack(trade_columns(grad_mixed), axis=0)
-    sends = [after(in_blocks[2 * j], grad_mixed) for j in range(local_experts)]
+    grad_mixed = jnp.concatenate(
+        [pieces[0]] + [swap(pieces[k], k) for k in range(1, replicas)], axis=0
+    )
+    sends = [
+        after(in_blocks[2 * j], grad_mixed, *[v[1] for v in out_traded]) for j in range(local_experts)
+    ]
     in_traded = [
         (in_blocks[2 * j + 1], swap(v, first_bit(j))) for j, v in enumerate(sends)
     ]
     grad_mixed = after(grad_mixed, *sends)
-    grad_qkv, gain_grads = attend_back(grad_mixed.reshape(replicas * length, part), raw, ready, totals, segments, cosine, sine, gains, heads
+    grad_qkv, gain_grads = attend_back(grad_mixed, raw, ready, totals, segments, cosine, sine, gains, heads
     )
-    query_gain_grad, key_gain_grad = jnp.sum(gain_grads, axis=0)
     qkv_grad = product(normed, grad_qkv)
-    w_late = after(w_qkv, qkv_grad, *[v[1] for v in in_traded])
-    attn_columns = [attn_pieces[0]] + [
-        swap(after(attn_pieces[k], *sends), k) for k in range(1, replicas)
+    part_normed = normed_grads(grad_qkv, w_qkv, replicas)
+    received = [v[1] for v in in_traded]
+    received[0] = after(received[0], *received[1:], moe_sum)
+    in_traded = [(v[0], got) for v, got in zip(in_traded, received)]
+    in_halves = [next_halves(v, j, 1, 10**11) for j, v in enumerate(in_traded)]
+    in_sends = [v for v, _ in in_halves]
+    in_done = [(keep, swap(v, next_bit(j, 1))) for j, (v, keep) in enumerate(in_halves)]
+    pieces = [after(part_normed[0], *in_sends)]
+    pieces += [swap(part_normed[k], k) for k in range(1, replicas)]
+    input_grad, small = input_step(
+        where, pieces, tokens, attn_gain[None, :], grad_hidden, ffn_gain_grad, gain_grads, tops, heads
+    )
+    second = [v[1] for v in in_done]
+    output_grad = dot_tn(jnp.concatenate(mixed_all, axis=0), grad_mixed[:, part:])
+    share_o = reduce(jnp.concatenate([output_grad.astype(BF), router_grad], axis=1))
+    share_qkv = reduce(qkv_grad)
+    blocks = spread(after(jnp.concatenate([share_qkv, share_o], axis=1), *second))
+    out_halves = [next_halves((k, after(v, input_grad)), j, 1) for j, (k, v) in enumerate(out_traded)]
+    out_done = [
+        (keep, swap(after(v, *second, moe_sum), next_bit(j, 1))) for j, (v, keep) in enumerate(out_halves)
     ]
-    in_halves = [next_halves(v, j, 1) for j, v in enumerate(in_traded)]
-    in_sends = [after(v, *attn_columns[1:]) for v, _ in in_halves]
-    in_done = [(keep, swap(v, next_bit(j, 1))) for j, (v, (_, keep)) in enumerate(zip(in_sends, in_halves))]
-    w_late = after(w_late, *in_sends)
-    part_normed = normed_grads(grad_qkv, w_late, replicas)
-    grad_normed = after(part_normed[0], *[v[1] for v in in_done]).astype(F32)
-    for k in range(1, replicas):
-        grad_normed = grad_normed + swap(part_normed[k], k).astype(F32)
-    attn_value, attn_back = jax.vjp(rms_norm, inputs, attn_gain)
-    grad_inputs_norm, attn_gain_grad = attn_back(grad_normed)
-    input_grad = (grad_hidden + grad_inputs_norm).astype(BF)
-
-    share_qkv = reduce(qkv_grad)
-    attn_columns = jnp.concatenate(attn_columns, axis=0)
-    output_grad = dot_tn(jnp.concatenate(mixed_all, axis=0), attn_columns)
-    share_qkv = after(share_qkv, output)
-    share_o = after(reduce(jnp.concatenate([output_grad.astype(BF), router_grad], axis=1)), share_qkv)
-    blocks_o = spread(share_o)
-    total_output = join_columns([b[:, :part].astype(F32) for b in blocks_o])
-    total_router = sum(b[:, part:].astype(F32) for b in blocks_o)
-    blocks_qkv = spread(share_qkv)
-    total_query, total_key, total_value = (
-        join_columns([b[:, i * part : (i + 1) * part].astype(F32) for b in blocks_qkv])
-        for i in range(3)
-    )
-
-    out_last = [(keep, after(got, grad_normed)) for keep, got in out_traded]
-    out_halves = [next_halves(v, j, 1) for j, v in enumerate(out_last)]
-    out_done = [
-        (keep, swap(after(v, *blocks_qkv[1:]), next_bit(j, 1)))
-        for j, (v, keep) in enumerate(out_halves)
-    ]
-
-    def settle(traded):
+    total_query, total_key, total_value, total_output, total_router = gather_step(where, blocks, 4)
+    total_router = total_router[:, :EXPERTS]
+
+    def settle(traded, cost):
         pairs = []
         for j, (keep, got) in enumerate(traded):
             for step in range(2, bits):
                 send, keep = next_halves((keep, got), j, step)
                 got = swap(send, next_bit(j, step))
             pairs.append((keep[0], got[0]))
-        return join(pairs)
-
-    expert_in_grad = settle(in_done)
-    expert_out_grad = settle(out_done)
-
-    top_heads = lax.dynamic_update_slice_in_dim(
-        jnp.full((replicas * heads,), -jnp.inf, F32), my_max, me_r * heads, 0
-    )
-    sums = jnp.concatenate([attn_gain_grad, query_gain_grad, key_gain_grad, ffn_gain_grad])
-    small = jnp.concatenate([sums, top_heads])
-    n_sums = sums.shape[0]
-    is_sum = jnp.arange(small.shape[0]) < n_sums
+        return join(pairs, cost)
+
+    expert_in_grad = settle(in_done, 10**11)
+    expert_out_grad = settle([(k, after(v, expert_in_grad)) for k, v in out_done], 0)
+
+    small = after(small, *second)
+    n_sums = 2 * width + 2 * HD
+    is_sum = jnp.arange(small.shape[1]) < n_sums
 
     def merge(a, b):
         return jnp.where(is_sum, a + b, jnp.maximum(a, b))
@@ -908,11 +969,12 @@
     small = functools.reduce(merge, spread(small))
     small = merge(small, cross(small, 1))
     small = functools.reduce(merge, [small] + [cross(small, 2 * k) for k in range(1, rounds)])
+    small = small[0]
     attn_gain_total = small[:width]
-    query_gain_total = small[width : width + HD]
-    key_gain_total = small[width + HD : width + 2 * HD]
-    ffn_gain_total = small[width + 2 * HD : n_sums]
-    head_max = small[n_sums:]
+    ffn_gain_total = small[width : 2 * width]
+    query_gain_total = small[2 * width : 2 * width + HD]
+    key_gain_total = small[2 * width + HD : n_sums]
+    head_max = small[n_sums : n_sums + replicas * heads]
     threshold = clip_threshold.astype(F32)
     factor = threshold / jnp.maximum(head_max, threshold)
     column_scale = jnp.repeat(jnp.sqrt(factor), HD)

time: 816 us -> 783 us (0.960)
  Pallas kernels: 278 us -> 294 us
  other arithmetic: 63.8 us -> 48.8 us
  waiting for transfers between devices: 300 us -> 285 us
    ppermute x41 -> x35, waiting for transfers between devices: 294 us -> 271 us  [swap(): return lax.ppermute(value, 'replica', [(r, r ^ k) for r in range(replicas)])]
    pallas_call x0 -> x2, Pallas kernels: none -> 11.6 us  [the longest x1 6.25 us: input_step(): pl.pallas_call(functools.partial(input_kernel, len(pieces), heads), in_sp...]
    dynamic_update_slice x10 -> x0, other arithmetic: 9.23 us -> none  [join_columns(): out = lax.dynamic_update_slice_in_dim(out, block, (me_r ^ k) * part, 1)]
    ppermute x41 -> x35, starting transfers between devices: 46.1 us -> 40.7 us  [swap(): return lax.ppermute(value, 'replica', [(r, r ^ k) for r in range(replicas)])]
    unnamed x212 -> x154, local copies, waits for them, and re-layouts: 46.9 us -> 42.9 us
  transfers between devices with their start and end apart: 70 -> 64, of which waited for: 31 -> 22; matrix products, arithmetic and copies ran while one was open for 11% -> 9% of each run, Pallas kernels for 34% -> 37%
where the time goes in v3:
time: 783 us; the launch traced here: 778 us
  Pallas kernels  294 us (38%)
  waiting for transfers between devices  285 us (36%)
  starting transfers between devices  67.4 us (9%)
  local copies, waits for them, and re-layouts  60.6 us (8%)
  other arithmetic  48.8 us (6%)
  between operations  15.6 us (2%)
    ppermute x35, waiting for transfers between devices, swap(): return lax.ppermute(value, 'replica', [(r, r ^ k) for r in range(replicas)])  271 us
    pallas_call x4, Pallas kernels, expert_block(): pl.pallas_call(functools.partial(expert_kernel, min(512, ff), min(1024, w...  131 us
    pallas_call x2, Pallas kernels, weight_grads(): pl.pallas_call(functools.partial(weight_grad_kernel, half), grid_spec=plt...  52.8 us
    unnamed x154, local copies, waits for them, and re-layouts  42.9 us
    ppermute x35, starting transfers between devices, swap(): return lax.ppermute(value, 'replica', [(r, r ^ k) for r in range(replicas)])  40.7 us
    ppermute x6, starting transfers between devices, pass_on(): return (lax.ppermute(up, 'fsdp', pairs), lax.ppermute(down, 'fsdp', back))  17.3 us
  transfers between devices with their start and end apart: 64, of which 22 were waited for; matrix products, arithmetic and copies ran while one was open for 9% of the time, Pallas kernels for 37%

profile of v3, /device:TPU:8, one launch (start us, length us, event | category | flops | bytes accessed | tf_op | source)
XLA Modules:
  0.0 778.4 jit_solution(17108635459929986547)
XLA Ops:
  22.8 2.5 collective-permute-start.5
  29.5 18.1 %collective-permute-done.3.refs_1_ = bf16[256,2048]{1,0:T(8,128)(2,1)S(1)} collective-permute-done((bf16[256,2048]{1,0:T(8,128)(2,1)}, bf16[256,2048]{1,0:T(8,128)(2,1)S(1)}, u32[]{:S(2)}, u32[]{:S(2)}) %collective-permute-start.3) | collective-permute-done | bytes 1048608 | tf_op jit(solution)/shard_map/ppermute | solution.py:743
  47.9 19.5 %collective-permute-done.4.refs_2_ = bf16[256,2048]{1,0:T(8,128)(2,1)S(1)} collective-permute-done((bf16[256,2048]{1,0:T(8,128)(2,1)}, bf16[256,2048]{1,0:T(8,128)(2,1)S(1)}, u32[]{:S(2)}, u32[]{:S(2)}) %collective-permute-start.4) | collective-permute-done | bytes 1048608 | tf_op jit(solution)/shard_map/ppermute | solution.py:743
  71.7 2.5 pad_maximum_fusion.refs_6_.refs_0_
  91.0 11.8 %collective-permute-done.6.refs_0_ = bf16[1024,512]{1,0:T(8,128)(2,1)S(1)} collective-permute-done((bf16[1024,512]{1,0:T(8,128)(2,1)}, bf16[1024,512]{1,0:T(8,128)(2,1)S(1)}, u32[]{:S(2)}, u32[]{:S(2)}) %collective-permute-start.6) | collective-permute-done | bytes 1048608 | tf_op jit(solution)/shard_map/ppermute | solution.py:743
  103.7 18.5 %collective-permute-done.7.refs_2_ = bf16[1024,512]{1,0:T(8,128)(2,1)} collective-permute-done((bf16[1024,512]{1,0:T(8,128)(2,1)}, bf16[1024,512]{1,0:T(8,128)(2,1)}, u32[]{:S(2)}, u32[]{:S(2)}) %collective-permute-start.7) | collective-permute-done | bytes 1048608 | tf_op jit(solution)/shard_map/ppermute | solution.py:743
  122.2 14.6 %attention.1 = (f32[1024,1024]{1,0:T(8,128)}, bf16[1024,1536]{1,0:T(8,128)(2,1)}, bf16[1024,512]{1,0:T(8,128)(2,1)}, f32[1024,128]{1,0:T(8,128)}, f32[4,1,128]{2,1,0:T(1,128)}) custom-call(bf16[1024,2048]{1,0:T(8,128)(2,1)} %after.32.normed.left, bf16[2048,1536]{1,0:T(8,128)(2,1)} %all-gather.6.cloned.1.call-done.weight, ...), custom_call_target="tpu_custom_call" | custom-call | tf_op jit(solution)/shard_map/attention/pallas_call | solution.py:379
  138.1 3.7 pad_maximum_fusion.1.refs_4_.refs_10_
  147.4 4.4 collective-permute-done.9.refs_1_
  151.8 5.5 collective-permute-done.10.refs_2_
  158.1 8.5 %attention_out.1 = (f32[256,2048]{1,0:T(8,128)}, bf16[256,2048]{1,0:T(8,128)(2,1)}, bf16[256,2048]{1,0:T(8,128)(2,1)}) custom-call(s32[3]{0:T(128)} %pad_add_fusion.2.who, bf16[256,512]{1,0:T(8,128)(2,1)} %get-tuple-element.229.refs_0_, bf16[256,512]{1,0:T(8,128)(2,1)} %copy-done.58, bf16[256,512]{1,0:T(8,128)(2,1)} %copy-done.59, ...), custom_call_target="tpu_custom_call" | custom-call | tf_op jit(solution)/shard_map/attention_out/pallas_call | solution.py:252
  167.2 3.5 collective-permute-start.13
  173.1 32.8 %experts.4 = (bf16[2,1152,2048]{2,1,0:T(8,128)(2,1)}, bf16[2,1152,2048]{2,1,0:T(8,128)(2,1)}, bf16[2,1152,2048]{2,1,0:T(8,128)(2,1)}, bf16[2,1152,1024]{2,1,0:T(...) custom-call(s32[5]{0:T(128)} %stack.125.who, ...), custom_call_target="tpu_custom_call" | custom-call | flops 28991029248 | bytes 46137344 | tf_op jit(solution)/shard_map/experts/pallas_call | solution.py:203
  205.9 5.8 collective-permute-done.13.refs_0_
  219.3 5.6 collective-permute-start.16
  226.9 32.8 %experts.5 = (bf16[2,1152,2048]{2,1,0:T(8,128)(2,1)}, bf16[2,1152,2048]{2,1,0:T(8,128)(2,1)}, bf16[2,1152,2048]{2,1,0:T(8,128)(2,1)}, bf16[2,1152,1024]{2,1,0:T(...) custom-call(s32[5]{0:T(128)} %stack.129.who, ...), custom_call_target="tpu_custom_call", output_to_operand_aliasing={{0}: (14, {}), {1}: (15, {}), {2}: (16, {}), {3}: (17, {}),... | custom-call | flops 28991029248 | bytes 46137344 | tf_op jit(solution)/shard_map/experts/pallas_call | solution.py:203
  270.8 33.1 %experts.6 = (bf16[2,1152,2048]{2,1,0:T(8,128)(2,1)}, bf16[2,1152,2048]{2,1,0:T(8,128)(2,1)}, bf16[2,1152,2048]{2,1,0:T(8,128)(2,1)}, bf16[2,1152,1024]{2,1,0:T(...) custom-call(s32[5]{0:T(128)} %stack.133.who, ...), custom_call_target="tpu_custom_call", output_to_operand_aliasing={{0}: (14, {}), {1}: (15, {}), {2}: (16, {}), {3}: (17, {}),... | custom-call | flops 28991029248 | bytes 46137344 | tf_op jit(solution)/shard_map/experts/pallas_call | solution.py:203
  306.5 2.7 add_convert_fusion.3.refs_18_
  309.2 2.7 add_convert_fusion.2.refs_19_
  311.9 4.2 collective-permute-start.30
  317.0 32.6 %experts.7 = (bf16[2,1152,2048]{2,1,0:T(8,128)(2,1)}, bf16[2,1152,2048]{2,1,0:T(8,128)(2,1)}, bf16[2,1152,2048]{2,1,0:T(8,128)(2,1)}, bf16[2,1152,1024]{2,1,0:T(...) custom-call(s32[5]{0:T(128)} %stack.122.who, ...), custom_call_target="tpu_custom_call", output_to_operand_aliasing={{0}: (14, {}), {1}: (15, {}), {2}: (16, {}), {3}: (17, {}),... | custom-call | flops 28991029248 | bytes 46137344 | tf_op jit(solution)/shard_map/experts/pallas_call | solution.py:203
  349.7 20.4 %weight_grads.2 = (bf16[2,256,2048]{2,1,0:T(8,128)(2,1)}, bf16[2,256,2048]{2,1,0:T(8,128)(2,1)}, bf16[2,256,2048]{2,1,0:T(8,128)(2,1)}, bf16[2,256,2048]{2,1,0:T(8,128)(2,1)}) custom-call(s32[2,4]{1,0:T(2,128)} %pad_add_fusion.1.quarters, bf16[2,1152,1024]{2,1,0:T(8,128)(2,1)} %after.40.left, bf16[2,1152,2048]{2,1,0:T(8,128)(2,1)} %get-tuple-element.117.right), custom_call_target="tpu_custom_call" | custom-call | tf_op jit(solution)/shard_map/weight_grads/pallas_call | solution.py:499
  374.5 2.7 add_convert_fusion.1.refs_1_
  377.2 32.5 %weight_grads.3 = (bf16[2,512,2048]{2,1,0:T(8,128)(2,1)}, bf16[2,512,2048]{2,1,0:T(8,128)(2,1)}, bf16[2,512,2048]{2,1,0:T(8,128)(2,1)}, bf16[2,512,2048]{2,1,0:T(8,128)(2,1)}) custom-call(s32[2,4]{1,0:T(2,128)} %pad_add_fusion.1.quarters, bf16[2,1152,2048]{2,1,0:T(8,128)(2,1)} %after.42.left, bf16[2,1152,2048]{2,1,0:T(8,128)(2,1)} %get-tuple-element.123.right), custom_call_target="tpu_custom_call" | custom-call | flops 99999997952 | tf_op jit(solution)/shard_map/weight_grads/pallas_call | solution.py:499
  409.7 10.1 %collective-permute-done.33.refs_5_.refs_2_.refs_0_ = bf16[2,256,2048]{2,1,0:T(8,128)(2,1)} collective-permute-done((bf16[2,256,2048]{2,1,0:T(8,128)(2,1)}, bf16[2,256,2048]{2,1,0:T(8,128)(2,1)}, u32[]{:S(2)}, u32[]{:S(2)}) %collective-permute-start.33) | collective-permute-done | bytes 2097184 | tf_op jit(solution)/shard_map/ppermute | solution.py:743
  421.1 6.8 collective-permute-done.32.refs_0_
  433.0 12.6 %attention_back.1 = (f32[256,2048]{1,0:T(8,128)}, f32[1,2048]{1,0:T(1,128)}, bf16[2048,128]{1,0:T(8,128)(2,1)}, bf16[256,1024]{1,0:T(8,128)(2,1)}, bf16[256,1024...) custom-call(s32[3]{0:T(128)} %pad_add_fusion.2.who, ...), custom_call_target="tpu_custom_call" | custom-call | flops 99999997952 | tf_op jit(solution)/shard_map/attention_back/pallas_call | solution.py:320
  450.2 10.4 %collective-permute-done.36 = bf16[256,1024]{1,0:T(8,128)(2,1)S(1)} collective-permute-done((bf16[256,1024]{1,0:T(8,128)(2,1)}, bf16[256,1024]{1,0:T(8,128)(2,1)S(1)}, u32[]{:S(2)}, u32[]{:S(2)}) %collective-permute-start.36) | collective-permute-done | bytes 524320 | tf_op jit(solution)/shard_map/ppermute | solution.py:743
  460.7 11.5 %collective-permute-done.37 = bf16[256,1024]{1,0:T(8,128)(2,1)S(1)} collective-permute-done((bf16[256,1024]{1,0:T(8,128)(2,1)}, bf16[256,1024]{1,0:T(8,128)(2,1)S(1)}, u32[]{:S(2)}, u32[]{:S(2)}) %collective-permute-start.37) | collective-permute-done | bytes 524320 | tf_op jit(solution)/shard_map/ppermute | solution.py:743
  473.6 5.0 fusion.9
  490.0 14.2 %attention_grad.1 = (bf16[1024,1536]{1,0:T(8,128)(2,1)S(1)}, f32[4,2,128]{2,1,0:T(2,128)S(1)}) custom-call(bf16[1024,1024]{1,0:T(8,128)(2,1)S(1)} %copy-done.6, f32[1024,1024]{1,0:T(8,128)S(1)} %copy-done.8, bf16[1024,1536]{1,0:T(8,128)(2,1)S(1)} %copy-done.16, f32[1024,128]{1,0:T(8,128)S(1)} %copy-done.26, s32[4,1,256]{2,1,0:T(1,128)S(1)} %copy-done.27, ...), custom_call_target="tpu_custom_call" | custom-call | tf_op jit(solution)/shard_map/attention_grad/pallas_call | solution.py:447
  504.3 8.7 %product.1 = bf16[2048,1536]{1,0:T(8,128)(2,1)S(1)} custom-call(bf16[1024,2048]{1,0:T(8,128)(2,1)S(1)} %copy-done.2, bf16[1024,1536]{1,0:T(8,128)(2,1)S(1)} %get-tuple-element.135.grad.right), custom_call_target="tpu_custom_call" | custom-call | tf_op jit(solution)/shard_map/product/pallas_call | solution.py:525
  513.0 2.6 copy-done.7
  517.2 12.5 %normed_grads.1 = (bf16[256,2048]{1,0:T(8,128)(2,1)S(1)}, bf16[256,2048]{1,0:T(8,128)(2,1)}, bf16[256,2048]{1,0:T(8,128)(2,1)}, bf16[256,2048]{1,0:T(8,128)(2,1)}) custom-call(bf16[1024,1536]{1,0:T(8,128)(2,1)} %copy-done.9, bf16[2048,1536]{1,0:T(8,128)(2,1)} %all-gather.6.cloned.1.call-done.weight), custom_call_target="tpu_custom_call" | custom-call | tf_op jit(solution)/shard_map/normed_grads/pallas_call | solution.py:553
  533.3 41.2 %collective-permute-done.40.refs_1_.got = bf16[2,512,2048]{2,1,0:T(8,128)(2,1)} collective-permute-done((bf16[2,512,2048]{2,1,0:T(8,128)(2,1)}, bf16[2,512,2048]{2,1,0:T(8,128)(2,1)}, u32[]{:S(2)}, u32[]{:S(2)}) %collective-permute-start.40) | collective-permute-done | bytes 4194336 | tf_op jit(solution)/shard_map/ppermute | solution.py:743
  576.6 5.8 halve.5
  587.1 4.4 halve.4
  594.1 6.5 collective-permute-done.41.refs_1_
  600.6 22.5 %collective-permute-done.43.refs_3_ = bf16[256,2048]{1,0:T(8,128)(2,1)} collective-permute-done((bf16[256,2048]{1,0:T(8,128)(2,1)}, bf16[256,2048]{1,0:T(8,128)(2,1)}, u32[]{:S(2)}, u32[]{:S(2)}) %collective-permute-start.43) | collective-permute-done | bytes 1048608 | tf_op jit(solution)/shard_map/ppermute | solution.py:743
  623.1 6.2 input_grad.1
  629.4 35.3 %collective-permute-done.45.refs_2_ = bf16[1,512,2048]{2,1,0:T(8,128)(2,1)} collective-permute-done((bf16[1,512,2048]{2,1,0:T(8,128)(2,1)}, bf16[1,512,2048]{2,1,0:T(8,128)(2,1)}, u32[]{:S(2)}, u32[]{:S(2)}) %collective-permute-start.45) | collective-permute-done | bytes 2097184 | tf_op jit(solution)/shard_map/ppermute | solution.py:743
  674.7 3.2 halve.6
  688.9 3.3 collective-permute-start.50
  692.2 7.6 join.2.refs_1_
  706.3 3.4 multiply_convert_fusion
  709.7 50.8 %collective-permute-done.56.refs_0_ = bf16[1,256,2048]{2,1,0:T(8,128)(2,1)} collective-permute-done((bf16[1,256,2048]{2,1,0:T(8,128)(2,1)S(1)}, bf16[1,256,2048]{2,1,0:T(8,128)(2,1)}, u32[]{:S(2)}, u32[]{:S(2)}) %collective-permute-start.56) | collective-permute-done | bytes 1048608 | tf_op jit(solution)/shard_map/ppermute | solution.py:743
  760.5 4.5 join.3
  765.0 5.4 gather_columns.1
  (388 shorter events, 147.3 us)
Async XLA Ops:
  7.2 67.0 %all-gather.4.cloned.1.call-start = ((), (), s32[]{:S(2)}) async-start(), calls=%async_computation.3 | async-start | bytes 2949120 | tf_op jit(solution)/shard_map/all_gather | solution.py:786
  9.9 112.3 %all-gather.6.cloned.1.call-start = ((), (), s32[]{:S(2)}) async-start(), calls=%async_computation.4 | async-start | bytes 7077888 | tf_op jit(solution)/shard_map/all_gather | solution.py:786
  13.1 213.7 %all-gather.8.cloned.1.call-start = ((), (), s32[]{:S(2)}) async-start(), calls=%async_computation.5 | async-start | bytes 9437184 | tf_op jit(solution)/shard_map/all_gather | solution.py:786
  16.7 568.1 %reduce-scatter.4.cloned.1.call-start = ((), (), s32[]{:S(2)}) async-start(), calls=%async_computation.6 | async-start | bytes 9437184 | tf_op jit(solution)/shard_map/reduce_scatter | solution.py:789
  21.3 26.3 %collective-permute-start.3 = (bf16[256,2048]{1,0:T(8,128)(2,1)}, bf16[256,2048]{1,0:T(8,128)(2,1)S(1)}, u32[]{:S(2)}, u32[]{:S(2)}) collective-permute-start(bf16[256,2048]{1,0:T(8,128)(2,1)} %after.29), channel_id=1, source_target_pairs={{0,8},{8,0},{16,24},{24,16},{1,9},{9,1},{17,25},{25,17},{2,10},{10... | collective-permute-start | bytes 3145736 | tf_op jit(solution)/shard_map/ppermute | solution.py:743
  21.8 45.6 %collective-permute-start.4 = (bf16[256,2048]{1,0:T(8,128)(2,1)}, bf16[256,2048]{1,0:T(8,128)(2,1)S(1)}, u32[]{:S(2)}, u32[]{:S(2)}) collective-permute-start(bf16[256,2048]{1,0:T(8,128)(2,1)} %after.29), channel_id=1, source_target_pairs={{0,16},{8,24},{16,0},{24,8},{1,17},{9,25},{17,1},{25,9},{2,18},{10... | collective-permute-start | bytes 3145736 | tf_op jit(solution)/shard_map/ppermute | solution.py:743
  22.8 44.9 %collective-permute-start.5 = (bf16[256,2048]{1,0:T(8,128)(2,1)}, bf16[256,2048]{1,0:T(8,128)(2,1)}, u32[]{:S(2)}, u32[]{:S(2)}) collective-permute-start(bf16[256,2048]{1,0:T(8,128)(2,1)} %after.29), channel_id=1, source_target_pairs={{0,24},{8,16},{16,8},{24,0},{1,25},{9,17},{17,9},{25,1},{2,26},{10... | collective-permute-start | bytes 3145736 | tf_op jit(solution)/shard_map/ppermute | solution.py:743
  76.5 26.3 %collective-permute-start.6 = (bf16[1024,512]{1,0:T(8,128)(2,1)}, bf16[1024,512]{1,0:T(8,128)(2,1)S(1)}, u32[]{:S(2)}, u32[]{:S(2)}) collective-permute-start(bf16[1024,512]{1,0:T(8,128)(2,1)} %after.30.refs_0_), channel_id=1, source_target_pairs={{0,8},{8,0},{16,24},{24,16},{1,9},{9,1},{17,25},{25,17},{2,10},{10... | collective-permute-start | bytes 3145736 | tf_op jit(solution)/shard_map/ppermute | solution.py:743
  77.9 44.3 %collective-permute-start.7 = (bf16[1024,512]{1,0:T(8,128)(2,1)}, bf16[1024,512]{1,0:T(8,128)(2,1)}, u32[]{:S(2)}, u32[]{:S(2)}) collective-permute-start(bf16[1024,512]{1,0:T(8,128)(2,1)} %after.30.refs_0_), channel_id=1, source_target_pairs={{0,16},{8,24},{16,0},{24,8},{1,17},{9,25},{17,1},{25,9},{2,18},{10... | collective-permute-start | bytes 3145736 | tf_op jit(solution)/shard_map/ppermute | solution.py:743
  78.4 43.9 %collective-permute-start.8 = (bf16[1024,512]{1,0:T(8,128)(2,1)}, bf16[1024,512]{1,0:T(8,128)(2,1)}, u32[]{:S(2)}, u32[]{:S(2)}) collective-permute-start(bf16[1024,512]{1,0:T(8,128)(2,1)} %after.30.refs_0_), channel_id=1, source_target_pairs={{0,24},{8,16},{16,8},{24,0},{1,25},{9,17},{17,9},{25,1},{2,26},{10... | collective-permute-start | bytes 3145736 | tf_op jit(solution)/shard_map/ppermute | solution.py:743
  141.8 15.4 %collective-permute-start.12 = (bf16[4,1024,512]{2,1,0:T(8,128)(2,1)}, bf16[4,1024,512]{2,1,0:T(8,128)(2,1)}, u32[]{:S(2)}, u32[]{:S(2)}) collective-permute-start(bf16[4,1024,512]{2,1,0:T(8,128)(2,1)} %pad_maximum_fusion.1.refs_4_.refs_10_), channel_id=1, source_target_pairs={{0,1},{1,0},{2,3},{3,2},{4,5},{5,4},{6,7},{7,6},{8,9},{9,8},{10,11... | collective-permute-start | bytes 12582920 | tf_op jit(solution)/shard_map/ppermute | solution.py:761
  143.2 14.0 %collective-permute-start.10 = (bf16[256,512]{1,0:T(8,128)(2,1)S(1)}, bf16[256,512]{1,0:T(8,128)(2,1)S(1)}, u32[]{:S(2)}, u32[]{:S(2)}) collective-permute-start(bf16[256,512]{1,0:T(8,128)(2,1)S(1)} %get-tuple-element.227), channel_id=1, source_target_pairs={{0,16},{8,24},{16,0},{24,8},{1,17},{9,25},{17,1},{25,9},{2,18},{10... | collective-permute-start | bytes 786440 | tf_op jit(solution)/shard_map/ppermute | solution.py:743
  146.2 26.9 %collective-permute-start.15 = (bf16[256,2048]{1,0:T(8,128)(2,1)S(1)}, bf16[256,2048]{1,0:T(8,128)(2,1)}, u32[]{:S(2)}, u32[]{:S(2)}) collective-permute-start(bf16[256,2048]{1,0:T(8,128)(2,1)S(1)} %copy-done.54), channel_id=1, source_target_pairs={{0,1},{1,0},{2,3},{3,2},{4,5},{5,4},{6,7},{7,6},{8,9},{9,8},{10,11... | collective-permute-start | bytes 3145736 | tf_op jit(solution)/shard_map/ppermute | solution.py:761
  167.2 44.5 %collective-permute-start.13 = (bf16[256,2048]{1,0:T(8,128)(2,1)}, bf16[256,2048]{1,0:T(8,128)(2,1)S(1)}, u32[]{:S(2)}, u32[]{:S(2)}) collective-permute-start(bf16[256,2048]{1,0:T(8,128)(2,1)} %get-tuple-element.91.refs_0_.refs_5_), channel_id=1, source_target_pairs={{0,2},{1,3},{2,4},{3,5},{4,6},{5,7},{8,10},{9,11},{10,12},{11,13},... | collective-permute-start | bytes 3145736 | tf_op jit(solution)/shard_map/ppermute | solution.py:767
  170.7 42.8 %collective-permute-start.17 = (bf16[256,2048]{1,0:T(8,128)(2,1)}, bf16[256,2048]{1,0:T(8,128)(2,1)S(1)}, u32[]{:S(2)}, u32[]{:S(2)}) collective-permute-start(bf16[256,2048]{1,0:T(8,128)(2,1)} %get-tuple-element.91.refs_0_.refs_5_), channel_id=1, source_target_pairs={{2,0},{3,1},{4,2},{5,3},{6,4},{7,5},{10,8},{11,9},{12,10},{13,11},... | collective-permute-start | bytes 3145736 | tf_op jit(solution)/shard_map/ppermute | solution.py:767
  216.3 53.9 %collective-permute-start.22 = (bf16[256,2048]{1,0:T(8,128)(2,1)}, bf16[256,2048]{1,0:T(8,128)(2,1)}, u32[]{:S(2)}, u32[]{:S(2)}) collective-permute-start(bf16[256,2048]{1,0:T(8,128)(2,1)} %get-tuple-element.104), channel_id=1, source_target_pairs={{0,8},{8,0},{16,24},{24,16},{1,9},{9,1},{17,25},{25,17},{2,10},{10... | collective-permute-start | bytes 3145736 | tf_op jit(solution)/shard_map/ppermute | solution.py:743
  217.8 52.9 %collective-permute-start.23 = (bf16[256,2048]{1,0:T(8,128)(2,1)}, bf16[256,2048]{1,0:T(8,128)(2,1)}, u32[]{:S(2)}, u32[]{:S(2)}) collective-permute-start(bf16[256,2048]{1,0:T(8,128)(2,1)} %get-tuple-element.104), channel_id=1, source_target_pairs={{0,16},{8,24},{16,0},{24,8},{1,17},{9,25},{17,1},{25,9},{2,18},{10... | collective-permute-start | bytes 3145736 | tf_op jit(solution)/shard_map/ppermute | solution.py:743
  219.3 40.4 %collective-permute-start.16 = (bf16[256,2048]{1,0:T(8,128)(2,1)S(1)}, bf16[256,2048]{1,0:T(8,128)(2,1)}, u32[]{:S(2)}, u32[]{:S(2)}) collective-permute-start(bf16[256,2048]{1,0:T(8,128)(2,1)S(1)} %copy-done.43), channel_id=1, source_target_pairs={{2,4},{3,5},{4,6},{5,7},{10,12},{11,13},{12,14},{13,15},{18,20},{1... | collective-permute-start | bytes 3145736 | tf_op jit(solution)/shard_map/ppermute | solution.py:767
  224.9 34.8 %collective-permute-start.20 = (bf16[256,2048]{1,0:T(8,128)(2,1)S(1)}, bf16[256,2048]{1,0:T(8,128)(2,1)S(1)}, u32[]{:S(2)}, u32[]{:S(2)}) collective-permute-start(bf16[256,2048]{1,0:T(8,128)(2,1)S(1)} %copy-done.41), channel_id=1, source_target_pairs={{2,0},{3,1},{4,2},{5,3},{10,8},{11,9},{12,10},{13,11},{18,16},{19,... | collective-permute-start | bytes 3145736 | tf_op jit(solution)/shard_map/ppermute | solution.py:767
  266.3 38.7 %collective-permute-start.19 = (bf16[256,2048]{1,0:T(8,128)(2,1)}, bf16[256,2048]{1,0:T(8,128)(2,1)}, u32[]{:S(2)}, u32[]{:S(2)}) collective-permute-start(bf16[256,2048]{1,0:T(8,128)(2,1)} %after.36), channel_id=1, source_target_pairs={{4,6},{5,7},{12,14},{13,15},{20,22},{21,23},{28,30},{29,31}} | collective-permute-start | bytes 3145736 | tf_op jit(solution)/shard_map/ppermute | solution.py:767
  268.0 37.0 %collective-permute-start.24 = (bf16[256,2048]{1,0:T(8,128)(2,1)S(1)}, bf16[256,2048]{1,0:T(8,128)(2,1)}, u32[]{:S(2)}, u32[]{:S(2)}) collective-permute-start(bf16[256,2048]{1,0:T(8,128)(2,1)S(1)} %copy-done.50), channel_id=1, source_target_pairs={{2,0},{3,1},{10,8},{11,9},{18,16},{19,17},{26,24},{27,25}} | collective-permute-start | bytes 3145736 | tf_op jit(solution)/shard_map/ppermute | solution.py:767
  270.2 35.3 %collective-permute-start.26 = (bf16[272,2048]{1,0:T(8,128)(2,1)}, bf16[272,2048]{1,0:T(8,128)(2,1)}, u32[]{:S(2)}, u32[]{:S(2)}) collective-permute-start(bf16[272,2048]{1,0:T(8,128)(2,1)} %get-tuple-element.111), channel_id=1, source_target_pairs={{0,1},{1,0},{2,3},{3,2},{4,5},{5,4},{6,7},{7,6},{8,9},{9,8},{10,11... | collective-permute-start | bytes 3342344 | tf_op jit(solution)/shard_map/ppermute | solution.py:761
  304.7 45.0 %collective-permute-start.28 = (bf16[256,2048]{1,0:T(8,128)(2,1)}, bf16[256,2048]{1,0:T(8,128)(2,1)}, u32[]{:S(2)}, u32[]{:S(2)}) collective-permute-start(bf16[256,2048]{1,0:T(8,128)(2,1)} %get-tuple-element.104), channel_id=1, source_target_pairs={{0,24},{8,16},{16,8},{24,0},{1,25},{9,17},{17,9},{25,1},{2,26},{10... | collective-permute-start | bytes 3145736 | tf_op jit(solution)/shard_map/ppermute | solution.py:743
  309.2 60.9 %collective-permute-start.29 = (bf16[272,2048]{1,0:T(8,128)(2,1)}, bf16[272,2048]{1,0:T(8,128)(2,1)S(1)}, u32[]{:S(2)}, u32[]{:S(2)}) collective-permute-start(bf16[272,2048]{1,0:T(8,128)(2,1)} %add_convert_fusion.3.refs_18_), channel_id=1, source_target_pairs={{0,2},{1,3},{2,0},{3,1},{4,6},{5,7},{6,4},{7,5},{8,10},{9,11},{10,... | collective-permute-start | bytes 3342344 | tf_op jit(solution)/shard_map/ppermute | solution.py:761
  311.9 58.2 %collective-permute-start.30 = (bf16[272,2048]{1,0:T(8,128)(2,1)}, bf16[272,2048]{1,0:T(8,128)(2,1)S(1)}, u32[]{:S(2)}, u32[]{:S(2)}) collective-permute-start(bf16[272,2048]{1,0:T(8,128)(2,1)} %add_convert_fusion.2.refs_19_), channel_id=1, source_target_pairs={{0,4},{1,5},{2,6},{3,7},{4,0},{5,1},{6,2},{7,3},{8,12},{9,13},{10,... | collective-permute-start | bytes 3342344 | tf_op jit(solution)/shard_map/ppermute | solution.py:761
  371.4 48.4 %collective-permute-start.33 = (bf16[2,256,2048]{2,1,0:T(8,128)(2,1)}, bf16[2,256,2048]{2,1,0:T(8,128)(2,1)}, u32[]{:S(2)}, u32[]{:S(2)}) collective-permute-start(bf16[2,256,2048]{2,1,0:T(8,128)(2,1)} %get-tuple-element.118.refs_1_), channel_id=1, source_target_pairs={{0,8},{8,0},{16,24},{24,16},{1,9},{9,1},{17,25},{25,17},{2,10},{10... | collective-permute-start | bytes 6291464 | tf_op jit(solution)/shard_map/ppermute | solution.py:743
  373.1 48.0 %collective-permute-start.34 = (bf16[2,256,2048]{2,1,0:T(8,128)(2,1)}, bf16[2,256,2048]{2,1,0:T(8,128)(2,1)S(1)}, u32[]{:S(2)}, u32[]{:S(2)}) collective-permute-start(bf16[2,256,2048]{2,1,0:T(8,128)(2,1)} %get-tuple-element.120.refs_3_), channel_id=1, source_target_pairs={{0,16},{8,24},{16,0},{24,8},{1,17},{9,25},{17,1},{25,9},{2,18},{10... | collective-permute-start | bytes 6291464 | tf_op jit(solution)/shard_map/ppermute | solution.py:743
  377.2 50.6 %collective-permute-start.32 = (bf16[272,2048]{1,0:T(8,128)(2,1)}, bf16[272,2048]{1,0:T(8,128)(2,1)}, u32[]{:S(2)}, u32[]{:S(2)}) collective-permute-start(bf16[272,2048]{1,0:T(8,128)(2,1)} %add_convert_fusion.1.refs_1_), channel_id=1, source_target_pairs={{0,6},{1,7},{2,4},{3,5},{4,2},{5,3},{6,0},{7,1},{8,14},{9,15},{10,... | collective-permute-start | bytes 3342344 | tf_op jit(solution)/shard_map/ppermute | solution.py:761
  427.9 240.4 %reduce-scatter.8.cloned.1.call-start = ((), (), s32[]{:S(2)}) async-start(), calls=%async_computation.8 | async-start | bytes 2949120 | tf_op jit(solution)/shard_map/reduce_scatter | solution.py:789
  445.7 15.0 %collective-permute-start.36 = (bf16[256,1024]{1,0:T(8,128)(2,1)}, bf16[256,1024]{1,0:T(8,128)(2,1)S(1)}, u32[]{:S(2)}, u32[]{:S(2)}) collective-permute-start(bf16[256,1024]{1,0:T(8,128)(2,1)} %get-tuple-element.130), channel_id=1, source_target_pairs={{0,8},{8,0},{16,24},{24,16},{1,9},{9,1},{17,25},{25,17},{2,10},{10... | collective-permute-start | bytes 1572872 | tf_op jit(solution)/shard_map/ppermute | solution.py:743
  447.2 25.0 %collective-permute-start.37 = (bf16[256,1024]{1,0:T(8,128)(2,1)}, bf16[256,1024]{1,0:T(8,128)(2,1)S(1)}, u32[]{:S(2)}, u32[]{:S(2)}) collective-permute-start(bf16[256,1024]{1,0:T(8,128)(2,1)} %get-tuple-element.131), channel_id=1, source_target_pairs={{0,16},{8,24},{16,0},{24,8},{1,17},{9,25},{17,1},{25,9},{2,18},{10... | collective-permute-start | bytes 1572872 | tf_op jit(solution)/shard_map/ppermute | solution.py:743
  448.7 23.6 %collective-permute-start.38 = (bf16[256,1024]{1,0:T(8,128)(2,1)}, bf16[256,1024]{1,0:T(8,128)(2,1)S(1)}, u32[]{:S(2)}, u32[]{:S(2)}) collective-permute-start(bf16[256,1024]{1,0:T(8,128)(2,1)} %get-tuple-element.132), channel_id=1, source_target_pairs={{0,24},{8,16},{16,8},{24,0},{1,25},{9,17},{17,9},{25,1},{2,26},{10... | collective-permute-start | bytes 1572872 | tf_op jit(solution)/shard_map/ppermute | solution.py:743
  480.5 187.8 %reduce-scatter.6.cloned.1.call-start = ((), (), s32[]{:S(2)}) async-start(), calls=%async_computation.7 | async-start | bytes 7077888 | tf_op jit(solution)/shard_map/reduce_scatter | solution.py:789
  480.5 93.9 %collective-permute-start.40 = (bf16[2,512,2048]{2,1,0:T(8,128)(2,1)}, bf16[2,512,2048]{2,1,0:T(8,128)(2,1)}, u32[]{:S(2)}, u32[]{:S(2)}) collective-permute-start(bf16[2,512,2048]{2,1,0:T(8,128)(2,1)} %after.46.refs_2_), channel_id=1, source_target_pairs={{0,16},{8,24},{16,0},{24,8},{1,17},{9,25},{17,1},{25,9},{2,18},{10... | collective-permute-start | bytes 12582920 | tf_op jit(solution)/shard_map/ppermute | solution.py:743
  484.3 100.6 %collective-permute-start.39 = (bf16[2,512,2048]{2,1,0:T(8,128)(2,1)}, bf16[2,512,2048]{2,1,0:T(8,128)(2,1)}, u32[]{:S(2)}, u32[]{:S(2)}) collective-permute-start(bf16[2,512,2048]{2,1,0:T(8,128)(2,1)} %after.45.refs_1_), channel_id=1, source_target_pairs={{0,8},{8,0},{16,24},{24,16},{1,9},{9,1},{17,25},{25,17},{2,10},{10... | collective-permute-start | bytes 12582920 | tf_op jit(solution)/shard_map/ppermute | solution.py:743
  529.7 70.9 %collective-permute-start.41 = (bf16[256,2048]{1,0:T(8,128)(2,1)}, bf16[256,2048]{1,0:T(8,128)(2,1)}, u32[]{:S(2)}, u32[]{:S(2)}) collective-permute-start(bf16[256,2048]{1,0:T(8,128)(2,1)} %get-tuple-element.139), channel_id=1, source_target_pairs={{0,8},{8,0},{16,24},{24,16},{1,9},{9,1},{17,25},{25,17},{2,10},{10... | collective-permute-start | bytes 3145736 | tf_op jit(solution)/shard_map/ppermute | solution.py:743
  531.3 69.3 %collective-permute-start.42 = (bf16[256,2048]{1,0:T(8,128)(2,1)}, bf16[256,2048]{1,0:T(8,128)(2,1)}, u32[]{:S(2)}, u32[]{:S(2)}) collective-permute-start(bf16[256,2048]{1,0:T(8,128)(2,1)} %get-tuple-element.140), channel_id=1, source_target_pairs={{0,16},{8,24},{16,0},{24,8},{1,17},{9,25},{17,1},{25,9},{2,18},{10... | collective-permute-start | bytes 3145736 | tf_op jit(solution)/shard_map/ppermute | solution.py:743
  531.8 91.3 %collective-permute-start.43 = (bf16[256,2048]{1,0:T(8,128)(2,1)}, bf16[256,2048]{1,0:T(8,128)(2,1)}, u32[]{:S(2)}, u32[]{:S(2)}) collective-permute-start(bf16[256,2048]{1,0:T(8,128)(2,1)} %get-tuple-element.141), channel_id=1, source_target_pairs={{0,24},{8,16},{16,8},{24,0},{1,25},{9,17},{17,9},{25,1},{2,26},{10... | collective-permute-start | bytes 3145736 | tf_op jit(solution)/shard_map/ppermute | solution.py:743
  583.7 81.0 %collective-permute-start.45 = (bf16[1,512,2048]{2,1,0:T(8,128)(2,1)}, bf16[1,512,2048]{2,1,0:T(8,128)(2,1)}, u32[]{:S(2)}, u32[]{:S(2)}) collective-permute-start(bf16[1,512,2048]{2,1,0:T(8,128)(2,1)} %get-tuple-element.138.refs_2_), channel_id=1, source_target_pairs={{0,8},{8,0},{16,24},{24,16},{1,9},{9,1},{17,25},{25,17},{2,10},{10... | collective-permute-start | bytes 6291464 | tf_op jit(solution)/shard_map/ppermute | solution.py:743
  592.8 71.9 %collective-permute-start.44 = (bf16[1,512,2048]{2,1,0:T(8,128)(2,1)S(1)}, bf16[1,512,2048]{2,1,0:T(8,128)(2,1)}, u32[]{:S(2)}, u32[]{:S(2)}) collective-permute-start(bf16[1,512,2048]{2,1,0:T(8,128)(2,1)S(1)} %get-tuple-element.137.refs_1_), channel_id=1, source_target_pairs={{0,16},{8,24},{16,0},{24,8},{1,17},{9,25},{17,1},{25,9},{2,18},{10... | collective-permute-start | bytes 6291464 | tf_op jit(solution)/shard_map/ppermute | solution.py:743
  671.7 17.0 %collective-permute-start.49 = (f32[1,4480]{1,0:T(1,128)S(1)}, f32[1,4480]{1,0:T(1,128)S(1)}, u32[]{:S(2)}, u32[]{:S(2)}) collective-permute-start(f32[1,4480]{1,0:T(1,128)S(1)} %maximum_select_fusion.2), channel_id=1, source_target_pairs={{0,1},{1,0},{2,3},{3,2},{4,5},{5,4},{6,7},{7,6},{8,9},{9,8},{10,11... | collective-permute-start | bytes 53768 | tf_op jit(solution)/shard_map/ppermute | solution.py:761
  686.6 78.4 %collective-permute-start.53 = (bf16[256,2176]{1,0:T(8,128)(2,1)}, bf16[256,2176]{1,0:T(8,128)(2,1)S(1)}, u32[]{:S(2)}, u32[]{:S(2)}) collective-permute-start(bf16[256,2176]{1,0:T(8,128)(2,1)} %after.51.refs_0_), channel_id=1, source_target_pairs={{0,8},{8,0},{16,24},{24,16},{1,9},{9,1},{17,25},{25,17},{2,10},{10... | collective-permute-start | bytes 3342344 | tf_op jit(solution)/shard_map/ppermute | solution.py:743
  687.2 77.8 %collective-permute-start.54 = (bf16[256,2176]{1,0:T(8,128)(2,1)}, bf16[256,2176]{1,0:T(8,128)(2,1)}, u32[]{:S(2)}, u32[]{:S(2)}) collective-permute-start(bf16[256,2176]{1,0:T(8,128)(2,1)} %after.51.refs_0_), channel_id=1, source_target_pairs={{0,16},{8,24},{16,0},{24,8},{1,17},{9,25},{17,1},{25,9},{2,18},{10... | collective-permute-start | bytes 3342344 | tf_op jit(solution)/shard_map/ppermute | solution.py:743
  688.9 13.6 %collective-permute-start.51 = (f32[1,4480]{1,0:T(1,128)S(1)}, f32[1,4480]{1,0:T(1,128)S(1)}, u32[]{:S(2)}, u32[]{:S(2)}) collective-permute-start(f32[1,4480]{1,0:T(1,128)S(1)} %maximum_select_fusion.1), channel_id=1, source_target_pairs={{0,4},{1,5},{2,6},{3,7},{4,0},{5,1},{6,2},{7,3},{8,12},{9,13},{10,... | collective-permute-start | bytes 53768 | tf_op jit(solution)/shard_map/ppermute | solution.py:761
  688.9 15.0 %collective-permute-start.50 = (f32[1,4480]{1,0:T(1,128)S(1)}, f32[1,4480]{1,0:T(1,128)S(1)}, u32[]{:S(2)}, u32[]{:S(2)}) collective-permute-start(f32[1,4480]{1,0:T(1,128)S(1)} %maximum_select_fusion.1), channel_id=1, source_target_pairs={{0,2},{1,3},{2,0},{3,1},{4,6},{5,7},{6,4},{7,5},{8,10},{9,11},{10,... | collective-permute-start | bytes 53768 | tf_op jit(solution)/shard_map/ppermute | solution.py:761
  701.1 64.0 %collective-permute-start.55 = (bf16[256,2176]{1,0:T(8,128)(2,1)S(1)}, bf16[256,2176]{1,0:T(8,128)(2,1)}, u32[]{:S(2)}, u32[]{:S(2)}) collective-permute-start(bf16[256,2176]{1,0:T(8,128)(2,1)S(1)} %copy-done.10), channel_id=1, source_target_pairs={{0,24},{8,16},{16,8},{24,0},{1,25},{9,17},{17,9},{25,1},{2,26},{10... | collective-permute-start | bytes 3342344 | tf_op jit(solution)/shard_map/ppermute | solution.py:743
  702.5 58.0 %collective-permute-start.56 = (bf16[1,256,2048]{2,1,0:T(8,128)(2,1)S(1)}, bf16[1,256,2048]{2,1,0:T(8,128)(2,1)}, u32[]{:S(2)}, u32[]{:S(2)}) collective-permute-start(bf16[1,256,2048]{2,1,0:T(8,128)(2,1)S(1)} %copy-done.21), channel_id=1, source_target_pairs={{0,16},{8,24},{16,0},{24,8},{1,17},{9,25},{17,1},{25,9},{2,18},{10... | collective-permute-start | bytes 3145736 | tf_op jit(solution)/shard_map/ppermute | solution.py:743
  704.0 56.6 %collective-permute-start.57 = (bf16[1,256,2048]{2,1,0:T(8,128)(2,1)}, bf16[1,256,2048]{2,1,0:T(8,128)(2,1)}, u32[]{:S(2)}, u32[]{:S(2)}) collective-permute-start(bf16[1,256,2048]{2,1,0:T(8,128)(2,1)} %after.56), channel_id=1, source_target_pairs={{0,8},{8,0},{16,24},{24,16},{1,9},{9,1},{17,25},{25,17},{2,10},{10... | collective-permute-start | bytes 3145736 | tf_op jit(solution)/shard_map/ppermute | solution.py:743
  (90 other events, 481.4 us)
Sparse Core Ops, SparseCore 0:
  10.2 34.3 all-gather.3
  46.9 62.1 all-gather.5
  110.7 96.9 all-gather.7
  428.0 85.9 reduce-scatter.3
  516.1 34.4 reduce-scatter.7
  552.8 70.3 reduce-scatter.5

commit v4 on v3

--- a/solution.py
+++ b/solution.py
@@ -826,9 +826,7 @@
     mask_wide = jnp.pad(mask.astype(F32), ((0, 0), (0, 0), (0, lanes - EXPERTS)))
     router_wide = jnp.pad(full_router, ((0, 0), (0, lanes - EXPERTS)))
     tables = (pick, spots, mask_wide, router_wide)
-    segments = spread(segment_ids)
-    tokens_all = spread(after(tokens, *segments[1:]))
-    segments = jnp.concatenate(segments, axis=0)
+    tokens_all = spread(tokens)
     normed = jnp.concatenate(
         [rms_norm(v.astype(F32), attn_gain).astype(BF) for v in tokens_all], axis=0
     )
@@ -836,7 +834,8 @@
     where = jnp.stack([me_r, me_f // 2, core]).astype(jnp.int32)
     half = lax.dynamic_slice(quarter, (core * (width // 2), 0), (width // 2, part))
     near = spread(after(half, *tokens_all[1:]))
-    near[1] = after(near[1], *tables, segments, normed)
+    near[1] = after(near[1], *tables, normed)
+    segments = jnp.concatenate(spread(after(segment_ids, near[2])), axis=0)
     normed = after(normed, *near[1:])
     w_qkv = gather(jnp.concatenate([columns(w, 0) for w in (w_query, w_key, w_value)], axis=1))
     cot_all = gather(cotangent)
@@ -919,7 +918,7 @@
     in_traded = [
         (in_blocks[2 * j + 1], swap(v, first_bit(j))) for j, v in enumerate(sends)
     ]
-    grad_mixed = after(grad_mixed, *sends)
+    ready = after(ready, *sends)
     grad_qkv, gain_grads = attend_back(grad_mixed, raw, ready, totals, segments, cosine, sine, gains, heads
     )
     qkv_grad = product(normed, grad_qkv)
@@ -930,17 +929,19 @@
     in_halves = [next_halves(v, j, 1, 10**11) for j, v in enumerate(in_traded)]
     in_sends = [v for v, _ in in_halves]
     in_done = [(keep, swap(v, next_bit(j, 1))) for j, (v, keep) in enumerate(in_halves)]
-    pieces = [after(part_normed[0], *in_sends)]
+    mixed_rows = after(jnp.concatenate(mixed_all, axis=0), *in_sends)
+    output_grad = dot_tn(mixed_rows, grad_mixed[:, part:])
+    o_grad = jnp.concatenate([output_grad.astype(BF), router_grad], axis=1)
+    share_o = reduce(o_grad)
+    out_halves = [next_halves((k, after(v, part_normed[0])), j, 1) for j, (k, v) in enumerate(out_traded)]
+    pieces = [after(part_normed[0], *in_sends, o_grad, *[v for v, _ in out_halves])]
     pieces += [swap(part_normed[k], k) for k in range(1, replicas)]
     input_grad, small = input_step(
         where, pieces, tokens, attn_gain[None, :], grad_hidden, ffn_gain_grad, gain_grads, tops, heads
     )
     second = [v[1] for v in in_done]
-    output_grad = dot_tn(jnp.concatenate(mixed_all, axis=0), grad_mixed[:, part:])
-    share_o = reduce(jnp.concatenate([output_grad.astype(BF), router_grad], axis=1))
     share_qkv = reduce(qkv_grad)
-    blocks = spread(after(jnp.concatenate([share_qkv, share_o], axis=1), *second))
-    out_halves = [next_halves((k, after(v, input_grad)), j, 1) for j, (k, v) in enumerate(out_traded)]
+    blocks = spread(after(jnp.concatenate([share_qkv, share_o], axis=1), *second, input_grad))
     out_done = [
         (keep, swap(after(v, *second, moe_sum), next_bit(j, 1))) for j, (v, keep) in enumerate(out_halves)
     ]
@@ -959,7 +960,6 @@
     expert_in_grad = settle(in_done, 10**11)
     expert_out_grad = settle([(k, after(v, expert_in_grad)) for k, v in out_done], 0)
 
-    small = after(small, *second)
     n_sums = 2 * width + 2 * HD
     is_sum = jnp.arange(small.shape[1]) < n_sums
 
@@ -967,8 +967,12 @@
         return jnp.where(is_sum, a + b, jnp.maximum(a, b))
 
     small = functools.reduce(merge, spread(small))
+    small = after(small, *blocks[1:], expert_in_grad)
     small = merge(small, cross(small, 1))
-    small = functools.reduce(merge, [small] + [cross(small, 2 * k) for k in range(1, rounds)])
+    step = 1
+    while step < rounds:
+        small = merge(small, cross(small, 2 * step))
+        step *= 2
     small = small[0]
     attn_gain_total = small[:width]
     ffn_gain_total = small[width : 2 * width]

time: 783 us -> 778 us (level)
  waiting for transfers between devices: 285 us -> 268 us
  other arithmetic: 48.8 us -> 56.9 us
    ppermute x35, waiting for transfers between devices: 271 us -> 257 us  [swap(): return lax.ppermute(value, 'replica', [(r, r ^ k) for r in range(replicas)])]
    unnamed x154 -> x146, local copies, waits for them, and re-layouts: 42.9 us -> 47.5 us
  transfers between devices with their start and end apart: 64 -> 63, of which waited for: 22 -> 20; matrix products, arithmetic and copies ran while one was open for 9% -> 10% of each run, Pallas kernels for 37% -> 38%
where the time goes in v4:
time: 778 us; the launch traced here: 770 us
  Pallas kernels  295 us (38%)
  waiting for transfers between devices  268 us (34%)
  local copies, waits for them, and re-layouts  66 us (8%)
  starting transfers between devices  62.4 us (8%)
  other arithmetic  56.9 us (7%)
  between operations  15.5 us (2%)
    ppermute x35, waiting for transfers between devices, swap(): return lax.ppermute(value, 'replica', [(r, r ^ k) for r in range(replicas)])  257 us
    pallas_call x4, Pallas kernels, expert_block(): pl.pallas_call(functools.partial(expert_kernel, min(512, ff), min(1024, w...  131 us
    pallas_call x2, Pallas kernels, weight_grads(): pl.pallas_call(functools.partial(weight_grad_kernel, half), grid_spec=plt...  52.7 us
    unnamed x146, local copies, waits for them, and re-layouts  47.5 us
    ppermute x35, starting transfers between devices, swap(): return lax.ppermute(value, 'replica', [(r, r ^ k) for r in range(replicas)])  38.4 us
    ppermute x6, starting transfers between devices, pass_on(): return (lax.ppermute(up, 'fsdp', pairs), lax.ppermute(down, 'fsdp', back))  17.7 us
    pallas_call x4, Pallas kernels, halve(): pl.pallas_call(functools.partial(halve_kernel, half), grid_spec=pltpu.Pre...  16.1 us
  transfers between devices with their start and end apart: 63, of which 20 were waited for; matrix products, arithmetic and copies ran while one was open for 10% of the time, Pallas kernels for 38%

profile of v4, /device:TPU:8, one launch (start us, length us, event | category | flops | bytes accessed | tf_op | source)
XLA Modules:
  0.0 770.2 jit_solution(9477502424283105017)
XLA Ops:
  20.9 19.6 %collective-permute-done.refs_1_ = bf16[256,2048]{1,0:T(8,128)(2,1)S(1)} collective-permute-done((bf16[256,2048]{1,0:T(8,128)(2,1)S(1)}, bf16[256,2048]{1,0:T(8,128)(2,1)S(1)}, u32[]{:S(2)}, u32[]{:S(2)}) %collective-permute-start) | collective-permute-done | bytes 1048608 | tf_op jit(solution)/shard_map/ppermute | solution.py:743
  40.8 22.2 %collective-permute-done.1.refs_2_ = bf16[256,2048]{1,0:T(8,128)(2,1)S(1)} collective-permute-done((bf16[256,2048]{1,0:T(8,128)(2,1)S(1)}, bf16[256,2048]{1,0:T(8,128)(2,1)S(1)}, u32[]{:S(2)}, u32[]{:S(2)}) %collective-permute-start.1) | collective-permute-done | bytes 1048608 | tf_op jit(solution)/shard_map/ppermute | solution.py:743
  84.8 34.6 %collective-permute-done.4.refs_2_.refs_1_ = bf16[1024,512]{1,0:T(8,128)(2,1)S(1)} collective-permute-done((bf16[1024,512]{1,0:T(8,128)(2,1)}, bf16[1024,512]{1,0:T(8,128)(2,1)S(1)}, u32[]{:S(2)}, u32[]{:S(2)}) %collective-permute-start.4) | collective-permute-done | bytes 1048608 | tf_op jit(solution)/shard_map/ppermute | solution.py:743
  130.4 14.6 %attention.1 = (f32[1024,1024]{1,0:T(8,128)}, bf16[1024,1536]{1,0:T(8,128)(2,1)}, bf16[1024,512]{1,0:T(8,128)(2,1)}, f32[1024,128]{1,0:T(8,128)}, f32[4,1,128]{2,1,0:T(1,128)}) custom-call(bf16[1024,2048]{1,0:T(8,128)(2,1)} %after.32.normed.left, bf16[2048,1536]{1,0:T(8,128)(2,1)} %all-gather.6.cloned.1.call-done.weight, ...), custom_call_target="tpu_custom_call" | custom-call | tf_op jit(solution)/shard_map/attention/pallas_call | solution.py:379
  146.7 3.5 pad_maximum_fusion.1.refs_4_.refs_10_
  151.7 2.8 collective-permute-start.11
  155.7 4.4 collective-permute-done.9.refs_1_
  160.1 5.5 collective-permute-done.10.refs_2_
  166.4 8.6 %attention_out.1 = (f32[256,2048]{1,0:T(8,128)}, bf16[256,2048]{1,0:T(8,128)(2,1)}, bf16[256,2048]{1,0:T(8,128)(2,1)}) custom-call(s32[3]{0:T(128)} %pad_add_fusion.2.who, bf16[256,512]{1,0:T(8,128)(2,1)} %get-tuple-element.229.refs_0_, bf16[256,512]{1,0:T(8,128)(2,1)} %copy-done.60, bf16[256,512]{1,0:T(8,128)(2,1)} %copy-done.61, ...), custom_call_target="tpu_custom_call" | custom-call | tf_op jit(solution)/shard_map/attention_out/pallas_call | solution.py:252
  175.6 3.3 collective-permute-start.13
  179.0 2.5 collective-permute-start.17
  181.5 32.8 %experts.4 = (bf16[2,1152,2048]{2,1,0:T(8,128)(2,1)}, bf16[2,1152,2048]{2,1,0:T(8,128)(2,1)}, bf16[2,1152,2048]{2,1,0:T(8,128)(2,1)}, bf16[2,1152,1024]{2,1,0:T(...) custom-call(s32[5]{0:T(128)} %stack.125.who, ...), custom_call_target="tpu_custom_call" | custom-call | flops 28991029248 | bytes 46137344 | tf_op jit(solution)/shard_map/experts/pallas_call | solution.py:203
  220.3 6.0 collective-permute-start.16
  228.3 32.8 %experts.5 = (bf16[2,1152,2048]{2,1,0:T(8,128)(2,1)}, bf16[2,1152,2048]{2,1,0:T(8,128)(2,1)}, bf16[2,1152,2048]{2,1,0:T(8,128)(2,1)}, bf16[2,1152,1024]{2,1,0:T(...) custom-call(s32[5]{0:T(128)} %stack.129.who, ...), custom_call_target="tpu_custom_call", output_to_operand_aliasing={{0}: (14, {}), {1}: (15, {}), {2}: (16, {}), {3}: (17, {}),... | custom-call | flops 28991029248 | bytes 46137344 | tf_op jit(solution)/shard_map/experts/pallas_call | solution.py:203
  272.1 33.0 %experts.6 = (bf16[2,1152,2048]{2,1,0:T(8,128)(2,1)}, bf16[2,1152,2048]{2,1,0:T(8,128)(2,1)}, bf16[2,1152,2048]{2,1,0:T(8,128)(2,1)}, bf16[2,1152,1024]{2,1,0:T(...) custom-call(s32[5]{0:T(128)} %stack.133.who, ...), custom_call_target="tpu_custom_call", output_to_operand_aliasing={{0}: (14, {}), {1}: (15, {}), {2}: (16, {}), {3}: (17, {}),... | custom-call | flops 28991029248 | bytes 46137344 | tf_op jit(solution)/shard_map/experts/pallas_call | solution.py:203
  308.8 2.7 add_convert_fusion.3.refs_18_
  311.5 2.7 add_convert_fusion.2.refs_19_
  314.2 4.4 collective-permute-start.30
  319.5 32.6 %experts.7 = (bf16[2,1152,2048]{2,1,0:T(8,128)(2,1)}, bf16[2,1152,2048]{2,1,0:T(8,128)(2,1)}, bf16[2,1152,2048]{2,1,0:T(8,128)(2,1)}, bf16[2,1152,1024]{2,1,0:T(...) custom-call(s32[5]{0:T(128)} %stack.122.who, ...), custom_call_target="tpu_custom_call", output_to_operand_aliasing={{0}: (14, {}), {1}: (15, {}), {2}: (16, {}), {3}: (17, {}),... | custom-call | flops 28991029248 | bytes 46137344 | tf_op jit(solution)/shard_map/experts/pallas_call | solution.py:203
  352.2 20.3 %weight_grads.2 = (bf16[2,256,2048]{2,1,0:T(8,128)(2,1)}, bf16[2,256,2048]{2,1,0:T(8,128)(2,1)}, bf16[2,256,2048]{2,1,0:T(8,128)(2,1)}, bf16[2,256,2048]{2,1,0:T(8,128)(2,1)}) custom-call(s32[2,4]{1,0:T(2,128)} %pad_add_fusion.1.quarters, bf16[2,1152,1024]{2,1,0:T(8,128)(2,1)} %after.41.left, bf16[2,1152,2048]{2,1,0:T(8,128)(2,1)} %get-tuple-element.117.right), custom_call_target="tpu_custom_call" | custom-call | tf_op jit(solution)/shard_map/weight_grads/pallas_call | solution.py:499
  376.9 2.7 add_convert_fusion.1.refs_1_
  379.5 32.4 %weight_grads.3 = (bf16[2,512,2048]{2,1,0:T(8,128)(2,1)}, bf16[2,512,2048]{2,1,0:T(8,128)(2,1)}, bf16[2,512,2048]{2,1,0:T(8,128)(2,1)}, bf16[2,512,2048]{2,1,0:T(8,128)(2,1)}) custom-call(s32[2,4]{1,0:T(2,128)} %pad_add_fusion.1.quarters, bf16[2,1152,2048]{2,1,0:T(8,128)(2,1)} %after.43.left, bf16[2,1152,2048]{2,1,0:T(8,128)(2,1)} %get-tuple-element.123.right), custom_call_target="tpu_custom_call" | custom-call | flops 99999997952 | tf_op jit(solution)/shard_map/weight_grads/pallas_call | solution.py:499
  411.9 10.3 %collective-permute-done.33.refs_5_.refs_2_.refs_0_ = bf16[2,256,2048]{2,1,0:T(8,128)(2,1)} collective-permute-done((bf16[2,256,2048]{2,1,0:T(8,128)(2,1)}, bf16[2,256,2048]{2,1,0:T(8,128)(2,1)}, u32[]{:S(2)}, u32[]{:S(2)}) %collective-permute-start.33) | collective-permute-done | bytes 2097184 | tf_op jit(solution)/shard_map/ppermute | solution.py:743
  423.5 6.8 collective-permute-done.32.refs_0_
  435.5 12.3 %attention_back.1 = (f32[256,2048]{1,0:T(8,128)}, f32[1,2048]{1,0:T(1,128)}, bf16[2048,128]{1,0:T(8,128)(2,1)}, bf16[256,1024]{1,0:T(8,128)(2,1)}, bf16[256,1024...) custom-call(s32[3]{0:T(128)} %pad_add_fusion.2.who, ...), custom_call_target="tpu_custom_call" | custom-call | flops 99999997952 | tf_op jit(solution)/shard_map/attention_back/pallas_call | solution.py:320
  452.4 10.4 %collective-permute-done.36 = bf16[256,1024]{1,0:T(8,128)(2,1)S(1)} collective-permute-done((bf16[256,1024]{1,0:T(8,128)(2,1)}, bf16[256,1024]{1,0:T(8,128)(2,1)S(1)}, u32[]{:S(2)}, u32[]{:S(2)}) %collective-permute-start.36) | collective-permute-done | bytes 524320 | tf_op jit(solution)/shard_map/ppermute | solution.py:743
  462.8 11.4 %collective-permute-done.37 = bf16[256,1024]{1,0:T(8,128)(2,1)S(1)} collective-permute-done((bf16[256,1024]{1,0:T(8,128)(2,1)}, bf16[256,1024]{1,0:T(8,128)(2,1)S(1)}, u32[]{:S(2)}, u32[]{:S(2)}) %collective-permute-start.37) | collective-permute-done | bytes 524320 | tf_op jit(solution)/shard_map/ppermute | solution.py:743
  478.5 3.8 pad_maximum_fusion.2.refs_0_
  489.1 14.2 %attention_grad.1 = (bf16[1024,1536]{1,0:T(8,128)(2,1)S(1)}, f32[4,2,128]{2,1,0:T(2,128)S(1)}) custom-call(bf16[1024,1024]{1,0:T(8,128)(2,1)S(1)} %copy-done.7, f32[1024,1024]{1,0:T(8,128)S(1)} %copy-done.8, bf16[1024,1536]{1,0:T(8,128)(2,1)S(1)} %copy-done.9, f32[1024,128]{1,0:T(8,128)S(1)} %copy-done.26, s32[4,1,256]{2,1,0:T(1,128)S(1)} %copy-done.27, ...), custom_call_target="tpu_custom_call" | custom-call | tf_op jit(solution)/shard_map/attention_grad/pallas_call | solution.py:447
  504.0 8.7 %product.1 = bf16[2048,1536]{1,0:T(8,128)(2,1)S(1)} custom-call(bf16[1024,2048]{1,0:T(8,128)(2,1)S(1)} %copy-done.2, bf16[1024,1536]{1,0:T(8,128)(2,1)S(1)} %get-tuple-element.135.grad.right), custom_call_target="tpu_custom_call" | custom-call | tf_op jit(solution)/shard_map/product/pallas_call | solution.py:525
  512.7 2.6 copy-done.5
  516.9 12.5 %normed_grads.1 = (bf16[256,2048]{1,0:T(8,128)(2,1)S(1)}, bf16[256,2048]{1,0:T(8,128)(2,1)}, bf16[256,2048]{1,0:T(8,128)(2,1)}, bf16[256,2048]{1,0:T(8,128)(2,1)}) custom-call(bf16[1024,1536]{1,0:T(8,128)(2,1)} %copy-done.10, bf16[2048,1536]{1,0:T(8,128)(2,1)} %all-gather.6.cloned.1.call-done.weight), custom_call_target="tpu_custom_call" | custom-call | tf_op jit(solution)/shard_map/normed_grads/pallas_call | solution.py:553
  535.5 2.9 halve.6
  547.5 22.0 %collective-permute-done.40.refs_1_.got = bf16[2,512,2048]{2,1,0:T(8,128)(2,1)} collective-permute-done((bf16[2,512,2048]{2,1,0:T(8,128)(2,1)}, bf16[2,512,2048]{2,1,0:T(8,128)(2,1)}, u32[]{:S(2)}, u32[]{:S(2)}) %collective-permute-start.40) | collective-permute-done | bytes 4194336 | tf_op jit(solution)/shard_map/ppermute | solution.py:743
  571.7 5.7 halve.5
  581.7 5.8 halve.4
  589.8 4.7 convolution_convert_fusion
  598.6 23.0 %collective-permute-done.43.refs_3_ = bf16[256,2048]{1,0:T(8,128)(2,1)} collective-permute-done((bf16[256,2048]{1,0:T(8,128)(2,1)}, bf16[256,2048]{1,0:T(8,128)(2,1)}, u32[]{:S(2)}, u32[]{:S(2)}) %collective-permute-start.43) | collective-permute-done | bytes 1048608 | tf_op jit(solution)/shard_map/ppermute | solution.py:743
  621.6 6.4 input_grad.1
  631.5 32.7 %collective-permute-done.46 = f32[1,4480]{1,0:T(1,128)S(1)} collective-permute-done((f32[1,4480]{1,0:T(1,128)}, f32[1,4480]{1,0:T(1,128)S(1)}, u32[]{:S(2)}, u32[]{:S(2)}) %collective-permute-start.46) | collective-permute-done | bytes 17952 | tf_op jit(solution)/shard_map/ppermute | solution.py:743
  671.4 7.6 join.2.refs_4_.refs_1_
  679.0 16.7 %collective-permute-done.49.refs_1_ = bf16[256,2176]{1,0:T(8,128)(2,1)S(1)} collective-permute-done((bf16[256,2176]{1,0:T(8,128)(2,1)}, bf16[256,2176]{1,0:T(8,128)(2,1)S(1)}, u32[]{:S(2)}, u32[]{:S(2)}) %collective-permute-start.49) | collective-permute-done | bytes 1114144 | tf_op jit(solution)/shard_map/ppermute | solution.py:743
  695.7 21.7 %collective-permute-done.50.refs_2_ = bf16[256,2176]{1,0:T(8,128)(2,1)} collective-permute-done((bf16[256,2176]{1,0:T(8,128)(2,1)}, bf16[256,2176]{1,0:T(8,128)(2,1)}, u32[]{:S(2)}, u32[]{:S(2)}) %collective-permute-start.50) | collective-permute-done | bytes 1114144 | tf_op jit(solution)/shard_map/ppermute | solution.py:743
  723.6 2.8 add_convert_fusion.4
  726.4 18.6 %collective-permute-done.55.refs_0_ = bf16[1,256,2048]{2,1,0:T(8,128)(2,1)S(1)} collective-permute-done((bf16[1,256,2048]{2,1,0:T(8,128)(2,1)}, bf16[1,256,2048]{2,1,0:T(8,128)(2,1)S(1)}, u32[]{:S(2)}, u32[]{:S(2)}) %collective-permute-start.55) | collective-permute-done | bytes 1048608 | tf_op jit(solution)/shard_map/ppermute | solution.py:743
  747.0 4.5 join.3
  751.6 5.4 gather_columns.1
  759.4 3.5 multiply_convert_fusion
  (381 shorter events, 153.5 us)
Async XLA Ops:
  7.2 62.5 %all-gather.4.cloned.1.call-start = ((), (), s32[]{:S(2)}) async-start(), calls=%async_computation.3 | async-start | bytes 2949120 | tf_op jit(solution)/shard_map/all_gather | solution.py:786
  11.2 119.2 %all-gather.6.cloned.1.call-start = ((), (), s32[]{:S(2)}) async-start(), calls=%async_computation.4 | async-start | bytes 7077888 | tf_op jit(solution)/shard_map/all_gather | solution.py:786
  14.3 213.9 %all-gather.8.cloned.1.call-start = ((), (), s32[]{:S(2)}) async-start(), calls=%async_computation.5 | async-start | bytes 9437184 | tf_op jit(solution)/shard_map/all_gather | solution.py:786
  14.4 26.1 %collective-permute-start = (bf16[256,2048]{1,0:T(8,128)(2,1)S(1)}, bf16[256,2048]{1,0:T(8,128)(2,1)S(1)}, u32[]{:S(2)}, u32[]{:S(2)}) collective-permute-start(bf16[256,2048]{1,0:T(8,128)(2,1)S(1)} %copy-done.37), channel_id=1, source_target_pairs={{0,8},{8,0},{16,24},{24,16},{1,9},{9,1},{17,25},{25,17},{2,10},{10... | collective-permute-start | bytes 3145736 | tf_op jit(solution)/shard_map/ppermute | solution.py:743
  16.0 47.1 %collective-permute-start.1 = (bf16[256,2048]{1,0:T(8,128)(2,1)S(1)}, bf16[256,2048]{1,0:T(8,128)(2,1)S(1)}, u32[]{:S(2)}, u32[]{:S(2)}) collective-permute-start(bf16[256,2048]{1,0:T(8,128)(2,1)S(1)} %copy-done.37), channel_id=1, source_target_pairs={{0,16},{8,24},{16,0},{24,8},{1,17},{9,25},{17,1},{25,9},{2,18},{10... | collective-permute-start | bytes 3145736 | tf_op jit(solution)/shard_map/ppermute | solution.py:743
  17.5 45.9 %collective-permute-start.2 = (bf16[256,2048]{1,0:T(8,128)(2,1)S(1)}, bf16[256,2048]{1,0:T(8,128)(2,1)}, u32[]{:S(2)}, u32[]{:S(2)}) collective-permute-start(bf16[256,2048]{1,0:T(8,128)(2,1)S(1)} %copy-done.37), channel_id=1, source_target_pairs={{0,24},{8,16},{16,8},{24,0},{1,25},{9,17},{17,9},{25,1},{2,26},{10... | collective-permute-start | bytes 3145736 | tf_op jit(solution)/shard_map/ppermute | solution.py:743
  18.0 561.5 %reduce-scatter.4.cloned.1.call-start = ((), (), s32[]{:S(2)}) async-start(), calls=%async_computation.6 | async-start | bytes 9437184 | tf_op jit(solution)/shard_map/reduce_scatter | solution.py:789
  72.0 55.1 %collective-permute-start.3 = (bf16[1024,512]{1,0:T(8,128)(2,1)}, bf16[1024,512]{1,0:T(8,128)(2,1)S(1)}, u32[]{:S(2)}, u32[]{:S(2)}) collective-permute-start(bf16[1024,512]{1,0:T(8,128)(2,1)} %after.30.refs_0_), channel_id=1, source_target_pairs={{0,8},{8,0},{16,24},{24,16},{1,9},{9,1},{17,25},{25,17},{2,10},{10... | collective-permute-start | bytes 3145736 | tf_op jit(solution)/shard_map/ppermute | solution.py:743
  73.0 46.5 %collective-permute-start.4 = (bf16[1024,512]{1,0:T(8,128)(2,1)}, bf16[1024,512]{1,0:T(8,128)(2,1)S(1)}, u32[]{:S(2)}, u32[]{:S(2)}) collective-permute-start(bf16[1024,512]{1,0:T(8,128)(2,1)} %after.30.refs_0_), channel_id=1, source_target_pairs={{0,16},{8,24},{16,0},{24,8},{1,17},{9,25},{17,1},{25,9},{2,18},{10... | collective-permute-start | bytes 3145736 | tf_op jit(solution)/shard_map/ppermute | solution.py:743
  74.1 53.9 %collective-permute-start.5 = (bf16[1024,512]{1,0:T(8,128)(2,1)}, bf16[1024,512]{1,0:T(8,128)(2,1)}, u32[]{:S(2)}, u32[]{:S(2)}) collective-permute-start(bf16[1024,512]{1,0:T(8,128)(2,1)} %after.30.refs_0_), channel_id=1, source_target_pairs={{0,24},{8,16},{16,8},{24,0},{1,25},{9,17},{17,9},{25,1},{2,26},{10... | collective-permute-start | bytes 3145736 | tf_op jit(solution)/shard_map/ppermute | solution.py:743
  150.2 15.4 %collective-permute-start.12 = (bf16[4,1024,512]{2,1,0:T(8,128)(2,1)}, bf16[4,1024,512]{2,1,0:T(8,128)(2,1)}, u32[]{:S(2)}, u32[]{:S(2)}) collective-permute-start(bf16[4,1024,512]{2,1,0:T(8,128)(2,1)} %pad_maximum_fusion.1.refs_4_.refs_10_), channel_id=1, source_target_pairs={{0,1},{1,0},{2,3},{3,2},{4,5},{5,4},{6,7},{7,6},{8,9},{9,8},{10,11... | collective-permute-start | bytes 12582920 | tf_op jit(solution)/shard_map/ppermute | solution.py:761
  154.5 27.0 %collective-permute-start.15 = (bf16[256,2048]{1,0:T(8,128)(2,1)S(1)}, bf16[256,2048]{1,0:T(8,128)(2,1)}, u32[]{:S(2)}, u32[]{:S(2)}) collective-permute-start(bf16[256,2048]{1,0:T(8,128)(2,1)S(1)} %copy-done.56), channel_id=1, source_target_pairs={{0,1},{1,0},{2,3},{3,2},{4,5},{5,4},{6,7},{7,6},{8,9},{9,8},{10,11... | collective-permute-start | bytes 3145736 | tf_op jit(solution)/shard_map/ppermute | solution.py:761
  175.6 38.7 %collective-permute-start.13 = (bf16[256,2048]{1,0:T(8,128)(2,1)}, bf16[256,2048]{1,0:T(8,128)(2,1)S(1)}, u32[]{:S(2)}, u32[]{:S(2)}) collective-permute-start(bf16[256,2048]{1,0:T(8,128)(2,1)} %get-tuple-element.91.refs_0_.refs_5_), channel_id=1, source_target_pairs={{0,2},{1,3},{2,4},{3,5},{4,6},{5,7},{8,10},{9,11},{10,12},{11,13},... | collective-permute-start | bytes 3145736 | tf_op jit(solution)/shard_map/ppermute | solution.py:767
  179.0 36.4 %collective-permute-start.17 = (bf16[256,2048]{1,0:T(8,128)(2,1)}, bf16[256,2048]{1,0:T(8,128)(2,1)S(1)}, u32[]{:S(2)}, u32[]{:S(2)}) collective-permute-start(bf16[256,2048]{1,0:T(8,128)(2,1)} %get-tuple-element.91.refs_0_.refs_5_), channel_id=1, source_target_pairs={{2,0},{3,1},{4,2},{5,3},{6,4},{7,5},{10,8},{11,9},{12,10},{13,11},... | collective-permute-start | bytes 3145736 | tf_op jit(solution)/shard_map/ppermute | solution.py:767
  218.6 53.0 %collective-permute-start.22 = (bf16[256,2048]{1,0:T(8,128)(2,1)}, bf16[256,2048]{1,0:T(8,128)(2,1)}, u32[]{:S(2)}, u32[]{:S(2)}) collective-permute-start(bf16[256,2048]{1,0:T(8,128)(2,1)} %get-tuple-element.104), channel_id=1, source_target_pairs={{0,8},{8,0},{16,24},{24,16},{1,9},{9,1},{17,25},{25,17},{2,10},{10... | collective-permute-start | bytes 3145736 | tf_op jit(solution)/shard_map/ppermute | solution.py:743
  220.1 52.0 %collective-permute-start.23 = (bf16[256,2048]{1,0:T(8,128)(2,1)}, bf16[256,2048]{1,0:T(8,128)(2,1)}, u32[]{:S(2)}, u32[]{:S(2)}) collective-permute-start(bf16[256,2048]{1,0:T(8,128)(2,1)} %get-tuple-element.104), channel_id=1, source_target_pairs={{0,16},{8,24},{16,0},{24,8},{1,17},{9,25},{17,1},{25,9},{2,18},{10... | collective-permute-start | bytes 3145736 | tf_op jit(solution)/shard_map/ppermute | solution.py:743
  220.3 40.8 %collective-permute-start.16 = (bf16[256,2048]{1,0:T(8,128)(2,1)S(1)}, bf16[256,2048]{1,0:T(8,128)(2,1)}, u32[]{:S(2)}, u32[]{:S(2)}) collective-permute-start(bf16[256,2048]{1,0:T(8,128)(2,1)S(1)} %copy-done.43), channel_id=1, source_target_pairs={{2,4},{3,5},{4,6},{5,7},{10,12},{11,13},{12,14},{13,15},{18,20},{1... | collective-permute-start | bytes 3145736 | tf_op jit(solution)/shard_map/ppermute | solution.py:767
  226.3 34.8 %collective-permute-start.20 = (bf16[256,2048]{1,0:T(8,128)(2,1)S(1)}, bf16[256,2048]{1,0:T(8,128)(2,1)S(1)}, u32[]{:S(2)}, u32[]{:S(2)}) collective-permute-start(bf16[256,2048]{1,0:T(8,128)(2,1)S(1)} %copy-done.41), channel_id=1, source_target_pairs={{2,0},{3,1},{4,2},{5,3},{10,8},{11,9},{12,10},{13,11},{18,16},{19,... | collective-permute-start | bytes 3145736 | tf_op jit(solution)/shard_map/ppermute | solution.py:767
  267.7 39.5 %collective-permute-start.19 = (bf16[256,2048]{1,0:T(8,128)(2,1)}, bf16[256,2048]{1,0:T(8,128)(2,1)}, u32[]{:S(2)}, u32[]{:S(2)}) collective-permute-start(bf16[256,2048]{1,0:T(8,128)(2,1)} %after.37), channel_id=1, source_target_pairs={{4,6},{5,7},{12,14},{13,15},{20,22},{21,23},{28,30},{29,31}} | collective-permute-start | bytes 3145736 | tf_op jit(solution)/shard_map/ppermute | solution.py:767
  269.4 37.9 %collective-permute-start.24 = (bf16[256,2048]{1,0:T(8,128)(2,1)S(1)}, bf16[256,2048]{1,0:T(8,128)(2,1)}, u32[]{:S(2)}, u32[]{:S(2)}) collective-permute-start(bf16[256,2048]{1,0:T(8,128)(2,1)S(1)} %copy-done.51), channel_id=1, source_target_pairs={{2,0},{3,1},{10,8},{11,9},{18,16},{19,17},{26,24},{27,25}} | collective-permute-start | bytes 3145736 | tf_op jit(solution)/shard_map/ppermute | solution.py:767
  271.6 36.2 %collective-permute-start.26 = (bf16[272,2048]{1,0:T(8,128)(2,1)}, bf16[272,2048]{1,0:T(8,128)(2,1)}, u32[]{:S(2)}, u32[]{:S(2)}) collective-permute-start(bf16[272,2048]{1,0:T(8,128)(2,1)} %get-tuple-element.111), channel_id=1, source_target_pairs={{0,1},{1,0},{2,3},{3,2},{4,5},{5,4},{6,7},{7,6},{8,9},{9,8},{10,11... | collective-permute-start | bytes 3342344 | tf_op jit(solution)/shard_map/ppermute | solution.py:761
  305.9 46.3 %collective-permute-start.28 = (bf16[256,2048]{1,0:T(8,128)(2,1)}, bf16[256,2048]{1,0:T(8,128)(2,1)}, u32[]{:S(2)}, u32[]{:S(2)}) collective-permute-start(bf16[256,2048]{1,0:T(8,128)(2,1)} %get-tuple-element.104), channel_id=1, source_target_pairs={{0,24},{8,16},{16,8},{24,0},{1,25},{9,17},{17,9},{25,1},{2,26},{10... | collective-permute-start | bytes 3145736 | tf_op jit(solution)/shard_map/ppermute | solution.py:743
  311.5 61.0 %collective-permute-start.29 = (bf16[272,2048]{1,0:T(8,128)(2,1)}, bf16[272,2048]{1,0:T(8,128)(2,1)S(1)}, u32[]{:S(2)}, u32[]{:S(2)}) collective-permute-start(bf16[272,2048]{1,0:T(8,128)(2,1)} %add_convert_fusion.3.refs_18_), channel_id=1, source_target_pairs={{0,2},{1,3},{2,0},{3,1},{4,6},{5,7},{6,4},{7,5},{8,10},{9,11},{10,... | collective-permute-start | bytes 3342344 | tf_op jit(solution)/shard_map/ppermute | solution.py:761
  314.2 58.3 %collective-permute-start.30 = (bf16[272,2048]{1,0:T(8,128)(2,1)}, bf16[272,2048]{1,0:T(8,128)(2,1)S(1)}, u32[]{:S(2)}, u32[]{:S(2)}) collective-permute-start(bf16[272,2048]{1,0:T(8,128)(2,1)} %add_convert_fusion.2.refs_19_), channel_id=1, source_target_pairs={{0,4},{1,5},{2,6},{3,7},{4,0},{5,1},{6,2},{7,3},{8,12},{9,13},{10,... | collective-permute-start | bytes 3342344 | tf_op jit(solution)/shard_map/ppermute | solution.py:761
  373.9 48.4 %collective-permute-start.33 = (bf16[2,256,2048]{2,1,0:T(8,128)(2,1)}, bf16[2,256,2048]{2,1,0:T(8,128)(2,1)}, u32[]{:S(2)}, u32[]{:S(2)}) collective-permute-start(bf16[2,256,2048]{2,1,0:T(8,128)(2,1)} %get-tuple-element.118.refs_1_), channel_id=1, source_target_pairs={{0,8},{8,0},{16,24},{24,16},{1,9},{9,1},{17,25},{25,17},{2,10},{10... | collective-permute-start | bytes 6291464 | tf_op jit(solution)/shard_map/ppermute | solution.py:743
  375.5 48.0 %collective-permute-start.34 = (bf16[2,256,2048]{2,1,0:T(8,128)(2,1)}, bf16[2,256,2048]{2,1,0:T(8,128)(2,1)S(1)}, u32[]{:S(2)}, u32[]{:S(2)}) collective-permute-start(bf16[2,256,2048]{2,1,0:T(8,128)(2,1)} %get-tuple-element.120.refs_3_), channel_id=1, source_target_pairs={{0,16},{8,24},{16,0},{24,8},{1,17},{9,25},{17,1},{25,9},{2,18},{10... | collective-permute-start | bytes 6291464 | tf_op jit(solution)/shard_map/ppermute | solution.py:743
  379.5 50.8 %collective-permute-start.32 = (bf16[272,2048]{1,0:T(8,128)(2,1)}, bf16[272,2048]{1,0:T(8,128)(2,1)}, u32[]{:S(2)}, u32[]{:S(2)}) collective-permute-start(bf16[272,2048]{1,0:T(8,128)(2,1)} %add_convert_fusion.1.refs_1_), channel_id=1, source_target_pairs={{0,6},{1,7},{2,4},{3,5},{4,2},{5,3},{6,0},{7,1},{8,14},{9,15},{10,... | collective-permute-start | bytes 3342344 | tf_op jit(solution)/shard_map/ppermute | solution.py:761
  430.4 235.2 %reduce-scatter.6.cloned.1.call-start = ((), (), s32[]{:S(2)}) async-start(), calls=%async_computation.7 | async-start | bytes 7077888 | tf_op jit(solution)/shard_map/reduce_scatter | solution.py:789
  447.8 15.0 %collective-permute-start.36 = (bf16[256,1024]{1,0:T(8,128)(2,1)}, bf16[256,1024]{1,0:T(8,128)(2,1)S(1)}, u32[]{:S(2)}, u32[]{:S(2)}) collective-permute-start(bf16[256,1024]{1,0:T(8,128)(2,1)} %get-tuple-element.130), channel_id=1, source_target_pairs={{0,8},{8,0},{16,24},{24,16},{1,9},{9,1},{17,25},{25,17},{2,10},{10... | collective-permute-start | bytes 1572872 | tf_op jit(solution)/shard_map/ppermute | solution.py:743
  449.4 24.9 %collective-permute-start.37 = (bf16[256,1024]{1,0:T(8,128)(2,1)}, bf16[256,1024]{1,0:T(8,128)(2,1)S(1)}, u32[]{:S(2)}, u32[]{:S(2)}) collective-permute-start(bf16[256,1024]{1,0:T(8,128)(2,1)} %get-tuple-element.131), channel_id=1, source_target_pairs={{0,16},{8,24},{16,0},{24,8},{1,17},{9,25},{17,1},{25,9},{2,18},{10... | collective-permute-start | bytes 1572872 | tf_op jit(solution)/shard_map/ppermute | solution.py:743
  450.2 24.1 %collective-permute-start.38 = (bf16[256,1024]{1,0:T(8,128)(2,1)}, bf16[256,1024]{1,0:T(8,128)(2,1)S(1)}, u32[]{:S(2)}, u32[]{:S(2)}) collective-permute-start(bf16[256,1024]{1,0:T(8,128)(2,1)} %get-tuple-element.132), channel_id=1, source_target_pairs={{0,24},{8,16},{16,8},{24,0},{1,25},{9,17},{17,9},{25,1},{2,26},{10... | collective-permute-start | bytes 1572872 | tf_op jit(solution)/shard_map/ppermute | solution.py:743
  475.6 93.8 %collective-permute-start.40 = (bf16[2,512,2048]{2,1,0:T(8,128)(2,1)}, bf16[2,512,2048]{2,1,0:T(8,128)(2,1)}, u32[]{:S(2)}, u32[]{:S(2)}) collective-permute-start(bf16[2,512,2048]{2,1,0:T(8,128)(2,1)} %after.47.refs_2_), channel_id=1, source_target_pairs={{0,16},{8,24},{16,0},{24,8},{1,17},{9,25},{17,1},{25,9},{2,18},{10... | collective-permute-start | bytes 12582920 | tf_op jit(solution)/shard_map/ppermute | solution.py:743
  482.3 97.1 %collective-permute-start.39 = (bf16[2,512,2048]{2,1,0:T(8,128)(2,1)}, bf16[2,512,2048]{2,1,0:T(8,128)(2,1)}, u32[]{:S(2)}, u32[]{:S(2)}) collective-permute-start(bf16[2,512,2048]{2,1,0:T(8,128)(2,1)} %after.46.refs_1_), channel_id=1, source_target_pairs={{0,8},{8,0},{16,24},{24,16},{1,9},{9,1},{17,25},{25,17},{2,10},{10... | collective-permute-start | bytes 12582920 | tf_op jit(solution)/shard_map/ppermute | solution.py:743
  530.4 68.3 %collective-permute-start.41 = (bf16[256,2048]{1,0:T(8,128)(2,1)}, bf16[256,2048]{1,0:T(8,128)(2,1)}, u32[]{:S(2)}, u32[]{:S(2)}) collective-permute-start(bf16[256,2048]{1,0:T(8,128)(2,1)} %get-tuple-element.142), channel_id=1, source_target_pairs={{0,8},{8,0},{16,24},{24,16},{1,9},{9,1},{17,25},{25,17},{2,10},{10... | collective-permute-start | bytes 3145736 | tf_op jit(solution)/shard_map/ppermute | solution.py:743
  531.7 66.9 %collective-permute-start.42 = (bf16[256,2048]{1,0:T(8,128)(2,1)}, bf16[256,2048]{1,0:T(8,128)(2,1)}, u32[]{:S(2)}, u32[]{:S(2)}) collective-permute-start(bf16[256,2048]{1,0:T(8,128)(2,1)} %get-tuple-element.143), channel_id=1, source_target_pairs={{0,16},{8,24},{16,0},{24,8},{1,17},{9,25},{17,1},{25,9},{2,18},{10... | collective-permute-start | bytes 3145736 | tf_op jit(solution)/shard_map/ppermute | solution.py:743
  532.8 88.8 %collective-permute-start.43 = (bf16[256,2048]{1,0:T(8,128)(2,1)}, bf16[256,2048]{1,0:T(8,128)(2,1)}, u32[]{:S(2)}, u32[]{:S(2)}) collective-permute-start(bf16[256,2048]{1,0:T(8,128)(2,1)} %get-tuple-element.144), channel_id=1, source_target_pairs={{0,24},{8,16},{16,8},{24,0},{1,25},{9,17},{17,9},{25,1},{2,26},{10... | collective-permute-start | bytes 3145736 | tf_op jit(solution)/shard_map/ppermute | solution.py:743
  547.2 118.4 %reduce-scatter.8.cloned.1.call-start = ((), (), s32[]{:S(2)}) async-start(), calls=%async_computation.8 | async-start | bytes 2949120 | tf_op jit(solution)/shard_map/reduce_scatter | solution.py:789
  578.8 89.1 %collective-permute-start.48 = (bf16[1,512,2048]{2,1,0:T(8,128)(2,1)}, bf16[1,512,2048]{2,1,0:T(8,128)(2,1)}, u32[]{:S(2)}, u32[]{:S(2)}) collective-permute-start(bf16[1,512,2048]{2,1,0:T(8,128)(2,1)} %get-tuple-element.138.refs_2_), channel_id=1, source_target_pairs={{0,8},{8,0},{16,24},{24,16},{1,9},{9,1},{17,25},{25,17},{2,10},{10... | collective-permute-start | bytes 6291464 | tf_op jit(solution)/shard_map/ppermute | solution.py:743
  588.8 79.1 %collective-permute-start.47 = (bf16[1,512,2048]{2,1,0:T(8,128)(2,1)}, bf16[1,512,2048]{2,1,0:T(8,128)(2,1)}, u32[]{:S(2)}, u32[]{:S(2)}) collective-permute-start(bf16[1,512,2048]{2,1,0:T(8,128)(2,1)} %get-tuple-element.137.refs_1_), channel_id=1, source_target_pairs={{0,16},{8,24},{16,0},{24,8},{1,17},{9,25},{17,1},{25,9},{2,18},{10... | collective-permute-start | bytes 6291464 | tf_op jit(solution)/shard_map/ppermute | solution.py:743
  628.0 36.2 %collective-permute-start.46 = (f32[1,4480]{1,0:T(1,128)}, f32[1,4480]{1,0:T(1,128)S(1)}, u32[]{:S(2)}, u32[]{:S(2)}) collective-permute-start(f32[1,4480]{1,0:T(1,128)} %get-tuple-element.150), channel_id=1, source_target_pairs={{0,24},{8,16},{16,8},{24,0},{1,25},{9,17},{17,9},{25,1},{2,26},{10... | collective-permute-start | bytes 53768 | tf_op jit(solution)/shard_map/ppermute | solution.py:743
  629.2 35.0 %collective-permute-start.45 = (f32[1,4480]{1,0:T(1,128)}, f32[1,4480]{1,0:T(1,128)S(1)}, u32[]{:S(2)}, u32[]{:S(2)}) collective-permute-start(f32[1,4480]{1,0:T(1,128)} %get-tuple-element.150), channel_id=1, source_target_pairs={{0,16},{8,24},{16,0},{24,8},{1,17},{9,25},{17,1},{25,9},{2,18},{10... | collective-permute-start | bytes 53768 | tf_op jit(solution)/shard_map/ppermute | solution.py:743
  630.2 34.0 %collective-permute-start.44 = (f32[1,4480]{1,0:T(1,128)}, f32[1,4480]{1,0:T(1,128)S(1)}, u32[]{:S(2)}, u32[]{:S(2)}) collective-permute-start(f32[1,4480]{1,0:T(1,128)} %get-tuple-element.150), channel_id=1, source_target_pairs={{0,8},{8,0},{16,24},{24,16},{1,9},{9,1},{17,25},{25,17},{2,10},{10... | collective-permute-start | bytes 53768 | tf_op jit(solution)/shard_map/ppermute | solution.py:743
  667.9 27.8 %collective-permute-start.49 = (bf16[256,2176]{1,0:T(8,128)(2,1)}, bf16[256,2176]{1,0:T(8,128)(2,1)S(1)}, u32[]{:S(2)}, u32[]{:S(2)}) collective-permute-start(bf16[256,2176]{1,0:T(8,128)(2,1)} %after.54.refs_0_), channel_id=1, source_target_pairs={{0,8},{8,0},{16,24},{24,16},{1,9},{9,1},{17,25},{25,17},{2,10},{10... | collective-permute-start | bytes 3342344 | tf_op jit(solution)/shard_map/ppermute | solution.py:743
  669.3 48.1 %collective-permute-start.50 = (bf16[256,2176]{1,0:T(8,128)(2,1)}, bf16[256,2176]{1,0:T(8,128)(2,1)}, u32[]{:S(2)}, u32[]{:S(2)}) collective-permute-start(bf16[256,2176]{1,0:T(8,128)(2,1)} %after.54.refs_0_), channel_id=1, source_target_pairs={{0,16},{8,24},{16,0},{24,8},{1,17},{9,25},{17,1},{25,9},{2,18},{10... | collective-permute-start | bytes 3342344 | tf_op jit(solution)/shard_map/ppermute | solution.py:743
  670.2 47.1 %collective-permute-start.51 = (bf16[256,2176]{1,0:T(8,128)(2,1)}, bf16[256,2176]{1,0:T(8,128)(2,1)}, u32[]{:S(2)}, u32[]{:S(2)}) collective-permute-start(bf16[256,2176]{1,0:T(8,128)(2,1)} %after.54.refs_0_), channel_id=1, source_target_pairs={{0,24},{8,16},{16,8},{24,0},{1,25},{9,17},{17,9},{25,1},{2,26},{10... | collective-permute-start | bytes 3342344 | tf_op jit(solution)/shard_map/ppermute | solution.py:743
  719.6 25.5 %collective-permute-start.55 = (bf16[1,256,2048]{2,1,0:T(8,128)(2,1)}, bf16[1,256,2048]{2,1,0:T(8,128)(2,1)S(1)}, u32[]{:S(2)}, u32[]{:S(2)}) collective-permute-start(bf16[1,256,2048]{2,1,0:T(8,128)(2,1)} %after.56), channel_id=1, source_target_pairs={{0,16},{8,24},{16,0},{24,8},{1,17},{9,25},{17,1},{25,9},{2,18},{10... | collective-permute-start | bytes 3145736 | tf_op jit(solution)/shard_map/ppermute | solution.py:743
  720.9 25.2 %collective-permute-start.56 = (bf16[1,256,2048]{2,1,0:T(8,128)(2,1)}, bf16[1,256,2048]{2,1,0:T(8,128)(2,1)S(1)}, u32[]{:S(2)}, u32[]{:S(2)}) collective-permute-start(bf16[1,256,2048]{2,1,0:T(8,128)(2,1)} %after.58), channel_id=1, source_target_pairs={{0,8},{8,0},{16,24},{24,16},{1,9},{9,1},{17,25},{25,17},{2,10},{10... | collective-permute-start | bytes 3145736 | tf_op jit(solution)/shard_map/ppermute | solution.py:743
  723.3 34.3 %collective-permute-start.54 = (f32[1,4480]{1,0:T(1,128)S(1)}, f32[1,4480]{1,0:T(1,128)S(1)}, u32[]{:S(2)}, u32[]{:S(2)}) collective-permute-start(f32[1,4480]{1,0:T(1,128)S(1)} %maximum_select_fusion.1), channel_id=1, source_target_pairs={{0,4},{1,5},{2,6},{3,7},{4,0},{5,1},{6,2},{7,3},{8,12},{9,13},{10,... | collective-permute-start | bytes 53768 | tf_op jit(solution)/shard_map/ppermute | solution.py:761
  (85 other events, 393.9 us)
Sparse Core Ops, SparseCore 0:
  11.3 34.3 all-gather.3
  47.9 62.2 all-gather.5
  111.8 89.7 all-gather.7
  430.5 85.0 reduce-scatter.3
  546.3 65.6 reduce-scatter.5
  614.8 34.7 reduce-scatter.7

commit v5 on v4

--- a/solution.py
+++ b/solution.py
@@ -705,6 +705,28 @@
     )(who, *blocks)
 
 
+def merge_kernel(sums, *refs):
+    out = refs[-1]
+    total = refs[0][...]
+    lane = lax.broadcasted_iota(jnp.int32, total.shape, 1)
+    for ref in refs[1:-1]:
+        other = ref[...]
+        total = jnp.where(lane < sums, total + other, jnp.maximum(total, other))
+    out[...] = total
+
+
+def merge(sums, *values):
+    vmem = pl.BlockSpec(memory_space=pltpu.VMEM)
+    return pl.pallas_call(
+        functools.partial(merge_kernel, sums),
+        in_specs=[vmem] * len(values),
+        out_specs=vmem,
+        out_shape=jax.ShapeDtypeStruct(values[0].shape, F32),
+        cost_estimate=pl.CostEstimate(flops=0, bytes_accessed=0, transcendentals=0),
+        name="merge",
+    )(*values)
+
+
 def local(
     tokens,
     cotangent,
@@ -826,7 +848,9 @@
     mask_wide = jnp.pad(mask.astype(F32), ((0, 0), (0, 0), (0, lanes - EXPERTS)))
     router_wide = jnp.pad(full_router, ((0, 0), (0, lanes - EXPERTS)))
     tables = (pick, spots, mask_wide, router_wide)
-    tokens_all = spread(tokens)
+    segments = spread(segment_ids)
+    tokens_all = spread(after(tokens, *segments[1:]))
+    segments = jnp.concatenate(segments, axis=0)
     normed = jnp.concatenate(
         [rms_norm(v.astype(F32), attn_gain).astype(BF) for v in tokens_all], axis=0
     )
@@ -834,8 +858,7 @@
     where = jnp.stack([me_r, me_f // 2, core]).astype(jnp.int32)
     half = lax.dynamic_slice(quarter, (core * (width // 2), 0), (width // 2, part))
     near = spread(after(half, *tokens_all[1:]))
-    near[1] = after(near[1], *tables, normed)
-    segments = jnp.concatenate(spread(after(segment_ids, near[2])), axis=0)
+    near[1] = after(near[1], *tables, segments, normed)
     normed = after(normed, *near[1:])
     w_qkv = gather(jnp.concatenate([columns(w, 0) for w in (w_query, w_key, w_value)], axis=1))
     cot_all = gather(cotangent)
@@ -929,7 +952,7 @@
     in_halves = [next_halves(v, j, 1, 10**11) for j, v in enumerate(in_traded)]
     in_sends = [v for v, _ in in_halves]
     in_done = [(keep, swap(v, next_bit(j, 1))) for j, (v, keep) in enumerate(in_halves)]
-    mixed_rows = after(jnp.concatenate(mixed_all, axis=0), *in_sends)
+    mixed_rows = jnp.concatenate([mixed_all[0], after(mixed_all[1], *in_sends), *mixed_all[2:]], axis=0)
     output_grad = dot_tn(mixed_rows, grad_mixed[:, part:])
     o_grad = jnp.concatenate([output_grad.astype(BF), router_grad], axis=1)
     share_o = reduce(o_grad)
@@ -945,8 +968,6 @@
     out_done = [
         (keep, swap(after(v, *second, moe_sum), next_bit(j, 1))) for j, (v, keep) in enumerate(out_halves)
     ]
-    total_query, total_key, total_value, total_output, total_router = gather_step(where, blocks, 4)
-    total_router = total_router[:, :EXPERTS]
 
     def settle(traded, cost):
         pairs = []
@@ -957,22 +978,10 @@
             pairs.append((keep[0], got[0]))
         return join(pairs, cost)
 
-    expert_in_grad = settle(in_done, 10**11)
-    expert_out_grad = settle([(k, after(v, expert_in_grad)) for k, v in out_done], 0)
-
     n_sums = 2 * width + 2 * HD
-    is_sum = jnp.arange(small.shape[1]) < n_sums
-
-    def merge(a, b):
-        return jnp.where(is_sum, a + b, jnp.maximum(a, b))
-
-    small = functools.reduce(merge, spread(small))
-    small = after(small, *blocks[1:], expert_in_grad)
-    small = merge(small, cross(small, 1))
-    step = 1
-    while step < rounds:
-        small = merge(small, cross(small, 2 * step))
-        step *= 2
+    small = merge(n_sums, small, cross(small, 1))
+    small = merge(n_sums, small, *[cross(small, 2 * k) for k in range(1, rounds)])
+    small = merge(n_sums, *spread(after(small, *second)))
     small = small[0]
     attn_gain_total = small[:width]
     ffn_gain_total = small[width : 2 * width]
@@ -984,6 +993,14 @@
     column_scale = jnp.repeat(jnp.sqrt(factor), HD)
     clipped_query = (w_query.astype(F32) * column_scale[None, :]).astype(BF)
     clipped_key = (w_key.astype(F32) * column_scale[None, :]).astype(BF)
+    expert_in_grad = settle(
+        [(keep, after(v, clipped_query, clipped_key, output)) for keep, v in in_done], 10**11
+    )
+    expert_out_grad = settle([(k, after(v, expert_in_grad)) for k, v in out_done], 0)
+
+    blocks[1] = after(blocks[1], expert_in_grad)
+    total_query, total_key, total_value, total_output, total_router = gather_step(where, blocks, 4)
+    total_router = total_router[:, :EXPERTS]
     return (
         output,
         input_grad,

time: 778 us -> 754 us (0.969)
  waiting for transfers between devices: 268 us -> 240 us
  other arithmetic: 56.9 us -> 48.9 us
    ppermute x35, waiting for transfers between devices: 257 us -> 222 us  [swap(): return lax.ppermute(value, 'replica', [(r, r ^ k) for r in range(replicas)])]
    unnamed x146 -> x172, local copies, waits for them, and re-layouts: 47.5 us -> 50.4 us
  transfers between devices with their start and end apart: 63 -> 64, of which waited for: 20 -> 27; matrix products, arithmetic and copies ran while one was open for 10% -> 10% of each run, Pallas kernels for 38% -> 39%
where the time goes in v5:
time: 754 us; the launch traced here: 748 us
  Pallas kernels  299 us (40%)
  waiting for transfers between devices  240 us (32%)
  local copies, waits for them, and re-layouts  69.2 us (9%)
  starting transfers between devices  68.4 us (9%)
  other arithmetic  48.9 us (6%)
  between operations  15.5 us (2%)
    ppermute x35, waiting for transfers between devices, swap(): return lax.ppermute(value, 'replica', [(r, r ^ k) for r in range(replicas)])  222 us
    pallas_call x4, Pallas kernels, expert_block(): pl.pallas_call(functools.partial(expert_kernel, min(512, ff), min(1024, w...  131 us
    pallas_call x2, Pallas kernels, weight_grads(): pl.pallas_call(functools.partial(weight_grad_kernel, half), grid_spec=plt...  52.8 us
    unnamed x172, local copies, waits for them, and re-layouts  50.4 us
    ppermute x35, starting transfers between devices, swap(): return lax.ppermute(value, 'replica', [(r, r ^ k) for r in range(replicas)])  41.5 us
    ppermute x6, starting transfers between devices, pass_on(): return (lax.ppermute(up, 'fsdp', pairs), lax.ppermute(down, 'fsdp', back))  17.3 us
    pallas_call x4, Pallas kernels, halve(): pl.pallas_call(functools.partial(halve_kernel, half), grid_spec=pltpu.Pre...  16.1 us
  transfers between devices with their start and end apart: 64, of which 27 were waited for; matrix products, arithmetic and copies ran while one was open for 10% of the time, Pallas kernels for 39%

profile of v5, /device:TPU:8, one launch (start us, length us, event | category | flops | bytes accessed | tf_op | source)
XLA Modules:
  0.0 748.2 jit_solution(278952273065705093)
XLA Ops:
  22.8 2.5 collective-permute-start.5
  29.5 18.1 %collective-permute-done.3.refs_1_ = bf16[256,2048]{1,0:T(8,128)(2,1)S(1)} collective-permute-done((bf16[256,2048]{1,0:T(8,128)(2,1)}, bf16[256,2048]{1,0:T(8,128)(2,1)S(1)}, u32[]{:S(2)}, u32[]{:S(2)}) %collective-permute-start.3) | collective-permute-done | bytes 1048608 | tf_op jit(solution)/shard_map/ppermute | solution.py:765
  47.9 19.5 %collective-permute-done.4.refs_2_ = bf16[256,2048]{1,0:T(8,128)(2,1)S(1)} collective-permute-done((bf16[256,2048]{1,0:T(8,128)(2,1)}, bf16[256,2048]{1,0:T(8,128)(2,1)S(1)}, u32[]{:S(2)}, u32[]{:S(2)}) %collective-permute-start.4) | collective-permute-done | bytes 1048608 | tf_op jit(solution)/shard_map/ppermute | solution.py:765
  71.7 2.5 pad_maximum_fusion.refs_6_.refs_0_
  90.9 11.8 %collective-permute-done.6.refs_0_ = bf16[1024,512]{1,0:T(8,128)(2,1)S(1)} collective-permute-done((bf16[1024,512]{1,0:T(8,128)(2,1)}, bf16[1024,512]{1,0:T(8,128)(2,1)S(1)}, u32[]{:S(2)}, u32[]{:S(2)}) %collective-permute-start.6) | collective-permute-done | bytes 1048608 | tf_op jit(solution)/shard_map/ppermute | solution.py:765
  103.7 18.5 %collective-permute-done.7.refs_2_ = bf16[1024,512]{1,0:T(8,128)(2,1)} collective-permute-done((bf16[1024,512]{1,0:T(8,128)(2,1)}, bf16[1024,512]{1,0:T(8,128)(2,1)}, u32[]{:S(2)}, u32[]{:S(2)}) %collective-permute-start.7) | collective-permute-done | bytes 1048608 | tf_op jit(solution)/shard_map/ppermute | solution.py:765
  122.2 14.6 %attention.1 = (f32[1024,1024]{1,0:T(8,128)}, bf16[1024,1536]{1,0:T(8,128)(2,1)}, bf16[1024,512]{1,0:T(8,128)(2,1)}, f32[1024,128]{1,0:T(8,128)}, f32[4,1,128]{2,1,0:T(1,128)}) custom-call(bf16[1024,2048]{1,0:T(8,128)(2,1)} %after.36.normed.left, bf16[2048,1536]{1,0:T(8,128)(2,1)} %all-gather.6.cloned.1.call-done.weight, ...), custom_call_target="tpu_custom_call" | custom-call | tf_op jit(solution)/shard_map/attention/pallas_call | solution.py:379
  138.1 3.7 pad_maximum_fusion.1.refs_4_.refs_10_
  147.3 4.4 collective-permute-done.9.refs_1_
  151.7 5.5 collective-permute-done.10.refs_2_
  158.0 8.5 %attention_out.1 = (f32[256,2048]{1,0:T(8,128)}, bf16[256,2048]{1,0:T(8,128)(2,1)}, bf16[256,2048]{1,0:T(8,128)(2,1)}) custom-call(s32[3]{0:T(128)} %pad_add_fusion.2.who, bf16[256,512]{1,0:T(8,128)(2,1)} %get-tuple-element.229.refs_0_, bf16[256,512]{1,0:T(8,128)(2,1)} %copy-done.61, bf16[256,512]{1,0:T(8,128)(2,1)} %copy-done.62, ...), custom_call_target="tpu_custom_call" | custom-call | tf_op jit(solution)/shard_map/attention_out/pallas_call | solution.py:252
  167.1 3.5 collective-permute-start.13
  173.1 32.8 %experts.4 = (bf16[2,1152,2048]{2,1,0:T(8,128)(2,1)}, bf16[2,1152,2048]{2,1,0:T(8,128)(2,1)}, bf16[2,1152,2048]{2,1,0:T(8,128)(2,1)}, bf16[2,1152,1024]{2,1,0:T(...) custom-call(s32[5]{0:T(128)} %stack.125.who, ...), custom_call_target="tpu_custom_call" | custom-call | flops 28991029248 | bytes 46137344 | tf_op jit(solution)/shard_map/experts/pallas_call | solution.py:203
  205.9 5.8 collective-permute-done.13.refs_0_
  219.2 5.6 collective-permute-start.16
  226.8 32.8 %experts.5 = (bf16[2,1152,2048]{2,1,0:T(8,128)(2,1)}, bf16[2,1152,2048]{2,1,0:T(8,128)(2,1)}, bf16[2,1152,2048]{2,1,0:T(8,128)(2,1)}, bf16[2,1152,1024]{2,1,0:T(...) custom-call(s32[5]{0:T(128)} %stack.129.who, ...), custom_call_target="tpu_custom_call", output_to_operand_aliasing={{0}: (14, {}), {1}: (15, {}), {2}: (16, {}), {3}: (17, {}),... | custom-call | flops 28991029248 | bytes 46137344 | tf_op jit(solution)/shard_map/experts/pallas_call | solution.py:203
  260.6 2.5 broadcast_select_fusion.refs_0_
  270.7 33.0 %experts.6 = (bf16[2,1152,2048]{2,1,0:T(8,128)(2,1)}, bf16[2,1152,2048]{2,1,0:T(8,128)(2,1)}, bf16[2,1152,2048]{2,1,0:T(8,128)(2,1)}, bf16[2,1152,1024]{2,1,0:T(...) custom-call(s32[5]{0:T(128)} %stack.133.who, ...), custom_call_target="tpu_custom_call", output_to_operand_aliasing={{0}: (14, {}), {1}: (15, {}), {2}: (16, {}), {3}: (17, {}),... | custom-call | flops 28991029248 | bytes 46137344 | tf_op jit(solution)/shard_map/experts/pallas_call | solution.py:203
  306.3 2.7 add_convert_fusion.3.refs_18_
  309.0 2.7 add_convert_fusion.2.refs_19_
  311.7 4.3 collective-permute-start.30
  317.0 32.6 %experts.7 = (bf16[2,1152,2048]{2,1,0:T(8,128)(2,1)}, bf16[2,1152,2048]{2,1,0:T(8,128)(2,1)}, bf16[2,1152,2048]{2,1,0:T(8,128)(2,1)}, bf16[2,1152,1024]{2,1,0:T(...) custom-call(s32[5]{0:T(128)} %stack.122.who, ...), custom_call_target="tpu_custom_call", output_to_operand_aliasing={{0}: (14, {}), {1}: (15, {}), {2}: (16, {}), {3}: (17, {}),... | custom-call | flops 28991029248 | bytes 46137344 | tf_op jit(solution)/shard_map/experts/pallas_call | solution.py:203
  349.6 20.4 %weight_grads.2 = (bf16[2,256,2048]{2,1,0:T(8,128)(2,1)}, bf16[2,256,2048]{2,1,0:T(8,128)(2,1)}, bf16[2,256,2048]{2,1,0:T(8,128)(2,1)}, bf16[2,256,2048]{2,1,0:T(8,128)(2,1)}) custom-call(s32[2,4]{1,0:T(2,128)} %pad_add_fusion.1.quarters, bf16[2,1152,1024]{2,1,0:T(8,128)(2,1)} %after.44.left, bf16[2,1152,2048]{2,1,0:T(8,128)(2,1)} %get-tuple-element.117.right), custom_call_target="tpu_custom_call" | custom-call | tf_op jit(solution)/shard_map/weight_grads/pallas_call | solution.py:499
  374.6 2.7 add_convert_fusion.1.refs_1_
  377.2 32.4 %weight_grads.3 = (bf16[2,512,2048]{2,1,0:T(8,128)(2,1)}, bf16[2,512,2048]{2,1,0:T(8,128)(2,1)}, bf16[2,512,2048]{2,1,0:T(8,128)(2,1)}, bf16[2,512,2048]{2,1,0:T(8,128)(2,1)}) custom-call(s32[2,4]{1,0:T(2,128)} %pad_add_fusion.1.quarters, bf16[2,1152,2048]{2,1,0:T(8,128)(2,1)} %after.46.left, bf16[2,1152,2048]{2,1,0:T(8,128)(2,1)} %get-tuple-element.123.right), custom_call_target="tpu_custom_call" | custom-call | flops 99999997952 | tf_op jit(solution)/shard_map/weight_grads/pallas_call | solution.py:499
  409.7 10.1 %collective-permute-done.33.refs_5_.refs_2_.refs_0_ = bf16[2,256,2048]{2,1,0:T(8,128)(2,1)} collective-permute-done((bf16[2,256,2048]{2,1,0:T(8,128)(2,1)}, bf16[2,256,2048]{2,1,0:T(8,128)(2,1)}, u32[]{:S(2)}, u32[]{:S(2)}) %collective-permute-start.33) | collective-permute-done | bytes 2097184 | tf_op jit(solution)/shard_map/ppermute | solution.py:765
  421.0 6.8 collective-permute-done.32.refs_0_
  433.0 12.7 %attention_back.1 = (f32[256,2048]{1,0:T(8,128)}, f32[1,2048]{1,0:T(1,128)}, bf16[2048,128]{1,0:T(8,128)(2,1)}, bf16[256,1024]{1,0:T(8,128)(2,1)}, bf16[256,1024...) custom-call(s32[3]{0:T(128)} %pad_add_fusion.2.who, ...), custom_call_target="tpu_custom_call" | custom-call | flops 99999997952 | tf_op jit(solution)/shard_map/attention_back/pallas_call | solution.py:320
  450.3 10.4 %collective-permute-done.36 = bf16[256,1024]{1,0:T(8,128)(2,1)S(1)} collective-permute-done((bf16[256,1024]{1,0:T(8,128)(2,1)}, bf16[256,1024]{1,0:T(8,128)(2,1)S(1)}, u32[]{:S(2)}, u32[]{:S(2)}) %collective-permute-start.36) | collective-permute-done | bytes 524320 | tf_op jit(solution)/shard_map/ppermute | solution.py:765
  460.7 11.5 %collective-permute-done.37 = bf16[256,1024]{1,0:T(8,128)(2,1)S(1)} collective-permute-done((bf16[256,1024]{1,0:T(8,128)(2,1)}, bf16[256,1024]{1,0:T(8,128)(2,1)S(1)}, u32[]{:S(2)}, u32[]{:S(2)}) %collective-permute-start.37) | collective-permute-done | bytes 524320 | tf_op jit(solution)/shard_map/ppermute | solution.py:765
  483.9 14.2 %attention_grad.1 = (bf16[1024,1536]{1,0:T(8,128)(2,1)S(1)}, f32[4,2,128]{2,1,0:T(2,128)S(1)}) custom-call(bf16[1024,1024]{1,0:T(8,128)(2,1)S(1)} %copy-done.7, f32[1024,1024]{1,0:T(8,128)S(1)} %copy-done.8, bf16[1024,1536]{1,0:T(8,128)(2,1)S(1)} %copy-done.9, f32[1024,128]{1,0:T(8,128)S(1)} %copy-done.26, s32[4,1,256]{2,1,0:T(1,128)S(1)} %copy-done.27, ...), custom_call_target="tpu_custom_call" | custom-call | tf_op jit(solution)/shard_map/attention_grad/pallas_call | solution.py:447
  498.7 8.7 %product.1 = bf16[2048,1536]{1,0:T(8,128)(2,1)S(1)} custom-call(bf16[1024,2048]{1,0:T(8,128)(2,1)S(1)} %copy-done.2, bf16[1024,1536]{1,0:T(8,128)(2,1)S(1)} %get-tuple-element.135.grad.right), custom_call_target="tpu_custom_call" | custom-call | tf_op jit(solution)/shard_map/product/pallas_call | solution.py:525
  507.4 2.6 copy-done.5
  511.7 12.5 %normed_grads.1 = (bf16[256,2048]{1,0:T(8,128)(2,1)S(1)}, bf16[256,2048]{1,0:T(8,128)(2,1)}, bf16[256,2048]{1,0:T(8,128)(2,1)}, bf16[256,2048]{1,0:T(8,128)(2,1)}) custom-call(bf16[1024,1536]{1,0:T(8,128)(2,1)} %copy-done.10, bf16[2048,1536]{1,0:T(8,128)(2,1)} %all-gather.6.cloned.1.call-done.weight), custom_call_target="tpu_custom_call" | custom-call | tf_op jit(solution)/shard_map/normed_grads/pallas_call | solution.py:553
  530.3 2.9 halve.6
  542.3 25.2 %collective-permute-done.40.refs_1_.got = bf16[2,512,2048]{2,1,0:T(8,128)(2,1)} collective-permute-done((bf16[2,512,2048]{2,1,0:T(8,128)(2,1)}, bf16[2,512,2048]{2,1,0:T(8,128)(2,1)}, u32[]{:S(2)}, u32[]{:S(2)}) %collective-permute-start.40) | collective-permute-done | bytes 4194336 | tf_op jit(solution)/shard_map/ppermute | solution.py:765
  569.8 5.8 halve.5
  580.3 5.8 halve.4
  588.2 4.7 fusion.9
  594.7 21.2 %collective-permute-done.43.refs_3_ = bf16[256,2048]{1,0:T(8,128)(2,1)} collective-permute-done((bf16[256,2048]{1,0:T(8,128)(2,1)}, bf16[256,2048]{1,0:T(8,128)(2,1)}, u32[]{:S(2)}, u32[]{:S(2)}) %collective-permute-start.43) | collective-permute-done | bytes 1048608 | tf_op jit(solution)/shard_map/ppermute | solution.py:765
  616.0 6.4 input_grad.1
  635.1 22.4 %collective-permute-done.49.refs_2_.refs_0_ = bf16[1,512,2048]{2,1,0:T(8,128)(2,1)} collective-permute-done((bf16[1,512,2048]{2,1,0:T(8,128)(2,1)}, bf16[1,512,2048]{2,1,0:T(8,128)(2,1)}, u32[]{:S(2)}, u32[]{:S(2)}) %collective-permute-start.49) | collective-permute-done | bytes 2097184 | tf_op jit(solution)/shard_map/ppermute | solution.py:765
  671.6 3.0 multiply_convert_fusion
  680.5 7.6 %join.2.refs_1_ = f32[2,512,2048]{2,1,0:T(8,128)} custom-call(bf16[512,2048]{1,0:T(8,128)(2,1)} %bitcast.71, bf16[512,2048]{1,0:T(8,128)(2,1)} %bitcast.38.refs_1_, bf16[512,2048]{1,0:T(8,128)(2,1)} %bitcast.70, bf16[512,2048]{1,0:T(8,128)(2,1)} %bitcast.40.refs_3_), custom_call_target="tpu_custom_call" | custom-call | flops 99999997952 | tf_op jit(solution)/shard_map/join/pallas_call | solution.py:623
  691.1 4.4 join.3
  695.5 18.5 %collective-permute-done.53.refs_0_ = bf16[256,2176]{1,0:T(8,128)(2,1)S(1)} collective-permute-done((bf16[256,2176]{1,0:T(8,128)(2,1)}, bf16[256,2176]{1,0:T(8,128)(2,1)S(1)}, u32[]{:S(2)}, u32[]{:S(2)}) %collective-permute-start.53) | collective-permute-done | bytes 1114144 | tf_op jit(solution)/shard_map/ppermute | solution.py:765
  715.0 18.7 %collective-permute-done.55.refs_3_ = bf16[256,2176]{1,0:T(8,128)(2,1)} collective-permute-done((bf16[256,2176]{1,0:T(8,128)(2,1)}, bf16[256,2176]{1,0:T(8,128)(2,1)}, u32[]{:S(2)}, u32[]{:S(2)}) %collective-permute-start.55) | collective-permute-done | bytes 1114144 | tf_op jit(solution)/shard_map/ppermute | solution.py:765
  734.9 5.4 gather_columns.1
  (410 shorter events, 167.8 us)
Async XLA Ops:
  7.2 67.0 %all-gather.4.cloned.1.call-start = ((), (), s32[]{:S(2)}) async-start(), calls=%async_computation.3 | async-start | bytes 2949120 | tf_op jit(solution)/shard_map/all_gather | solution.py:808
  9.9 112.3 %all-gather.6.cloned.1.call-start = ((), (), s32[]{:S(2)}) async-start(), calls=%async_computation.4 | async-start | bytes 7077888 | tf_op jit(solution)/shard_map/all_gather | solution.py:808
  13.1 213.7 %all-gather.8.cloned.1.call-start = ((), (), s32[]{:S(2)}) async-start(), calls=%async_computation.5 | async-start | bytes 9437184 | tf_op jit(solution)/shard_map/all_gather | solution.py:808
  16.7 561.3 %reduce-scatter.4.cloned.1.call-start = ((), (), s32[]{:S(2)}) async-start(), calls=%async_computation.6 | async-start | bytes 9437184 | tf_op jit(solution)/shard_map/reduce_scatter | solution.py:811
  21.3 26.3 %collective-permute-start.3 = (bf16[256,2048]{1,0:T(8,128)(2,1)}, bf16[256,2048]{1,0:T(8,128)(2,1)S(1)}, u32[]{:S(2)}, u32[]{:S(2)}) collective-permute-start(bf16[256,2048]{1,0:T(8,128)(2,1)} %after.33), channel_id=1, source_target_pairs={{0,8},{8,0},{16,24},{24,16},{1,9},{9,1},{17,25},{25,17},{2,10},{10... | collective-permute-start | bytes 3145736 | tf_op jit(solution)/shard_map/ppermute | solution.py:765
  21.8 45.6 %collective-permute-start.4 = (bf16[256,2048]{1,0:T(8,128)(2,1)}, bf16[256,2048]{1,0:T(8,128)(2,1)S(1)}, u32[]{:S(2)}, u32[]{:S(2)}) collective-permute-start(bf16[256,2048]{1,0:T(8,128)(2,1)} %after.33), channel_id=1, source_target_pairs={{0,16},{8,24},{16,0},{24,8},{1,17},{9,25},{17,1},{25,9},{2,18},{10... | collective-permute-start | bytes 3145736 | tf_op jit(solution)/shard_map/ppermute | solution.py:765
  22.8 44.9 %collective-permute-start.5 = (bf16[256,2048]{1,0:T(8,128)(2,1)}, bf16[256,2048]{1,0:T(8,128)(2,1)}, u32[]{:S(2)}, u32[]{:S(2)}) collective-permute-start(bf16[256,2048]{1,0:T(8,128)(2,1)} %after.33), channel_id=1, source_target_pairs={{0,24},{8,16},{16,8},{24,0},{1,25},{9,17},{17,9},{25,1},{2,26},{10... | collective-permute-start | bytes 3145736 | tf_op jit(solution)/shard_map/ppermute | solution.py:765
  76.5 26.3 %collective-permute-start.6 = (bf16[1024,512]{1,0:T(8,128)(2,1)}, bf16[1024,512]{1,0:T(8,128)(2,1)S(1)}, u32[]{:S(2)}, u32[]{:S(2)}) collective-permute-start(bf16[1024,512]{1,0:T(8,128)(2,1)} %after.34.refs_0_), channel_id=1, source_target_pairs={{0,8},{8,0},{16,24},{24,16},{1,9},{9,1},{17,25},{25,17},{2,10},{10... | collective-permute-start | bytes 3145736 | tf_op jit(solution)/shard_map/ppermute | solution.py:765
  77.9 44.3 %collective-permute-start.7 = (bf16[1024,512]{1,0:T(8,128)(2,1)}, bf16[1024,512]{1,0:T(8,128)(2,1)}, u32[]{:S(2)}, u32[]{:S(2)}) collective-permute-start(bf16[1024,512]{1,0:T(8,128)(2,1)} %after.34.refs_0_), channel_id=1, source_target_pairs={{0,16},{8,24},{16,0},{24,8},{1,17},{9,25},{17,1},{25,9},{2,18},{10... | collective-permute-start | bytes 3145736 | tf_op jit(solution)/shard_map/ppermute | solution.py:765
  78.4 43.9 %collective-permute-start.8 = (bf16[1024,512]{1,0:T(8,128)(2,1)}, bf16[1024,512]{1,0:T(8,128)(2,1)}, u32[]{:S(2)}, u32[]{:S(2)}) collective-permute-start(bf16[1024,512]{1,0:T(8,128)(2,1)} %after.34.refs_0_), channel_id=1, source_target_pairs={{0,24},{8,16},{16,8},{24,0},{1,25},{9,17},{17,9},{25,1},{2,26},{10... | collective-permute-start | bytes 3145736 | tf_op jit(solution)/shard_map/ppermute | solution.py:765
  141.8 15.4 %collective-permute-start.12 = (bf16[4,1024,512]{2,1,0:T(8,128)(2,1)}, bf16[4,1024,512]{2,1,0:T(8,128)(2,1)}, u32[]{:S(2)}, u32[]{:S(2)}) collective-permute-start(bf16[4,1024,512]{2,1,0:T(8,128)(2,1)} %pad_maximum_fusion.1.refs_4_.refs_10_), channel_id=1, source_target_pairs={{0,1},{1,0},{2,3},{3,2},{4,5},{5,4},{6,7},{7,6},{8,9},{9,8},{10,11... | collective-permute-start | bytes 12582920 | tf_op jit(solution)/shard_map/ppermute | solution.py:783
  143.2 14.0 %collective-permute-start.10 = (bf16[256,512]{1,0:T(8,128)(2,1)S(1)}, bf16[256,512]{1,0:T(8,128)(2,1)S(1)}, u32[]{:S(2)}, u32[]{:S(2)}) collective-permute-start(bf16[256,512]{1,0:T(8,128)(2,1)S(1)} %get-tuple-element.227), channel_id=1, source_target_pairs={{0,16},{8,24},{16,0},{24,8},{1,17},{9,25},{17,1},{25,9},{2,18},{10... | collective-permute-start | bytes 786440 | tf_op jit(solution)/shard_map/ppermute | solution.py:765
  144.7 12.6 %collective-permute-start.11 = (bf16[256,512]{1,0:T(8,128)(2,1)S(1)}, bf16[256,512]{1,0:T(8,128)(2,1)S(1)}, u32[]{:S(2)}, u32[]{:S(2)}) collective-permute-start(bf16[256,512]{1,0:T(8,128)(2,1)S(1)} %get-tuple-element.226), channel_id=1, source_target_pairs={{0,24},{8,16},{16,8},{24,0},{1,25},{9,17},{17,9},{25,1},{2,26},{10... | collective-permute-start | bytes 786440 | tf_op jit(solution)/shard_map/ppermute | solution.py:765
  146.1 26.9 %collective-permute-start.15 = (bf16[256,2048]{1,0:T(8,128)(2,1)S(1)}, bf16[256,2048]{1,0:T(8,128)(2,1)}, u32[]{:S(2)}, u32[]{:S(2)}) collective-permute-start(bf16[256,2048]{1,0:T(8,128)(2,1)S(1)} %copy-done.57), channel_id=1, source_target_pairs={{0,1},{1,0},{2,3},{3,2},{4,5},{5,4},{6,7},{7,6},{8,9},{9,8},{10,11... | collective-permute-start | bytes 3145736 | tf_op jit(solution)/shard_map/ppermute | solution.py:783
  167.1 44.5 %collective-permute-start.13 = (bf16[256,2048]{1,0:T(8,128)(2,1)}, bf16[256,2048]{1,0:T(8,128)(2,1)S(1)}, u32[]{:S(2)}, u32[]{:S(2)}) collective-permute-start(bf16[256,2048]{1,0:T(8,128)(2,1)} %get-tuple-element.91.refs_0_.refs_5_), channel_id=1, source_target_pairs={{0,2},{1,3},{2,4},{3,5},{4,6},{5,7},{8,10},{9,11},{10,12},{11,13},... | collective-permute-start | bytes 3145736 | tf_op jit(solution)/shard_map/ppermute | solution.py:789
  170.7 42.8 %collective-permute-start.17 = (bf16[256,2048]{1,0:T(8,128)(2,1)}, bf16[256,2048]{1,0:T(8,128)(2,1)S(1)}, u32[]{:S(2)}, u32[]{:S(2)}) collective-permute-start(bf16[256,2048]{1,0:T(8,128)(2,1)} %get-tuple-element.91.refs_0_.refs_5_), channel_id=1, source_target_pairs={{2,0},{3,1},{4,2},{5,3},{6,4},{7,5},{10,8},{11,9},{12,10},{13,11},... | collective-permute-start | bytes 3145736 | tf_op jit(solution)/shard_map/ppermute | solution.py:789
  215.5 11.2 %collective-permute-start.18 = (bf16[256,2048]{1,0:T(8,128)(2,1)}, bf16[256,2048]{1,0:T(8,128)(2,1)}, u32[]{:S(2)}, u32[]{:S(2)}) collective-permute-start(bf16[256,2048]{1,0:T(8,128)(2,1)} %broadcast_select_fusion.1.refs_0_), channel_id=1, source_target_pairs={{0,1},{1,0},{2,3},{3,2},{4,5},{5,4},{6,7},{7,6},{8,9},{9,8},{10,11... | collective-permute-start | bytes 3145736 | tf_op jit(solution)/shard_map/ppermute | solution.py:783
  216.3 53.9 %collective-permute-start.22 = (bf16[256,2048]{1,0:T(8,128)(2,1)}, bf16[256,2048]{1,0:T(8,128)(2,1)}, u32[]{:S(2)}, u32[]{:S(2)}) collective-permute-start(bf16[256,2048]{1,0:T(8,128)(2,1)} %get-tuple-element.104), channel_id=1, source_target_pairs={{0,8},{8,0},{16,24},{24,16},{1,9},{9,1},{17,25},{25,17},{2,10},{10... | collective-permute-start | bytes 3145736 | tf_op jit(solution)/shard_map/ppermute | solution.py:765
  217.8 52.9 %collective-permute-start.23 = (bf16[256,2048]{1,0:T(8,128)(2,1)}, bf16[256,2048]{1,0:T(8,128)(2,1)}, u32[]{:S(2)}, u32[]{:S(2)}) collective-permute-start(bf16[256,2048]{1,0:T(8,128)(2,1)} %get-tuple-element.104), channel_id=1, source_target_pairs={{0,16},{8,24},{16,0},{24,8},{1,17},{9,25},{17,1},{25,9},{2,18},{10... | collective-permute-start | bytes 3145736 | tf_op jit(solution)/shard_map/ppermute | solution.py:765
  219.2 40.4 %collective-permute-start.16 = (bf16[256,2048]{1,0:T(8,128)(2,1)S(1)}, bf16[256,2048]{1,0:T(8,128)(2,1)}, u32[]{:S(2)}, u32[]{:S(2)}) collective-permute-start(bf16[256,2048]{1,0:T(8,128)(2,1)S(1)} %copy-done.43), channel_id=1, source_target_pairs={{2,4},{3,5},{4,6},{5,7},{10,12},{11,13},{12,14},{13,15},{18,20},{1... | collective-permute-start | bytes 3145736 | tf_op jit(solution)/shard_map/ppermute | solution.py:789
  224.8 34.8 %collective-permute-start.20 = (bf16[256,2048]{1,0:T(8,128)(2,1)S(1)}, bf16[256,2048]{1,0:T(8,128)(2,1)S(1)}, u32[]{:S(2)}, u32[]{:S(2)}) collective-permute-start(bf16[256,2048]{1,0:T(8,128)(2,1)S(1)} %copy-done.41), channel_id=1, source_target_pairs={{2,0},{3,1},{4,2},{5,3},{10,8},{11,9},{12,10},{13,11},{18,16},{19,... | collective-permute-start | bytes 3145736 | tf_op jit(solution)/shard_map/ppermute | solution.py:789
  266.3 38.5 %collective-permute-start.19 = (bf16[256,2048]{1,0:T(8,128)(2,1)}, bf16[256,2048]{1,0:T(8,128)(2,1)}, u32[]{:S(2)}, u32[]{:S(2)}) collective-permute-start(bf16[256,2048]{1,0:T(8,128)(2,1)} %after.40), channel_id=1, source_target_pairs={{4,6},{5,7},{12,14},{13,15},{20,22},{21,23},{28,30},{29,31}} | collective-permute-start | bytes 3145736 | tf_op jit(solution)/shard_map/ppermute | solution.py:789
  267.9 36.9 %collective-permute-start.24 = (bf16[256,2048]{1,0:T(8,128)(2,1)S(1)}, bf16[256,2048]{1,0:T(8,128)(2,1)}, u32[]{:S(2)}, u32[]{:S(2)}) collective-permute-start(bf16[256,2048]{1,0:T(8,128)(2,1)S(1)} %copy-done.50), channel_id=1, source_target_pairs={{2,0},{3,1},{10,8},{11,9},{18,16},{19,17},{26,24},{27,25}} | collective-permute-start | bytes 3145736 | tf_op jit(solution)/shard_map/ppermute | solution.py:789
  270.2 35.1 %collective-permute-start.26 = (bf16[272,2048]{1,0:T(8,128)(2,1)}, bf16[272,2048]{1,0:T(8,128)(2,1)}, u32[]{:S(2)}, u32[]{:S(2)}) collective-permute-start(bf16[272,2048]{1,0:T(8,128)(2,1)} %get-tuple-element.111), channel_id=1, source_target_pairs={{0,1},{1,0},{2,3},{3,2},{4,5},{5,4},{6,7},{7,6},{8,9},{9,8},{10,11... | collective-permute-start | bytes 3342344 | tf_op jit(solution)/shard_map/ppermute | solution.py:783
  304.4 45.2 %collective-permute-start.28 = (bf16[256,2048]{1,0:T(8,128)(2,1)}, bf16[256,2048]{1,0:T(8,128)(2,1)}, u32[]{:S(2)}, u32[]{:S(2)}) collective-permute-start(bf16[256,2048]{1,0:T(8,128)(2,1)} %get-tuple-element.104), channel_id=1, source_target_pairs={{0,24},{8,16},{16,8},{24,0},{1,25},{9,17},{17,9},{25,1},{2,26},{10... | collective-permute-start | bytes 3145736 | tf_op jit(solution)/shard_map/ppermute | solution.py:765
  305.1 11.0 %collective-permute-start.25 = (bf16[256,2048]{1,0:T(8,128)(2,1)S(1)}, bf16[256,2048]{1,0:T(8,128)(2,1)S(1)}, u32[]{:S(2)}, u32[]{:S(2)}) collective-permute-start(bf16[256,2048]{1,0:T(8,128)(2,1)S(1)} %select_select_fusion.refs_0_), channel_id=1, source_target_pairs={{0,1},{1,0},{2,3},{3,2},{4,5},{5,4},{6,7},{7,6},{8,9},{9,8},{10,11... | collective-permute-start | bytes 3145736 | tf_op jit(solution)/shard_map/ppermute | solution.py:783
  309.0 61.0 %collective-permute-start.29 = (bf16[272,2048]{1,0:T(8,128)(2,1)}, bf16[272,2048]{1,0:T(8,128)(2,1)S(1)}, u32[]{:S(2)}, u32[]{:S(2)}) collective-permute-start(bf16[272,2048]{1,0:T(8,128)(2,1)} %add_convert_fusion.3.refs_18_), channel_id=1, source_target_pairs={{0,2},{1,3},{2,0},{3,1},{4,6},{5,7},{6,4},{7,5},{8,10},{9,11},{10,... | collective-permute-start | bytes 3342344 | tf_op jit(solution)/shard_map/ppermute | solution.py:783
  311.7 58.3 %collective-permute-start.30 = (bf16[272,2048]{1,0:T(8,128)(2,1)}, bf16[272,2048]{1,0:T(8,128)(2,1)S(1)}, u32[]{:S(2)}, u32[]{:S(2)}) collective-permute-start(bf16[272,2048]{1,0:T(8,128)(2,1)} %add_convert_fusion.2.refs_19_), channel_id=1, source_target_pairs={{0,4},{1,5},{2,6},{3,7},{4,0},{5,1},{6,2},{7,3},{8,12},{9,13},{10,... | collective-permute-start | bytes 3342344 | tf_op jit(solution)/shard_map/ppermute | solution.py:783
  371.4 48.4 %collective-permute-start.33 = (bf16[2,256,2048]{2,1,0:T(8,128)(2,1)}, bf16[2,256,2048]{2,1,0:T(8,128)(2,1)}, u32[]{:S(2)}, u32[]{:S(2)}) collective-permute-start(bf16[2,256,2048]{2,1,0:T(8,128)(2,1)} %get-tuple-element.118.refs_1_), channel_id=1, source_target_pairs={{0,8},{8,0},{16,24},{24,16},{1,9},{9,1},{17,25},{25,17},{2,10},{10... | collective-permute-start | bytes 6291464 | tf_op jit(solution)/shard_map/ppermute | solution.py:765
  373.1 48.0 %collective-permute-start.34 = (bf16[2,256,2048]{2,1,0:T(8,128)(2,1)}, bf16[2,256,2048]{2,1,0:T(8,128)(2,1)S(1)}, u32[]{:S(2)}, u32[]{:S(2)}) collective-permute-start(bf16[2,256,2048]{2,1,0:T(8,128)(2,1)} %get-tuple-element.120.refs_3_), channel_id=1, source_target_pairs={{0,16},{8,24},{16,0},{24,8},{1,17},{9,25},{17,1},{25,9},{2,18},{10... | collective-permute-start | bytes 6291464 | tf_op jit(solution)/shard_map/ppermute | solution.py:765
  377.2 50.6 %collective-permute-start.32 = (bf16[272,2048]{1,0:T(8,128)(2,1)}, bf16[272,2048]{1,0:T(8,128)(2,1)}, u32[]{:S(2)}, u32[]{:S(2)}) collective-permute-start(bf16[272,2048]{1,0:T(8,128)(2,1)} %add_convert_fusion.1.refs_1_), channel_id=1, source_target_pairs={{0,6},{1,7},{2,4},{3,5},{4,2},{5,3},{6,0},{7,1},{8,14},{9,15},{10,... | collective-permute-start | bytes 3342344 | tf_op jit(solution)/shard_map/ppermute | solution.py:783
  427.9 246.8 %reduce-scatter.6.cloned.1.call-start = ((), (), s32[]{:S(2)}) async-start(), calls=%async_computation.7 | async-start | bytes 7077888 | tf_op jit(solution)/shard_map/reduce_scatter | solution.py:811
  445.7 15.0 %collective-permute-start.36 = (bf16[256,1024]{1,0:T(8,128)(2,1)}, bf16[256,1024]{1,0:T(8,128)(2,1)S(1)}, u32[]{:S(2)}, u32[]{:S(2)}) collective-permute-start(bf16[256,1024]{1,0:T(8,128)(2,1)} %get-tuple-element.130), channel_id=1, source_target_pairs={{0,8},{8,0},{16,24},{24,16},{1,9},{9,1},{17,25},{25,17},{2,10},{10... | collective-permute-start | bytes 1572872 | tf_op jit(solution)/shard_map/ppermute | solution.py:765
  447.2 25.0 %collective-permute-start.37 = (bf16[256,1024]{1,0:T(8,128)(2,1)}, bf16[256,1024]{1,0:T(8,128)(2,1)S(1)}, u32[]{:S(2)}, u32[]{:S(2)}) collective-permute-start(bf16[256,1024]{1,0:T(8,128)(2,1)} %get-tuple-element.131), channel_id=1, source_target_pairs={{0,16},{8,24},{16,0},{24,8},{1,17},{9,25},{17,1},{25,9},{2,18},{10... | collective-permute-start | bytes 1572872 | tf_op jit(solution)/shard_map/ppermute | solution.py:765
  448.7 23.6 %collective-permute-start.38 = (bf16[256,1024]{1,0:T(8,128)(2,1)}, bf16[256,1024]{1,0:T(8,128)(2,1)S(1)}, u32[]{:S(2)}, u32[]{:S(2)}) collective-permute-start(bf16[256,1024]{1,0:T(8,128)(2,1)} %get-tuple-element.132), channel_id=1, source_target_pairs={{0,24},{8,16},{16,8},{24,0},{1,25},{9,17},{17,9},{25,1},{2,26},{10... | collective-permute-start | bytes 1572872 | tf_op jit(solution)/shard_map/ppermute | solution.py:765
  473.7 93.8 %collective-permute-start.40 = (bf16[2,512,2048]{2,1,0:T(8,128)(2,1)}, bf16[2,512,2048]{2,1,0:T(8,128)(2,1)}, u32[]{:S(2)}, u32[]{:S(2)}) collective-permute-start(bf16[2,512,2048]{2,1,0:T(8,128)(2,1)} %after.50.refs_2_), channel_id=1, source_target_pairs={{0,16},{8,24},{16,0},{24,8},{1,17},{9,25},{17,1},{25,9},{2,18},{10... | collective-permute-start | bytes 12582920 | tf_op jit(solution)/shard_map/ppermute | solution.py:765
  477.1 100.9 %collective-permute-start.39 = (bf16[2,512,2048]{2,1,0:T(8,128)(2,1)}, bf16[2,512,2048]{2,1,0:T(8,128)(2,1)}, u32[]{:S(2)}, u32[]{:S(2)}) collective-permute-start(bf16[2,512,2048]{2,1,0:T(8,128)(2,1)} %after.49.refs_1_), channel_id=1, source_target_pairs={{0,8},{8,0},{16,24},{24,16},{1,9},{9,1},{17,25},{25,17},{2,10},{10... | collective-permute-start | bytes 12582920 | tf_op jit(solution)/shard_map/ppermute | solution.py:765
  525.2 69.5 %collective-permute-start.41 = (bf16[256,2048]{1,0:T(8,128)(2,1)}, bf16[256,2048]{1,0:T(8,128)(2,1)}, u32[]{:S(2)}, u32[]{:S(2)}) collective-permute-start(bf16[256,2048]{1,0:T(8,128)(2,1)} %get-tuple-element.142), channel_id=1, source_target_pairs={{0,8},{8,0},{16,24},{24,16},{1,9},{9,1},{17,25},{25,17},{2,10},{10... | collective-permute-start | bytes 3145736 | tf_op jit(solution)/shard_map/ppermute | solution.py:765
  526.6 68.1 %collective-permute-start.42 = (bf16[256,2048]{1,0:T(8,128)(2,1)}, bf16[256,2048]{1,0:T(8,128)(2,1)}, u32[]{:S(2)}, u32[]{:S(2)}) collective-permute-start(bf16[256,2048]{1,0:T(8,128)(2,1)} %get-tuple-element.143), channel_id=1, source_target_pairs={{0,16},{8,24},{16,0},{24,8},{1,17},{9,25},{17,1},{25,9},{2,18},{10... | collective-permute-start | bytes 3145736 | tf_op jit(solution)/shard_map/ppermute | solution.py:765
  527.1 88.9 %collective-permute-start.43 = (bf16[256,2048]{1,0:T(8,128)(2,1)}, bf16[256,2048]{1,0:T(8,128)(2,1)}, u32[]{:S(2)}, u32[]{:S(2)}) collective-permute-start(bf16[256,2048]{1,0:T(8,128)(2,1)} %get-tuple-element.144), channel_id=1, source_target_pairs={{0,24},{8,16},{16,8},{24,0},{1,25},{9,17},{17,9},{25,1},{2,26},{10... | collective-permute-start | bytes 3145736 | tf_op jit(solution)/shard_map/ppermute | solution.py:765
  542.1 132.6 %reduce-scatter.8.cloned.1.call-start = ((), (), s32[]{:S(2)}) async-start(), calls=%async_computation.8 | async-start | bytes 2949120 | tf_op jit(solution)/shard_map/reduce_scatter | solution.py:811
  576.9 80.6 %collective-permute-start.49 = (bf16[1,512,2048]{2,1,0:T(8,128)(2,1)}, bf16[1,512,2048]{2,1,0:T(8,128)(2,1)}, u32[]{:S(2)}, u32[]{:S(2)}) collective-permute-start(bf16[1,512,2048]{2,1,0:T(8,128)(2,1)} %get-tuple-element.138.refs_2_), channel_id=1, source_target_pairs={{0,8},{8,0},{16,24},{24,16},{1,9},{9,1},{17,25},{25,17},{2,10},{10... | collective-permute-start | bytes 6291464 | tf_op jit(solution)/shard_map/ppermute | solution.py:765
  587.4 70.0 %collective-permute-start.48 = (bf16[1,512,2048]{2,1,0:T(8,128)(2,1)}, bf16[1,512,2048]{2,1,0:T(8,128)(2,1)}, u32[]{:S(2)}, u32[]{:S(2)}) collective-permute-start(bf16[1,512,2048]{2,1,0:T(8,128)(2,1)} %get-tuple-element.137.refs_1_), channel_id=1, source_target_pairs={{0,16},{8,24},{16,0},{24,8},{1,17},{9,25},{17,1},{25,9},{2,18},{10... | collective-permute-start | bytes 6291464 | tf_op jit(solution)/shard_map/ppermute | solution.py:765
  662.2 26.3 %collective-permute-start.56 = (bf16[1,256,2048]{2,1,0:T(8,128)(2,1)}, bf16[1,256,2048]{2,1,0:T(8,128)(2,1)S(1)}, u32[]{:S(2)}, u32[]{:S(2)}) collective-permute-start(bf16[1,256,2048]{2,1,0:T(8,128)(2,1)} %after.62), channel_id=1, source_target_pairs={{0,16},{8,24},{16,0},{24,8},{1,17},{9,25},{17,1},{25,9},{2,18},{10... | collective-permute-start | bytes 3145736 | tf_op jit(solution)/shard_map/ppermute | solution.py:765
  663.8 26.3 %collective-permute-start.57 = (bf16[1,256,2048]{2,1,0:T(8,128)(2,1)}, bf16[1,256,2048]{2,1,0:T(8,128)(2,1)S(1)}, u32[]{:S(2)}, u32[]{:S(2)}) collective-permute-start(bf16[1,256,2048]{2,1,0:T(8,128)(2,1)} %after.64), channel_id=1, source_target_pairs={{0,8},{8,0},{16,24},{24,16},{1,9},{9,1},{17,25},{25,17},{2,10},{10... | collective-permute-start | bytes 3145736 | tf_op jit(solution)/shard_map/ppermute | solution.py:765
  677.0 37.0 %collective-permute-start.53 = (bf16[256,2176]{1,0:T(8,128)(2,1)}, bf16[256,2176]{1,0:T(8,128)(2,1)S(1)}, u32[]{:S(2)}, u32[]{:S(2)}) collective-permute-start(bf16[256,2176]{1,0:T(8,128)(2,1)} %after.58.refs_0_), channel_id=1, source_target_pairs={{0,8},{8,0},{16,24},{24,16},{1,9},{9,1},{17,25},{25,17},{2,10},{10... | collective-permute-start | bytes 3342344 | tf_op jit(solution)/shard_map/ppermute | solution.py:765
  677.6 37.4 %collective-permute-start.54 = (bf16[256,2176]{1,0:T(8,128)(2,1)}, bf16[256,2176]{1,0:T(8,128)(2,1)}, u32[]{:S(2)}, u32[]{:S(2)}) collective-permute-start(bf16[256,2176]{1,0:T(8,128)(2,1)} %after.58.refs_0_), channel_id=1, source_target_pairs={{0,16},{8,24},{16,0},{24,8},{1,17},{9,25},{17,1},{25,9},{2,18},{10... | collective-permute-start | bytes 3342344 | tf_op jit(solution)/shard_map/ppermute | solution.py:765
  678.0 55.6 %collective-permute-start.55 = (bf16[256,2176]{1,0:T(8,128)(2,1)}, bf16[256,2176]{1,0:T(8,128)(2,1)}, u32[]{:S(2)}, u32[]{:S(2)}) collective-permute-start(bf16[256,2176]{1,0:T(8,128)(2,1)} %after.58.refs_0_), channel_id=1, source_target_pairs={{0,24},{8,16},{16,8},{24,0},{1,25},{9,17},{17,9},{25,1},{2,26},{10... | collective-permute-start | bytes 3342344 | tf_op jit(solution)/shard_map/ppermute | solution.py:765
  (99 other events, 565.6 us)
Sparse Core Ops, SparseCore 0:
  10.2 34.3 all-gather.3
  46.9 62.1 all-gather.5
  110.7 96.9 all-gather.7
  428.0 85.9 reduce-scatter.3
  541.2 65.0 reduce-scatter.5
  609.1 35.2 reduce-scatter.7

commit v6 on v5

--- a/solution.py
+++ b/solution.py
@@ -224,10 +224,10 @@
 
 def out_kernel(replicas, groups, who, *refs):
     pieces = refs[:replicas]
-    near, far, tokens, gain = refs[replicas : replicas + 4]
-    hidden, normed, mixed = refs[replicas + 4 :]
+    near, far = refs[replicas : 2 * replicas], refs[2 * replicas : 3 * replicas]
+    tokens, gain, hidden, normed, mixed = refs[3 * replicas :]
     part = pieces[0].shape[1]
-    depth = near.shape[1] // (groups // 2)
+    depth = near[0].shape[0] // (groups // 2)
     for q in range(replicas):
         mixed[:, pl.ds(pl.multiple_of((who[0] ^ q) * part, part), part)] = pieces[q][...]
     for q in range(replicas):
@@ -236,7 +236,7 @@
             for flip, source in enumerate((near, far)):
                 at = ((who[2] ^ flip) * (groups // 2) + k) * depth
                 left = mixed[:, pl.ds(pl.multiple_of(at, depth), depth)]
-                total += dot(left, source[q, k * depth : (k + 1) * depth])
+                total += dot(left, source[q][k * depth : (k + 1) * depth])
         here = pl.ds(pl.multiple_of((who[0] ^ q) * part, part), part)
         hidden[:, here] = tokens[:, here].astype(F32) + total
     value = hidden[...]
@@ -251,7 +251,7 @@
     vmem = pl.BlockSpec(memory_space=pltpu.VMEM)
     return pl.pallas_call(
         functools.partial(out_kernel, replicas, groups),
-        in_specs=[pl.BlockSpec(memory_space=pltpu.SMEM)] + [vmem] * (replicas + 4),
+        in_specs=[pl.BlockSpec(memory_space=pltpu.SMEM)] + [vmem] * (3 * replicas + 2),
         out_specs=[vmem] * 3,
         out_shape=[
             jax.ShapeDtypeStruct((length, width), F32),
@@ -260,16 +260,18 @@
         ],
         compiler_params=pltpu.CompilerParams(vmem_limit_bytes=60 * 2**20),
         name="attention_out",
-    )(who, *pieces, near, far, tokens, gain)
+    )(who, *pieces, *near, *far, tokens, gain)
 
 
 def back_kernel(replicas, groups, experts, who, *refs):
     rounds = groups // 2
     shares = refs[:rounds]
-    hidden, normed, cot, gain, gates, router, near, far = refs[rounds : rounds + 8]
-    grad_hidden, gain_grad, router_grad = refs[rounds + 8 : rounds + 11]
-    pieces = refs[rounds + 11 : rounds + 11 + replicas]
-    mixed = refs[rounds + 11 + replicas]
+    hidden, normed, cot, gain, gates, router = refs[rounds : rounds + 6]
+    refs = refs[rounds + 6 :]
+    near, far, refs = refs[:replicas], refs[replicas : 2 * replicas], refs[2 * replicas :]
+    grad_hidden, gain_grad, router_grad = refs[:3]
+    pieces = refs[3 : 3 + replicas]
+    mixed = refs[3 + replicas]
     length, width = hidden.shape
     lanes = router.shape[1]
     part = width // replicas
@@ -303,7 +305,7 @@
         for flip, source in enumerate((near, far)):
             block = jnp.zeros((length, depth), F32)
             for q in range(replicas):
-                block += dot_nt(pieces[q][:, part:], source[q, k * depth : (k + 1) * depth])
+                block += dot_nt(pieces[q][:, part:], source[q][k * depth : (k + 1) * depth])
             at = ((who[2] ^ flip) * (groups // 2) + k) * depth
             mixed[:, pl.ds(pl.multiple_of(at, depth), depth)] = block.astype(BF)
     for q in range(replicas):
@@ -312,14 +314,14 @@
 
 
 def back_step(who, shares, hidden, normed, cot, gain, gates, router, near, far, experts):
-    replicas = near.shape[0]
+    replicas = len(near)
     length, width = hidden.shape
     groups = 2 * len(shares)
     vmem = pl.BlockSpec(memory_space=pltpu.VMEM)
     piece = jax.ShapeDtypeStruct((length, 2 * width // replicas), BF)
     results = pl.pallas_call(
         functools.partial(back_kernel, replicas, groups, experts),
-        in_specs=[pl.BlockSpec(memory_space=pltpu.SMEM)] + [vmem] * (len(shares) + 8),
+        in_specs=[pl.BlockSpec(memory_space=pltpu.SMEM)] + [vmem] * (len(shares) + 6 + 2 * replicas),
         out_specs=[vmem] * (3 + replicas),
         scratch_shapes=[pltpu.VMEM((length, width), BF)],
         out_shape=[
@@ -331,7 +333,7 @@
         compiler_params=pltpu.CompilerParams(vmem_limit_bytes=60 * 2**20),
         cost_estimate=pl.CostEstimate(flops=10**11, bytes_accessed=0, transcendentals=0),
         name="attention_back",
-    )(who, *shares, hidden, normed, cot, gain, gates, router, near, far)
+    )(who, *shares, hidden, normed, cot, gain, gates, router, *near, *far)
     return results[0], results[1], results[2], results[3:]
 
 
@@ -725,6 +727,33 @@
         cost_estimate=pl.CostEstimate(flops=0, bytes_accessed=0, transcendentals=0),
         name="merge",
     )(*values)
+
+
+def norm_kernel(count, gain, *refs):
+    out = refs[-1]
+    for k in range(count):
+
+        @pl.when(pl.program_id(0) == k)
+        def _(k=k):
+            value = refs[k][...].astype(F32)
+            scale = lax.rsqrt(jnp.mean(value * value, axis=1, keepdims=True) + epsilon)
+            out[...] = (value * scale * gain[...]).astype(BF)
+
+
+def norm_rows(values, gain):
+    count = len(values)
+    length, width = values[0].shape
+    return pl.pallas_call(
+        functools.partial(norm_kernel, count),
+        grid=(count,),
+        in_specs=[pl.BlockSpec((1, width), lambda n: (0, 0))]
+        + [pl.BlockSpec((length, width), lambda n: (0, 0))] * count,
+        out_specs=pl.BlockSpec((length, width), lambda n: (n, 0)),
+        out_shape=jax.ShapeDtypeStruct((count * length, width), BF),
+        compiler_params=pltpu.CompilerParams(vmem_limit_bytes=32 * 2**20),
+        cost_estimate=pl.CostEstimate(flops=10**11, bytes_accessed=0, transcendentals=0),
+        name="norm_rows",
+    )(gain, *values)
 
 
 def local(
@@ -848,18 +877,16 @@
     mask_wide = jnp.pad(mask.astype(F32), ((0, 0), (0, 0), (0, lanes - EXPERTS)))
     router_wide = jnp.pad(full_router, ((0, 0), (0, lanes - EXPERTS)))
     tables = (pick, spots, mask_wide, router_wide)
-    segments = spread(segment_ids)
-    tokens_all = spread(after(tokens, *segments[1:]))
-    segments = jnp.concatenate(segments, axis=0)
-    normed = jnp.concatenate(
-        [rms_norm(v.astype(F32), attn_gain).astype(BF) for v in tokens_all], axis=0
-    )
+    tokens_all = spread(tokens)
+    segments = jnp.concatenate(spread(after(segment_ids, *tokens_all[1:])), axis=0)
+    normed = norm_rows(tokens_all, attn_gain[None, :])
     rounds = groups // 2
     where = jnp.stack([me_r, me_f // 2, core]).astype(jnp.int32)
     half = lax.dynamic_slice(quarter, (core * (width // 2), 0), (width // 2, part))
     near = spread(after(half, *tokens_all[1:]))
     near[1] = after(near[1], *tables, segments, normed)
     normed = after(normed, *near[1:])
+    far = [cross(v, 1) for v in near]
     w_qkv = gather(jnp.concatenate([columns(w, 0) for w in (w_query, w_key, w_value)], axis=1))
     cot_all = gather(cotangent)
     cot_pair = (cotangent, cross(cotangent, 1))
@@ -870,8 +897,6 @@
     gains = jnp.stack([gain_query, gain_key])
     raw, ready, mixed_heads, totals, tops = attend(normed, w_qkv, segments, cosine, sine, gains, heads
     )
-    near = jnp.stack([after(near[0], raw), *near[1:]])
-    far = cross(near, 1)
     mixed_heads = mixed_heads.reshape(replicas, length, part)
     pieces = [mixed_heads[0]] + [swap(mixed_heads[k], k) for k in range(1, replicas)]
     inputs = tokens.astype(F32)

time: 754 us -> 760 us (level)
  other arithmetic: 48.9 us -> 37.8 us
  local copies, waits for them, and re-layouts: 69.2 us -> 77.1 us
    unnamed x172 -> x170, local copies, waits for them, and re-layouts: 50.4 us -> 57 us
  transfers between devices with their start and end apart: 64 -> 67, of which waited for: 27 -> 26; matrix products, arithmetic and copies ran while one was open for 10% -> 9% of each run, Pallas kernels for 39% -> 39%
where the time goes in v6:
time: 760 us; the launch traced here: 749 us
  Pallas kernels  301 us (40%)
  waiting for transfers between devices  241 us (32%)
  local copies, waits for them, and re-layouts  77.1 us (10%)
  starting transfers between devices  70 us (9%)
  other arithmetic  37.8 us (5%)
  between operations  15.5 us (2%)
    ppermute x35, waiting for transfers between devices, swap(): return lax.ppermute(value, 'replica', [(r, r ^ k) for r in range(replicas)])  226 us
    pallas_call x4, Pallas kernels, expert_block(): pl.pallas_call(functools.partial(expert_kernel, min(512, ff), min(1024, w...  130 us
    unnamed x170, local copies, waits for them, and re-layouts  57 us
    pallas_call x2, Pallas kernels, weight_grads(): pl.pallas_call(functools.partial(weight_grad_kernel, half), grid_spec=plt...  52.8 us
    ppermute x35, starting transfers between devices, swap(): return lax.ppermute(value, 'replica', [(r, r ^ k) for r in range(replicas)])  41.3 us
    ppermute x6, starting transfers between devices, pass_on(): return (lax.ppermute(up, 'fsdp', pairs), lax.ppermute(down, 'fsdp', back))  18.5 us
    pallas_call x4, Pallas kernels, halve(): pl.pallas_call(functools.partial(halve_kernel, half), grid_spec=pltpu.Pre...  16.1 us
  transfers between devices with their start and end apart: 67, of which 26 were waited for; matrix products, arithmetic and copies ran while one was open for 9% of the time, Pallas kernels for 39%

profile of v6, /device:TPU:8, one launch (start us, length us, event | category | flops | bytes accessed | tf_op | source)
XLA Modules:
  0.0 749.5 jit_solution(40438069129052325)
XLA Ops:
  18.0 22.6 %collective-permute-done.refs_1_ = bf16[256,2048]{1,0:T(8,128)(2,1)S(1)} collective-permute-done((bf16[256,2048]{1,0:T(8,128)(2,1)}, bf16[256,2048]{1,0:T(8,128)(2,1)S(1)}, u32[]{:S(2)}, u32[]{:S(2)}) %collective-permute-start) | collective-permute-done | bytes 1048608 | tf_op jit(solution)/shard_map/ppermute | solution.py:794
  40.6 22.5 %collective-permute-done.1.refs_2_ = bf16[256,2048]{1,0:T(8,128)(2,1)S(1)} collective-permute-done((bf16[256,2048]{1,0:T(8,128)(2,1)}, bf16[256,2048]{1,0:T(8,128)(2,1)S(1)}, u32[]{:S(2)}, u32[]{:S(2)}) %collective-permute-start.1) | collective-permute-done | bytes 1048608 | tf_op jit(solution)/shard_map/ppermute | solution.py:794
  72.3 3.0 norm_rows.1.refs_6_.refs_0_
  95.3 11.8 %collective-permute-done.3.refs_0_ = bf16[1024,512]{1,0:T(8,128)(2,1)S(1)} collective-permute-done((bf16[1024,512]{1,0:T(8,128)(2,1)}, bf16[1024,512]{1,0:T(8,128)(2,1)S(1)}, u32[]{:S(2)}, u32[]{:S(2)}) %collective-permute-start.3) | collective-permute-done | bytes 1048608 | tf_op jit(solution)/shard_map/ppermute | solution.py:794
  108.1 18.7 %collective-permute-done.7.refs_2_.refs_6_.refs_12_ = bf16[1024,512]{1,0:T(8,128)(2,1)} collective-permute-done((bf16[1024,512]{1,0:T(8,128)(2,1)}, bf16[1024,512]{1,0:T(8,128)(2,1)}, u32[]{:S(2)}, u32[]{:S(2)}) %collective-permute-start.7) | collective-permute-done | bytes 1048608 | tf_op jit(solution)/shard_map/ppermute | solution.py:794
  130.9 14.6 %attention.1 = (f32[1024,1024]{1,0:T(8,128)}, bf16[1024,1536]{1,0:T(8,128)(2,1)}, bf16[1024,512]{1,0:T(8,128)(2,1)}, f32[1024,128]{1,0:T(8,128)}, f32[4,1,128]{2,1,0:T(1,128)}) custom-call(bf16[1024,2048]{1,0:T(8,128)(2,1)} %after.35.normed.left, bf16[2048,1536]{1,0:T(8,128)(2,1)} %all-gather.6.cloned.1.call-done.weight, ...), custom_call_target="tpu_custom_call" | custom-call | tf_op jit(solution)/shard_map/attention/pallas_call | solution.py:381
  152.5 4.6 collective-permute-done.9.refs_1_
  157.5 4.7 collective-permute-done.11.refs_3_
  162.2 8.6 %attention_out.1 = (f32[256,2048]{1,0:T(8,128)}, bf16[256,2048]{1,0:T(8,128)(2,1)}, bf16[256,2048]{1,0:T(8,128)(2,1)}) custom-call(s32[3]{0:T(128)} %pad_add_fusion.2.who, bf16[256,512]{1,0:T(8,128)(2,1)} %get-tuple-element.229.refs_0_, bf16[256,512]{1,0:T(8,128)(2,1)} %copy-done.65, bf16[256,512]{1,0:T(8,128)(2,1)} %collective-permute-done.10.refs_2_, ...), custom_call_target="tpu_custom_call" | custom-call | tf_op jit(solution)/shard_map/attention_out/pallas_call | solution.py:252
  171.5 3.7 collective-permute-start.16
  175.2 2.4 collective-permute-start.20
  178.6 32.5 %experts.4 = (bf16[2,1152,2048]{2,1,0:T(8,128)(2,1)}, bf16[2,1152,2048]{2,1,0:T(8,128)(2,1)}, bf16[2,1152,2048]{2,1,0:T(8,128)(2,1)}, bf16[2,1152,1024]{2,1,0:T(...) custom-call(s32[5]{0:T(128)} %stack.105.who, ...), custom_call_target="tpu_custom_call" | custom-call | flops 28991029248 | bytes 46137344 | tf_op jit(solution)/shard_map/experts/pallas_call | solution.py:203
  220.4 5.8 collective-permute-start.19
  228.4 32.5 %experts.5 = (bf16[2,1152,2048]{2,1,0:T(8,128)(2,1)}, bf16[2,1152,2048]{2,1,0:T(8,128)(2,1)}, bf16[2,1152,2048]{2,1,0:T(8,128)(2,1)}, bf16[2,1152,1024]{2,1,0:T(...) custom-call(s32[5]{0:T(128)} %stack.109.who, ...), custom_call_target="tpu_custom_call", output_to_operand_aliasing={{0}: (14, {}), {1}: (15, {}), {2}: (16, {}), {3}: (17, {}),... | custom-call | flops 28991029248 | bytes 46137344 | tf_op jit(solution)/shard_map/experts/pallas_call | solution.py:203
  262.0 2.4 broadcast_select_fusion.refs_0_
  269.3 2.7 collective-permute-start.27
  272.6 32.5 %experts.6 = (bf16[2,1152,2048]{2,1,0:T(8,128)(2,1)}, bf16[2,1152,2048]{2,1,0:T(8,128)(2,1)}, bf16[2,1152,2048]{2,1,0:T(8,128)(2,1)}, bf16[2,1152,1024]{2,1,0:T(...) custom-call(s32[5]{0:T(128)} %stack.113.who, ...), custom_call_target="tpu_custom_call", output_to_operand_aliasing={{0}: (14, {}), {1}: (15, {}), {2}: (16, {}), {3}: (17, {}),... | custom-call | flops 28991029248 | bytes 46137344 | tf_op jit(solution)/shard_map/experts/pallas_call | solution.py:203
  307.4 2.7 add_convert_fusion.3.refs_18_
  310.1 2.7 add_convert_fusion.2.refs_19_
  312.8 4.3 collective-permute-start.33
  318.1 32.7 %experts.7 = (bf16[2,1152,2048]{2,1,0:T(8,128)(2,1)}, bf16[2,1152,2048]{2,1,0:T(8,128)(2,1)}, bf16[2,1152,2048]{2,1,0:T(8,128)(2,1)}, bf16[2,1152,1024]{2,1,0:T(...) custom-call(s32[5]{0:T(128)} %stack.102.who, ...), custom_call_target="tpu_custom_call", output_to_operand_aliasing={{0}: (14, {}), {1}: (15, {}), {2}: (16, {}), {3}: (17, {}),... | custom-call | flops 28991029248 | bytes 46137344 | tf_op jit(solution)/shard_map/experts/pallas_call | solution.py:203
  350.8 20.4 %weight_grads.2 = (bf16[2,256,2048]{2,1,0:T(8,128)(2,1)}, bf16[2,256,2048]{2,1,0:T(8,128)(2,1)}, bf16[2,256,2048]{2,1,0:T(8,128)(2,1)}, bf16[2,256,2048]{2,1,0:T(8,128)(2,1)}) custom-call(s32[2,4]{1,0:T(2,128)} %pad_add_fusion.1.quarters, bf16[2,1152,1024]{2,1,0:T(8,128)(2,1)} %after.42.left, bf16[2,1152,2048]{2,1,0:T(8,128)(2,1)} %get-tuple-element.116.right), custom_call_target="tpu_custom_call" | custom-call | tf_op jit(solution)/shard_map/weight_grads/pallas_call | solution.py:501
  375.9 2.7 add_convert_fusion.1.refs_1_
  378.6 32.4 %weight_grads.3 = (bf16[2,512,2048]{2,1,0:T(8,128)(2,1)}, bf16[2,512,2048]{2,1,0:T(8,128)(2,1)}, bf16[2,512,2048]{2,1,0:T(8,128)(2,1)}, bf16[2,512,2048]{2,1,0:T(8,128)(2,1)}) custom-call(s32[2,4]{1,0:T(2,128)} %pad_add_fusion.1.quarters, bf16[2,1152,2048]{2,1,0:T(8,128)(2,1)} %after.44.left, bf16[2,1152,2048]{2,1,0:T(8,128)(2,1)} %get-tuple-element.122.right), custom_call_target="tpu_custom_call" | custom-call | flops 99999997952 | tf_op jit(solution)/shard_map/weight_grads/pallas_call | solution.py:501
  411.0 10.0 %collective-permute-done.36.refs_5_.refs_2_.refs_0_ = bf16[2,256,2048]{2,1,0:T(8,128)(2,1)} collective-permute-done((bf16[2,256,2048]{2,1,0:T(8,128)(2,1)}, bf16[2,256,2048]{2,1,0:T(8,128)(2,1)}, u32[]{:S(2)}, u32[]{:S(2)}) %collective-permute-start.36) | collective-permute-done | bytes 2097184 | tf_op jit(solution)/shard_map/ppermute | solution.py:794
  422.3 6.8 collective-permute-done.35.refs_0_
  434.4 12.6 %attention_back.1 = (f32[256,2048]{1,0:T(8,128)}, f32[1,2048]{1,0:T(1,128)}, bf16[2048,128]{1,0:T(8,128)(2,1)}, bf16[256,1024]{1,0:T(8,128)(2,1)}, bf16[256,1024...) custom-call(s32[3]{0:T(128)} %pad_add_fusion.2.who, ...), custom_call_target="tpu_custom_call" | custom-call | flops 99999997952 | tf_op jit(solution)/shard_map/attention_back/pallas_call | solution.py:322
  451.6 10.4 %collective-permute-done.39 = bf16[256,1024]{1,0:T(8,128)(2,1)S(1)} collective-permute-done((bf16[256,1024]{1,0:T(8,128)(2,1)}, bf16[256,1024]{1,0:T(8,128)(2,1)S(1)}, u32[]{:S(2)}, u32[]{:S(2)}) %collective-permute-start.39) | collective-permute-done | bytes 524320 | tf_op jit(solution)/shard_map/ppermute | solution.py:794
  462.0 11.5 %collective-permute-done.40 = bf16[256,1024]{1,0:T(8,128)(2,1)S(1)} collective-permute-done((bf16[256,1024]{1,0:T(8,128)(2,1)}, bf16[256,1024]{1,0:T(8,128)(2,1)S(1)}, u32[]{:S(2)}, u32[]{:S(2)}) %collective-permute-start.40) | collective-permute-done | bytes 524320 | tf_op jit(solution)/shard_map/ppermute | solution.py:794
  485.1 14.2 %attention_grad.1 = (bf16[1024,1536]{1,0:T(8,128)(2,1)S(1)}, f32[4,2,128]{2,1,0:T(2,128)S(1)}) custom-call(bf16[1024,1024]{1,0:T(8,128)(2,1)S(1)} %copy-done.8, f32[1024,1024]{1,0:T(8,128)S(1)} %copy-done.18, bf16[1024,1536]{1,0:T(8,128)(2,1)S(1)} %copy-done.9, f32[1024,128]{1,0:T(8,128)S(1)} %copy-done.33, s32[4,1,256]{2,1,0:T(1,128)S(1)} %copy-done.34, ...), custom_call_target="tpu_custom_call" | custom-call | tf_op jit(solution)/shard_map/attention_grad/pallas_call | solution.py:449
  500.0 8.7 %product.1 = bf16[2048,1536]{1,0:T(8,128)(2,1)S(1)} custom-call(bf16[1024,2048]{1,0:T(8,128)(2,1)S(1)} %copy-done.3, bf16[1024,1536]{1,0:T(8,128)(2,1)S(1)} %get-tuple-element.135.grad.right), custom_call_target="tpu_custom_call" | custom-call | tf_op jit(solution)/shard_map/product/pallas_call | solution.py:527
  508.7 2.6 copy-done.6
  512.9 12.5 %normed_grads.1 = (bf16[256,2048]{1,0:T(8,128)(2,1)S(1)}, bf16[256,2048]{1,0:T(8,128)(2,1)}, bf16[256,2048]{1,0:T(8,128)(2,1)}, bf16[256,2048]{1,0:T(8,128)(2,1)}) custom-call(bf16[1024,1536]{1,0:T(8,128)(2,1)} %copy-done.10, bf16[2048,1536]{1,0:T(8,128)(2,1)} %all-gather.6.cloned.1.call-done.weight), custom_call_target="tpu_custom_call" | custom-call | tf_op jit(solution)/shard_map/normed_grads/pallas_call | solution.py:555
  531.5 2.9 halve.6
  543.5 25.3 %collective-permute-done.43.refs_1_.got = bf16[2,512,2048]{2,1,0:T(8,128)(2,1)} collective-permute-done((bf16[2,512,2048]{2,1,0:T(8,128)(2,1)}, bf16[2,512,2048]{2,1,0:T(8,128)(2,1)}, u32[]{:S(2)}, u32[]{:S(2)}) %collective-permute-start.43) | collective-permute-done | bytes 4194336 | tf_op jit(solution)/shard_map/ppermute | solution.py:794
  571.1 5.8 halve.5
  581.6 5.8 halve.4
  589.6 4.7 fusion.9
  596.0 21.2 %collective-permute-done.46.refs_3_ = bf16[256,2048]{1,0:T(8,128)(2,1)} collective-permute-done((bf16[256,2048]{1,0:T(8,128)(2,1)}, bf16[256,2048]{1,0:T(8,128)(2,1)}, u32[]{:S(2)}, u32[]{:S(2)}) %collective-permute-start.46) | collective-permute-done | bytes 1048608 | tf_op jit(solution)/shard_map/ppermute | solution.py:794
  617.3 6.3 input_grad.1
  636.4 22.4 %collective-permute-done.52.refs_2_.refs_0_ = bf16[1,512,2048]{2,1,0:T(8,128)(2,1)} collective-permute-done((bf16[1,512,2048]{2,1,0:T(8,128)(2,1)}, bf16[1,512,2048]{2,1,0:T(8,128)(2,1)}, u32[]{:S(2)}, u32[]{:S(2)}) %collective-permute-start.52) | collective-permute-done | bytes 2097184 | tf_op jit(solution)/shard_map/ppermute | solution.py:794
  672.9 3.0 multiply_convert_fusion
  679.4 2.3 collective-permute-start.58
  681.7 7.6 %join.2.refs_1_ = f32[2,512,2048]{2,1,0:T(8,128)} custom-call(bf16[512,2048]{1,0:T(8,128)(2,1)} %bitcast.69, bf16[512,2048]{1,0:T(8,128)(2,1)} %bitcast.34.refs_1_, bf16[512,2048]{1,0:T(8,128)(2,1)} %bitcast.68, bf16[512,2048]{1,0:T(8,128)(2,1)} %bitcast.36.refs_3_), custom_call_target="tpu_custom_call" | custom-call | flops 99999997952 | tf_op jit(solution)/shard_map/join/pallas_call | solution.py:625
  692.4 4.4 join.3
  696.8 18.5 %collective-permute-done.56.refs_0_ = bf16[256,2176]{1,0:T(8,128)(2,1)S(1)} collective-permute-done((bf16[256,2176]{1,0:T(8,128)(2,1)}, bf16[256,2176]{1,0:T(8,128)(2,1)S(1)}, u32[]{:S(2)}, u32[]{:S(2)}) %collective-permute-start.56) | collective-permute-done | bytes 1114144 | tf_op jit(solution)/shard_map/ppermute | solution.py:794
  716.3 18.6 %collective-permute-done.58.refs_3_ = bf16[256,2176]{1,0:T(8,128)(2,1)} collective-permute-done((bf16[256,2176]{1,0:T(8,128)(2,1)}, bf16[256,2176]{1,0:T(8,128)(2,1)}, u32[]{:S(2)}, u32[]{:S(2)}) %collective-permute-start.58) | collective-permute-done | bytes 1114144 | tf_op jit(solution)/shard_map/ppermute | solution.py:794
  736.1 5.4 gather_columns.1
  (403 shorter events, 166.8 us)
Async XLA Ops:
  7.2 71.3 %all-gather.4.cloned.1.call-start = ((), (), s32[]{:S(2)}) async-start(), calls=%async_computation.3 | async-start | bytes 2949120 | tf_op jit(solution)/shard_map/all_gather | solution.py:837
  11.2 119.7 %all-gather.6.cloned.1.call-start = ((), (), s32[]{:S(2)}) async-start(), calls=%async_computation.4 | async-start | bytes 7077888 | tf_op jit(solution)/shard_map/all_gather | solution.py:837
  14.3 214.2 %all-gather.8.cloned.1.call-start = ((), (), s32[]{:S(2)}) async-start(), calls=%async_computation.5 | async-start | bytes 9437184 | tf_op jit(solution)/shard_map/all_gather | solution.py:837
  14.3 26.3 %collective-permute-start = (bf16[256,2048]{1,0:T(8,128)(2,1)}, bf16[256,2048]{1,0:T(8,128)(2,1)S(1)}, u32[]{:S(2)}, u32[]{:S(2)}) collective-permute-start(bf16[256,2048]{1,0:T(8,128)(2,1)} %refs_4_.1), channel_id=1, source_target_pairs={{0,8},{8,0},{16,24},{24,16},{1,9},{9,1},{17,25},{25,17},{2,10},{10... | collective-permute-start | bytes 3145736 | tf_op jit(solution)/shard_map/ppermute | solution.py:794
  15.9 47.3 %collective-permute-start.1 = (bf16[256,2048]{1,0:T(8,128)(2,1)}, bf16[256,2048]{1,0:T(8,128)(2,1)S(1)}, u32[]{:S(2)}, u32[]{:S(2)}) collective-permute-start(bf16[256,2048]{1,0:T(8,128)(2,1)} %refs_4_.1), channel_id=1, source_target_pairs={{0,16},{8,24},{16,0},{24,8},{1,17},{9,25},{17,1},{25,9},{2,18},{10... | collective-permute-start | bytes 3145736 | tf_op jit(solution)/shard_map/ppermute | solution.py:794
  17.4 45.8 %collective-permute-start.2 = (bf16[256,2048]{1,0:T(8,128)(2,1)}, bf16[256,2048]{1,0:T(8,128)(2,1)S(1)}, u32[]{:S(2)}, u32[]{:S(2)}) collective-permute-start(bf16[256,2048]{1,0:T(8,128)(2,1)} %refs_4_.1), channel_id=1, source_target_pairs={{0,24},{8,16},{16,8},{24,0},{1,25},{9,17},{17,9},{25,1},{2,26},{10... | collective-permute-start | bytes 3145736 | tf_op jit(solution)/shard_map/ppermute | solution.py:794
  17.9 561.4 %reduce-scatter.4.cloned.1.call-start = ((), (), s32[]{:S(2)}) async-start(), calls=%async_computation.6 | async-start | bytes 9437184 | tf_op jit(solution)/shard_map/reduce_scatter | solution.py:840
  80.8 26.3 %collective-permute-start.3 = (bf16[1024,512]{1,0:T(8,128)(2,1)}, bf16[1024,512]{1,0:T(8,128)(2,1)S(1)}, u32[]{:S(2)}, u32[]{:S(2)}) collective-permute-start(bf16[1024,512]{1,0:T(8,128)(2,1)} %after.32.refs_4_.refs_10_), channel_id=1, source_target_pairs={{0,8},{8,0},{16,24},{24,16},{1,9},{9,1},{17,25},{25,17},{2,10},{10... | collective-permute-start | bytes 3145736 | tf_op jit(solution)/shard_map/ppermute | solution.py:794
  81.0 45.7 %collective-permute-start.7 = (bf16[1024,512]{1,0:T(8,128)(2,1)}, bf16[1024,512]{1,0:T(8,128)(2,1)}, u32[]{:S(2)}, u32[]{:S(2)}) collective-permute-start(bf16[1024,512]{1,0:T(8,128)(2,1)} %after.32.refs_4_.refs_10_), channel_id=1, source_target_pairs={{0,16},{8,24},{16,0},{24,8},{1,17},{9,25},{17,1},{25,9},{2,18},{10... | collective-permute-start | bytes 3145736 | tf_op jit(solution)/shard_map/ppermute | solution.py:794
  82.8 43.9 %collective-permute-start.8 = (bf16[1024,512]{1,0:T(8,128)(2,1)}, bf16[1024,512]{1,0:T(8,128)(2,1)}, u32[]{:S(2)}, u32[]{:S(2)}) collective-permute-start(bf16[1024,512]{1,0:T(8,128)(2,1)} %after.32.refs_4_.refs_10_), channel_id=1, source_target_pairs={{0,24},{8,16},{16,8},{24,0},{1,25},{9,17},{17,9},{25,1},{2,26},{10... | collective-permute-start | bytes 3145736 | tf_op jit(solution)/shard_map/ppermute | solution.py:794
  84.3 63.6 %collective-permute-start.12 = (bf16[1024,512]{1,0:T(8,128)(2,1)}, bf16[1024,512]{1,0:T(8,128)(2,1)}, u32[]{:S(2)}, u32[]{:S(2)}) collective-permute-start(bf16[1024,512]{1,0:T(8,128)(2,1)} %after.32.refs_4_.refs_10_), channel_id=1, source_target_pairs={{0,1},{1,0},{2,3},{3,2},{4,5},{5,4},{6,7},{7,6},{8,9},{9,8},{10,11... | collective-permute-start | bytes 3145736 | tf_op jit(solution)/shard_map/ppermute | solution.py:812
  108.1 41.0 %collective-permute-start.13 = (bf16[1024,512]{1,0:T(8,128)(2,1)}, bf16[1024,512]{1,0:T(8,128)(2,1)S(1)}, u32[]{:S(2)}, u32[]{:S(2)}) collective-permute-start(bf16[1024,512]{1,0:T(8,128)(2,1)} %after.34.refs_1_.refs_5_.refs_11_), channel_id=1, source_target_pairs={{0,1},{1,0},{2,3},{3,2},{4,5},{5,4},{6,7},{7,6},{8,9},{9,8},{10,11... | collective-permute-start | bytes 3145736 | tf_op jit(solution)/shard_map/ppermute | solution.py:812
  126.7 25.7 %collective-permute-start.14 = (bf16[1024,512]{1,0:T(8,128)(2,1)}, bf16[1024,512]{1,0:T(8,128)(2,1)S(1)}, u32[]{:S(2)}, u32[]{:S(2)}) collective-permute-start(bf16[1024,512]{1,0:T(8,128)(2,1)} %collective-permute-done.7.refs_2_.refs_6_.refs_12_), channel_id=1, source_target_pairs={{0,1},{1,0},{2,3},{3,2},{4,5},{5,4},{6,7},{7,6},{8,9},{9,8},{10,11... | collective-permute-start | bytes 3145736 | tf_op jit(solution)/shard_map/ppermute | solution.py:812
  126.7 25.7 %collective-permute-start.15 = (bf16[1024,512]{1,0:T(8,128)(2,1)}, bf16[1024,512]{1,0:T(8,128)(2,1)S(1)}, u32[]{:S(2)}, u32[]{:S(2)}) collective-permute-start(bf16[1024,512]{1,0:T(8,128)(2,1)} %collective-permute-done.8.refs_3_.refs_7_.refs_13_), channel_id=1, source_target_pairs={{0,1},{1,0},{2,3},{3,2},{4,5},{5,4},{6,7},{7,6},{8,9},{9,8},{10,11... | collective-permute-start | bytes 3145736 | tf_op jit(solution)/shard_map/ppermute | solution.py:812
  149.0 13.1 %collective-permute-start.11 = (bf16[256,512]{1,0:T(8,128)(2,1)}, bf16[256,512]{1,0:T(8,128)(2,1)}, u32[]{:S(2)}, u32[]{:S(2)}) collective-permute-start(bf16[256,512]{1,0:T(8,128)(2,1)} %get-tuple-element.226), channel_id=1, source_target_pairs={{0,24},{8,16},{16,8},{24,0},{1,25},{9,17},{17,9},{25,1},{2,26},{10... | collective-permute-start | bytes 786440 | tf_op jit(solution)/shard_map/ppermute | solution.py:794
  152.4 25.2 %collective-permute-start.18 = (bf16[256,2048]{1,0:T(8,128)(2,1)}, bf16[256,2048]{1,0:T(8,128)(2,1)}, u32[]{:S(2)}, u32[]{:S(2)}) collective-permute-start(bf16[256,2048]{1,0:T(8,128)(2,1)} %refs_6_.1), channel_id=1, source_target_pairs={{0,1},{1,0},{2,3},{3,2},{4,5},{5,4},{6,7},{7,6},{8,9},{9,8},{10,11... | collective-permute-start | bytes 3145736 | tf_op jit(solution)/shard_map/ppermute | solution.py:812
  171.5 41.5 %collective-permute-start.16 = (bf16[256,2048]{1,0:T(8,128)(2,1)}, bf16[256,2048]{1,0:T(8,128)(2,1)S(1)}, u32[]{:S(2)}, u32[]{:S(2)}) collective-permute-start(bf16[256,2048]{1,0:T(8,128)(2,1)} %get-tuple-element.90.refs_0_.refs_5_), channel_id=1, source_target_pairs={{0,2},{1,3},{2,4},{3,5},{4,6},{5,7},{8,10},{9,11},{10,12},{11,13},... | collective-permute-start | bytes 3145736 | tf_op jit(solution)/shard_map/ppermute | solution.py:818
  175.2 39.6 %collective-permute-start.20 = (bf16[256,2048]{1,0:T(8,128)(2,1)}, bf16[256,2048]{1,0:T(8,128)(2,1)S(1)}, u32[]{:S(2)}, u32[]{:S(2)}) collective-permute-start(bf16[256,2048]{1,0:T(8,128)(2,1)} %get-tuple-element.90.refs_0_.refs_5_), channel_id=1, source_target_pairs={{2,0},{3,1},{4,2},{5,3},{6,4},{7,5},{10,8},{11,9},{12,10},{13,11},... | collective-permute-start | bytes 3145736 | tf_op jit(solution)/shard_map/ppermute | solution.py:818
  217.5 54.5 %collective-permute-start.25 = (bf16[256,2048]{1,0:T(8,128)(2,1)}, bf16[256,2048]{1,0:T(8,128)(2,1)}, u32[]{:S(2)}, u32[]{:S(2)}) collective-permute-start(bf16[256,2048]{1,0:T(8,128)(2,1)} %get-tuple-element.103), channel_id=1, source_target_pairs={{0,8},{8,0},{16,24},{24,16},{1,9},{9,1},{17,25},{25,17},{2,10},{10... | collective-permute-start | bytes 3145736 | tf_op jit(solution)/shard_map/ppermute | solution.py:794
  219.0 53.6 %collective-permute-start.26 = (bf16[256,2048]{1,0:T(8,128)(2,1)}, bf16[256,2048]{1,0:T(8,128)(2,1)}, u32[]{:S(2)}, u32[]{:S(2)}) collective-permute-start(bf16[256,2048]{1,0:T(8,128)(2,1)} %get-tuple-element.103), channel_id=1, source_target_pairs={{0,16},{8,24},{16,0},{24,8},{1,17},{9,25},{17,1},{25,9},{2,18},{10... | collective-permute-start | bytes 3145736 | tf_op jit(solution)/shard_map/ppermute | solution.py:794
  220.4 40.6 %collective-permute-start.19 = (bf16[256,2048]{1,0:T(8,128)(2,1)S(1)}, bf16[256,2048]{1,0:T(8,128)(2,1)}, u32[]{:S(2)}, u32[]{:S(2)}) collective-permute-start(bf16[256,2048]{1,0:T(8,128)(2,1)S(1)} %copy-done.48), channel_id=1, source_target_pairs={{2,4},{3,5},{4,6},{5,7},{10,12},{11,13},{12,14},{13,15},{18,20},{1... | collective-permute-start | bytes 3145736 | tf_op jit(solution)/shard_map/ppermute | solution.py:818
  226.2 34.8 %collective-permute-start.23 = (bf16[256,2048]{1,0:T(8,128)(2,1)S(1)}, bf16[256,2048]{1,0:T(8,128)(2,1)S(1)}, u32[]{:S(2)}, u32[]{:S(2)}) collective-permute-start(bf16[256,2048]{1,0:T(8,128)(2,1)S(1)} %copy-done.46), channel_id=1, source_target_pairs={{2,0},{3,1},{4,2},{5,3},{10,8},{11,9},{12,10},{13,11},{18,16},{19,... | collective-permute-start | bytes 3145736 | tf_op jit(solution)/shard_map/ppermute | solution.py:818
  267.6 38.3 %collective-permute-start.22 = (bf16[256,2048]{1,0:T(8,128)(2,1)}, bf16[256,2048]{1,0:T(8,128)(2,1)}, u32[]{:S(2)}, u32[]{:S(2)}) collective-permute-start(bf16[256,2048]{1,0:T(8,128)(2,1)} %after.38), channel_id=1, source_target_pairs={{4,6},{5,7},{12,14},{13,15},{20,22},{21,23},{28,30},{29,31}} | collective-permute-start | bytes 3145736 | tf_op jit(solution)/shard_map/ppermute | solution.py:818
  269.3 36.7 %collective-permute-start.27 = (bf16[256,2048]{1,0:T(8,128)(2,1)S(1)}, bf16[256,2048]{1,0:T(8,128)(2,1)}, u32[]{:S(2)}, u32[]{:S(2)}) collective-permute-start(bf16[256,2048]{1,0:T(8,128)(2,1)S(1)} %copy-done.53), channel_id=1, source_target_pairs={{2,0},{3,1},{10,8},{11,9},{18,16},{19,17},{26,24},{27,25}} | collective-permute-start | bytes 3145736 | tf_op jit(solution)/shard_map/ppermute | solution.py:818
  272.0 34.6 %collective-permute-start.29 = (bf16[272,2048]{1,0:T(8,128)(2,1)}, bf16[272,2048]{1,0:T(8,128)(2,1)}, u32[]{:S(2)}, u32[]{:S(2)}) collective-permute-start(bf16[272,2048]{1,0:T(8,128)(2,1)} %get-tuple-element.110), channel_id=1, source_target_pairs={{0,1},{1,0},{2,3},{3,2},{4,5},{5,4},{6,7},{7,6},{8,9},{9,8},{10,11... | collective-permute-start | bytes 3342344 | tf_op jit(solution)/shard_map/ppermute | solution.py:812
  305.9 44.9 %collective-permute-start.31 = (bf16[256,2048]{1,0:T(8,128)(2,1)}, bf16[256,2048]{1,0:T(8,128)(2,1)}, u32[]{:S(2)}, u32[]{:S(2)}) collective-permute-start(bf16[256,2048]{1,0:T(8,128)(2,1)} %get-tuple-element.103), channel_id=1, source_target_pairs={{0,24},{8,16},{16,8},{24,0},{1,25},{9,17},{17,9},{25,1},{2,26},{10... | collective-permute-start | bytes 3145736 | tf_op jit(solution)/shard_map/ppermute | solution.py:794
  310.1 61.1 %collective-permute-start.32 = (bf16[272,2048]{1,0:T(8,128)(2,1)}, bf16[272,2048]{1,0:T(8,128)(2,1)S(1)}, u32[]{:S(2)}, u32[]{:S(2)}) collective-permute-start(bf16[272,2048]{1,0:T(8,128)(2,1)} %add_convert_fusion.3.refs_18_), channel_id=1, source_target_pairs={{0,2},{1,3},{2,0},{3,1},{4,6},{5,7},{6,4},{7,5},{8,10},{9,11},{10,... | collective-permute-start | bytes 3342344 | tf_op jit(solution)/shard_map/ppermute | solution.py:812
  312.8 58.4 %collective-permute-start.33 = (bf16[272,2048]{1,0:T(8,128)(2,1)}, bf16[272,2048]{1,0:T(8,128)(2,1)S(1)}, u32[]{:S(2)}, u32[]{:S(2)}) collective-permute-start(bf16[272,2048]{1,0:T(8,128)(2,1)} %add_convert_fusion.2.refs_19_), channel_id=1, source_target_pairs={{0,4},{1,5},{2,6},{3,7},{4,0},{5,1},{6,2},{7,3},{8,12},{9,13},{10,... | collective-permute-start | bytes 3342344 | tf_op jit(solution)/shard_map/ppermute | solution.py:812
  372.5 48.5 %collective-permute-start.36 = (bf16[2,256,2048]{2,1,0:T(8,128)(2,1)}, bf16[2,256,2048]{2,1,0:T(8,128)(2,1)}, u32[]{:S(2)}, u32[]{:S(2)}) collective-permute-start(bf16[2,256,2048]{2,1,0:T(8,128)(2,1)} %get-tuple-element.117.refs_1_), channel_id=1, source_target_pairs={{0,8},{8,0},{16,24},{24,16},{1,9},{9,1},{17,25},{25,17},{2,10},{10... | collective-permute-start | bytes 6291464 | tf_op jit(solution)/shard_map/ppermute | solution.py:794
  374.4 48.0 %collective-permute-start.37 = (bf16[2,256,2048]{2,1,0:T(8,128)(2,1)}, bf16[2,256,2048]{2,1,0:T(8,128)(2,1)S(1)}, u32[]{:S(2)}, u32[]{:S(2)}) collective-permute-start(bf16[2,256,2048]{2,1,0:T(8,128)(2,1)} %get-tuple-element.119.refs_3_), channel_id=1, source_target_pairs={{0,16},{8,24},{16,0},{24,8},{1,17},{9,25},{17,1},{25,9},{2,18},{10... | collective-permute-start | bytes 6291464 | tf_op jit(solution)/shard_map/ppermute | solution.py:794
  378.6 50.6 %collective-permute-start.35 = (bf16[272,2048]{1,0:T(8,128)(2,1)}, bf16[272,2048]{1,0:T(8,128)(2,1)}, u32[]{:S(2)}, u32[]{:S(2)}) collective-permute-start(bf16[272,2048]{1,0:T(8,128)(2,1)} %add_convert_fusion.1.refs_1_), channel_id=1, source_target_pairs={{0,6},{1,7},{2,4},{3,5},{4,2},{5,3},{6,0},{7,1},{8,14},{9,15},{10,... | collective-permute-start | bytes 3342344 | tf_op jit(solution)/shard_map/ppermute | solution.py:812
  429.2 246.7 %reduce-scatter.6.cloned.1.call-start = ((), (), s32[]{:S(2)}) async-start(), calls=%async_computation.7 | async-start | bytes 7077888 | tf_op jit(solution)/shard_map/reduce_scatter | solution.py:840
  447.0 15.0 %collective-permute-start.39 = (bf16[256,1024]{1,0:T(8,128)(2,1)}, bf16[256,1024]{1,0:T(8,128)(2,1)S(1)}, u32[]{:S(2)}, u32[]{:S(2)}) collective-permute-start(bf16[256,1024]{1,0:T(8,128)(2,1)} %get-tuple-element.129), channel_id=1, source_target_pairs={{0,8},{8,0},{16,24},{24,16},{1,9},{9,1},{17,25},{25,17},{2,10},{10... | collective-permute-start | bytes 1572872 | tf_op jit(solution)/shard_map/ppermute | solution.py:794
  448.6 25.0 %collective-permute-start.40 = (bf16[256,1024]{1,0:T(8,128)(2,1)}, bf16[256,1024]{1,0:T(8,128)(2,1)S(1)}, u32[]{:S(2)}, u32[]{:S(2)}) collective-permute-start(bf16[256,1024]{1,0:T(8,128)(2,1)} %get-tuple-element.130), channel_id=1, source_target_pairs={{0,16},{8,24},{16,0},{24,8},{1,17},{9,25},{17,1},{25,9},{2,18},{10... | collective-permute-start | bytes 1572872 | tf_op jit(solution)/shard_map/ppermute | solution.py:794
  450.1 23.5 %collective-permute-start.41 = (bf16[256,1024]{1,0:T(8,128)(2,1)}, bf16[256,1024]{1,0:T(8,128)(2,1)S(1)}, u32[]{:S(2)}, u32[]{:S(2)}) collective-permute-start(bf16[256,1024]{1,0:T(8,128)(2,1)} %get-tuple-element.131), channel_id=1, source_target_pairs={{0,24},{8,16},{16,8},{24,0},{1,25},{9,17},{17,9},{25,1},{2,26},{10... | collective-permute-start | bytes 1572872 | tf_op jit(solution)/shard_map/ppermute | solution.py:794
  475.0 93.8 %collective-permute-start.43 = (bf16[2,512,2048]{2,1,0:T(8,128)(2,1)}, bf16[2,512,2048]{2,1,0:T(8,128)(2,1)}, u32[]{:S(2)}, u32[]{:S(2)}) collective-permute-start(bf16[2,512,2048]{2,1,0:T(8,128)(2,1)} %after.48.refs_2_), channel_id=1, source_target_pairs={{0,16},{8,24},{16,0},{24,8},{1,17},{9,25},{17,1},{25,9},{2,18},{10... | collective-permute-start | bytes 12582920 | tf_op jit(solution)/shard_map/ppermute | solution.py:794
  478.4 100.9 %collective-permute-start.42 = (bf16[2,512,2048]{2,1,0:T(8,128)(2,1)}, bf16[2,512,2048]{2,1,0:T(8,128)(2,1)}, u32[]{:S(2)}, u32[]{:S(2)}) collective-permute-start(bf16[2,512,2048]{2,1,0:T(8,128)(2,1)} %after.47.refs_1_), channel_id=1, source_target_pairs={{0,8},{8,0},{16,24},{24,16},{1,9},{9,1},{17,25},{25,17},{2,10},{10... | collective-permute-start | bytes 12582920 | tf_op jit(solution)/shard_map/ppermute | solution.py:794
  526.4 69.6 %collective-permute-start.44 = (bf16[256,2048]{1,0:T(8,128)(2,1)}, bf16[256,2048]{1,0:T(8,128)(2,1)}, u32[]{:S(2)}, u32[]{:S(2)}) collective-permute-start(bf16[256,2048]{1,0:T(8,128)(2,1)} %get-tuple-element.142), channel_id=1, source_target_pairs={{0,8},{8,0},{16,24},{24,16},{1,9},{9,1},{17,25},{25,17},{2,10},{10... | collective-permute-start | bytes 3145736 | tf_op jit(solution)/shard_map/ppermute | solution.py:794
  527.9 68.1 %collective-permute-start.45 = (bf16[256,2048]{1,0:T(8,128)(2,1)}, bf16[256,2048]{1,0:T(8,128)(2,1)}, u32[]{:S(2)}, u32[]{:S(2)}) collective-permute-start(bf16[256,2048]{1,0:T(8,128)(2,1)} %get-tuple-element.143), channel_id=1, source_target_pairs={{0,16},{8,24},{16,0},{24,8},{1,17},{9,25},{17,1},{25,9},{2,18},{10... | collective-permute-start | bytes 3145736 | tf_op jit(solution)/shard_map/ppermute | solution.py:794
  528.4 88.8 %collective-permute-start.46 = (bf16[256,2048]{1,0:T(8,128)(2,1)}, bf16[256,2048]{1,0:T(8,128)(2,1)}, u32[]{:S(2)}, u32[]{:S(2)}) collective-permute-start(bf16[256,2048]{1,0:T(8,128)(2,1)} %get-tuple-element.144), channel_id=1, source_target_pairs={{0,24},{8,16},{16,8},{24,0},{1,25},{9,17},{17,9},{25,1},{2,26},{10... | collective-permute-start | bytes 3145736 | tf_op jit(solution)/shard_map/ppermute | solution.py:794
  543.3 132.7 %reduce-scatter.8.cloned.1.call-start = ((), (), s32[]{:S(2)}) async-start(), calls=%async_computation.8 | async-start | bytes 2949120 | tf_op jit(solution)/shard_map/reduce_scatter | solution.py:840
  578.1 80.7 %collective-permute-start.52 = (bf16[1,512,2048]{2,1,0:T(8,128)(2,1)}, bf16[1,512,2048]{2,1,0:T(8,128)(2,1)}, u32[]{:S(2)}, u32[]{:S(2)}) collective-permute-start(bf16[1,512,2048]{2,1,0:T(8,128)(2,1)} %get-tuple-element.138.refs_2_), channel_id=1, source_target_pairs={{0,8},{8,0},{16,24},{24,16},{1,9},{9,1},{17,25},{25,17},{2,10},{10... | collective-permute-start | bytes 6291464 | tf_op jit(solution)/shard_map/ppermute | solution.py:794
  588.7 70.1 %collective-permute-start.51 = (bf16[1,512,2048]{2,1,0:T(8,128)(2,1)}, bf16[1,512,2048]{2,1,0:T(8,128)(2,1)}, u32[]{:S(2)}, u32[]{:S(2)}) collective-permute-start(bf16[1,512,2048]{2,1,0:T(8,128)(2,1)} %get-tuple-element.137.refs_1_), channel_id=1, source_target_pairs={{0,16},{8,24},{16,0},{24,8},{1,17},{9,25},{17,1},{25,9},{2,18},{10... | collective-permute-start | bytes 6291464 | tf_op jit(solution)/shard_map/ppermute | solution.py:794
  663.6 26.3 %collective-permute-start.59 = (bf16[1,256,2048]{2,1,0:T(8,128)(2,1)}, bf16[1,256,2048]{2,1,0:T(8,128)(2,1)S(1)}, u32[]{:S(2)}, u32[]{:S(2)}) collective-permute-start(bf16[1,256,2048]{2,1,0:T(8,128)(2,1)} %after.60), channel_id=1, source_target_pairs={{0,16},{8,24},{16,0},{24,8},{1,17},{9,25},{17,1},{25,9},{2,18},{10... | collective-permute-start | bytes 3145736 | tf_op jit(solution)/shard_map/ppermute | solution.py:794
  665.1 26.3 %collective-permute-start.60 = (bf16[1,256,2048]{2,1,0:T(8,128)(2,1)}, bf16[1,256,2048]{2,1,0:T(8,128)(2,1)S(1)}, u32[]{:S(2)}, u32[]{:S(2)}) collective-permute-start(bf16[1,256,2048]{2,1,0:T(8,128)(2,1)} %after.62), channel_id=1, source_target_pairs={{0,8},{8,0},{16,24},{24,16},{1,9},{9,1},{17,25},{25,17},{2,10},{10... | collective-permute-start | bytes 3145736 | tf_op jit(solution)/shard_map/ppermute | solution.py:794
  678.2 37.1 %collective-permute-start.56 = (bf16[256,2176]{1,0:T(8,128)(2,1)}, bf16[256,2176]{1,0:T(8,128)(2,1)S(1)}, u32[]{:S(2)}, u32[]{:S(2)}) collective-permute-start(bf16[256,2176]{1,0:T(8,128)(2,1)} %after.56.refs_0_), channel_id=1, source_target_pairs={{0,8},{8,0},{16,24},{24,16},{1,9},{9,1},{17,25},{25,17},{2,10},{10... | collective-permute-start | bytes 3342344 | tf_op jit(solution)/shard_map/ppermute | solution.py:794
  678.9 37.4 %collective-permute-start.57 = (bf16[256,2176]{1,0:T(8,128)(2,1)}, bf16[256,2176]{1,0:T(8,128)(2,1)}, u32[]{:S(2)}, u32[]{:S(2)}) collective-permute-start(bf16[256,2176]{1,0:T(8,128)(2,1)} %after.56.refs_0_), channel_id=1, source_target_pairs={{0,16},{8,24},{16,0},{24,8},{1,17},{9,25},{17,1},{25,9},{2,18},{10... | collective-permute-start | bytes 3342344 | tf_op jit(solution)/shard_map/ppermute | solution.py:794
  679.4 55.5 %collective-permute-start.58 = (bf16[256,2176]{1,0:T(8,128)(2,1)}, bf16[256,2176]{1,0:T(8,128)(2,1)}, u32[]{:S(2)}, u32[]{:S(2)}) collective-permute-start(bf16[256,2176]{1,0:T(8,128)(2,1)} %after.56.refs_0_), channel_id=1, source_target_pairs={{0,24},{8,16},{16,8},{24,0},{1,25},{9,17},{17,9},{25,1},{2,26},{10... | collective-permute-start | bytes 3342344 | tf_op jit(solution)/shard_map/ppermute | solution.py:794
  (101 other events, 581.0 us)
Sparse Core Ops, SparseCore 0:
  11.3 34.3 all-gather.3
  47.9 62.9 all-gather.5
  112.5 93.4 all-gather.7
  429.3 86.0 reduce-scatter.3
  542.4 65.0 reduce-scatter.5
  610.3 35.2 reduce-scatter.7

commit v7 on v5

--- a/solution.py
+++ b/solution.py
@@ -964,7 +964,15 @@
     )
     second = [v[1] for v in in_done]
     share_qkv = reduce(qkv_grad)
-    blocks = spread(after(jnp.concatenate([share_qkv, share_o], axis=1), *second, input_grad))
+    payload = after(jnp.concatenate([share_qkv, share_o], axis=1), *second, input_grad)
+    if replicas == 4:
+        across, along = swap(payload, 1), swap(payload, 2)
+        cut_at = payload.shape[0] // 2
+        upper = swap(across[:cut_at], 2)
+        lower = swap(along[cut_at:], 1)
+        blocks = [payload, across, along, jnp.concatenate([upper, lower], axis=0)]
+    else:
+        blocks = spread(payload)
     out_done = [
         (keep, swap(after(v, *second, moe_sum), next_bit(j, 1))) for j, (v, keep) in enumerate(out_halves)
     ]

time: 754 us -> 746 us (0.989)
    ppermute x35 -> x36, waiting for transfers between devices: 222 us -> 215 us  [swap(): return lax.ppermute(value, 'replica', [(r, r ^ k) for r in range(replicas)])]
    unnamed x172 -> x170, local copies, waits for them, and re-layouts: 50.4 us -> 47.6 us
    ppermute x35 -> x36, starting transfers between devices: 41.5 us -> 42.1 us  [swap(): return lax.ppermute(value, 'replica', [(r, r ^ k) for r in range(replicas)])]
  transfers between devices with their start and end apart: 64 -> 65, of which waited for: 27 -> 24; matrix products, arithmetic and copies ran while one was open for 10% -> 10% of each run, Pallas kernels for 39% -> 40%
where the time goes in v7:
time: 746 us; the launch traced here: 741 us
  Pallas kernels  298 us (40%)
  waiting for transfers between devices  234 us (31%)
  starting transfers between devices  68.9 us (9%)
  local copies, waits for them, and re-layouts  66.7 us (9%)
  other arithmetic  50.8 us (7%)
  between operations  15.5 us (2%)
    ppermute x36, waiting for transfers between devices, swap(): return lax.ppermute(value, 'replica', [(r, r ^ k) for r in range(replicas)])  215 us
    pallas_call x4, Pallas kernels, expert_block(): pl.pallas_call(functools.partial(expert_kernel, min(512, ff), min(1024, w...  131 us
    pallas_call x2, Pallas kernels, weight_grads(): pl.pallas_call(functools.partial(weight_grad_kernel, half), grid_spec=plt...  52.8 us
    unnamed x170, local copies, waits for them, and re-layouts  47.6 us
    ppermute x36, starting transfers between devices, swap(): return lax.ppermute(value, 'replica', [(r, r ^ k) for r in range(replicas)])  42.1 us
    ppermute x6, starting transfers between devices, pass_on(): return (lax.ppermute(up, 'fsdp', pairs), lax.ppermute(down, 'fsdp', back))  17.3 us
    pallas_call x4, Pallas kernels, halve(): pl.pallas_call(functools.partial(halve_kernel, half), grid_spec=pltpu.Pre...  16.1 us
  transfers between devices with their start and end apart: 65, of which 24 were waited for; matrix products, arithmetic and copies ran while one was open for 10% of the time, Pallas kernels for 40%

profile of v7, /device:TPU:8, one launch (start us, length us, event | category | flops | bytes accessed | tf_op | source)
XLA Modules:
  0.0 740.6 jit_solution(5970384828157358466)
XLA Ops:
  18.3 2.4 collective-permute-done.2.refs_3_
  22.8 2.5 collective-permute-start.5
  29.5 18.1 %collective-permute-done.3.refs_1_ = bf16[256,2048]{1,0:T(8,128)(2,1)S(1)} collective-permute-done((bf16[256,2048]{1,0:T(8,128)(2,1)}, bf16[256,2048]{1,0:T(8,128)(2,1)S(1)}, u32[]{:S(2)}, u32[]{:S(2)}) %collective-permute-start.3) | collective-permute-done | bytes 1048608 | tf_op jit(solution)/shard_map/ppermute | solution.py:765
  47.9 19.5 %collective-permute-done.4.refs_2_ = bf16[256,2048]{1,0:T(8,128)(2,1)S(1)} collective-permute-done((bf16[256,2048]{1,0:T(8,128)(2,1)}, bf16[256,2048]{1,0:T(8,128)(2,1)S(1)}, u32[]{:S(2)}, u32[]{:S(2)}) %collective-permute-start.4) | collective-permute-done | bytes 1048608 | tf_op jit(solution)/shard_map/ppermute | solution.py:765
  71.7 2.5 pad_maximum_fusion.refs_6_.refs_0_
  90.9 11.8 %collective-permute-done.6.refs_0_ = bf16[1024,512]{1,0:T(8,128)(2,1)S(1)} collective-permute-done((bf16[1024,512]{1,0:T(8,128)(2,1)}, bf16[1024,512]{1,0:T(8,128)(2,1)S(1)}, u32[]{:S(2)}, u32[]{:S(2)}) %collective-permute-start.6) | collective-permute-done | bytes 1048608 | tf_op jit(solution)/shard_map/ppermute | solution.py:765
  103.7 18.5 %collective-permute-done.7.refs_2_ = bf16[1024,512]{1,0:T(8,128)(2,1)} collective-permute-done((bf16[1024,512]{1,0:T(8,128)(2,1)}, bf16[1024,512]{1,0:T(8,128)(2,1)}, u32[]{:S(2)}, u32[]{:S(2)}) %collective-permute-start.7) | collective-permute-done | bytes 1048608 | tf_op jit(solution)/shard_map/ppermute | solution.py:765
  122.2 14.6 %attention.1 = (f32[1024,1024]{1,0:T(8,128)}, bf16[1024,1536]{1,0:T(8,128)(2,1)}, bf16[1024,512]{1,0:T(8,128)(2,1)}, f32[1024,128]{1,0:T(8,128)}, f32[4,1,128]{2,1,0:T(1,128)}) custom-call(bf16[1024,2048]{1,0:T(8,128)(2,1)} %after.36.normed.left, bf16[2048,1536]{1,0:T(8,128)(2,1)} %all-gather.6.cloned.1.call-done.weight, ...), custom_call_target="tpu_custom_call" | custom-call | tf_op jit(solution)/shard_map/attention/pallas_call | solution.py:379
  138.1 3.7 pad_maximum_fusion.1.refs_4_.refs_10_
  147.3 4.4 collective-permute-done.9.refs_1_
  151.7 5.5 collective-permute-done.10.refs_2_
  158.0 8.5 %attention_out.1 = (f32[256,2048]{1,0:T(8,128)}, bf16[256,2048]{1,0:T(8,128)(2,1)}, bf16[256,2048]{1,0:T(8,128)(2,1)}) custom-call(s32[3]{0:T(128)} %pad_add_fusion.2.who, bf16[256,512]{1,0:T(8,128)(2,1)} %get-tuple-element.229.refs_0_, bf16[256,512]{1,0:T(8,128)(2,1)} %copy-done.59, bf16[256,512]{1,0:T(8,128)(2,1)} %copy-done.60, ...), custom_call_target="tpu_custom_call" | custom-call | tf_op jit(solution)/shard_map/attention_out/pallas_call | solution.py:252
  167.1 3.5 collective-permute-start.13
  173.1 32.8 %experts.4 = (bf16[2,1152,2048]{2,1,0:T(8,128)(2,1)}, bf16[2,1152,2048]{2,1,0:T(8,128)(2,1)}, bf16[2,1152,2048]{2,1,0:T(8,128)(2,1)}, bf16[2,1152,1024]{2,1,0:T(...) custom-call(s32[5]{0:T(128)} %stack.125.who, ...), custom_call_target="tpu_custom_call" | custom-call | flops 28991029248 | bytes 46137344 | tf_op jit(solution)/shard_map/experts/pallas_call | solution.py:203
  205.9 5.8 collective-permute-done.13.refs_0_
  219.2 5.6 collective-permute-start.16
  226.8 32.8 %experts.5 = (bf16[2,1152,2048]{2,1,0:T(8,128)(2,1)}, bf16[2,1152,2048]{2,1,0:T(8,128)(2,1)}, bf16[2,1152,2048]{2,1,0:T(8,128)(2,1)}, bf16[2,1152,1024]{2,1,0:T(...) custom-call(s32[5]{0:T(128)} %stack.129.who, ...), custom_call_target="tpu_custom_call", output_to_operand_aliasing={{0}: (14, {}), {1}: (15, {}), {2}: (16, {}), {3}: (17, {}),... | custom-call | flops 28991029248 | bytes 46137344 | tf_op jit(solution)/shard_map/experts/pallas_call | solution.py:203
  260.6 2.5 broadcast_select_fusion.refs_0_
  270.7 33.0 %experts.6 = (bf16[2,1152,2048]{2,1,0:T(8,128)(2,1)}, bf16[2,1152,2048]{2,1,0:T(8,128)(2,1)}, bf16[2,1152,2048]{2,1,0:T(8,128)(2,1)}, bf16[2,1152,1024]{2,1,0:T(...) custom-call(s32[5]{0:T(128)} %stack.133.who, ...), custom_call_target="tpu_custom_call", output_to_operand_aliasing={{0}: (14, {}), {1}: (15, {}), {2}: (16, {}), {3}: (17, {}),... | custom-call | flops 28991029248 | bytes 46137344 | tf_op jit(solution)/shard_map/experts/pallas_call | solution.py:203
  306.3 2.7 add_convert_fusion.3.refs_18_
  309.0 2.7 add_convert_fusion.2.refs_19_
  311.7 4.3 collective-permute-start.30
  317.0 32.6 %experts.7 = (bf16[2,1152,2048]{2,1,0:T(8,128)(2,1)}, bf16[2,1152,2048]{2,1,0:T(8,128)(2,1)}, bf16[2,1152,2048]{2,1,0:T(8,128)(2,1)}, bf16[2,1152,1024]{2,1,0:T(...) custom-call(s32[5]{0:T(128)} %stack.122.who, ...), custom_call_target="tpu_custom_call", output_to_operand_aliasing={{0}: (14, {}), {1}: (15, {}), {2}: (16, {}), {3}: (17, {}),... | custom-call | flops 28991029248 | bytes 46137344 | tf_op jit(solution)/shard_map/experts/pallas_call | solution.py:203
  349.6 20.4 %weight_grads.2 = (bf16[2,256,2048]{2,1,0:T(8,128)(2,1)}, bf16[2,256,2048]{2,1,0:T(8,128)(2,1)}, bf16[2,256,2048]{2,1,0:T(8,128)(2,1)}, bf16[2,256,2048]{2,1,0:T(8,128)(2,1)}) custom-call(s32[2,4]{1,0:T(2,128)} %pad_add_fusion.1.quarters, bf16[2,1152,1024]{2,1,0:T(8,128)(2,1)} %after.44.left, bf16[2,1152,2048]{2,1,0:T(8,128)(2,1)} %get-tuple-element.117.right), custom_call_target="tpu_custom_call" | custom-call | tf_op jit(solution)/shard_map/weight_grads/pallas_call | solution.py:499
  374.6 2.7 add_convert_fusion.1.refs_1_
  377.2 32.4 %weight_grads.3 = (bf16[2,512,2048]{2,1,0:T(8,128)(2,1)}, bf16[2,512,2048]{2,1,0:T(8,128)(2,1)}, bf16[2,512,2048]{2,1,0:T(8,128)(2,1)}, bf16[2,512,2048]{2,1,0:T(8,128)(2,1)}) custom-call(s32[2,4]{1,0:T(2,128)} %pad_add_fusion.1.quarters, bf16[2,1152,2048]{2,1,0:T(8,128)(2,1)} %after.46.left, bf16[2,1152,2048]{2,1,0:T(8,128)(2,1)} %get-tuple-element.123.right), custom_call_target="tpu_custom_call" | custom-call | flops 99999997952 | tf_op jit(solution)/shard_map/weight_grads/pallas_call | solution.py:499
  409.7 10.1 %collective-permute-done.33.refs_5_.refs_2_.refs_0_ = bf16[2,256,2048]{2,1,0:T(8,128)(2,1)} collective-permute-done((bf16[2,256,2048]{2,1,0:T(8,128)(2,1)}, bf16[2,256,2048]{2,1,0:T(8,128)(2,1)}, u32[]{:S(2)}, u32[]{:S(2)}) %collective-permute-start.33) | collective-permute-done | bytes 2097184 | tf_op jit(solution)/shard_map/ppermute | solution.py:765
  421.0 6.8 collective-permute-done.32.refs_0_
  433.0 12.7 %attention_back.1 = (f32[256,2048]{1,0:T(8,128)}, f32[1,2048]{1,0:T(1,128)}, bf16[2048,128]{1,0:T(8,128)(2,1)}, bf16[256,1024]{1,0:T(8,128)(2,1)}, bf16[256,1024...) custom-call(s32[3]{0:T(128)} %pad_add_fusion.2.who, ...), custom_call_target="tpu_custom_call" | custom-call | flops 99999997952 | tf_op jit(solution)/shard_map/attention_back/pallas_call | solution.py:320
  450.3 10.4 %collective-permute-done.36 = bf16[256,1024]{1,0:T(8,128)(2,1)S(1)} collective-permute-done((bf16[256,1024]{1,0:T(8,128)(2,1)}, bf16[256,1024]{1,0:T(8,128)(2,1)S(1)}, u32[]{:S(2)}, u32[]{:S(2)}) %collective-permute-start.36) | collective-permute-done | bytes 524320 | tf_op jit(solution)/shard_map/ppermute | solution.py:765
  460.7 11.5 %collective-permute-done.37 = bf16[256,1024]{1,0:T(8,128)(2,1)S(1)} collective-permute-done((bf16[256,1024]{1,0:T(8,128)(2,1)}, bf16[256,1024]{1,0:T(8,128)(2,1)S(1)}, u32[]{:S(2)}, u32[]{:S(2)}) %collective-permute-start.37) | collective-permute-done | bytes 524320 | tf_op jit(solution)/shard_map/ppermute | solution.py:765
  483.9 14.2 %attention_grad.1 = (bf16[1024,1536]{1,0:T(8,128)(2,1)S(1)}, f32[4,2,128]{2,1,0:T(2,128)S(1)}) custom-call(bf16[1024,1024]{1,0:T(8,128)(2,1)S(1)} %copy-done.7, f32[1024,1024]{1,0:T(8,128)S(1)} %copy-done.8, bf16[1024,1536]{1,0:T(8,128)(2,1)S(1)} %copy-done.9, f32[1024,128]{1,0:T(8,128)S(1)} %copy-done.26, s32[4,1,256]{2,1,0:T(1,128)S(1)} %copy-done.27, ...), custom_call_target="tpu_custom_call" | custom-call | tf_op jit(solution)/shard_map/attention_grad/pallas_call | solution.py:447
  498.7 8.7 %product.1 = bf16[2048,1536]{1,0:T(8,128)(2,1)S(1)} custom-call(bf16[1024,2048]{1,0:T(8,128)(2,1)S(1)} %copy-done.2, bf16[1024,1536]{1,0:T(8,128)(2,1)S(1)} %get-tuple-element.135.grad.right), custom_call_target="tpu_custom_call" | custom-call | tf_op jit(solution)/shard_map/product/pallas_call | solution.py:525
  507.4 2.6 copy-done.5
  511.7 12.5 %normed_grads.1 = (bf16[256,2048]{1,0:T(8,128)(2,1)S(1)}, bf16[256,2048]{1,0:T(8,128)(2,1)}, bf16[256,2048]{1,0:T(8,128)(2,1)}, bf16[256,2048]{1,0:T(8,128)(2,1)}) custom-call(bf16[1024,1536]{1,0:T(8,128)(2,1)} %copy-done.10, bf16[2048,1536]{1,0:T(8,128)(2,1)} %all-gather.6.cloned.1.call-done.weight), custom_call_target="tpu_custom_call" | custom-call | tf_op jit(solution)/shard_map/normed_grads/pallas_call | solution.py:553
  530.3 2.9 halve.6
  542.3 25.2 %collective-permute-done.40.refs_1_.got = bf16[2,512,2048]{2,1,0:T(8,128)(2,1)} collective-permute-done((bf16[2,512,2048]{2,1,0:T(8,128)(2,1)}, bf16[2,512,2048]{2,1,0:T(8,128)(2,1)}, u32[]{:S(2)}, u32[]{:S(2)}) %collective-permute-start.40) | collective-permute-done | bytes 4194336 | tf_op jit(solution)/shard_map/ppermute | solution.py:765
  569.8 5.8 halve.5
  580.3 5.8 halve.4
  588.2 4.7 fusion.9
  594.7 21.2 %collective-permute-done.43.refs_3_ = bf16[256,2048]{1,0:T(8,128)(2,1)} collective-permute-done((bf16[256,2048]{1,0:T(8,128)(2,1)}, bf16[256,2048]{1,0:T(8,128)(2,1)}, u32[]{:S(2)}, u32[]{:S(2)}) %collective-permute-start.43) | collective-permute-done | bytes 1048608 | tf_op jit(solution)/shard_map/ppermute | solution.py:765
  616.0 6.4 input_grad.1
  635.1 22.4 %collective-permute-done.49.refs_2_.refs_0_ = bf16[1,512,2048]{2,1,0:T(8,128)(2,1)} collective-permute-done((bf16[1,512,2048]{2,1,0:T(8,128)(2,1)}, bf16[1,512,2048]{2,1,0:T(8,128)(2,1)}, u32[]{:S(2)}, u32[]{:S(2)}) %collective-permute-start.49) | collective-permute-done | bytes 2097184 | tf_op jit(solution)/shard_map/ppermute | solution.py:765
  673.6 3.4 multiply_convert_fusion
  677.0 31.7 %collective-permute-done.54.refs_2_ = bf16[256,2176]{1,0:T(8,128)(2,1)S(1)} collective-permute-done((bf16[256,2176]{1,0:T(8,128)(2,1)}, bf16[256,2176]{1,0:T(8,128)(2,1)S(1)}, u32[]{:S(2)}, u32[]{:S(2)}) %collective-permute-start.54) | collective-permute-done | bytes 1114144 | tf_op jit(solution)/shard_map/ppermute | solution.py:765
  713.5 7.6 %join.2.refs_1_ = f32[2,512,2048]{2,1,0:T(8,128)} custom-call(bf16[512,2048]{1,0:T(8,128)(2,1)} %bitcast.71, bf16[512,2048]{1,0:T(8,128)(2,1)} %bitcast.38.refs_1_, bf16[512,2048]{1,0:T(8,128)(2,1)} %bitcast.70, bf16[512,2048]{1,0:T(8,128)(2,1)} %bitcast.40.refs_3_), custom_call_target="tpu_custom_call" | custom-call | flops 99999997952 | tf_op jit(solution)/shard_map/join/pallas_call | solution.py:623
  722.0 4.4 join.3
  728.3 4.3 gather_columns.1
  (413 shorter events, 163.9 us)
Async XLA Ops:
  7.2 67.0 %all-gather.4.cloned.1.call-start = ((), (), s32[]{:S(2)}) async-start(), calls=%async_computation.3 | async-start | bytes 2949120 | tf_op jit(solution)/shard_map/all_gather | solution.py:808
  9.9 112.3 %all-gather.6.cloned.1.call-start = ((), (), s32[]{:S(2)}) async-start(), calls=%async_computation.4 | async-start | bytes 7077888 | tf_op jit(solution)/shard_map/all_gather | solution.py:808
  13.1 213.7 %all-gather.8.cloned.1.call-start = ((), (), s32[]{:S(2)}) async-start(), calls=%async_computation.5 | async-start | bytes 9437184 | tf_op jit(solution)/shard_map/all_gather | solution.py:808
  16.7 561.3 %reduce-scatter.4.cloned.1.call-start = ((), (), s32[]{:S(2)}) async-start(), calls=%async_computation.6 | async-start | bytes 9437184 | tf_op jit(solution)/shard_map/reduce_scatter | solution.py:811
  21.3 26.3 %collective-permute-start.3 = (bf16[256,2048]{1,0:T(8,128)(2,1)}, bf16[256,2048]{1,0:T(8,128)(2,1)S(1)}, u32[]{:S(2)}, u32[]{:S(2)}) collective-permute-start(bf16[256,2048]{1,0:T(8,128)(2,1)} %after.33), channel_id=1, source_target_pairs={{0,8},{8,0},{16,24},{24,16},{1,9},{9,1},{17,25},{25,17},{2,10},{10... | collective-permute-start | bytes 3145736 | tf_op jit(solution)/shard_map/ppermute | solution.py:765
  21.8 45.6 %collective-permute-start.4 = (bf16[256,2048]{1,0:T(8,128)(2,1)}, bf16[256,2048]{1,0:T(8,128)(2,1)S(1)}, u32[]{:S(2)}, u32[]{:S(2)}) collective-permute-start(bf16[256,2048]{1,0:T(8,128)(2,1)} %after.33), channel_id=1, source_target_pairs={{0,16},{8,24},{16,0},{24,8},{1,17},{9,25},{17,1},{25,9},{2,18},{10... | collective-permute-start | bytes 3145736 | tf_op jit(solution)/shard_map/ppermute | solution.py:765
  22.8 44.9 %collective-permute-start.5 = (bf16[256,2048]{1,0:T(8,128)(2,1)}, bf16[256,2048]{1,0:T(8,128)(2,1)}, u32[]{:S(2)}, u32[]{:S(2)}) collective-permute-start(bf16[256,2048]{1,0:T(8,128)(2,1)} %after.33), channel_id=1, source_target_pairs={{0,24},{8,16},{16,8},{24,0},{1,25},{9,17},{17,9},{25,1},{2,26},{10... | collective-permute-start | bytes 3145736 | tf_op jit(solution)/shard_map/ppermute | solution.py:765
  76.5 26.3 %collective-permute-start.6 = (bf16[1024,512]{1,0:T(8,128)(2,1)}, bf16[1024,512]{1,0:T(8,128)(2,1)S(1)}, u32[]{:S(2)}, u32[]{:S(2)}) collective-permute-start(bf16[1024,512]{1,0:T(8,128)(2,1)} %after.34.refs_0_), channel_id=1, source_target_pairs={{0,8},{8,0},{16,24},{24,16},{1,9},{9,1},{17,25},{25,17},{2,10},{10... | collective-permute-start | bytes 3145736 | tf_op jit(solution)/shard_map/ppermute | solution.py:765
  77.9 44.3 %collective-permute-start.7 = (bf16[1024,512]{1,0:T(8,128)(2,1)}, bf16[1024,512]{1,0:T(8,128)(2,1)}, u32[]{:S(2)}, u32[]{:S(2)}) collective-permute-start(bf16[1024,512]{1,0:T(8,128)(2,1)} %after.34.refs_0_), channel_id=1, source_target_pairs={{0,16},{8,24},{16,0},{24,8},{1,17},{9,25},{17,1},{25,9},{2,18},{10... | collective-permute-start | bytes 3145736 | tf_op jit(solution)/shard_map/ppermute | solution.py:765
  78.4 43.9 %collective-permute-start.8 = (bf16[1024,512]{1,0:T(8,128)(2,1)}, bf16[1024,512]{1,0:T(8,128)(2,1)}, u32[]{:S(2)}, u32[]{:S(2)}) collective-permute-start(bf16[1024,512]{1,0:T(8,128)(2,1)} %after.34.refs_0_), channel_id=1, source_target_pairs={{0,24},{8,16},{16,8},{24,0},{1,25},{9,17},{17,9},{25,1},{2,26},{10... | collective-permute-start | bytes 3145736 | tf_op jit(solution)/shard_map/ppermute | solution.py:765
  141.8 15.4 %collective-permute-start.12 = (bf16[4,1024,512]{2,1,0:T(8,128)(2,1)}, bf16[4,1024,512]{2,1,0:T(8,128)(2,1)}, u32[]{:S(2)}, u32[]{:S(2)}) collective-permute-start(bf16[4,1024,512]{2,1,0:T(8,128)(2,1)} %pad_maximum_fusion.1.refs_4_.refs_10_), channel_id=1, source_target_pairs={{0,1},{1,0},{2,3},{3,2},{4,5},{5,4},{6,7},{7,6},{8,9},{9,8},{10,11... | collective-permute-start | bytes 12582920 | tf_op jit(solution)/shard_map/ppermute | solution.py:783
  143.2 14.0 %collective-permute-start.10 = (bf16[256,512]{1,0:T(8,128)(2,1)S(1)}, bf16[256,512]{1,0:T(8,128)(2,1)S(1)}, u32[]{:S(2)}, u32[]{:S(2)}) collective-permute-start(bf16[256,512]{1,0:T(8,128)(2,1)S(1)} %get-tuple-element.227), channel_id=1, source_target_pairs={{0,16},{8,24},{16,0},{24,8},{1,17},{9,25},{17,1},{25,9},{2,18},{10... | collective-permute-start | bytes 786440 | tf_op jit(solution)/shard_map/ppermute | solution.py:765
  144.7 12.6 %collective-permute-start.11 = (bf16[256,512]{1,0:T(8,128)(2,1)S(1)}, bf16[256,512]{1,0:T(8,128)(2,1)S(1)}, u32[]{:S(2)}, u32[]{:S(2)}) collective-permute-start(bf16[256,512]{1,0:T(8,128)(2,1)S(1)} %get-tuple-element.226), channel_id=1, source_target_pairs={{0,24},{8,16},{16,8},{24,0},{1,25},{9,17},{17,9},{25,1},{2,26},{10... | collective-permute-start | bytes 786440 | tf_op jit(solution)/shard_map/ppermute | solution.py:765
  146.1 26.9 %collective-permute-start.15 = (bf16[256,2048]{1,0:T(8,128)(2,1)S(1)}, bf16[256,2048]{1,0:T(8,128)(2,1)}, u32[]{:S(2)}, u32[]{:S(2)}) collective-permute-start(bf16[256,2048]{1,0:T(8,128)(2,1)S(1)} %copy-done.55), channel_id=1, source_target_pairs={{0,1},{1,0},{2,3},{3,2},{4,5},{5,4},{6,7},{7,6},{8,9},{9,8},{10,11... | collective-permute-start | bytes 3145736 | tf_op jit(solution)/shard_map/ppermute | solution.py:783
  167.1 44.5 %collective-permute-start.13 = (bf16[256,2048]{1,0:T(8,128)(2,1)}, bf16[256,2048]{1,0:T(8,128)(2,1)S(1)}, u32[]{:S(2)}, u32[]{:S(2)}) collective-permute-start(bf16[256,2048]{1,0:T(8,128)(2,1)} %get-tuple-element.91.refs_0_.refs_5_), channel_id=1, source_target_pairs={{0,2},{1,3},{2,4},{3,5},{4,6},{5,7},{8,10},{9,11},{10,12},{11,13},... | collective-permute-start | bytes 3145736 | tf_op jit(solution)/shard_map/ppermute | solution.py:789
  170.7 42.8 %collective-permute-start.17 = (bf16[256,2048]{1,0:T(8,128)(2,1)}, bf16[256,2048]{1,0:T(8,128)(2,1)S(1)}, u32[]{:S(2)}, u32[]{:S(2)}) collective-permute-start(bf16[256,2048]{1,0:T(8,128)(2,1)} %get-tuple-element.91.refs_0_.refs_5_), channel_id=1, source_target_pairs={{2,0},{3,1},{4,2},{5,3},{6,4},{7,5},{10,8},{11,9},{12,10},{13,11},... | collective-permute-start | bytes 3145736 | tf_op jit(solution)/shard_map/ppermute | solution.py:789
  215.5 11.2 %collective-permute-start.18 = (bf16[256,2048]{1,0:T(8,128)(2,1)}, bf16[256,2048]{1,0:T(8,128)(2,1)}, u32[]{:S(2)}, u32[]{:S(2)}) collective-permute-start(bf16[256,2048]{1,0:T(8,128)(2,1)} %broadcast_select_fusion.1.refs_0_), channel_id=1, source_target_pairs={{0,1},{1,0},{2,3},{3,2},{4,5},{5,4},{6,7},{7,6},{8,9},{9,8},{10,11... | collective-permute-start | bytes 3145736 | tf_op jit(solution)/shard_map/ppermute | solution.py:783
  216.3 53.9 %collective-permute-start.22 = (bf16[256,2048]{1,0:T(8,128)(2,1)}, bf16[256,2048]{1,0:T(8,128)(2,1)}, u32[]{:S(2)}, u32[]{:S(2)}) collective-permute-start(bf16[256,2048]{1,0:T(8,128)(2,1)} %get-tuple-element.104), channel_id=1, source_target_pairs={{0,8},{8,0},{16,24},{24,16},{1,9},{9,1},{17,25},{25,17},{2,10},{10... | collective-permute-start | bytes 3145736 | tf_op jit(solution)/shard_map/ppermute | solution.py:765
  217.8 52.9 %collective-permute-start.23 = (bf16[256,2048]{1,0:T(8,128)(2,1)}, bf16[256,2048]{1,0:T(8,128)(2,1)}, u32[]{:S(2)}, u32[]{:S(2)}) collective-permute-start(bf16[256,2048]{1,0:T(8,128)(2,1)} %get-tuple-element.104), channel_id=1, source_target_pairs={{0,16},{8,24},{16,0},{24,8},{1,17},{9,25},{17,1},{25,9},{2,18},{10... | collective-permute-start | bytes 3145736 | tf_op jit(solution)/shard_map/ppermute | solution.py:765
  219.2 40.4 %collective-permute-start.16 = (bf16[256,2048]{1,0:T(8,128)(2,1)S(1)}, bf16[256,2048]{1,0:T(8,128)(2,1)}, u32[]{:S(2)}, u32[]{:S(2)}) collective-permute-start(bf16[256,2048]{1,0:T(8,128)(2,1)S(1)} %copy-done.43), channel_id=1, source_target_pairs={{2,4},{3,5},{4,6},{5,7},{10,12},{11,13},{12,14},{13,15},{18,20},{1... | collective-permute-start | bytes 3145736 | tf_op jit(solution)/shard_map/ppermute | solution.py:789
  224.8 34.8 %collective-permute-start.20 = (bf16[256,2048]{1,0:T(8,128)(2,1)S(1)}, bf16[256,2048]{1,0:T(8,128)(2,1)S(1)}, u32[]{:S(2)}, u32[]{:S(2)}) collective-permute-start(bf16[256,2048]{1,0:T(8,128)(2,1)S(1)} %copy-done.41), channel_id=1, source_target_pairs={{2,0},{3,1},{4,2},{5,3},{10,8},{11,9},{12,10},{13,11},{18,16},{19,... | collective-permute-start | bytes 3145736 | tf_op jit(solution)/shard_map/ppermute | solution.py:789
  266.3 38.5 %collective-permute-start.19 = (bf16[256,2048]{1,0:T(8,128)(2,1)}, bf16[256,2048]{1,0:T(8,128)(2,1)}, u32[]{:S(2)}, u32[]{:S(2)}) collective-permute-start(bf16[256,2048]{1,0:T(8,128)(2,1)} %after.40), channel_id=1, source_target_pairs={{4,6},{5,7},{12,14},{13,15},{20,22},{21,23},{28,30},{29,31}} | collective-permute-start | bytes 3145736 | tf_op jit(solution)/shard_map/ppermute | solution.py:789
  267.9 36.9 %collective-permute-start.24 = (bf16[256,2048]{1,0:T(8,128)(2,1)S(1)}, bf16[256,2048]{1,0:T(8,128)(2,1)}, u32[]{:S(2)}, u32[]{:S(2)}) collective-permute-start(bf16[256,2048]{1,0:T(8,128)(2,1)S(1)} %copy-done.50), channel_id=1, source_target_pairs={{2,0},{3,1},{10,8},{11,9},{18,16},{19,17},{26,24},{27,25}} | collective-permute-start | bytes 3145736 | tf_op jit(solution)/shard_map/ppermute | solution.py:789
  270.2 35.1 %collective-permute-start.26 = (bf16[272,2048]{1,0:T(8,128)(2,1)}, bf16[272,2048]{1,0:T(8,128)(2,1)}, u32[]{:S(2)}, u32[]{:S(2)}) collective-permute-start(bf16[272,2048]{1,0:T(8,128)(2,1)} %get-tuple-element.111), channel_id=1, source_target_pairs={{0,1},{1,0},{2,3},{3,2},{4,5},{5,4},{6,7},{7,6},{8,9},{9,8},{10,11... | collective-permute-start | bytes 3342344 | tf_op jit(solution)/shard_map/ppermute | solution.py:783
  304.4 45.2 %collective-permute-start.28 = (bf16[256,2048]{1,0:T(8,128)(2,1)}, bf16[256,2048]{1,0:T(8,128)(2,1)}, u32[]{:S(2)}, u32[]{:S(2)}) collective-permute-start(bf16[256,2048]{1,0:T(8,128)(2,1)} %get-tuple-element.104), channel_id=1, source_target_pairs={{0,24},{8,16},{16,8},{24,0},{1,25},{9,17},{17,9},{25,1},{2,26},{10... | collective-permute-start | bytes 3145736 | tf_op jit(solution)/shard_map/ppermute | solution.py:765
  309.0 61.0 %collective-permute-start.29 = (bf16[272,2048]{1,0:T(8,128)(2,1)}, bf16[272,2048]{1,0:T(8,128)(2,1)S(1)}, u32[]{:S(2)}, u32[]{:S(2)}) collective-permute-start(bf16[272,2048]{1,0:T(8,128)(2,1)} %add_convert_fusion.3.refs_18_), channel_id=1, source_target_pairs={{0,2},{1,3},{2,0},{3,1},{4,6},{5,7},{6,4},{7,5},{8,10},{9,11},{10,... | collective-permute-start | bytes 3342344 | tf_op jit(solution)/shard_map/ppermute | solution.py:783
  311.7 58.3 %collective-permute-start.30 = (bf16[272,2048]{1,0:T(8,128)(2,1)}, bf16[272,2048]{1,0:T(8,128)(2,1)S(1)}, u32[]{:S(2)}, u32[]{:S(2)}) collective-permute-start(bf16[272,2048]{1,0:T(8,128)(2,1)} %add_convert_fusion.2.refs_19_), channel_id=1, source_target_pairs={{0,4},{1,5},{2,6},{3,7},{4,0},{5,1},{6,2},{7,3},{8,12},{9,13},{10,... | collective-permute-start | bytes 3342344 | tf_op jit(solution)/shard_map/ppermute | solution.py:783
  371.4 48.4 %collective-permute-start.33 = (bf16[2,256,2048]{2,1,0:T(8,128)(2,1)}, bf16[2,256,2048]{2,1,0:T(8,128)(2,1)}, u32[]{:S(2)}, u32[]{:S(2)}) collective-permute-start(bf16[2,256,2048]{2,1,0:T(8,128)(2,1)} %get-tuple-element.118.refs_1_), channel_id=1, source_target_pairs={{0,8},{8,0},{16,24},{24,16},{1,9},{9,1},{17,25},{25,17},{2,10},{10... | collective-permute-start | bytes 6291464 | tf_op jit(solution)/shard_map/ppermute | solution.py:765
  373.1 48.0 %collective-permute-start.34 = (bf16[2,256,2048]{2,1,0:T(8,128)(2,1)}, bf16[2,256,2048]{2,1,0:T(8,128)(2,1)S(1)}, u32[]{:S(2)}, u32[]{:S(2)}) collective-permute-start(bf16[2,256,2048]{2,1,0:T(8,128)(2,1)} %get-tuple-element.120.refs_3_), channel_id=1, source_target_pairs={{0,16},{8,24},{16,0},{24,8},{1,17},{9,25},{17,1},{25,9},{2,18},{10... | collective-permute-start | bytes 6291464 | tf_op jit(solution)/shard_map/ppermute | solution.py:765
  377.2 50.6 %collective-permute-start.32 = (bf16[272,2048]{1,0:T(8,128)(2,1)}, bf16[272,2048]{1,0:T(8,128)(2,1)}, u32[]{:S(2)}, u32[]{:S(2)}) collective-permute-start(bf16[272,2048]{1,0:T(8,128)(2,1)} %add_convert_fusion.1.refs_1_), channel_id=1, source_target_pairs={{0,6},{1,7},{2,4},{3,5},{4,2},{5,3},{6,0},{7,1},{8,14},{9,15},{10,... | collective-permute-start | bytes 3342344 | tf_op jit(solution)/shard_map/ppermute | solution.py:783
  427.9 241.2 %reduce-scatter.6.cloned.1.call-start = ((), (), s32[]{:S(2)}) async-start(), calls=%async_computation.7 | async-start | bytes 7077888 | tf_op jit(solution)/shard_map/reduce_scatter | solution.py:811
  445.7 15.0 %collective-permute-start.36 = (bf16[256,1024]{1,0:T(8,128)(2,1)}, bf16[256,1024]{1,0:T(8,128)(2,1)S(1)}, u32[]{:S(2)}, u32[]{:S(2)}) collective-permute-start(bf16[256,1024]{1,0:T(8,128)(2,1)} %get-tuple-element.130), channel_id=1, source_target_pairs={{0,8},{8,0},{16,24},{24,16},{1,9},{9,1},{17,25},{25,17},{2,10},{10... | collective-permute-start | bytes 1572872 | tf_op jit(solution)/shard_map/ppermute | solution.py:765
  447.2 25.0 %collective-permute-start.37 = (bf16[256,1024]{1,0:T(8,128)(2,1)}, bf16[256,1024]{1,0:T(8,128)(2,1)S(1)}, u32[]{:S(2)}, u32[]{:S(2)}) collective-permute-start(bf16[256,1024]{1,0:T(8,128)(2,1)} %get-tuple-element.131), channel_id=1, source_target_pairs={{0,16},{8,24},{16,0},{24,8},{1,17},{9,25},{17,1},{25,9},{2,18},{10... | collective-permute-start | bytes 1572872 | tf_op jit(solution)/shard_map/ppermute | solution.py:765
  448.7 23.6 %collective-permute-start.38 = (bf16[256,1024]{1,0:T(8,128)(2,1)}, bf16[256,1024]{1,0:T(8,128)(2,1)S(1)}, u32[]{:S(2)}, u32[]{:S(2)}) collective-permute-start(bf16[256,1024]{1,0:T(8,128)(2,1)} %get-tuple-element.132), channel_id=1, source_target_pairs={{0,24},{8,16},{16,8},{24,0},{1,25},{9,17},{17,9},{25,1},{2,26},{10... | collective-permute-start | bytes 1572872 | tf_op jit(solution)/shard_map/ppermute | solution.py:765
  473.7 93.8 %collective-permute-start.40 = (bf16[2,512,2048]{2,1,0:T(8,128)(2,1)}, bf16[2,512,2048]{2,1,0:T(8,128)(2,1)}, u32[]{:S(2)}, u32[]{:S(2)}) collective-permute-start(bf16[2,512,2048]{2,1,0:T(8,128)(2,1)} %after.50.refs_2_), channel_id=1, source_target_pairs={{0,16},{8,24},{16,0},{24,8},{1,17},{9,25},{17,1},{25,9},{2,18},{10... | collective-permute-start | bytes 12582920 | tf_op jit(solution)/shard_map/ppermute | solution.py:765
  477.1 100.9 %collective-permute-start.39 = (bf16[2,512,2048]{2,1,0:T(8,128)(2,1)}, bf16[2,512,2048]{2,1,0:T(8,128)(2,1)}, u32[]{:S(2)}, u32[]{:S(2)}) collective-permute-start(bf16[2,512,2048]{2,1,0:T(8,128)(2,1)} %after.49.refs_1_), channel_id=1, source_target_pairs={{0,8},{8,0},{16,24},{24,16},{1,9},{9,1},{17,25},{25,17},{2,10},{10... | collective-permute-start | bytes 12582920 | tf_op jit(solution)/shard_map/ppermute | solution.py:765
  525.2 69.5 %collective-permute-start.41 = (bf16[256,2048]{1,0:T(8,128)(2,1)}, bf16[256,2048]{1,0:T(8,128)(2,1)}, u32[]{:S(2)}, u32[]{:S(2)}) collective-permute-start(bf16[256,2048]{1,0:T(8,128)(2,1)} %get-tuple-element.142), channel_id=1, source_target_pairs={{0,8},{8,0},{16,24},{24,16},{1,9},{9,1},{17,25},{25,17},{2,10},{10... | collective-permute-start | bytes 3145736 | tf_op jit(solution)/shard_map/ppermute | solution.py:765
  526.6 68.1 %collective-permute-start.42 = (bf16[256,2048]{1,0:T(8,128)(2,1)}, bf16[256,2048]{1,0:T(8,128)(2,1)}, u32[]{:S(2)}, u32[]{:S(2)}) collective-permute-start(bf16[256,2048]{1,0:T(8,128)(2,1)} %get-tuple-element.143), channel_id=1, source_target_pairs={{0,16},{8,24},{16,0},{24,8},{1,17},{9,25},{17,1},{25,9},{2,18},{10... | collective-permute-start | bytes 3145736 | tf_op jit(solution)/shard_map/ppermute | solution.py:765
  527.1 88.9 %collective-permute-start.43 = (bf16[256,2048]{1,0:T(8,128)(2,1)}, bf16[256,2048]{1,0:T(8,128)(2,1)}, u32[]{:S(2)}, u32[]{:S(2)}) collective-permute-start(bf16[256,2048]{1,0:T(8,128)(2,1)} %get-tuple-element.144), channel_id=1, source_target_pairs={{0,24},{8,16},{16,8},{24,0},{1,25},{9,17},{17,9},{25,1},{2,26},{10... | collective-permute-start | bytes 3145736 | tf_op jit(solution)/shard_map/ppermute | solution.py:765
  542.1 127.0 %reduce-scatter.8.cloned.1.call-start = ((), (), s32[]{:S(2)}) async-start(), calls=%async_computation.8 | async-start | bytes 2949120 | tf_op jit(solution)/shard_map/reduce_scatter | solution.py:811
  576.9 80.6 %collective-permute-start.49 = (bf16[1,512,2048]{2,1,0:T(8,128)(2,1)}, bf16[1,512,2048]{2,1,0:T(8,128)(2,1)}, u32[]{:S(2)}, u32[]{:S(2)}) collective-permute-start(bf16[1,512,2048]{2,1,0:T(8,128)(2,1)} %get-tuple-element.138.refs_2_), channel_id=1, source_target_pairs={{0,8},{8,0},{16,24},{24,16},{1,9},{9,1},{17,25},{25,17},{2,10},{10... | collective-permute-start | bytes 6291464 | tf_op jit(solution)/shard_map/ppermute | solution.py:765
  587.4 70.0 %collective-permute-start.48 = (bf16[1,512,2048]{2,1,0:T(8,128)(2,1)}, bf16[1,512,2048]{2,1,0:T(8,128)(2,1)}, u32[]{:S(2)}, u32[]{:S(2)}) collective-permute-start(bf16[1,512,2048]{2,1,0:T(8,128)(2,1)} %get-tuple-element.137.refs_1_), channel_id=1, source_target_pairs={{0,16},{8,24},{16,0},{24,8},{1,17},{9,25},{17,1},{25,9},{2,18},{10... | collective-permute-start | bytes 6291464 | tf_op jit(solution)/shard_map/ppermute | solution.py:765
  662.2 58.8 %collective-permute-start.57 = (bf16[1,256,2048]{2,1,0:T(8,128)(2,1)}, bf16[1,256,2048]{2,1,0:T(8,128)(2,1)S(1)}, u32[]{:S(2)}, u32[]{:S(2)}) collective-permute-start(bf16[1,256,2048]{2,1,0:T(8,128)(2,1)} %after.62), channel_id=1, source_target_pairs={{0,16},{8,24},{16,0},{24,8},{1,17},{9,25},{17,1},{25,9},{2,18},{10... | collective-permute-start | bytes 3145736 | tf_op jit(solution)/shard_map/ppermute | solution.py:765
  663.8 58.2 %collective-permute-start.58 = (bf16[1,256,2048]{2,1,0:T(8,128)(2,1)}, bf16[1,256,2048]{2,1,0:T(8,128)(2,1)}, u32[]{:S(2)}, u32[]{:S(2)}) collective-permute-start(bf16[1,256,2048]{2,1,0:T(8,128)(2,1)} %after.64), channel_id=1, source_target_pairs={{0,8},{8,0},{16,24},{24,16},{1,9},{9,1},{17,25},{25,17},{2,10},{10... | collective-permute-start | bytes 3145736 | tf_op jit(solution)/shard_map/ppermute | solution.py:765
  671.4 39.4 %collective-permute-start.53 = (bf16[256,2176]{1,0:T(8,128)(2,1)}, bf16[256,2176]{1,0:T(8,128)(2,1)S(1)}, u32[]{:S(2)}, u32[]{:S(2)}) collective-permute-start(bf16[256,2176]{1,0:T(8,128)(2,1)} %after.58.refs_0_), channel_id=1, source_target_pairs={{0,8},{8,0},{16,24},{24,16},{1,9},{9,1},{17,25},{25,17},{2,10},{10... | collective-permute-start | bytes 3342344 | tf_op jit(solution)/shard_map/ppermute | solution.py:765
  672.0 36.7 %collective-permute-start.54 = (bf16[256,2176]{1,0:T(8,128)(2,1)}, bf16[256,2176]{1,0:T(8,128)(2,1)S(1)}, u32[]{:S(2)}, u32[]{:S(2)}) collective-permute-start(bf16[256,2176]{1,0:T(8,128)(2,1)} %after.58.refs_0_), channel_id=1, source_target_pairs={{0,16},{8,24},{16,0},{24,8},{1,17},{9,25},{17,1},{25,9},{2,18},{10... | collective-permute-start | bytes 3342344 | tf_op jit(solution)/shard_map/ppermute | solution.py:765
  709.5 16.9 %collective-permute-start.56 = (bf16[128,2176]{1,0:T(8,128)(2,1)}, bf16[128,2176]{1,0:T(8,128)(2,1)}, u32[]{:S(2)}, u32[]{:S(2)}) collective-permute-start(bf16[128,2176]{1,0:T(8,128)(2,1)} %slice.90), channel_id=1, source_target_pairs={{0,8},{8,0},{16,24},{24,16},{1,9},{9,1},{17,25},{25,17},{2,10},{10... | collective-permute-start | bytes 1671176 | tf_op jit(solution)/shard_map/ppermute | solution.py:765
  711.8 14.7 %collective-permute-start.55 = (bf16[128,2176]{1,0:T(8,128)(2,1)}, bf16[128,2176]{1,0:T(8,128)(2,1)}, u32[]{:S(2)}, u32[]{:S(2)}) collective-permute-start(bf16[128,2176]{1,0:T(8,128)(2,1)} %slice.89), channel_id=1, source_target_pairs={{0,16},{8,24},{16,0},{24,8},{1,17},{9,25},{17,1},{25,9},{2,18},{10... | collective-permute-start | bytes 1671176 | tf_op jit(solution)/shard_map/ppermute | solution.py:765
  (99 other events, 483.5 us)
Sparse Core Ops, SparseCore 0:
  10.2 34.3 all-gather.3
  46.9 62.1 all-gather.5
  110.7 96.9 all-gather.7
  428.0 85.9 reduce-scatter.3
  541.2 65.0 reduce-scatter.5
  609.1 35.2 reduce-scatter.7

commit v8 on v7

--- a/solution.py
+++ b/solution.py
@@ -258,7 +258,7 @@
             jax.ShapeDtypeStruct((length, width), BF),
             jax.ShapeDtypeStruct((length, width), BF),
         ],
-        compiler_params=pltpu.CompilerParams(vmem_limit_bytes=60 * 2**20),
+        compiler_params=pltpu.CompilerParams(vmem_limit_bytes=48 * 2**20),
         name="attention_out",
     )(who, *pieces, near, far, tokens, gain)
 
@@ -328,7 +328,7 @@
             jax.ShapeDtypeStruct((width, router.shape[1]), BF),
             *[piece] * replicas,
         ],
-        compiler_params=pltpu.CompilerParams(vmem_limit_bytes=60 * 2**20),
+        compiler_params=pltpu.CompilerParams(vmem_limit_bytes=48 * 2**20),
         cost_estimate=pl.CostEstimate(flops=10**11, bytes_accessed=0, transcendentals=0),
         name="attention_back",
     )(who, *shares, hidden, normed, cot, gain, gates, router, near, far)
@@ -692,11 +692,16 @@
     lanes = 128 if wide % (arrays * 256) else 0
     part = (wide - lanes) // arrays
     count = len(blocks)
-    vmem = pl.BlockSpec(memory_space=pltpu.VMEM)
+    step = rows // 4
+
+    def spec(n):
+        return pl.BlockSpec((step, n), lambda i: (i, 0))
+
     return pl.pallas_call(
         functools.partial(gather_kernel, count, arrays),
-        in_specs=[pl.BlockSpec(memory_space=pltpu.SMEM)] + [vmem] * count,
-        out_specs=[vmem] * (arrays + (lanes > 0)),
+        grid=(rows // step,),
+        in_specs=[pl.BlockSpec(memory_space=pltpu.SMEM)] + [spec(wide)] * count,
+        out_specs=[spec(part * count)] * arrays + [spec(lanes)] * (lanes > 0),
         out_shape=[jax.ShapeDtypeStruct((rows, part * count), F32)] * arrays
         + [jax.ShapeDtypeStruct((rows, lanes), F32)] * (lanes > 0),
         compiler_params=pltpu.CompilerParams(vmem_limit_bytes=48 * 2**20),

time: 746 us -> 744 us (level)
    unnamed x170 -> x190, local copies, waits for them, and re-layouts: 47.6 us -> 51.6 us
  transfers between devices with their start and end apart: 65 -> 65, of which waited for: 24 -> 25; matrix products, arithmetic and copies ran while one was open for 10% -> 11% of each run, Pallas kernels for 40% -> 39%
where the time goes in v8:
time: 744 us; the launch traced here: 739 us
  Pallas kernels  295 us (40%)
  waiting for transfers between devices  228 us (31%)
  local copies, waits for them, and re-layouts  71.9 us (10%)
  starting transfers between devices  68.2 us (9%)
  other arithmetic  54 us (7%)
  between operations  15.6 us (2%)
    ppermute x36, waiting for transfers between devices, swap(): return lax.ppermute(value, 'replica', [(r, r ^ k) for r in range(replicas)])  213 us
    pallas_call x4, Pallas kernels, expert_block(): pl.pallas_call(functools.partial(expert_kernel, min(512, ff), min(1024, w...  131 us
    pallas_call x2, Pallas kernels, weight_grads(): pl.pallas_call(functools.partial(weight_grad_kernel, half), grid_spec=plt...  52.8 us
    unnamed x190, local copies, waits for them, and re-layouts  51.6 us
    ppermute x36, starting transfers between devices, swap(): return lax.ppermute(value, 'replica', [(r, r ^ k) for r in range(replicas)])  42 us
    ppermute x6, starting transfers between devices, pass_on(): return (lax.ppermute(up, 'fsdp', pairs), lax.ppermute(down, 'fsdp', back))  16.4 us
    pallas_call x4, Pallas kernels, halve(): pl.pallas_call(functools.partial(halve_kernel, half), grid_spec=pltpu.Pre...  16.2 us
  transfers between devices with their start and end apart: 65, of which 25 were waited for; matrix products, arithmetic and copies ran while one was open for 11% of the time, Pallas kernels for 39%

profile of v8, /device:TPU:8, one launch (start us, length us, event | category | flops | bytes accessed | tf_op | source)
XLA Modules:
  0.0 738.6 jit_solution(14520104067763918373)
XLA Ops:
  22.8 2.5 collective-permute-start.5
  29.5 18.1 %collective-permute-done.3.refs_1_ = bf16[256,2048]{1,0:T(8,128)(2,1)S(1)} collective-permute-done((bf16[256,2048]{1,0:T(8,128)(2,1)}, bf16[256,2048]{1,0:T(8,128)(2,1)S(1)}, u32[]{:S(2)}, u32[]{:S(2)}) %collective-permute-start.3) | collective-permute-done | bytes 1048608 | tf_op jit(solution)/shard_map/ppermute | solution.py:770
  47.9 19.6 %collective-permute-done.4.refs_2_ = bf16[256,2048]{1,0:T(8,128)(2,1)} collective-permute-done((bf16[256,2048]{1,0:T(8,128)(2,1)}, bf16[256,2048]{1,0:T(8,128)(2,1)}, u32[]{:S(2)}, u32[]{:S(2)}) %collective-permute-start.4) | collective-permute-done | bytes 1048608 | tf_op jit(solution)/shard_map/ppermute | solution.py:770
  70.6 2.6 fusion.15
  73.2 2.5 pad_maximum_fusion.refs_6_.refs_0_
  94.7 9.5 %collective-permute-done.6.refs_0_ = bf16[1024,512]{1,0:T(8,128)(2,1)S(1)} collective-permute-done((bf16[1024,512]{1,0:T(8,128)(2,1)}, bf16[1024,512]{1,0:T(8,128)(2,1)S(1)}, u32[]{:S(2)}, u32[]{:S(2)}) %collective-permute-start.6) | collective-permute-done | bytes 1048608 | tf_op jit(solution)/shard_map/ppermute | solution.py:770
  105.2 17.3 %collective-permute-done.7.refs_2_ = bf16[1024,512]{1,0:T(8,128)(2,1)} collective-permute-done((bf16[1024,512]{1,0:T(8,128)(2,1)}, bf16[1024,512]{1,0:T(8,128)(2,1)}, u32[]{:S(2)}, u32[]{:S(2)}) %collective-permute-start.7) | collective-permute-done | bytes 1048608 | tf_op jit(solution)/shard_map/ppermute | solution.py:770
  122.5 14.6 %attention.1 = (f32[1024,1024]{1,0:T(8,128)}, bf16[1024,1536]{1,0:T(8,128)(2,1)}, bf16[1024,512]{1,0:T(8,128)(2,1)}, f32[1024,128]{1,0:T(8,128)}, f32[4,1,128]{2,1,0:T(1,128)}) custom-call(bf16[1024,2048]{1,0:T(8,128)(2,1)} %after.36.normed.left, bf16[2048,1536]{1,0:T(8,128)(2,1)} %all-gather.6.cloned.1.call-done.weight, ...), custom_call_target="tpu_custom_call" | custom-call | tf_op jit(solution)/shard_map/attention/pallas_call | solution.py:379
  138.4 3.7 pad_maximum_fusion.1.refs_4_.refs_10_
  146.7 5.7 collective-permute-done.9.refs_1_
  153.1 4.7 collective-permute-done.10.refs_2_
  162.1 7.3 attention_out.1
  171.6 3.7 collective-permute-start.13
  175.3 3.1 collective-permute-start.17
  178.5 32.8 %experts.4 = (bf16[2,1152,2048]{2,1,0:T(8,128)(2,1)}, bf16[2,1152,2048]{2,1,0:T(8,128)(2,1)}, bf16[2,1152,2048]{2,1,0:T(8,128)(2,1)}, bf16[2,1152,1024]{2,1,0:T(...) custom-call(s32[5]{0:T(128)} %stack.125.who, ...), custom_call_target="tpu_custom_call" | custom-call | flops 28991029248 | bytes 46137344 | tf_op jit(solution)/shard_map/experts/pallas_call | solution.py:203
  220.5 3.7 collective-permute-start.16
  226.2 32.8 %experts.5 = (bf16[2,1152,2048]{2,1,0:T(8,128)(2,1)}, bf16[2,1152,2048]{2,1,0:T(8,128)(2,1)}, bf16[2,1152,2048]{2,1,0:T(8,128)(2,1)}, bf16[2,1152,1024]{2,1,0:T(...) custom-call(s32[5]{0:T(128)} %stack.129.who, ...), custom_call_target="tpu_custom_call", output_to_operand_aliasing={{0}: (14, {}), {1}: (15, {}), {2}: (16, {}), {3}: (17, {}),... | custom-call | flops 28991029248 | bytes 46137344 | tf_op jit(solution)/shard_map/experts/pallas_call | solution.py:203
  270.0 33.0 %experts.6 = (bf16[2,1152,2048]{2,1,0:T(8,128)(2,1)}, bf16[2,1152,2048]{2,1,0:T(8,128)(2,1)}, bf16[2,1152,2048]{2,1,0:T(8,128)(2,1)}, bf16[2,1152,1024]{2,1,0:T(...) custom-call(s32[5]{0:T(128)} %stack.133.who, ...), custom_call_target="tpu_custom_call", output_to_operand_aliasing={{0}: (14, {}), {1}: (15, {}), {2}: (16, {}), {3}: (17, {}),... | custom-call | flops 28991029248 | bytes 46137344 | tf_op jit(solution)/shard_map/experts/pallas_call | solution.py:203
  305.7 2.7 add_convert_fusion.3.refs_18_
  308.4 2.7 add_convert_fusion.2.refs_19_
  311.1 4.6 collective-permute-start.30
  316.7 32.6 %experts.7 = (bf16[2,1152,2048]{2,1,0:T(8,128)(2,1)}, bf16[2,1152,2048]{2,1,0:T(8,128)(2,1)}, bf16[2,1152,2048]{2,1,0:T(8,128)(2,1)}, bf16[2,1152,1024]{2,1,0:T(...) custom-call(s32[5]{0:T(128)} %stack.122.who, ...), custom_call_target="tpu_custom_call", output_to_operand_aliasing={{0}: (14, {}), {1}: (15, {}), {2}: (16, {}), {3}: (17, {}),... | custom-call | flops 28991029248 | bytes 46137344 | tf_op jit(solution)/shard_map/experts/pallas_call | solution.py:203
  349.4 20.4 %weight_grads.2 = (bf16[2,256,2048]{2,1,0:T(8,128)(2,1)}, bf16[2,256,2048]{2,1,0:T(8,128)(2,1)}, bf16[2,256,2048]{2,1,0:T(8,128)(2,1)}, bf16[2,256,2048]{2,1,0:T(8,128)(2,1)}) custom-call(s32[2,4]{1,0:T(2,128)} %pad_add_fusion.1.quarters, bf16[2,1152,1024]{2,1,0:T(8,128)(2,1)} %after.44.left, bf16[2,1152,2048]{2,1,0:T(8,128)(2,1)} %get-tuple-element.117.right), custom_call_target="tpu_custom_call" | custom-call | tf_op jit(solution)/shard_map/weight_grads/pallas_call | solution.py:499
  374.1 2.6 add_convert_fusion.1.refs_1_
  376.7 32.4 %weight_grads.3 = (bf16[2,512,2048]{2,1,0:T(8,128)(2,1)}, bf16[2,512,2048]{2,1,0:T(8,128)(2,1)}, bf16[2,512,2048]{2,1,0:T(8,128)(2,1)}, bf16[2,512,2048]{2,1,0:T(8,128)(2,1)}) custom-call(s32[2,4]{1,0:T(2,128)} %pad_add_fusion.1.quarters, bf16[2,1152,2048]{2,1,0:T(8,128)(2,1)} %after.46.left, bf16[2,1152,2048]{2,1,0:T(8,128)(2,1)} %get-tuple-element.123.right), custom_call_target="tpu_custom_call" | custom-call | flops 99999997952 | tf_op jit(solution)/shard_map/weight_grads/pallas_call | solution.py:499
  409.1 10.3 %collective-permute-done.33.refs_5_.refs_2_.refs_0_ = bf16[2,256,2048]{2,1,0:T(8,128)(2,1)} collective-permute-done((bf16[2,256,2048]{2,1,0:T(8,128)(2,1)}, bf16[2,256,2048]{2,1,0:T(8,128)(2,1)}, u32[]{:S(2)}, u32[]{:S(2)}) %collective-permute-start.33) | collective-permute-done | bytes 2097184 | tf_op jit(solution)/shard_map/ppermute | solution.py:770
  420.5 7.0 collective-permute-done.32.refs_0_
  431.0 2.7 add_convert_fusion.refs_0_
  433.6 10.4 %attention_back.1 = (f32[256,2048]{1,0:T(8,128)}, f32[1,2048]{1,0:T(1,128)S(1)}, bf16[2048,128]{1,0:T(8,128)(2,1)S(1)}, bf16[256,1024]{1,0:T(8,128)(2,1)S(1)}, b...) custom-call(s32[3]{0:T(128)S(1)} %copy-done.44, ...), custom_call_target="tpu_custom_call" | custom-call | flops 99999997952 | tf_op jit(solution)/shard_map/attention_back/pallas_call | solution.py:320
  447.6 11.3 %collective-permute-done.36 = bf16[256,1024]{1,0:T(8,128)(2,1)S(1)} collective-permute-done((bf16[256,1024]{1,0:T(8,128)(2,1)S(1)}, bf16[256,1024]{1,0:T(8,128)(2,1)S(1)}, u32[]{:S(2)}, u32[]{:S(2)}) %collective-permute-start.36) | collective-permute-done | bytes 524320 | tf_op jit(solution)/shard_map/ppermute | solution.py:770
  458.9 11.5 %collective-permute-done.37 = bf16[256,1024]{1,0:T(8,128)(2,1)S(1)} collective-permute-done((bf16[256,1024]{1,0:T(8,128)(2,1)S(1)}, bf16[256,1024]{1,0:T(8,128)(2,1)S(1)}, u32[]{:S(2)}, u32[]{:S(2)}) %collective-permute-start.37) | collective-permute-done | bytes 524320 | tf_op jit(solution)/shard_map/ppermute | solution.py:770
  482.0 14.2 %attention_grad.1 = (bf16[1024,1536]{1,0:T(8,128)(2,1)S(1)}, f32[4,2,128]{2,1,0:T(2,128)S(1)}) custom-call(bf16[1024,1024]{1,0:T(8,128)(2,1)S(1)} %copy-done.7, f32[1024,1024]{1,0:T(8,128)S(1)} %copy-done.8, bf16[1024,1536]{1,0:T(8,128)(2,1)S(1)} %copy-done.9, f32[1024,128]{1,0:T(8,128)S(1)} %copy-done.32, s32[4,1,256]{2,1,0:T(1,128)S(1)} %copy-done.41, ...), custom_call_target="tpu_custom_call" | custom-call | tf_op jit(solution)/shard_map/attention_grad/pallas_call | solution.py:447
  496.8 8.7 %product.1 = bf16[2048,1536]{1,0:T(8,128)(2,1)S(1)} custom-call(bf16[1024,2048]{1,0:T(8,128)(2,1)S(1)} %copy-done.2, bf16[1024,1536]{1,0:T(8,128)(2,1)S(1)} %get-tuple-element.135.grad.right), custom_call_target="tpu_custom_call" | custom-call | tf_op jit(solution)/shard_map/product/pallas_call | solution.py:525
  505.5 2.6 copy-done.5
  509.8 12.5 %normed_grads.1 = (bf16[256,2048]{1,0:T(8,128)(2,1)S(1)}, bf16[256,2048]{1,0:T(8,128)(2,1)}, bf16[256,2048]{1,0:T(8,128)(2,1)}, bf16[256,2048]{1,0:T(8,128)(2,1)}) custom-call(bf16[1024,1536]{1,0:T(8,128)(2,1)} %copy-done.10, bf16[2048,1536]{1,0:T(8,128)(2,1)} %all-gather.6.cloned.1.call-done.weight), custom_call_target="tpu_custom_call" | custom-call | tf_op jit(solution)/shard_map/normed_grads/pallas_call | solution.py:553
  528.4 2.9 halve.6
  540.4 25.3 %collective-permute-done.40.refs_1_.got = bf16[2,512,2048]{2,1,0:T(8,128)(2,1)} collective-permute-done((bf16[2,512,2048]{2,1,0:T(8,128)(2,1)}, bf16[2,512,2048]{2,1,0:T(8,128)(2,1)}, u32[]{:S(2)}, u32[]{:S(2)}) %collective-permute-start.40) | collective-permute-done | bytes 4194336 | tf_op jit(solution)/shard_map/ppermute | solution.py:770
  568.0 5.8 halve.5
  578.5 5.8 halve.4
  586.4 4.7 fusion.9
  592.8 21.3 %collective-permute-done.43.refs_3_ = bf16[256,2048]{1,0:T(8,128)(2,1)} collective-permute-done((bf16[256,2048]{1,0:T(8,128)(2,1)}, bf16[256,2048]{1,0:T(8,128)(2,1)}, u32[]{:S(2)}, u32[]{:S(2)}) %collective-permute-start.43) | collective-permute-done | bytes 1048608 | tf_op jit(solution)/shard_map/ppermute | solution.py:770
  614.2 6.4 input_grad.1
  633.4 22.4 %collective-permute-done.49.refs_2_.refs_0_ = bf16[1,512,2048]{2,1,0:T(8,128)(2,1)} collective-permute-done((bf16[1,512,2048]{2,1,0:T(8,128)(2,1)}, bf16[1,512,2048]{2,1,0:T(8,128)(2,1)}, u32[]{:S(2)}, u32[]{:S(2)}) %collective-permute-start.49) | collective-permute-done | bytes 2097184 | tf_op jit(solution)/shard_map/ppermute | solution.py:770
  671.9 3.4 multiply_convert_fusion
  675.3 31.6 %collective-permute-done.54.refs_2_ = bf16[256,2176]{1,0:T(8,128)(2,1)S(1)} collective-permute-done((bf16[256,2176]{1,0:T(8,128)(2,1)}, bf16[256,2176]{1,0:T(8,128)(2,1)S(1)}, u32[]{:S(2)}, u32[]{:S(2)}) %collective-permute-start.54) | collective-permute-done | bytes 1114144 | tf_op jit(solution)/shard_map/ppermute | solution.py:770
  711.7 7.6 %join.2.refs_1_ = f32[2,512,2048]{2,1,0:T(8,128)} custom-call(bf16[512,2048]{1,0:T(8,128)(2,1)} %bitcast.73, bf16[512,2048]{1,0:T(8,128)(2,1)} %bitcast.38.refs_1_, bf16[512,2048]{1,0:T(8,128)(2,1)} %bitcast.72, bf16[512,2048]{1,0:T(8,128)(2,1)} %bitcast.40.refs_3_), custom_call_target="tpu_custom_call" | custom-call | flops 99999997952 | tf_op jit(solution)/shard_map/join/pallas_call | solution.py:623
  720.3 4.4 join.3
  726.6 4.0 gather_columns.1
  (433 shorter events, 170.6 us)
Async XLA Ops:
  7.2 68.5 %all-gather.4.cloned.1.call-start = ((), (), s32[]{:S(2)}) async-start(), calls=%async_computation.3 | async-start | bytes 2949120 | tf_op jit(solution)/shard_map/all_gather | solution.py:813
  9.9 112.6 %all-gather.6.cloned.1.call-start = ((), (), s32[]{:S(2)}) async-start(), calls=%async_computation.4 | async-start | bytes 7077888 | tf_op jit(solution)/shard_map/all_gather | solution.py:813
  13.1 213.1 %all-gather.8.cloned.1.call-start = ((), (), s32[]{:S(2)}) async-start(), calls=%async_computation.5 | async-start | bytes 9437184 | tf_op jit(solution)/shard_map/all_gather | solution.py:813
  16.7 559.5 %reduce-scatter.4.cloned.1.call-start = ((), (), s32[]{:S(2)}) async-start(), calls=%async_computation.6 | async-start | bytes 9437184 | tf_op jit(solution)/shard_map/reduce_scatter | solution.py:816
  21.3 26.3 %collective-permute-start.3 = (bf16[256,2048]{1,0:T(8,128)(2,1)}, bf16[256,2048]{1,0:T(8,128)(2,1)S(1)}, u32[]{:S(2)}, u32[]{:S(2)}) collective-permute-start(bf16[256,2048]{1,0:T(8,128)(2,1)} %after.33), channel_id=1, source_target_pairs={{0,8},{8,0},{16,24},{24,16},{1,9},{9,1},{17,25},{25,17},{2,10},{10... | collective-permute-start | bytes 3145736 | tf_op jit(solution)/shard_map/ppermute | solution.py:770
  21.8 45.7 %collective-permute-start.4 = (bf16[256,2048]{1,0:T(8,128)(2,1)}, bf16[256,2048]{1,0:T(8,128)(2,1)}, u32[]{:S(2)}, u32[]{:S(2)}) collective-permute-start(bf16[256,2048]{1,0:T(8,128)(2,1)} %after.33), channel_id=1, source_target_pairs={{0,16},{8,24},{16,0},{24,8},{1,17},{9,25},{17,1},{25,9},{2,18},{10... | collective-permute-start | bytes 3145736 | tf_op jit(solution)/shard_map/ppermute | solution.py:770
  22.8 46.2 %collective-permute-start.5 = (bf16[256,2048]{1,0:T(8,128)(2,1)}, bf16[256,2048]{1,0:T(8,128)(2,1)}, u32[]{:S(2)}, u32[]{:S(2)}) collective-permute-start(bf16[256,2048]{1,0:T(8,128)(2,1)} %after.33), channel_id=1, source_target_pairs={{0,24},{8,16},{16,8},{24,0},{1,25},{9,17},{17,9},{25,1},{2,26},{10... | collective-permute-start | bytes 3145736 | tf_op jit(solution)/shard_map/ppermute | solution.py:770
  77.9 26.3 %collective-permute-start.6 = (bf16[1024,512]{1,0:T(8,128)(2,1)}, bf16[1024,512]{1,0:T(8,128)(2,1)S(1)}, u32[]{:S(2)}, u32[]{:S(2)}) collective-permute-start(bf16[1024,512]{1,0:T(8,128)(2,1)} %after.34.refs_0_), channel_id=1, source_target_pairs={{0,8},{8,0},{16,24},{24,16},{1,9},{9,1},{17,25},{25,17},{2,10},{10... | collective-permute-start | bytes 3145736 | tf_op jit(solution)/shard_map/ppermute | solution.py:770
  79.4 43.1 %collective-permute-start.7 = (bf16[1024,512]{1,0:T(8,128)(2,1)}, bf16[1024,512]{1,0:T(8,128)(2,1)}, u32[]{:S(2)}, u32[]{:S(2)}) collective-permute-start(bf16[1024,512]{1,0:T(8,128)(2,1)} %after.34.refs_0_), channel_id=1, source_target_pairs={{0,16},{8,24},{16,0},{24,8},{1,17},{9,25},{17,1},{25,9},{2,18},{10... | collective-permute-start | bytes 3145736 | tf_op jit(solution)/shard_map/ppermute | solution.py:770
  80.0 42.5 %collective-permute-start.8 = (bf16[1024,512]{1,0:T(8,128)(2,1)}, bf16[1024,512]{1,0:T(8,128)(2,1)}, u32[]{:S(2)}, u32[]{:S(2)}) collective-permute-start(bf16[1024,512]{1,0:T(8,128)(2,1)} %after.34.refs_0_), channel_id=1, source_target_pairs={{0,24},{8,16},{16,8},{24,0},{1,25},{9,17},{17,9},{25,1},{2,26},{10... | collective-permute-start | bytes 3145736 | tf_op jit(solution)/shard_map/ppermute | solution.py:770
  142.2 17.1 %collective-permute-start.12 = (bf16[4,1024,512]{2,1,0:T(8,128)(2,1)}, bf16[4,1024,512]{2,1,0:T(8,128)(2,1)}, u32[]{:S(2)}, u32[]{:S(2)}) collective-permute-start(bf16[4,1024,512]{2,1,0:T(8,128)(2,1)} %pad_maximum_fusion.1.refs_4_.refs_10_), channel_id=1, source_target_pairs={{0,1},{1,0},{2,3},{3,2},{4,5},{5,4},{6,7},{7,6},{8,9},{9,8},{10,11... | collective-permute-start | bytes 12582920 | tf_op jit(solution)/shard_map/ppermute | solution.py:788
  143.6 14.3 %collective-permute-start.10 = (bf16[256,512]{1,0:T(8,128)(2,1)}, bf16[256,512]{1,0:T(8,128)(2,1)S(1)}, u32[]{:S(2)}, u32[]{:S(2)}) collective-permute-start(bf16[256,512]{1,0:T(8,128)(2,1)} %get-tuple-element.227), channel_id=1, source_target_pairs={{0,16},{8,24},{16,0},{24,8},{1,17},{9,25},{17,1},{25,9},{2,18},{10... | collective-permute-start | bytes 786440 | tf_op jit(solution)/shard_map/ppermute | solution.py:770
  145.0 13.5 %collective-permute-start.11 = (bf16[256,512]{1,0:T(8,128)(2,1)}, bf16[256,512]{1,0:T(8,128)(2,1)S(1)}, u32[]{:S(2)}, u32[]{:S(2)}) collective-permute-start(bf16[256,512]{1,0:T(8,128)(2,1)} %get-tuple-element.226), channel_id=1, source_target_pairs={{0,24},{8,16},{16,8},{24,0},{1,25},{9,17},{17,9},{25,1},{2,26},{10... | collective-permute-start | bytes 786440 | tf_op jit(solution)/shard_map/ppermute | solution.py:770
  146.6 31.9 %collective-permute-start.15 = (bf16[256,2048]{1,0:T(8,128)(2,1)S(1)}, bf16[256,2048]{1,0:T(8,128)(2,1)}, u32[]{:S(2)}, u32[]{:S(2)}) collective-permute-start(bf16[256,2048]{1,0:T(8,128)(2,1)S(1)} %copy-done.26), channel_id=1, source_target_pairs={{0,1},{1,0},{2,3},{3,2},{4,5},{5,4},{6,7},{7,6},{8,9},{9,8},{10,11... | collective-permute-start | bytes 3145736 | tf_op jit(solution)/shard_map/ppermute | solution.py:788
  171.6 40.2 %collective-permute-start.13 = (bf16[256,2048]{1,0:T(8,128)(2,1)S(1)}, bf16[256,2048]{1,0:T(8,128)(2,1)}, u32[]{:S(2)}, u32[]{:S(2)}) collective-permute-start(bf16[256,2048]{1,0:T(8,128)(2,1)S(1)} %get-tuple-element.91.refs_0_.refs_5_), channel_id=1, source_target_pairs={{0,2},{1,3},{2,4},{3,5},{4,6},{5,7},{8,10},{9,11},{10,12},{11,13},... | collective-permute-start | bytes 3145736 | tf_op jit(solution)/shard_map/ppermute | solution.py:794
  175.3 38.2 %collective-permute-start.17 = (bf16[256,2048]{1,0:T(8,128)(2,1)S(1)}, bf16[256,2048]{1,0:T(8,128)(2,1)S(1)}, u32[]{:S(2)}, u32[]{:S(2)}) collective-permute-start(bf16[256,2048]{1,0:T(8,128)(2,1)S(1)} %get-tuple-element.91.refs_0_.refs_5_), channel_id=1, source_target_pairs={{2,0},{3,1},{4,2},{5,3},{6,4},{7,5},{10,8},{11,9},{12,10},{13,11},... | collective-permute-start | bytes 3145736 | tf_op jit(solution)/shard_map/ppermute | solution.py:794
  217.6 51.9 %collective-permute-start.22 = (bf16[256,2048]{1,0:T(8,128)(2,1)S(1)}, bf16[256,2048]{1,0:T(8,128)(2,1)}, u32[]{:S(2)}, u32[]{:S(2)}) collective-permute-start(bf16[256,2048]{1,0:T(8,128)(2,1)S(1)} %copy-done.47), channel_id=1, source_target_pairs={{0,8},{8,0},{16,24},{24,16},{1,9},{9,1},{17,25},{25,17},{2,10},{10... | collective-permute-start | bytes 3145736 | tf_op jit(solution)/shard_map/ppermute | solution.py:770
  219.1 50.9 %collective-permute-start.23 = (bf16[256,2048]{1,0:T(8,128)(2,1)S(1)}, bf16[256,2048]{1,0:T(8,128)(2,1)}, u32[]{:S(2)}, u32[]{:S(2)}) collective-permute-start(bf16[256,2048]{1,0:T(8,128)(2,1)S(1)} %copy-done.47), channel_id=1, source_target_pairs={{0,16},{8,24},{16,0},{24,8},{1,17},{9,25},{17,1},{25,9},{2,18},{10... | collective-permute-start | bytes 3145736 | tf_op jit(solution)/shard_map/ppermute | solution.py:770
  220.5 38.5 %collective-permute-start.16 = (bf16[256,2048]{1,0:T(8,128)(2,1)}, bf16[256,2048]{1,0:T(8,128)(2,1)}, u32[]{:S(2)}, u32[]{:S(2)}) collective-permute-start(bf16[256,2048]{1,0:T(8,128)(2,1)} %after.38), channel_id=1, source_target_pairs={{2,4},{3,5},{4,6},{5,7},{10,12},{11,13},{12,14},{13,15},{18,20},{1... | collective-permute-start | bytes 3145736 | tf_op jit(solution)/shard_map/ppermute | solution.py:794
  224.3 34.8 %collective-permute-start.20 = (bf16[256,2048]{1,0:T(8,128)(2,1)S(1)}, bf16[256,2048]{1,0:T(8,128)(2,1)S(1)}, u32[]{:S(2)}, u32[]{:S(2)}) collective-permute-start(bf16[256,2048]{1,0:T(8,128)(2,1)S(1)} %copy-done.59), channel_id=1, source_target_pairs={{2,0},{3,1},{4,2},{5,3},{10,8},{11,9},{12,10},{13,11},{18,16},{19,... | collective-permute-start | bytes 3145736 | tf_op jit(solution)/shard_map/ppermute | solution.py:794
  265.6 38.7 %collective-permute-start.19 = (bf16[256,2048]{1,0:T(8,128)(2,1)}, bf16[256,2048]{1,0:T(8,128)(2,1)}, u32[]{:S(2)}, u32[]{:S(2)}) collective-permute-start(bf16[256,2048]{1,0:T(8,128)(2,1)} %after.40), channel_id=1, source_target_pairs={{4,6},{5,7},{12,14},{13,15},{20,22},{21,23},{28,30},{29,31}} | collective-permute-start | bytes 3145736 | tf_op jit(solution)/shard_map/ppermute | solution.py:794
  267.2 37.0 %collective-permute-start.24 = (bf16[256,2048]{1,0:T(8,128)(2,1)S(1)}, bf16[256,2048]{1,0:T(8,128)(2,1)}, u32[]{:S(2)}, u32[]{:S(2)}) collective-permute-start(bf16[256,2048]{1,0:T(8,128)(2,1)S(1)} %copy-done.65), channel_id=1, source_target_pairs={{2,0},{3,1},{10,8},{11,9},{18,16},{19,17},{26,24},{27,25}} | collective-permute-start | bytes 3145736 | tf_op jit(solution)/shard_map/ppermute | solution.py:794
  269.5 35.2 %collective-permute-start.26 = (bf16[272,2048]{1,0:T(8,128)(2,1)}, bf16[272,2048]{1,0:T(8,128)(2,1)}, u32[]{:S(2)}, u32[]{:S(2)}) collective-permute-start(bf16[272,2048]{1,0:T(8,128)(2,1)} %get-tuple-element.111), channel_id=1, source_target_pairs={{0,1},{1,0},{2,3},{3,2},{4,5},{5,4},{6,7},{7,6},{8,9},{9,8},{10,11... | collective-permute-start | bytes 3342344 | tf_op jit(solution)/shard_map/ppermute | solution.py:788
  303.6 45.7 %collective-permute-start.28 = (bf16[256,2048]{1,0:T(8,128)(2,1)S(1)}, bf16[256,2048]{1,0:T(8,128)(2,1)}, u32[]{:S(2)}, u32[]{:S(2)}) collective-permute-start(bf16[256,2048]{1,0:T(8,128)(2,1)S(1)} %copy-done.47), channel_id=1, source_target_pairs={{0,24},{8,16},{16,8},{24,0},{1,25},{9,17},{17,9},{25,1},{2,26},{10... | collective-permute-start | bytes 3145736 | tf_op jit(solution)/shard_map/ppermute | solution.py:770
  304.5 11.3 %collective-permute-start.25 = (bf16[256,2048]{1,0:T(8,128)(2,1)S(1)}, bf16[256,2048]{1,0:T(8,128)(2,1)S(1)}, u32[]{:S(2)}, u32[]{:S(2)}) collective-permute-start(bf16[256,2048]{1,0:T(8,128)(2,1)S(1)} %select_select_fusion.refs_0_), channel_id=1, source_target_pairs={{0,1},{1,0},{2,3},{3,2},{4,5},{5,4},{6,7},{7,6},{8,9},{9,8},{10,11... | collective-permute-start | bytes 3145736 | tf_op jit(solution)/shard_map/ppermute | solution.py:788
  308.4 61.3 %collective-permute-start.29 = (bf16[272,2048]{1,0:T(8,128)(2,1)}, bf16[272,2048]{1,0:T(8,128)(2,1)S(1)}, u32[]{:S(2)}, u32[]{:S(2)}) collective-permute-start(bf16[272,2048]{1,0:T(8,128)(2,1)} %add_convert_fusion.3.refs_18_), channel_id=1, source_target_pairs={{0,2},{1,3},{2,0},{3,1},{4,6},{5,7},{6,4},{7,5},{8,10},{9,11},{10,... | collective-permute-start | bytes 3342344 | tf_op jit(solution)/shard_map/ppermute | solution.py:788
  311.1 58.6 %collective-permute-start.30 = (bf16[272,2048]{1,0:T(8,128)(2,1)}, bf16[272,2048]{1,0:T(8,128)(2,1)S(1)}, u32[]{:S(2)}, u32[]{:S(2)}) collective-permute-start(bf16[272,2048]{1,0:T(8,128)(2,1)} %add_convert_fusion.2.refs_19_), channel_id=1, source_target_pairs={{0,4},{1,5},{2,6},{3,7},{4,0},{5,1},{6,2},{7,3},{8,12},{9,13},{10,... | collective-permute-start | bytes 3342344 | tf_op jit(solution)/shard_map/ppermute | solution.py:788
  371.1 48.4 %collective-permute-start.33 = (bf16[2,256,2048]{2,1,0:T(8,128)(2,1)}, bf16[2,256,2048]{2,1,0:T(8,128)(2,1)}, u32[]{:S(2)}, u32[]{:S(2)}) collective-permute-start(bf16[2,256,2048]{2,1,0:T(8,128)(2,1)} %get-tuple-element.118.refs_1_), channel_id=1, source_target_pairs={{0,8},{8,0},{16,24},{24,16},{1,9},{9,1},{17,25},{25,17},{2,10},{10... | collective-permute-start | bytes 6291464 | tf_op jit(solution)/shard_map/ppermute | solution.py:770
  372.6 48.0 %collective-permute-start.34 = (bf16[2,256,2048]{2,1,0:T(8,128)(2,1)}, bf16[2,256,2048]{2,1,0:T(8,128)(2,1)S(1)}, u32[]{:S(2)}, u32[]{:S(2)}) collective-permute-start(bf16[2,256,2048]{2,1,0:T(8,128)(2,1)} %get-tuple-element.120.refs_3_), channel_id=1, source_target_pairs={{0,16},{8,24},{16,0},{24,8},{1,17},{9,25},{17,1},{25,9},{2,18},{10... | collective-permute-start | bytes 6291464 | tf_op jit(solution)/shard_map/ppermute | solution.py:770
  376.7 50.8 %collective-permute-start.32 = (bf16[272,2048]{1,0:T(8,128)(2,1)}, bf16[272,2048]{1,0:T(8,128)(2,1)}, u32[]{:S(2)}, u32[]{:S(2)}) collective-permute-start(bf16[272,2048]{1,0:T(8,128)(2,1)} %add_convert_fusion.1.refs_1_), channel_id=1, source_target_pairs={{0,6},{1,7},{2,4},{3,5},{4,2},{5,3},{6,0},{7,1},{8,14},{9,15},{10,... | collective-permute-start | bytes 3342344 | tf_op jit(solution)/shard_map/ppermute | solution.py:788
  427.6 239.8 %reduce-scatter.6.cloned.1.call-start = ((), (), s32[]{:S(2)}) async-start(), calls=%async_computation.7 | async-start | bytes 7077888 | tf_op jit(solution)/shard_map/reduce_scatter | solution.py:816
  444.1 14.8 %collective-permute-start.36 = (bf16[256,1024]{1,0:T(8,128)(2,1)S(1)}, bf16[256,1024]{1,0:T(8,128)(2,1)S(1)}, u32[]{:S(2)}, u32[]{:S(2)}) collective-permute-start(bf16[256,1024]{1,0:T(8,128)(2,1)S(1)} %get-tuple-element.130), channel_id=1, source_target_pairs={{0,8},{8,0},{16,24},{24,16},{1,9},{9,1},{17,25},{25,17},{2,10},{10... | collective-permute-start | bytes 1572872 | tf_op jit(solution)/shard_map/ppermute | solution.py:770
  445.6 24.8 %collective-permute-start.37 = (bf16[256,1024]{1,0:T(8,128)(2,1)S(1)}, bf16[256,1024]{1,0:T(8,128)(2,1)S(1)}, u32[]{:S(2)}, u32[]{:S(2)}) collective-permute-start(bf16[256,1024]{1,0:T(8,128)(2,1)S(1)} %get-tuple-element.131), channel_id=1, source_target_pairs={{0,16},{8,24},{16,0},{24,8},{1,17},{9,25},{17,1},{25,9},{2,18},{10... | collective-permute-start | bytes 1572872 | tf_op jit(solution)/shard_map/ppermute | solution.py:770
  447.0 23.4 %collective-permute-start.38 = (bf16[256,1024]{1,0:T(8,128)(2,1)S(1)}, bf16[256,1024]{1,0:T(8,128)(2,1)S(1)}, u32[]{:S(2)}, u32[]{:S(2)}) collective-permute-start(bf16[256,1024]{1,0:T(8,128)(2,1)S(1)} %get-tuple-element.132), channel_id=1, source_target_pairs={{0,24},{8,16},{16,8},{24,0},{1,25},{9,17},{17,9},{25,1},{2,26},{10... | collective-permute-start | bytes 1572872 | tf_op jit(solution)/shard_map/ppermute | solution.py:770
  471.9 93.8 %collective-permute-start.40 = (bf16[2,512,2048]{2,1,0:T(8,128)(2,1)}, bf16[2,512,2048]{2,1,0:T(8,128)(2,1)}, u32[]{:S(2)}, u32[]{:S(2)}) collective-permute-start(bf16[2,512,2048]{2,1,0:T(8,128)(2,1)} %after.50.refs_2_), channel_id=1, source_target_pairs={{0,16},{8,24},{16,0},{24,8},{1,17},{9,25},{17,1},{25,9},{2,18},{10... | collective-permute-start | bytes 12582920 | tf_op jit(solution)/shard_map/ppermute | solution.py:770
  475.3 100.9 %collective-permute-start.39 = (bf16[2,512,2048]{2,1,0:T(8,128)(2,1)}, bf16[2,512,2048]{2,1,0:T(8,128)(2,1)}, u32[]{:S(2)}, u32[]{:S(2)}) collective-permute-start(bf16[2,512,2048]{2,1,0:T(8,128)(2,1)} %after.49.refs_1_), channel_id=1, source_target_pairs={{0,8},{8,0},{16,24},{24,16},{1,9},{9,1},{17,25},{25,17},{2,10},{10... | collective-permute-start | bytes 12582920 | tf_op jit(solution)/shard_map/ppermute | solution.py:770
  523.3 69.5 %collective-permute-start.41 = (bf16[256,2048]{1,0:T(8,128)(2,1)}, bf16[256,2048]{1,0:T(8,128)(2,1)}, u32[]{:S(2)}, u32[]{:S(2)}) collective-permute-start(bf16[256,2048]{1,0:T(8,128)(2,1)} %get-tuple-element.142), channel_id=1, source_target_pairs={{0,8},{8,0},{16,24},{24,16},{1,9},{9,1},{17,25},{25,17},{2,10},{10... | collective-permute-start | bytes 3145736 | tf_op jit(solution)/shard_map/ppermute | solution.py:770
  524.8 68.0 %collective-permute-start.42 = (bf16[256,2048]{1,0:T(8,128)(2,1)}, bf16[256,2048]{1,0:T(8,128)(2,1)}, u32[]{:S(2)}, u32[]{:S(2)}) collective-permute-start(bf16[256,2048]{1,0:T(8,128)(2,1)} %get-tuple-element.143), channel_id=1, source_target_pairs={{0,16},{8,24},{16,0},{24,8},{1,17},{9,25},{17,1},{25,9},{2,18},{10... | collective-permute-start | bytes 3145736 | tf_op jit(solution)/shard_map/ppermute | solution.py:770
  525.4 88.8 %collective-permute-start.43 = (bf16[256,2048]{1,0:T(8,128)(2,1)}, bf16[256,2048]{1,0:T(8,128)(2,1)}, u32[]{:S(2)}, u32[]{:S(2)}) collective-permute-start(bf16[256,2048]{1,0:T(8,128)(2,1)} %get-tuple-element.144), channel_id=1, source_target_pairs={{0,24},{8,16},{16,8},{24,0},{1,25},{9,17},{17,9},{25,1},{2,26},{10... | collective-permute-start | bytes 3145736 | tf_op jit(solution)/shard_map/ppermute | solution.py:770
  540.1 127.2 %reduce-scatter.8.cloned.1.call-start = ((), (), s32[]{:S(2)}) async-start(), calls=%async_computation.8 | async-start | bytes 2949120 | tf_op jit(solution)/shard_map/reduce_scatter | solution.py:816
  575.1 80.7 %collective-permute-start.49 = (bf16[1,512,2048]{2,1,0:T(8,128)(2,1)}, bf16[1,512,2048]{2,1,0:T(8,128)(2,1)}, u32[]{:S(2)}, u32[]{:S(2)}) collective-permute-start(bf16[1,512,2048]{2,1,0:T(8,128)(2,1)} %get-tuple-element.138.refs_2_), channel_id=1, source_target_pairs={{0,8},{8,0},{16,24},{24,16},{1,9},{9,1},{17,25},{25,17},{2,10},{10... | collective-permute-start | bytes 6291464 | tf_op jit(solution)/shard_map/ppermute | solution.py:770
  585.6 70.2 %collective-permute-start.48 = (bf16[1,512,2048]{2,1,0:T(8,128)(2,1)}, bf16[1,512,2048]{2,1,0:T(8,128)(2,1)}, u32[]{:S(2)}, u32[]{:S(2)}) collective-permute-start(bf16[1,512,2048]{2,1,0:T(8,128)(2,1)} %get-tuple-element.137.refs_1_), channel_id=1, source_target_pairs={{0,16},{8,24},{16,0},{24,8},{1,17},{9,25},{17,1},{25,9},{2,18},{10... | collective-permute-start | bytes 6291464 | tf_op jit(solution)/shard_map/ppermute | solution.py:770
  660.5 58.8 %collective-permute-start.57 = (bf16[1,256,2048]{2,1,0:T(8,128)(2,1)}, bf16[1,256,2048]{2,1,0:T(8,128)(2,1)S(1)}, u32[]{:S(2)}, u32[]{:S(2)}) collective-permute-start(bf16[1,256,2048]{2,1,0:T(8,128)(2,1)} %after.62), channel_id=1, source_target_pairs={{0,16},{8,24},{16,0},{24,8},{1,17},{9,25},{17,1},{25,9},{2,18},{10... | collective-permute-start | bytes 3145736 | tf_op jit(solution)/shard_map/ppermute | solution.py:770
  662.0 58.3 %collective-permute-start.58 = (bf16[1,256,2048]{2,1,0:T(8,128)(2,1)}, bf16[1,256,2048]{2,1,0:T(8,128)(2,1)}, u32[]{:S(2)}, u32[]{:S(2)}) collective-permute-start(bf16[1,256,2048]{2,1,0:T(8,128)(2,1)} %after.64), channel_id=1, source_target_pairs={{0,8},{8,0},{16,24},{24,16},{1,9},{9,1},{17,25},{25,17},{2,10},{10... | collective-permute-start | bytes 3145736 | tf_op jit(solution)/shard_map/ppermute | solution.py:770
  669.6 39.5 %collective-permute-start.53 = (bf16[256,2176]{1,0:T(8,128)(2,1)}, bf16[256,2176]{1,0:T(8,128)(2,1)S(1)}, u32[]{:S(2)}, u32[]{:S(2)}) collective-permute-start(bf16[256,2176]{1,0:T(8,128)(2,1)} %after.58.refs_0_), channel_id=1, source_target_pairs={{0,8},{8,0},{16,24},{24,16},{1,9},{9,1},{17,25},{25,17},{2,10},{10... | collective-permute-start | bytes 3342344 | tf_op jit(solution)/shard_map/ppermute | solution.py:770
  670.2 36.7 %collective-permute-start.54 = (bf16[256,2176]{1,0:T(8,128)(2,1)}, bf16[256,2176]{1,0:T(8,128)(2,1)S(1)}, u32[]{:S(2)}, u32[]{:S(2)}) collective-permute-start(bf16[256,2176]{1,0:T(8,128)(2,1)} %after.58.refs_0_), channel_id=1, source_target_pairs={{0,16},{8,24},{16,0},{24,8},{1,17},{9,25},{17,1},{25,9},{2,18},{10... | collective-permute-start | bytes 3342344 | tf_op jit(solution)/shard_map/ppermute | solution.py:770
  707.8 16.9 %collective-permute-start.56 = (bf16[128,2176]{1,0:T(8,128)(2,1)}, bf16[128,2176]{1,0:T(8,128)(2,1)}, u32[]{:S(2)}, u32[]{:S(2)}) collective-permute-start(bf16[128,2176]{1,0:T(8,128)(2,1)} %slice.90), channel_id=1, source_target_pairs={{0,8},{8,0},{16,24},{24,16},{1,9},{9,1},{17,25},{25,17},{2,10},{10... | collective-permute-start | bytes 1671176 | tf_op jit(solution)/shard_map/ppermute | solution.py:770
  710.1 14.6 %collective-permute-start.55 = (bf16[128,2176]{1,0:T(8,128)(2,1)}, bf16[128,2176]{1,0:T(8,128)(2,1)}, u32[]{:S(2)}, u32[]{:S(2)}) collective-permute-start(bf16[128,2176]{1,0:T(8,128)(2,1)} %slice.89), channel_id=1, source_target_pairs={{0,16},{8,24},{16,0},{24,8},{1,17},{9,25},{17,1},{25,9},{2,18},{10... | collective-permute-start | bytes 1671176 | tf_op jit(solution)/shard_map/ppermute | solution.py:770
  (109 other events, 552.4 us)
Sparse Core Ops, SparseCore 0:
  10.2 34.3 all-gather.3
  46.9 62.2 all-gather.5
  110.7 92.8 all-gather.7
  427.7 85.7 reduce-scatter.3
  539.3 65.3 reduce-scatter.5
  607.4 35.3 reduce-scatter.7
